TPU v7x, 32 devices: a whole 2x2x4 slice. The times are simulated.
32 devices in a mesh: gz: 4 (over z), gx: 4 (over y, core), gy: 2 (over x).
Axes of the slice: x: 2, y: 2, z: 4, core: 2. Of those that a mesh axis runs over, the one named last changes fastest.
Arguments:
- right_side: float32 [40, 32, 6, 1024], P('gz', 'gy', None, 'gx'), may hold values from -0.0625 to 0.0625
- previous: float32 [40, 32, 6, 1024], P('gz', 'gy', None, 'gx'), may hold values from -0.15625 to 0.15625
- diag_inverse: bfloat16 [40, 32, 6, 6, 1024], P('gz', 'gy', None, None, 'gx'), may hold values from -0.6 to 2.6, as said below
- jacobians: bfloat16 [40, 32, 6, 6, 6, 1024], P('gz', 'gy', None, None, None, 'gx'), may hold values from -3 to 3, as said below
Outputs:
- update: float32 [40, 32, 6, 1024], P('gz', 'gy', None, 'gx')
Inputs may be any that keep to these rules, and one draw needn't show every extreme that they name: `diag_inverse`: entries of the cells' inverted diagonal blocks. `jacobians`: entries of the cells' coupling blocks.
All inputs are finite; a program needn't handle non-finite values.
Results may differ from a plain program's by a relative error of at most 0.0003.
Values sent between devices are 32-bit elements; how exact they have to be, the bound alone decides.
No kernel may reach another device: no remote copies, remote signals or barrier semaphores. Data moves between devices by JAX's collectives and lax.ppermute only.
A program may use at most 128 MiB of HBM per device.

v0:
```python
import jax
import jax.numpy as jnp
from jax import lax
from jax.sharding import PartitionSpec as P


def extended(x, sides, width):
    for axis, dim in sides:
        devices, length = (lax.axis_size(axis), x.shape[dim])
        up = [(i, (i + 1) % devices) for i in range(devices - 1)]
        down = [(j, i) for i, j in up]
        last = lax.slice_in_dim(x, length - width, length, axis=dim)
        initial = lax.slice_in_dim(x, 0, width, axis=dim)
        before = lax.ppermute(last, axis, up)
        after = lax.ppermute(initial, axis, down)
        x = jnp.concatenate([before, x, after], axis=dim)
    return x


def shifted(x, axis, by):
    devices = lax.axis_size(axis)
    pairs = [(i, i + by) for i in range(devices) if 0 <= i + by < devices]
    return lax.ppermute(x, axis, pairs)


def block_apply(blocks, vector):
    return jnp.sum(blocks * vector[..., None, :, :], axis=-2)


def slab_inplane(jacobians, padded):
    total = block_apply(jacobians[:, :, 0].astype(jnp.float32), padded[:, 1:-1, :, :-2])
    total = total + block_apply(jacobians[:, :, 1].astype(jnp.float32), padded[:, 1:-1, :, 2:])
    total = total + block_apply(jacobians[:, :, 2].astype(jnp.float32), padded[:, :-2, :, 1:-1])
    total = total + block_apply(jacobians[:, :, 3].astype(jnp.float32), padded[:, 2:, :, 1:-1])
    return total


def body(right_side, previous, diag_inverse, jacobians):
    planes_y = right_side.shape[1]
    planes_x = right_side.shape[3]
    zeros_plane = jnp.zeros((planes_y, 6, planes_x), jnp.float32)
    inverse_all = diag_inverse.astype(jnp.float32)
    lower_all = jacobians[:, :, 4].astype(jnp.float32)
    upper_all = jacobians[:, :, 5].astype(jnp.float32)
    padded_old = extended(previous, (("gx", 3), ("gy", 1)), 1)
    source_all = right_side - slab_inplane(jacobians, padded_old)

    def forward_sweep(incoming):

        def forward_step(earlier, planes):
            source, inverse, lower = planes
            result = block_apply(inverse, source - block_apply(lower, earlier))
            return (result, result)

        return lax.scan(forward_step, incoming, (source_all, inverse_all, lower_all), unroll=True)

    incoming = zeros_plane
    for handoff_step in range(lax.axis_size("gz") - 1):
        final_plane, sweep_values = forward_sweep(incoming)
        incoming = shifted(final_plane, "gz", 1)
    final_plane, sweep_values = forward_sweep(incoming)
    padded_new = extended(sweep_values - previous, (("gx", 3), ("gy", 1)), 1)
    inner_all = slab_inplane(jacobians, padded_new)

    def backward_sweep(incoming):

        def backward_step(later, planes):
            forward_plane, inner, inverse, upper = planes
            change = block_apply(upper, later) + inner
            result = forward_plane - block_apply(inverse, change)
            return (result, result)

        return lax.scan(
            backward_step,
            incoming,
            (sweep_values, inner_all, inverse_all, upper_all),
            reverse=True,
            unroll=True,
        )

    incoming = zeros_plane
    for handoff_step in range(lax.axis_size("gz") - 1):
        bottom_plane, update = backward_sweep(incoming)
        incoming = shifted(bottom_plane, "gz", -1)
    bottom_plane, update = backward_sweep(incoming)
    return update


def solution(mesh):
    placed = (
        P("gz", "gy", None, "gx"),
        P("gz", "gy", None, "gx"),
        P("gz", "gy", None, None, "gx"),
        P("gz", "gy", None, None, None, "gx"),
    )
    return jax.shard_map(
        body, mesh=mesh, in_specs=placed, out_specs=P("gz", "gy", None, "gx"), check_vma=False
    )
```

profile of v0, /device:TPU:14, one launch (start us, length us, event | category | flops | bytes accessed | tf_op | source)
XLA Modules:
  0.0 130.5 jit_solution(1309203401651174341)
XLA Ops:
  0.0 1.4 %fusion.99 = (f32[10,16,6,1]{3,1,2,0:T(8,128)S(1)}, f32[10,16,6,1]{3,1,2,0:T(8,128)S(1)}) fusion(f32[10,16,6,256]{3,1,2,0:T(8,128)} %param.5), kind=kLoop, calls=%fused_computation.363 | loop fusion | bytes 15360 | tf_op jit(solution)/shard_map/slice | solution.py:12
  1.9 1.9 %collective-permute-start.1 = (f32[10,16,6,1]{1,2,3,0:T(8,128)S(1)}, f32[10,16,6,1]{1,2,3,0:T(8,128)S(1)}, u32[]{:S(2)}, u32[]{:S(2)}) collective-permute-start(f32[10,16,6,1]{1,2,3,0:T(8,128)S(1)} %copy.22), channel_id=1, source_target_pairs={{2,0},{4,2},{6,4},{3,1},{5,3},{7,5},{10,8},{12,10},{14,12},{11,9},... | collective-permute-start | bytes 11528 | tf_op jit(solution)/shard_map/ppermute | solution.py:15
  4.4 2.7 %collective-permute-start = (f32[10,16,6,1]{1,2,3,0:T(8,128)S(1)}, f32[10,16,6,1]{1,2,3,0:T(8,128)S(1)}, u32[]{:S(2)}, u32[]{:S(2)}) collective-permute-start(f32[10,16,6,1]{1,2,3,0:T(8,128)S(1)} %copy.21), channel_id=1, source_target_pairs={{0,2},{2,4},{4,6},{1,3},{3,5},{5,7},{8,10},{10,12},{12,14},{9,11},... | collective-permute-start | bytes 11528 | tf_op jit(solution)/shard_map/ppermute | solution.py:14
  7.0 6.3 %slice_convert_fusion.1 = (f32[10,16,1,6,6,256]{5,1,4,3,2,0:T(8,128)S(1)}, f32[10,16,1,6,6,256]{5,1,4,3,2,0:T(8,128)}) fusion(bf16[10,16,6,6,6,256]{5,1,4,3,2,0:T(8,128)(2,1)} %param.7), kind=kLoop, calls=%fused_computation.17 | loop fusion | flops 2949120 | bytes 17694720 | tf_op jit(solution)/shard_map/convert_element_type | solution.py:43
  14.1 3.6 %convert_element_type.39 = f32[10,16,6,6,256]{4,1,3,2,0:T(8,128)} convert(bf16[10,16,6,6,256]{4,1,3,2,0:T(8,128)(2,1)S(1)} %copy-done.2) | non-fusion elementwise | flops 1474560 | bytes 8847360 | tf_op jit(solution)/shard_map/convert_element_type | solution.py:42
  18.3 1.4 %copy.16 = f32[10,16,6,1]{3,2,1,0:T(8,128)} copy(f32[10,16,6,1]{1,2,3,0:T(8,128)S(1)} %collective-permute-done) | data formatting | bytes 7680 | tf_op jit(solution)/shard_map/ppermute | solution.py:14
  19.6 1.6 %pad_maximum_fusion.18 = (f32[10,1,6,258]{3,2,1,0:T(8,128)}, f32[10,1,6,258]{3,2,1,0:T(8,128)}) fusion(f32[10,16,6,1]{3,2,1,0:T(8,128)S(1)} %copy.18, f32[10,16,6,256]{3,2,1,0:T(8,128)S(1)} %copy.17, f32[10,16,6,1]{3,2,1,0:T(8,128)} %copy.16), kind=kLoop, calls=%fused_computation.228 | loop fusion | flops 61920 | bytes 1114560 | tf_op jit(solution)/shard_map/slice | solution.py:12
  22.6 5.8 %collective-permute-start.3 = (f32[10,1,6,258]{3,2,1,0:T(8,128)}, f32[10,1,6,258]{3,2,1,0:T(8,128)}, u32[]{:S(2)}, u32[]{:S(2)}) collective-permute-start(f32[10,1,6,258]{3,2,1,0:T(8,128)} %get-tuple-element.18), channel_id=1, source_target_pairs={{1,0},{3,2},{5,4},{7,6},{9,8},{11,10},{13,12},{15,14},{17,16},{19,... | collective-permute-start | bytes 185768 | tf_op jit(solution)/shard_map/ppermute | solution.py:15
  29.6 2.0 %copy.15 = f32[10,16,6,1]{3,1,2,0:T(8,128)} copy(f32[10,16,6,1]{1,2,3,0:T(8,128)} %copy-done.4) | data formatting | bytes 7680 | tf_op jit(solution)/shard_map/ppermute | solution.py:15
  31.6 1.7 %pad_maximum_fusion.15 = (f32[10,16,6,256]{3,1,2,0:T(8,128)S(1)}, f32[10,16,6,256]{3,1,2,0:T(8,128)S(1)}) fusion(f32[10,16,6,256]{3,1,2,0:T(8,128)S(1)} %copy-done.1, f32[10,16,6,1]{3,1,2,0:T(8,128)S(1)} %copy.13, f32[10,16,6,1]{3,1,2,0:T(8,128)} %copy.15), kind=kLoop, calls=%fused_computation.33 | loop fusion | flops 491520 | bytes 2956800 | tf_op jit(solution)/shard_map/concatenate | solution.py:16
  33.3 1.9 %pad_maximum_fusion.3 = (f32[10,16,6,256]{3,2,1,0:T(8,128)S(1)}, f32[10,16,6,256]{3,2,1,0:T(8,128)S(1)}) fusion(f32[10,1,6,258]{3,2,1,0:T(8,128)} %collective-permute-done.2, f32[10,16,6,1]{3,2,1,0:T(8,128)S(1)} %copy.18, f32[10,16,6,256]{3,2,1,0:T(8,128)S(1)} %copy.17, f32[10,16,6,1]{3,2,1,0:T(8,128)} %copy.16, f32[10,1,6,258]{3,2,1,0:T(8,128)} %collective-permute-done.3), kind=kLoop, calls=%fused_computation.21 | loop fusion | flops 1474560 | bytes 3080640 | tf_op jit(solution)/shard_map/concatenate | solution.py:16
  35.9 7.6 %fusion.2 = (f32[10,16,6,256]{3,1,2,0:T(8,128)S(1)}, f32[10,16,6,256]{3,1,2,0:T(8,128)S(1)}, f32[10,16,6,256]{3,1,2,0:T(8,128)S(1)}, f32[10,16,6,256]{3,1,2,0:T(8,128)S(1)}) fusion(f32[10,16,6,256]{3,1,2,0:T(8,128)S(1)} %get-tuple-element.28, bf16[10,16,6,6,6,256]{5,1,4,3,2,0:T(8,128)(2,1)} %param.7, f32[10,16,6,256]{3,1,2,0:T(8,128)S(1)} %copy.20, ...), kind=kLoop, calls=%fused_computation.10 | loop fusion | flops 16711680 | bytes 19660800 | tf_op jit(solution)/shard_map/reduce_sum | solution.py:27
  45.6 3.7 %collective-permute-start.4 = (f32[16,6,256]{2,0,1:T(8,128)S(1)}, f32[16,6,256]{2,0,1:T(8,128)S(1)}, u32[]{:S(2)}, u32[]{:S(2)}) collective-permute-start(f32[16,6,256]{2,0,1:T(8,128)S(1)} %multiply_reduce_fusion.140), channel_id=1, source_target_pairs={{0,8},{8,16},{16,24},{1,9},{9,17},{17,25},{2,10},{10,18},{18,26},{... | collective-permute-start | bytes 294920 | tf_op jit(solution)/shard_map/ppermute | solution.py:23
  49.3 2.8 %collective-permute-done.4 = f32[16,6,256]{2,0,1:T(8,128)S(1)} collective-permute-done((f32[16,6,256]{2,0,1:T(8,128)S(1)}, f32[16,6,256]{2,0,1:T(8,128)S(1)}, u32[]{:S(2)}, u32[]{:S(2)}) %collective-permute-start.4) | collective-permute-done | bytes 98336 | tf_op jit(solution)/shard_map/ppermute | solution.py:23
  53.8 3.5 %collective-permute-start.5 = (f32[16,6,256]{2,0,1:T(8,128)S(1)}, f32[16,6,256]{2,0,1:T(8,128)S(1)}, u32[]{:S(2)}, u32[]{:S(2)}) collective-permute-start(f32[16,6,256]{2,0,1:T(8,128)S(1)} %multiply_reduce_fusion.120), channel_id=1, source_target_pairs={{0,8},{8,16},{16,24},{1,9},{9,17},{17,25},{2,10},{10,18},{18,26},{... | collective-permute-start | bytes 294920 | tf_op jit(solution)/shard_map/ppermute | solution.py:23
  57.3 3.0 %collective-permute-done.5 = f32[16,6,256]{2,0,1:T(8,128)S(1)} collective-permute-done((f32[16,6,256]{2,0,1:T(8,128)S(1)}, f32[16,6,256]{2,0,1:T(8,128)S(1)}, u32[]{:S(2)}, u32[]{:S(2)}) %collective-permute-start.5) | collective-permute-done | bytes 98336 | tf_op jit(solution)/shard_map/ppermute | solution.py:23
  61.9 3.5 %collective-permute-start.6 = (f32[16,6,256]{2,0,1:T(8,128)S(1)}, f32[16,6,256]{2,0,1:T(8,128)S(1)}, u32[]{:S(2)}, u32[]{:S(2)}) collective-permute-start(f32[16,6,256]{2,0,1:T(8,128)S(1)} %multiply_reduce_fusion.100), channel_id=1, source_target_pairs={{0,8},{8,16},{16,24},{1,9},{9,17},{17,25},{2,10},{10,18},{18,26},{... | collective-permute-start | bytes 294920 | tf_op jit(solution)/shard_map/ppermute | solution.py:23
  65.4 3.0 %collective-permute-done.6 = f32[16,6,256]{2,0,1:T(8,128)S(1)} collective-permute-done((f32[16,6,256]{2,0,1:T(8,128)S(1)}, f32[16,6,256]{2,0,1:T(8,128)S(1)}, u32[]{:S(2)}, u32[]{:S(2)}) %collective-permute-start.6) | collective-permute-done | bytes 98336 | tf_op jit(solution)/shard_map/ppermute | solution.py:23
  72.2 1.9 %collective-permute-start.7 = (f32[10,16,6,1]{3,1,2,0:T(8,128)S(1)}, f32[10,16,6,1]{3,1,2,0:T(8,128)S(1)}, u32[]{:S(2)}, u32[]{:S(2)}) collective-permute-start(f32[10,16,6,1]{3,1,2,0:T(8,128)S(1)} %get-tuple-element.25), channel_id=1, source_target_pairs={{0,2},{2,4},{4,6},{1,3},{3,5},{5,7},{8,10},{10,12},{12,14},{9,11},... | collective-permute-start | bytes 11528 | tf_op jit(solution)/shard_map/ppermute | solution.py:14
  74.1 3.6 %collective-permute-start.8 = (f32[10,16,6,1]{3,1,2,0:T(8,128)S(1)}, f32[10,16,6,1]{3,1,2,0:T(8,128)S(1)}, u32[]{:S(2)}, u32[]{:S(2)}) collective-permute-start(f32[10,16,6,1]{3,1,2,0:T(8,128)S(1)} %get-tuple-element.26), channel_id=1, source_target_pairs={{2,0},{4,2},{6,4},{3,1},{5,3},{7,5},{10,8},{12,10},{14,12},{11,9},... | collective-permute-start | bytes 11528 | tf_op jit(solution)/shard_map/ppermute | solution.py:15
  77.8 4.6 %collective-permute-done.7 = f32[10,16,6,1]{3,1,2,0:T(8,128)S(1)} collective-permute-done((f32[10,16,6,1]{3,1,2,0:T(8,128)S(1)}, f32[10,16,6,1]{3,1,2,0:T(8,128)S(1)}, u32[]{:S(2)}, u32[]{:S(2)}) %collective-permute-start.7) | collective-permute-done | bytes 3872 | tf_op jit(solution)/shard_map/ppermute | solution.py:14
  82.4 1.8 %collective-permute-done.8 = f32[10,16,6,1]{3,1,2,0:T(8,128)S(1)} collective-permute-done((f32[10,16,6,1]{3,1,2,0:T(8,128)S(1)}, f32[10,16,6,1]{3,1,2,0:T(8,128)S(1)}, u32[]{:S(2)}, u32[]{:S(2)}) %collective-permute-start.8) | collective-permute-done | bytes 3872 | tf_op jit(solution)/shard_map/ppermute | solution.py:15
  84.7 1.5 %collective-permute-start.10 = (f32[10,1,6,258]{3,1,2,0:T(1,128)S(1)}, f32[10,1,6,258]{3,1,2,0:T(1,128)S(1)}, u32[]{:S(2)}, u32[]{:S(2)}) collective-permute-start(f32[10,1,6,258]{3,1,2,0:T(1,128)S(1)} %get-tuple-element.21), channel_id=1, source_target_pairs={{1,0},{3,2},{5,4},{7,6},{9,8},{11,10},{13,12},{15,14},{17,16},{19,... | collective-permute-start | bytes 185768 | tf_op jit(solution)/shard_map/ppermute | solution.py:15
  86.2 1.5 %collective-permute-start.9 = (f32[10,1,6,258]{3,1,2,0:T(1,128)S(1)}, f32[10,1,6,258]{3,1,2,0:T(1,128)S(1)}, u32[]{:S(2)}, u32[]{:S(2)}) collective-permute-start(f32[10,1,6,258]{3,1,2,0:T(1,128)S(1)} %get-tuple-element.22), channel_id=1, source_target_pairs={{0,1},{2,3},{4,5},{6,7},{8,9},{10,11},{12,13},{14,15},{16,17},{18,... | collective-permute-start | bytes 185768 | tf_op jit(solution)/shard_map/ppermute | solution.py:14
  88.4 4.3 %collective-permute-done.9 = f32[10,1,6,258]{3,1,2,0:T(1,128)S(1)} collective-permute-done((f32[10,1,6,258]{3,1,2,0:T(1,128)S(1)}, f32[10,1,6,258]{3,1,2,0:T(1,128)S(1)}, u32[]{:S(2)}, u32[]{:S(2)}) %collective-permute-start.9) | collective-permute-done | bytes 61952 | tf_op jit(solution)/shard_map/ppermute | solution.py:14
  93.9 7.4 %fusion.3 = (f32[10,16,6,256]{3,1,2,0:T(8,128)S(1)}, f32[10,16,6,256]{3,1,2,0:T(8,128)S(1)}, f32[10,16,6,256]{3,1,2,0:T(8,128)S(1)}, f32[10,16,6,256]{3,1,2,0:T(8,128)S(1)}) fusion(f32[10,16,6,256]{3,1,2,0:T(8,128)S(1)} %get-tuple-element.24, bf16[10,16,6,6,6,256]{5,1,4,3,2,0:T(8,128)(2,1)} %param.7, f32[10,16,6,256]{3,1,2,0:T(8,128)S(1)} %get-tuple-element.23, ...), kind=kLoop, calls=%fused_computation.11 | loop fusion | flops 16711680 | bytes 19660800 | tf_op jit(solution)/shard_map/reduce_sum | solution.py:27
  103.6 1.9 %collective-permute-start.11 = (f32[16,6,256]{2,0,1:T(8,128)S(1)}, f32[16,6,256]{2,0,1:T(8,128)S(1)}, u32[]{:S(2)}, u32[]{:S(2)}) collective-permute-start(f32[16,6,256]{2,0,1:T(8,128)S(1)} %sub.689), channel_id=1, source_target_pairs={{8,0},{16,8},{24,16},{9,1},{17,9},{25,17},{10,2},{18,10},{26,18},{... | collective-permute-start | bytes 294920 | tf_op jit(solution)/shard_map/ppermute | solution.py:23
  105.5 4.6 %collective-permute-done.11 = f32[16,6,256]{2,0,1:T(8,128)S(1)} collective-permute-done((f32[16,6,256]{2,0,1:T(8,128)S(1)}, f32[16,6,256]{2,0,1:T(8,128)S(1)}, u32[]{:S(2)}, u32[]{:S(2)}) %collective-permute-start.11) | collective-permute-done | bytes 98336 | tf_op jit(solution)/shard_map/ppermute | solution.py:23
  112.0 2.0 %collective-permute-start.12 = (f32[16,6,256]{2,0,1:T(8,128)S(1)}, f32[16,6,256]{2,0,1:T(8,128)S(1)}, u32[]{:S(2)}, u32[]{:S(2)}) collective-permute-start(f32[16,6,256]{2,0,1:T(8,128)S(1)} %sub.699), channel_id=1, source_target_pairs={{8,0},{16,8},{24,16},{9,1},{17,9},{25,17},{10,2},{18,10},{26,18},{... | collective-permute-start | bytes 294920 | tf_op jit(solution)/shard_map/ppermute | solution.py:23
  114.0 4.5 %collective-permute-done.12 = f32[16,6,256]{2,0,1:T(8,128)S(1)} collective-permute-done((f32[16,6,256]{2,0,1:T(8,128)S(1)}, f32[16,6,256]{2,0,1:T(8,128)S(1)}, u32[]{:S(2)}, u32[]{:S(2)}) %collective-permute-start.12) | collective-permute-done | bytes 98336 | tf_op jit(solution)/shard_map/ppermute | solution.py:23
  120.3 2.0 %collective-permute-start.13 = (f32[16,6,256]{2,0,1:T(8,128)S(1)}, f32[16,6,256]{2,0,1:T(8,128)S(1)}, u32[]{:S(2)}, u32[]{:S(2)}) collective-permute-start(f32[16,6,256]{2,0,1:T(8,128)S(1)} %sub.709), channel_id=1, source_target_pairs={{8,0},{16,8},{24,16},{9,1},{17,9},{25,17},{10,2},{18,10},{26,18},{... | collective-permute-start | bytes 294920 | tf_op jit(solution)/shard_map/ppermute | solution.py:23
  122.4 4.5 %collective-permute-done.13 = f32[16,6,256]{2,0,1:T(8,128)S(1)} collective-permute-done((f32[16,6,256]{2,0,1:T(8,128)S(1)}, f32[16,6,256]{2,0,1:T(8,128)S(1)}, u32[]{:S(2)}, u32[]{:S(2)}) %collective-permute-start.13) | collective-permute-done | bytes 98336 | tf_op jit(solution)/shard_map/ppermute | solution.py:23
  (346 shorter events, 24.3 us)
Async XLA Ops:
  1.9 15.8 %collective-permute-start.1 = (f32[10,16,6,1]{1,2,3,0:T(8,128)S(1)}, f32[10,16,6,1]{1,2,3,0:T(8,128)S(1)}, u32[]{:S(2)}, u32[]{:S(2)}) collective-permute-start(f32[10,16,6,1]{1,2,3,0:T(8,128)S(1)} %copy.22), channel_id=1, source_target_pairs={{2,0},{4,2},{6,4},{3,1},{5,3},{7,5},{10,8},{12,10},{14,12},{11,9},... | collective-permute-start | bytes 11528 | tf_op jit(solution)/shard_map/ppermute | solution.py:15
  4.4 9.1 %copy-start.1 = (f32[10,16,6,256]{3,1,2,0:T(8,128)S(1)}, f32[10,16,6,256]{3,1,2,0:T(8,128)}, u32[]{:S(2)}) copy-start(f32[10,16,6,256]{3,1,2,0:T(8,128)} %param.5) | copy-start | bytes 2949124
  4.4 9.7 %copy-start.2 = (bf16[10,16,6,6,256]{4,1,3,2,0:T(8,128)(2,1)S(1)}, bf16[10,16,6,6,256]{4,1,3,2,0:T(8,128)(2,1)}, u32[]{:S(2)}) copy-start(bf16[10,16,6,6,256]{4,1,3,2,0:T(8,128)(2,1)} %param.6) | copy-start | bytes 8847364
  4.4 13.9 %collective-permute-start = (f32[10,16,6,1]{1,2,3,0:T(8,128)S(1)}, f32[10,16,6,1]{1,2,3,0:T(8,128)S(1)}, u32[]{:S(2)}, u32[]{:S(2)}) collective-permute-start(f32[10,16,6,1]{1,2,3,0:T(8,128)S(1)} %copy.21), channel_id=1, source_target_pairs={{0,2},{2,4},{4,6},{1,3},{3,5},{5,7},{8,10},{10,12},{12,14},{9,11},... | collective-permute-start | bytes 11528 | tf_op jit(solution)/shard_map/ppermute | solution.py:14
  13.4 4.3 %copy-start = (f32[10,16,1,6,6,256]{5,1,4,3,2,0:T(8,128)}, f32[10,16,1,6,6,256]{5,1,4,3,2,0:T(8,128)S(1)}, u32[]{:S(2)}) copy-start(f32[10,16,1,6,6,256]{5,1,4,3,2,0:T(8,128)S(1)} %get-tuple-element.13) | copy-start | bytes 17694724
  17.7 4.9 %copy-start.4 = (f32[10,16,6,1]{1,2,3,0:T(8,128)}, f32[10,16,6,1]{1,2,3,0:T(8,128)S(1)}, u32[]{:S(2)}) copy-start(f32[10,16,6,1]{1,2,3,0:T(8,128)S(1)} %collective-permute-done.1) | copy-start | bytes 11524
  18.2 4.3 %copy-start.5 = (f32[10,16,6,1]{1,2,3,0:T(8,128)}, f32[10,16,6,1]{1,2,3,0:T(8,128)S(1)}, u32[]{:S(2)}) copy-start(f32[10,16,6,1]{1,2,3,0:T(8,128)S(1)} %collective-permute-done) | copy-start | bytes 11524
  21.3 12.0 %collective-permute-start.2 = (f32[10,1,6,258]{3,2,1,0:T(8,128)}, f32[10,1,6,258]{3,2,1,0:T(8,128)}, u32[]{:S(2)}, u32[]{:S(2)}) collective-permute-start(f32[10,1,6,258]{3,2,1,0:T(8,128)} %get-tuple-element.17), channel_id=1, source_target_pairs={{0,1},{2,3},{4,5},{6,7},{8,9},{10,11},{12,13},{14,15},{16,17},{18,... | collective-permute-start | bytes 185768 | tf_op jit(solution)/shard_map/ppermute | solution.py:14
  22.6 10.7 %collective-permute-start.3 = (f32[10,1,6,258]{3,2,1,0:T(8,128)}, f32[10,1,6,258]{3,2,1,0:T(8,128)}, u32[]{:S(2)}, u32[]{:S(2)}) collective-permute-start(f32[10,1,6,258]{3,2,1,0:T(8,128)} %get-tuple-element.18), channel_id=1, source_target_pairs={{1,0},{3,2},{5,4},{7,6},{9,8},{11,10},{13,12},{15,14},{17,16},{19,... | collective-permute-start | bytes 185768 | tf_op jit(solution)/shard_map/ppermute | solution.py:15
  35.8 8.3 %slice-start = ((s8[5898240]{0:T(1024)(128)(4,1)}), s8[4194304]{0:T(1024)(128)(4,1)S(1)}, s32[]{:S(2)}) async-start(s8[5898240]{0:T(1024)(128)(4,1)} %bitcast.666), calls=%async_computation | async-start | bytes 8388608
  35.8 8.3 %slice-start.4 = ((s8[5898240]{0:T(1024)(128)(4,1)}), s8[4194304]{0:T(1024)(128)(4,1)S(1)}, s32[]{:S(2)}) async-start(s8[5898240]{0:T(1024)(128)(4,1)} %bitcast.670), calls=%async_computation.4 | async-start | bytes 8388608
  35.8 7.6 %copy-start.3 = (f32[10,16,6,256]{3,1,2,0:T(8,128)S(1)}, f32[10,16,6,256]{3,1,2,0:T(8,128)}, u32[]{:S(2)}) copy-start(f32[10,16,6,256]{3,1,2,0:T(8,128)} %param.4) | copy-start | bytes 2949124
  35.8 8.2 %slice-start.1 = ((s8[5898240]{0:T(1024)(128)(4,1)}), s8[1703936]{0:T(1024)(128)(4,1)S(1)}, s32[]{:S(2)}) async-start(s8[5898240]{0:T(1024)(128)(4,1)} %bitcast.666), calls=%async_computation.1 | async-start | bytes 3407872
  35.8 8.3 %slice-start.5 = ((s8[5898240]{0:T(1024)(128)(4,1)}), s8[1703936]{0:T(1024)(128)(4,1)S(1)}, s32[]{:S(2)}) async-start(s8[5898240]{0:T(1024)(128)(4,1)} %bitcast.670), calls=%async_computation.5 | async-start | bytes 3407872
  45.6 6.5 %collective-permute-start.4 = (f32[16,6,256]{2,0,1:T(8,128)S(1)}, f32[16,6,256]{2,0,1:T(8,128)S(1)}, u32[]{:S(2)}, u32[]{:S(2)}) collective-permute-start(f32[16,6,256]{2,0,1:T(8,128)S(1)} %multiply_reduce_fusion.140), channel_id=1, source_target_pairs={{0,8},{8,16},{16,24},{1,9},{9,17},{17,25},{2,10},{10,18},{18,26},{... | collective-permute-start | bytes 294920 | tf_op jit(solution)/shard_map/ppermute | solution.py:23
  53.8 6.5 %collective-permute-start.5 = (f32[16,6,256]{2,0,1:T(8,128)S(1)}, f32[16,6,256]{2,0,1:T(8,128)S(1)}, u32[]{:S(2)}, u32[]{:S(2)}) collective-permute-start(f32[16,6,256]{2,0,1:T(8,128)S(1)} %multiply_reduce_fusion.120), channel_id=1, source_target_pairs={{0,8},{8,16},{16,24},{1,9},{9,17},{17,25},{2,10},{10,18},{18,26},{... | collective-permute-start | bytes 294920 | tf_op jit(solution)/shard_map/ppermute | solution.py:23
  61.9 6.5 %collective-permute-start.6 = (f32[16,6,256]{2,0,1:T(8,128)S(1)}, f32[16,6,256]{2,0,1:T(8,128)S(1)}, u32[]{:S(2)}, u32[]{:S(2)}) collective-permute-start(f32[16,6,256]{2,0,1:T(8,128)S(1)} %multiply_reduce_fusion.100), channel_id=1, source_target_pairs={{0,8},{8,16},{16,24},{1,9},{9,17},{17,25},{2,10},{10,18},{18,26},{... | collective-permute-start | bytes 294920 | tf_op jit(solution)/shard_map/ppermute | solution.py:23
  68.5 2.2 %slice-start.2 = ((s8[5898240]{0:T(1024)(128)(4,1)}), s8[4194304]{0:T(1024)(128)(4,1)S(1)}, s32[]{:S(2)}) async-start(s8[5898240]{0:T(1024)(128)(4,1)} %bitcast.668), calls=%async_computation.2 | async-start | bytes 8388608
  69.2 2.3 %slice-start.3 = ((s8[5898240]{0:T(1024)(128)(4,1)}), s8[1703936]{0:T(1024)(128)(4,1)S(1)}, s32[]{:S(2)}) async-start(s8[5898240]{0:T(1024)(128)(4,1)} %bitcast.668), calls=%async_computation.3 | async-start | bytes 3407872
  72.2 10.1 %collective-permute-start.7 = (f32[10,16,6,1]{3,1,2,0:T(8,128)S(1)}, f32[10,16,6,1]{3,1,2,0:T(8,128)S(1)}, u32[]{:S(2)}, u32[]{:S(2)}) collective-permute-start(f32[10,16,6,1]{3,1,2,0:T(8,128)S(1)} %get-tuple-element.25), channel_id=1, source_target_pairs={{0,2},{2,4},{4,6},{1,3},{3,5},{5,7},{8,10},{10,12},{12,14},{9,11},... | collective-permute-start | bytes 11528 | tf_op jit(solution)/shard_map/ppermute | solution.py:14
  74.1 10.0 %collective-permute-start.8 = (f32[10,16,6,1]{3,1,2,0:T(8,128)S(1)}, f32[10,16,6,1]{3,1,2,0:T(8,128)S(1)}, u32[]{:S(2)}, u32[]{:S(2)}) collective-permute-start(f32[10,16,6,1]{3,1,2,0:T(8,128)S(1)} %get-tuple-element.26), channel_id=1, source_target_pairs={{2,0},{4,2},{6,4},{3,1},{5,3},{7,5},{10,8},{12,10},{14,12},{11,9},... | collective-permute-start | bytes 11528 | tf_op jit(solution)/shard_map/ppermute | solution.py:15
  84.7 3.7 %collective-permute-start.10 = (f32[10,1,6,258]{3,1,2,0:T(1,128)S(1)}, f32[10,1,6,258]{3,1,2,0:T(1,128)S(1)}, u32[]{:S(2)}, u32[]{:S(2)}) collective-permute-start(f32[10,1,6,258]{3,1,2,0:T(1,128)S(1)} %get-tuple-element.21), channel_id=1, source_target_pairs={{1,0},{3,2},{5,4},{7,6},{9,8},{11,10},{13,12},{15,14},{17,16},{19,... | collective-permute-start | bytes 185768 | tf_op jit(solution)/shard_map/ppermute | solution.py:15
  86.2 6.4 %collective-permute-start.9 = (f32[10,1,6,258]{3,1,2,0:T(1,128)S(1)}, f32[10,1,6,258]{3,1,2,0:T(1,128)S(1)}, u32[]{:S(2)}, u32[]{:S(2)}) collective-permute-start(f32[10,1,6,258]{3,1,2,0:T(1,128)S(1)} %get-tuple-element.22), channel_id=1, source_target_pairs={{0,1},{2,3},{4,5},{6,7},{8,9},{10,11},{12,13},{14,15},{16,17},{18,... | collective-permute-start | bytes 185768 | tf_op jit(solution)/shard_map/ppermute | solution.py:14
  103.6 6.5 %collective-permute-start.11 = (f32[16,6,256]{2,0,1:T(8,128)S(1)}, f32[16,6,256]{2,0,1:T(8,128)S(1)}, u32[]{:S(2)}, u32[]{:S(2)}) collective-permute-start(f32[16,6,256]{2,0,1:T(8,128)S(1)} %sub.689), channel_id=1, source_target_pairs={{8,0},{16,8},{24,16},{9,1},{17,9},{25,17},{10,2},{18,10},{26,18},{... | collective-permute-start | bytes 294920 | tf_op jit(solution)/shard_map/ppermute | solution.py:23
  112.0 6.5 %collective-permute-start.12 = (f32[16,6,256]{2,0,1:T(8,128)S(1)}, f32[16,6,256]{2,0,1:T(8,128)S(1)}, u32[]{:S(2)}, u32[]{:S(2)}) collective-permute-start(f32[16,6,256]{2,0,1:T(8,128)S(1)} %sub.699), channel_id=1, source_target_pairs={{8,0},{16,8},{24,16},{9,1},{17,9},{25,17},{10,2},{18,10},{26,18},{... | collective-permute-start | bytes 294920 | tf_op jit(solution)/shard_map/ppermute | solution.py:23
  120.3 6.5 %collective-permute-start.13 = (f32[16,6,256]{2,0,1:T(8,128)S(1)}, f32[16,6,256]{2,0,1:T(8,128)S(1)}, u32[]{:S(2)}, u32[]{:S(2)}) collective-permute-start(f32[16,6,256]{2,0,1:T(8,128)S(1)} %sub.709), channel_id=1, source_target_pairs={{8,0},{16,8},{24,16},{9,1},{17,9},{25,17},{10,2},{18,10},{26,18},{... | collective-permute-start | bytes 294920 | tf_op jit(solution)/shard_map/ppermute | solution.py:23
  128.9 0.9 copy-start.6
where the time goes:
time: 131 us; the launch traced here: 130 us
  other arithmetic  45.8 us (35%)
  starting transfers between devices  36.9 us (28%)
  waiting for transfers between devices  33.6 us (26%)
  local copies, waits for them, and re-layouts  11.5 us (9%)
  between operations  2.54 us (2%)
    reduce_sum x161, other arithmetic, block_apply(): return jnp.sum(blocks * vector[..., None, :, :], axis=-2)  24.8 us
    ppermute x6, waiting for transfers between devices, shifted(): return lax.ppermute(x, axis, pairs)  22.4 us
    ppermute x6, starting transfers between devices, shifted(): return lax.ppermute(x, axis, pairs)  16.6 us
    ppermute x4, starting transfers between devices, extended(): after = lax.ppermute(initial, axis, down)  12.9 us
    ppermute x4, waiting for transfers between devices, extended(): before = lax.ppermute(last, axis, up)  8.89 us
    ppermute x4, starting transfers between devices, extended(): before = lax.ppermute(last, axis, up)  7.38 us
    convert_element_type x1, other arithmetic, body(): lower_all = jacobians[:, :, 4].astype(jnp.float32)  6.34 us
    concatenate x4, other arithmetic, extended(): x = jnp.concatenate([before, x, after], axis=dim)  5.4 us
  transfers between devices with their start and end apart: 14, of which 10 were waited for; matrix products, arithmetic and copies ran while one was open for 13% of the time, Pallas kernels for 0%

commit v1 on v0

v1 whole, which is shorter than its diff:
```python
import functools

import jax
import jax.numpy as jnp
from jax import lax
from jax.experimental import pallas as pl
from jax.experimental.pallas import tpu as pltpu
from jax.sharding import PartitionSpec as P

VARS = 6
LANES = 128
F32 = jnp.float32
WHOLE = pl.BlockSpec(memory_space=pltpu.VMEM)


def in_vmem(x):
    return pltpu.with_memory_space_constraint(x, pltpu.VMEM)


def call(body, outs, *args, flops, limit=16 << 20):
    moved = sum(a.size * a.dtype.itemsize for a in args)
    return pl.pallas_call(
        body,
        out_shape=[pltpu.VMEM(s, F32) for s in outs],
        in_specs=[WHOLE] * len(args),
        out_specs=[WHOLE] * len(outs),
        cost_estimate=pl.CostEstimate(flops=flops, bytes_accessed=moved, transcendentals=0),
        compiler_params=pltpu.CompilerParams(vmem_limit_bytes=limit),
    )(*[in_vmem(a) for a in args])


def lane_iota(rows):
    return lax.broadcasted_iota(jnp.int32, (rows, LANES), 1)


def row_iota(rows):
    return lax.broadcasted_iota(jnp.int32, (rows, LANES), 0)


def dot6(blocks, values):
    terms = [b.astype(F32) * v for b, v in zip(blocks, values)]
    return (terms[0] + terms[1]) + (terms[2] + terms[3]) + (terms[4] + terms[5])


def block(ref, *index, at):
    return lambda r, c: ref[(*index, r, c, slice(None), at)]


def apply_block(get, values):
    return [dot6([get(r, c) for c in range(VARS)], values) for r in range(VARS)]


def write_faces(value, left, right, rows, z_count, swap):
    y_count = value.shape[2]
    x_count = value.shape[3]
    lane = lane_iota(y_count)
    for face, start, source_lane in ((left, 0, 0), (right, x_count - LANES, LANES - 1)):
        for group in range(face.shape[0]):
            held = jnp.zeros((y_count, LANES), F32)
            for slot in range(min(LANES, z_count * VARS - group * LANES)):
                z, var = divmod(group * LANES + slot, VARS)
                tile = value[z, var, :, start : start + LANES]
                moved = pltpu.roll(tile, (slot - source_lane) % LANES, 1)
                held = jnp.where(lane == slot, moved, held)
            face[group] = held
    if swap:
        first = lax.axis_index("gy") == 0
        for j in range(z_count * VARS):
            z, var = divmod(j, VARS)
            low = value[z, var, 0:1, :]
            high = value[z, var, y_count - 1 : y_count, :]
            rows[0][z, var : var + 1, :] = jnp.where(first, high, low)
    else:
        for j in range(z_count * VARS):
            z, var = divmod(j, VARS)
            rows[0][z, var : var + 1, :] = value[z, var, 0:1, :]
            rows[1][z, var : var + 1, :] = value[z, var, y_count - 1 : y_count, :]


def halo_reader(before_x, after_x, rows, swap):
    def column(face, z, var, lane):
        j = z * VARS + var
        return pltpu.roll(face[j // LANES], (lane - j % LANES) % LANES, 1)

    def row(which, z, var, at):
        if not swap:
            return rows[which][z, var : var + 1, at]
        here = rows[0][z, var : var + 1, at]
        wanted = lax.axis_index("gy") == 1 - which
        return jnp.where(wanted, here, jnp.zeros_like(here))

    return (
        lambda z, var: column(before_x, z, var, 0),
        lambda z, var: column(after_x, z, var, LANES - 1),
        lambda z, var, at: row(0, z, var, at),
        lambda z, var, at: row(1, z, var, at),
    )


def neighbours(value, z, tile, tiles, halo):
    y_count = value.shape[2]
    lane = lane_iota(y_count)
    row = row_iota(y_count)
    at = slice(tile * LANES, (tile + 1) * LANES)
    result = ([], [], [], [])
    for var in range(VARS):
        here = value[z, var, :, at]
        if tile > 0:
            before = pltpu.roll(value[z, var, :, at.start - LANES : at.start], 1, 1)
        else:
            before = halo[0](z, var)
        if tile < tiles - 1:
            after = pltpu.roll(value[z, var, :, at.stop : at.stop + LANES], LANES - 1, 1)
        else:
            after = halo[1](z, var)
        result[0].append(jnp.where(lane == 0, before, pltpu.roll(here, 1, 1)))
        result[1].append(jnp.where(lane == LANES - 1, after, pltpu.roll(here, LANES - 1, 1)))
        result[2].append(jnp.where(row == 0, halo[2](z, var, at), pltpu.roll(here, 1, 0)))
        result[3].append(
            jnp.where(row == y_count - 1, halo[3](z, var, at), pltpu.roll(here, y_count - 1, 0))
        )
    return result


def inplane(jacobians, value, z, tile, tiles, halo):
    at = slice(tile * LANES, (tile + 1) * LANES)
    total = None
    for n, values in enumerate(neighbours(value, z, tile, tiles, halo)):
        part = apply_block(block(jacobians, z, n, at=at), values)
        total = part if total is None else [a + b for a, b in zip(total, part)]
    return total


def planes_of(ref, z, at):
    return [ref[z, var, :, at] for var in range(VARS)]


def solution(mesh):
    gz, gx, gy = (mesh.shape[a] for a in ("gz", "gx", "gy"))
    swap = gy == 2

    def body(right_side, previous, diag_inverse, jacobians):
        rhs = jnp.transpose(right_side, (0, 2, 1, 3))
        prev = jnp.transpose(previous, (0, 2, 1, 3))
        inv = jnp.transpose(diag_inverse, (0, 2, 3, 1, 4))
        jac = jnp.transpose(jacobians, (0, 2, 3, 4, 1, 5))
        nz, _, ny, nx = rhs.shape
        tiles = nx // LANES
        assert nx % LANES == 0
        spans = [slice(t * LANES, (t + 1) * LANES) for t in range(tiles)]
        plane = (VARS, ny, nx)
        volume = (nz, VARS, ny, nx)
        x_face = (-(-nz * VARS // LANES), ny, LANES)
        y_face = (nz, VARS, nx)
        face_shapes = [x_face, x_face] + [y_face] * (1 if swap else 2)
        cells = nz * ny * nx
        block_flops = 2 * VARS * VARS * cells

        def exchange(left, right, *rows):
            up = [(i, i + 1) for i in range(gx - 1)]
            before_x = lax.ppermute(right, "gx", up)
            after_x = lax.ppermute(left, "gx", [(j, i) for i, j in up])
            if swap:
                return before_x, after_x, lax.ppermute(rows[0], "gy", [(0, 1), (1, 0)])
            up = [(i, i + 1) for i in range(gy - 1)]
            before_y = lax.ppermute(rows[1], "gy", up)
            after_y = lax.ppermute(rows[0], "gy", [(j, i) for i, j in up])
            return before_x, after_x, before_y, after_y

        def faces_kernel(value, left, right, *rows):
            write_faces(value, left, right, rows, nz, swap)

        def forward_plane(source, inv_ref, jac_ref, z, at, earlier):
            lagged = apply_block(block(jac_ref, z, 4, at=at), earlier)
            return apply_block(block(inv_ref, z, at=at), [a - b for a, b in zip(source, lagged)])

        def first_kernel(rhs_ref, prev_ref, inv_ref, jac_ref, *rest):
            halo_refs, (source_ref, top_ref) = rest[:-2], rest[-2:]
            halo = halo_reader(halo_refs[0], halo_refs[1], halo_refs[2:], swap)
            for tile, at in enumerate(spans):

                def step(z, earlier, tile=tile, at=at):
                    lagged = inplane(jac_ref, prev_ref, z, tile, tiles, halo)
                    source = [a - b for a, b in zip(planes_of(rhs_ref, z, at), lagged)]
                    for var in range(VARS):
                        source_ref[z, var, :, at] = source[var]
                    return tuple(forward_plane(source, inv_ref, jac_ref, z, at, earlier))

                zero = tuple(jnp.zeros((ny, LANES), F32) for _ in range(VARS))
                top = lax.fori_loop(0, nz, step, zero)
                for var in range(VARS):
                    top_ref[var, :, at] = top[var]

        def incoming(refs, at):
            total = [refs[0][var, :, at] for var in range(VARS)]
            for ref in refs[1:]:
                total = [a + ref[var, :, at] for var, a in enumerate(total)]
            return tuple(total)

        def forward_kernel(source_ref, inv_ref, jac_ref, *rest):
            came, top_ref = rest[:-1], rest[-1]
            for at in spans:

                def step(z, earlier, at=at):
                    source = planes_of(source_ref, z, at)
                    return tuple(forward_plane(source, inv_ref, jac_ref, z, at, earlier))

                top = lax.fori_loop(0, nz, step, incoming(came, at))
                for var in range(VARS):
                    top_ref[var, :, at] = top[var]

        def forward_last_kernel(source_ref, prev_ref, inv_ref, jac_ref, *rest):
            came, (sweep_ref, change_ref, left, right, *rows) = rest[: gz - 1], rest[gz - 1 :]
            for at in spans:

                def step(z, earlier, at=at):
                    source = planes_of(source_ref, z, at)
                    result = forward_plane(source, inv_ref, jac_ref, z, at, earlier)
                    before = planes_of(prev_ref, z, at)
                    for var in range(VARS):
                        sweep_ref[z, var, :, at] = result[var]
                        change_ref[z, var, :, at] = result[var] - before[var]
                    return tuple(result)

                lax.fori_loop(0, nz, step, incoming(came, at))
            write_faces(change_ref, left, right, rows, nz, swap)

        def backward_plane(sweep, inner, inv_ref, jac_ref, z, at, later):
            change = apply_block(block(jac_ref, z, 5, at=at), later)
            change = apply_block(block(inv_ref, z, at=at), [a + b for a, b in zip(change, inner)])
            return [a - b for a, b in zip(sweep, change)]

        def inner_kernel(sweep_ref, change_ref, inv_ref, jac_ref, *rest):
            halo_refs, (inner_ref, low_ref) = rest[:-2], rest[-2:]
            halo = halo_reader(halo_refs[0], halo_refs[1], halo_refs[2:], swap)
            for tile, at in enumerate(spans):

                def step(i, later, tile=tile, at=at):
                    z = nz - 1 - i
                    inner = inplane(jac_ref, change_ref, z, tile, tiles, halo)
                    for var in range(VARS):
                        inner_ref[z, var, :, at] = inner[var]
                    sweep = planes_of(sweep_ref, z, at)
                    return tuple(backward_plane(sweep, inner, inv_ref, jac_ref, z, at, later))

                zero = tuple(jnp.zeros((ny, LANES), F32) for _ in range(VARS))
                low = lax.fori_loop(0, nz, step, zero)
                for var in range(VARS):
                    low_ref[var, :, at] = low[var]

        def backward_kernel(keep, sweep_ref, inner_ref, inv_ref, jac_ref, *rest):
            came, out_ref = rest[:-1], rest[-1]
            for at in spans:

                def step(i, later, at=at):
                    z = nz - 1 - i
                    sweep, inner = planes_of(sweep_ref, z, at), planes_of(inner_ref, z, at)
                    result = backward_plane(sweep, inner, inv_ref, jac_ref, z, at, later)
                    if keep:
                        for var in range(VARS):
                            out_ref[z, var, :, at] = result[var]
                    return tuple(result)

                low = lax.fori_loop(0, nz, step, incoming(came, at))
                if not keep:
                    for var in range(VARS):
                        out_ref[var, :, at] = low[var]

        faces = call(faces_kernel, face_shapes, prev, flops=cells)
        halo = exchange(*faces)
        source, top = call(
            first_kernel, [volume, plane], rhs, prev, inv, jac, *halo, flops=6 * block_flops
        )
        came = []
        for hop in range(gz - 1):
            if hop:
                (top,) = call(
                    forward_kernel, [plane], source, inv, jac, *came, flops=2 * block_flops
                )
            came.append(lax.ppermute(top, "gz", [(hop, hop + 1)]))
        sweep, change, *faces = call(
            forward_last_kernel,
            [volume, volume, *face_shapes],
            source,
            prev,
            inv,
            jac,
            *came,
            flops=2 * block_flops,
        )
        halo = exchange(*faces)
        inner, low = call(
            inner_kernel, [volume, plane], sweep, change, inv, jac, *halo, flops=6 * block_flops
        )
        came = []
        for hop in range(gz - 1, 0, -1):
            if came:
                (low,) = call(
                    functools.partial(backward_kernel, False),
                    [plane],
                    sweep,
                    inner,
                    inv,
                    jac,
                    *came,
                    flops=2 * block_flops,
                )
            came.append(lax.ppermute(low, "gz", [(hop, hop - 1)]))
        (update,) = call(
            functools.partial(backward_kernel, True),
            [volume],
            sweep,
            inner,
            inv,
            jac,
            *came,
            flops=2 * block_flops,
        )
        return jnp.transpose(update, (0, 2, 1, 3))

    placed = (
        P("gz", "gy", None, "gx"),
        P("gz", "gy", None, "gx"),
        P("gz", "gy", None, None, "gx"),
        P("gz", "gy", None, None, None, "gx"),
    )
    return jax.shard_map(
        body, mesh=mesh, in_specs=placed, out_specs=P("gz", "gy", None, "gx"), check_vma=False
    )
```

time: 131 us -> 78.9 us (0.60)
  the two profiles are of different devices: /device:TPU:14 before, /device:TPU:0 now
where the time goes in v1:
time: 78.9 us; the launch traced here: 78.4 us
  waiting for transfers between devices  31.2 us (40%)
  starting transfers between devices  18.4 us (23%)
  Pallas kernels  17.4 us (22%)
  local copies, waits for them, and re-layouts  11.2 us (14%)
    ppermute x3, waiting for transfers between devices, body(): came.append(lax.ppermute(low, 'gz', [(hop, hop - 1)]))  23.2 us
    pallas_call x9, Pallas kernels, call(): pl.pallas_call(body, out_shape=[pltpu.VMEM(s, F32) for s in outs], in_spe...  17.4 us
    unnamed x11, local copies, waits for them, and re-layouts  11.2 us
    ppermute x2, waiting for transfers between devices, exchange(): after_x = lax.ppermute(left, 'gx', [(j, i) for i, j in up])  5.77 us
    ppermute x3, starting transfers between devices, body(): came.append(lax.ppermute(top, 'gz', [(hop, hop + 1)]))  4.95 us
    ppermute x2, starting transfers between devices, exchange(): before_x = lax.ppermute(right, 'gx', up)  4.61 us
    ppermute x2, starting transfers between devices, exchange(): return (before_x, after_x, lax.ppermute(rows[0], 'gy', [(0, 1), (1, 0)]))  3.6 us
    ppermute x3, starting transfers between devices, body(): came.append(lax.ppermute(low, 'gz', [(hop, hop - 1)]))  2.63 us
  transfers between devices with their start and end apart: 12, of which 4 were waited for; matrix products, arithmetic and copies ran while one was open for 0% of the time, Pallas kernels for 0%

profile of v1, /device:TPU:0, one launch (start us, length us, event | category | flops | bytes accessed | tf_op | source)
XLA Modules:
  0.0 78.4 jit_solution(14444238070429491573)
XLA Ops:
  0.0 1.2 %copy-done.3 = f32[10,16,6,256]{3,1,2,0:T(8,128)S(1)} copy-done((f32[10,16,6,256]{3,1,2,0:T(8,128)S(1)}, f32[10,16,6,256]{3,1,2,0:T(8,128)}, u32[]{:S(2)}) %copy-start.3) | copy-done | bytes 983064
  1.2 0.3 shard_map.46
  1.5 3.0 %collective-permute-start.2 = (f32[10,6,256]{2,1,0:T(8,128)S(1)}, f32[10,6,256]{2,1,0:T(8,128)S(1)}, u32[]{:S(2)}, u32[]{:S(2)}) collective-permute-start(f32[10,6,256]{2,1,0:T(8,128)S(1)} %get-tuple-element.19), channel_id=1, source_target_pairs={{0,1},{1,0},{2,3},{3,2},{4,5},{5,4},{6,7},{7,6},{8,9},{9,8},{10,11... | collective-permute-start | bytes 184328 | tf_op jit(solution)/shard_map/ppermute | solution.py:164
  4.5 1.4 %collective-permute-start = (f32[1,16,128]{2,1,0:T(8,128)S(1)}, f32[1,16,128]{2,1,0:T(8,128)S(1)}, u32[]{:S(2)}, u32[]{:S(2)}) collective-permute-start(f32[1,16,128]{2,1,0:T(8,128)S(1)} %get-tuple-element.17), channel_id=1, source_target_pairs={{0,2},{2,4},{4,6},{1,3},{3,5},{5,7},{8,10},{10,12},{12,14},{9,11},... | collective-permute-start | bytes 24584 | tf_op jit(solution)/shard_map/ppermute | solution.py:161
  6.0 1.3 %collective-permute-start.1 = (f32[1,16,128]{2,1,0:T(8,128)S(1)}, f32[1,16,128]{2,1,0:T(8,128)S(1)}, u32[]{:S(2)}, u32[]{:S(2)}) collective-permute-start(f32[1,16,128]{2,1,0:T(8,128)S(1)} %get-tuple-element.18), channel_id=1, source_target_pairs={{2,0},{4,2},{6,4},{3,1},{5,3},{7,5},{10,8},{12,10},{14,12},{11,9},... | collective-permute-start | bytes 24584 | tf_op jit(solution)/shard_map/ppermute | solution.py:162
  7.3 3.3 %collective-permute-done.1.rest_1_ = f32[1,16,128]{2,1,0:T(8,128)S(1)} collective-permute-done((f32[1,16,128]{2,1,0:T(8,128)S(1)}, f32[1,16,128]{2,1,0:T(8,128)S(1)}, u32[]{:S(2)}, u32[]{:S(2)}) %collective-permute-start.1) | collective-permute-done | bytes 8224 | tf_op jit(solution)/shard_map/ppermute | solution.py:162
  10.6 6.0 %copy-done = bf16[10,16,6,6,6,256]{5,1,4,3,2,0:T(8,128)(2,1)S(1)} copy-done((bf16[10,16,6,6,6,256]{5,1,4,3,2,0:T(8,128)(2,1)S(1)}, bf16[10,16,6,6,6,256]{5,1,4,3,2,0:T(8,128)(2,1)}, u32[]{:S(2)}) %copy-start) | copy-done | bytes 17694744
  16.7 1.8 %copy-done.2 = bf16[10,16,6,6,256]{4,1,3,2,0:T(8,128)(2,1)S(1)} copy-done((bf16[10,16,6,6,256]{4,1,3,2,0:T(8,128)(2,1)S(1)}, bf16[10,16,6,6,256]{4,1,3,2,0:T(8,128)(2,1)}, u32[]{:S(2)}) %copy-start.2) | copy-done | bytes 2949144
  18.5 1.2 %copy-done.4 = f32[10,16,6,256]{3,1,2,0:T(8,128)S(1)} copy-done((f32[10,16,6,256]{3,1,2,0:T(8,128)S(1)}, f32[10,16,6,256]{3,1,2,0:T(8,128)}, u32[]{:S(2)}) %copy-start.4) | copy-done | bytes 983064
  19.7 4.6 %shard_map.47 = (f32[10,6,16,256]{3,2,1,0:T(8,128)S(1)}, f32[6,16,256]{2,1,0:T(8,128)S(1)}) custom-call(f32[10,6,16,256]{3,2,1,0:T(8,128)S(1)} %bitcast.25, f32[10,6,16,256]{3,2,1,0:T(8,128)S(1)} %bitcast.23, bf16[10,6,6,16,256]{4,3,2,1,0:T(8,128)(2,1)S(1)} %bitcast.14, bf16[10,6,6,6,16,256]{5,4,3,2,1,0:T(8,128)(2,1)S(1)} %bitcast.6, ...), custom_call_target="tpu_custom_call" | custom-call | flops 17694720 | bytes 22687744 | tf_op jit(solution)/shard_map/pallas_call | solution.py:22
  24.4 3.6 %collective-permute-start.3 = (f32[6,16,256]{2,1,0:T(8,128)S(1)}, f32[6,16,256]{2,1,0:T(8,128)S(1)}, u32[]{:S(2)}, u32[]{:S(2)}) collective-permute-start(f32[6,16,256]{2,1,0:T(8,128)S(1)} %get-tuple-element.21), channel_id=1, source_target_pairs={{0,8},{1,9},{2,10},{3,11},{4,12},{5,13},{6,14},{7,15}} | collective-permute-start | bytes 294920 | tf_op jit(solution)/shard_map/ppermute | solution.py:280
  28.0 2.2 %collective-permute-done.3.rest_0_ = f32[6,16,256]{2,1,0:T(8,128)S(1)} collective-permute-done((f32[6,16,256]{2,1,0:T(8,128)S(1)}, f32[6,16,256]{2,1,0:T(8,128)S(1)}, u32[]{:S(2)}, u32[]{:S(2)}) %collective-permute-start.3) | collective-permute-done | bytes 98336 | tf_op jit(solution)/shard_map/ppermute | solution.py:280
  30.2 1.2 %shard_map.48 = f32[6,16,256]{2,1,0:T(8,128)S(1)} custom-call(f32[10,6,16,256]{3,2,1,0:T(8,128)S(1)} %get-tuple-element.20.source_ref, bf16[10,6,6,16,256]{4,3,2,1,0:T(8,128)(2,1)S(1)} %bitcast.15, bf16[10,6,6,6,16,256]{5,4,3,2,1,0:T(8,128)(2,1)S(1)} %bitcast.7, f32[6,16,256]{2,1,0:T(8,128)S(1)} %collective-permute-done.3.rest_0_), custom_call_target="tpu_custom_call" | custom-call | flops 5898240 | bytes 21725184 | tf_op jit(solution)/shard_map/pallas_call | solution.py:22
  31.4 0.7 collective-permute-start.4
  32.1 1.2 %shard_map.49 = f32[6,16,256]{2,1,0:T(8,128)S(1)} custom-call(f32[10,6,16,256]{3,2,1,0:T(8,128)S(1)} %get-tuple-element.20.source_ref, bf16[10,6,6,16,256]{4,3,2,1,0:T(8,128)(2,1)S(1)} %bitcast.16, bf16[10,6,6,6,16,256]{5,4,3,2,1,0:T(8,128)(2,1)S(1)} %bitcast.8, f32[6,16,256]{2,1,0:T(8,128)S(1)} %collective-permute-done.3.rest_0_, ...), custom_call_target="tpu_custom_call" | custom-call | flops 5898240 | bytes 21823488 | tf_op jit(solution)/shard_map/pallas_call | solution.py:22
  33.3 0.7 collective-permute-start.5
  34.0 0.0 collective-permute-done.5.rest_2_
  34.0 1.6 %shard_map.50 = (f32[10,6,16,256]{3,2,1,0:T(8,128)S(1)}, f32[10,6,16,256]{3,2,1,0:T(8,128)S(1)}, f32[1,16,128]{2,1,0:T(8,128)S(1)}, f32[1,16,128]{2,1,0:T(8,128)S(1)}, f32[10,6,256]{2,1,0:T(8,128)S(1)}) custom-call(f32[10,6,16,256]{3,2,1,0:T(8,128)S(1)} %get-tuple-element.20.source_ref, f32[10,6,16,256]{3,2,1,0:T(8,128)S(1)} %bitcast.24, ...), custom_call_target="tpu_custom_call" | custom-call | flops 5898240 | bytes 22904832 | tf_op jit(solution)/shard_map/pallas_call | solution.py:22
  35.6 0.6 collective-permute-start.8
  36.2 3.2 %collective-permute-start.6 = (f32[1,16,128]{2,1,0:T(8,128)S(1)}, f32[1,16,128]{2,1,0:T(8,128)S(1)}, u32[]{:S(2)}, u32[]{:S(2)}) collective-permute-start(f32[1,16,128]{2,1,0:T(8,128)S(1)} %get-tuple-element.24), channel_id=1, source_target_pairs={{0,2},{2,4},{4,6},{1,3},{3,5},{5,7},{8,10},{10,12},{12,14},{9,11},... | collective-permute-start | bytes 24584 | tf_op jit(solution)/shard_map/ppermute | solution.py:161
  39.4 1.3 %collective-permute-start.7 = (f32[1,16,128]{2,1,0:T(8,128)S(1)}, f32[1,16,128]{2,1,0:T(8,128)S(1)}, u32[]{:S(2)}, u32[]{:S(2)}) collective-permute-start(f32[1,16,128]{2,1,0:T(8,128)S(1)} %get-tuple-element.25), channel_id=1, source_target_pairs={{2,0},{4,2},{6,4},{3,1},{5,3},{7,5},{10,8},{12,10},{14,12},{11,9},... | collective-permute-start | bytes 24584 | tf_op jit(solution)/shard_map/ppermute | solution.py:162
  40.7 2.4 %collective-permute-done.7.rest_1_ = f32[1,16,128]{2,1,0:T(8,128)S(1)} collective-permute-done((f32[1,16,128]{2,1,0:T(8,128)S(1)}, f32[1,16,128]{2,1,0:T(8,128)S(1)}, u32[]{:S(2)}, u32[]{:S(2)}) %collective-permute-start.7) | collective-permute-done | bytes 8224 | tf_op jit(solution)/shard_map/ppermute | solution.py:162
  43.1 4.7 %shard_map.51 = (f32[10,6,16,256]{3,2,1,0:T(8,128)S(1)}, f32[6,16,256]{2,1,0:T(8,128)S(1)}) custom-call(f32[10,6,16,256]{3,2,1,0:T(8,128)S(1)} %get-tuple-element.22.sweep_ref, f32[10,6,16,256]{3,2,1,0:T(8,128)S(1)} %get-tuple-element.23.change_ref, bf16[10,6,6,16,256]{4,3,2,1,0:T(8,128)(2,1)S(1)} %bitcast.18, bf16[10,6,6,6,16,256]{5,4,3,2,1,0:T(8,128)(2,1)S(1)} %bitcast.10, ...), custom_call_target="tpu_custom_call" | custom-call | flops 17694720 | bytes 22687744 | tf_op jit(solution)/shard_map/pallas_call | solution.py:22
  47.8 0.7 collective-permute-start.9
  48.5 1.2 %shard_map.52 = f32[6,16,256]{2,1,0:T(8,128)S(1)} custom-call(f32[10,6,16,256]{3,2,1,0:T(8,128)S(1)} %get-tuple-element.22.sweep_ref, f32[10,6,16,256]{3,2,1,0:T(8,128)S(1)} %get-tuple-element.27.inner_ref, bf16[10,6,6,16,256]{4,3,2,1,0:T(8,128)(2,1)S(1)} %bitcast.19, bf16[10,6,6,6,16,256]{5,4,3,2,1,0:T(8,128)(2,1)S(1)} %bitcast.11, ...), custom_call_target="tpu_custom_call" | custom-call | flops 5898240 | bytes 22708224 | tf_op jit(solution)/shard_map/pallas_call | solution.py:22
  49.7 0.7 collective-permute-start.10
  50.4 0.0 collective-permute-done.10.rest_1_
  50.4 1.2 %shard_map.53 = f32[6,16,256]{2,1,0:T(8,128)S(1)} custom-call(f32[10,6,16,256]{3,2,1,0:T(8,128)S(1)} %get-tuple-element.22.sweep_ref, f32[10,6,16,256]{3,2,1,0:T(8,128)S(1)} %get-tuple-element.27.inner_ref, bf16[10,6,6,16,256]{4,3,2,1,0:T(8,128)(2,1)S(1)} %bitcast.20, bf16[10,6,6,6,16,256]{5,4,3,2,1,0:T(8,128)(2,1)S(1)} %bitcast.12, ...), custom_call_target="tpu_custom_call" | custom-call | flops 5898240 | bytes 22806528 | tf_op jit(solution)/shard_map/pallas_call | solution.py:22
  51.7 1.3 %collective-permute-start.11 = (f32[6,16,256]{2,1,0:T(8,128)S(1)}, f32[6,16,256]{2,1,0:T(8,128)S(1)}, u32[]{:S(2)}, u32[]{:S(2)}) collective-permute-start(f32[6,16,256]{2,1,0:T(8,128)S(1)} %shard_map.53), channel_id=1, source_target_pairs={{8,0},{9,1},{10,2},{11,3},{12,4},{13,5},{14,6},{15,7}} | collective-permute-start | bytes 294920 | tf_op jit(solution)/shard_map/ppermute | solution.py:308
  53.0 23.2 %collective-permute-done.11.rest_2_ = f32[6,16,256]{2,1,0:T(8,128)S(1)} collective-permute-done((f32[6,16,256]{2,1,0:T(8,128)S(1)}, f32[6,16,256]{2,1,0:T(8,128)S(1)}, u32[]{:S(2)}, u32[]{:S(2)}) %collective-permute-start.11) | collective-permute-done | bytes 98336 | tf_op jit(solution)/shard_map/ppermute | solution.py:308
  76.2 1.3 %shard_map.54 = f32[10,6,16,256]{3,2,1,0:T(8,128)S(1)} custom-call(f32[10,6,16,256]{3,2,1,0:T(8,128)S(1)} %get-tuple-element.22.sweep_ref, f32[10,6,16,256]{3,2,1,0:T(8,128)S(1)} %get-tuple-element.27.inner_ref, bf16[10,6,6,16,256]{4,3,2,1,0:T(8,128)(2,1)S(1)} %bitcast.21, bf16[10,6,6,6,16,256]{5,4,3,2,1,0:T(8,128)(2,1)S(1)} %bitcast.13, ...), custom_call_target="tpu_custom_call" | custom-call | flops 5898240 | bytes 22904832 | tf_op jit(solution)/shard_map/pallas_call | solution.py:22
  77.5 0.9 %copy.5 = f32[10,16,6,256]{3,1,2,0:T(8,128)} copy(f32[10,16,6,256]{3,1,2,0:T(8,128)S(1)} %bitcast.5) | data formatting | bytes 1966080
  (12 shorter events, 0.0 us)
Async XLA Ops:
  0.0 1.2 %copy-start.3 = (f32[10,16,6,256]{3,1,2,0:T(8,128)S(1)}, f32[10,16,6,256]{3,1,2,0:T(8,128)}, u32[]{:S(2)}) copy-start(f32[10,16,6,256]{3,1,2,0:T(8,128)} %param.5) | copy-start | bytes 2949124
  1.5 9.1 %collective-permute-start.2 = (f32[10,6,256]{2,1,0:T(8,128)S(1)}, f32[10,6,256]{2,1,0:T(8,128)S(1)}, u32[]{:S(2)}, u32[]{:S(2)}) collective-permute-start(f32[10,6,256]{2,1,0:T(8,128)S(1)} %get-tuple-element.19), channel_id=1, source_target_pairs={{0,1},{1,0},{2,3},{3,2},{4,5},{5,4},{6,7},{7,6},{8,9},{9,8},{10,11... | collective-permute-start | bytes 184328 | tf_op jit(solution)/shard_map/ppermute | solution.py:164
  4.5 2.8 %collective-permute-start = (f32[1,16,128]{2,1,0:T(8,128)S(1)}, f32[1,16,128]{2,1,0:T(8,128)S(1)}, u32[]{:S(2)}, u32[]{:S(2)}) collective-permute-start(f32[1,16,128]{2,1,0:T(8,128)S(1)} %get-tuple-element.17), channel_id=1, source_target_pairs={{0,2},{2,4},{4,6},{1,3},{3,5},{5,7},{8,10},{10,12},{12,14},{9,11},... | collective-permute-start | bytes 24584 | tf_op jit(solution)/shard_map/ppermute | solution.py:161
  6.0 4.7 %collective-permute-start.1 = (f32[1,16,128]{2,1,0:T(8,128)S(1)}, f32[1,16,128]{2,1,0:T(8,128)S(1)}, u32[]{:S(2)}, u32[]{:S(2)}) collective-permute-start(f32[1,16,128]{2,1,0:T(8,128)S(1)} %get-tuple-element.18), channel_id=1, source_target_pairs={{2,0},{4,2},{6,4},{3,1},{5,3},{7,5},{10,8},{12,10},{14,12},{11,9},... | collective-permute-start | bytes 24584 | tf_op jit(solution)/shard_map/ppermute | solution.py:162
  10.6 6.0 %copy-start = (bf16[10,16,6,6,6,256]{5,1,4,3,2,0:T(8,128)(2,1)S(1)}, bf16[10,16,6,6,6,256]{5,1,4,3,2,0:T(8,128)(2,1)}, u32[]{:S(2)}) copy-start(bf16[10,16,6,6,6,256]{5,1,4,3,2,0:T(8,128)(2,1)} %param.7) | copy-start | bytes 53084164
  16.7 1.8 %copy-start.2 = (bf16[10,16,6,6,256]{4,1,3,2,0:T(8,128)(2,1)S(1)}, bf16[10,16,6,6,256]{4,1,3,2,0:T(8,128)(2,1)}, u32[]{:S(2)}) copy-start(bf16[10,16,6,6,256]{4,1,3,2,0:T(8,128)(2,1)} %param.6) | copy-start | bytes 8847364
  18.5 1.2 %copy-start.4 = (f32[10,16,6,256]{3,1,2,0:T(8,128)S(1)}, f32[10,16,6,256]{3,1,2,0:T(8,128)}, u32[]{:S(2)}) copy-start(f32[10,16,6,256]{3,1,2,0:T(8,128)} %param.4) | copy-start | bytes 2949124
  19.7 10.5 %copy-start.1 = (bf16[10,16,6,6,6,256]{5,1,4,3,2,0:T(8,128)(2,1)S(1)}, bf16[10,16,6,6,6,256]{5,1,4,3,2,0:T(8,128)(2,1)}, u32[]{:S(2)}) copy-start(bf16[10,16,6,6,6,256]{5,1,4,3,2,0:T(8,128)(2,1)} %param.7) | copy-start | bytes 53084164
  24.4 5.8 %collective-permute-start.3 = (f32[6,16,256]{2,1,0:T(8,128)S(1)}, f32[6,16,256]{2,1,0:T(8,128)S(1)}, u32[]{:S(2)}, u32[]{:S(2)}) collective-permute-start(f32[6,16,256]{2,1,0:T(8,128)S(1)} %get-tuple-element.21), channel_id=1, source_target_pairs={{0,8},{1,9},{2,10},{3,11},{4,12},{5,13},{6,14},{7,15}} | collective-permute-start | bytes 294920 | tf_op jit(solution)/shard_map/ppermute | solution.py:280
  31.4 0.7 collective-permute-start.4
  33.3 0.7 collective-permute-start.5
  35.6 7.5 %collective-permute-start.8 = (f32[10,6,256]{2,1,0:T(8,128)S(1)}, f32[10,6,256]{2,1,0:T(8,128)S(1)}, u32[]{:S(2)}, u32[]{:S(2)}) collective-permute-start(f32[10,6,256]{2,1,0:T(8,128)S(1)} %get-tuple-element.26), channel_id=1, source_target_pairs={{0,1},{1,0},{2,3},{3,2},{4,5},{5,4},{6,7},{7,6},{8,9},{9,8},{10,11... | collective-permute-start | bytes 184328 | tf_op jit(solution)/shard_map/ppermute | solution.py:164
  36.2 4.5 %collective-permute-start.6 = (f32[1,16,128]{2,1,0:T(8,128)S(1)}, f32[1,16,128]{2,1,0:T(8,128)S(1)}, u32[]{:S(2)}, u32[]{:S(2)}) collective-permute-start(f32[1,16,128]{2,1,0:T(8,128)S(1)} %get-tuple-element.24), channel_id=1, source_target_pairs={{0,2},{2,4},{4,6},{1,3},{3,5},{5,7},{8,10},{10,12},{12,14},{9,11},... | collective-permute-start | bytes 24584 | tf_op jit(solution)/shard_map/ppermute | solution.py:161
  39.4 3.7 %collective-permute-start.7 = (f32[1,16,128]{2,1,0:T(8,128)S(1)}, f32[1,16,128]{2,1,0:T(8,128)S(1)}, u32[]{:S(2)}, u32[]{:S(2)}) collective-permute-start(f32[1,16,128]{2,1,0:T(8,128)S(1)} %get-tuple-element.25), channel_id=1, source_target_pairs={{2,0},{4,2},{6,4},{3,1},{5,3},{7,5},{10,8},{12,10},{14,12},{11,9},... | collective-permute-start | bytes 24584 | tf_op jit(solution)/shard_map/ppermute | solution.py:162
  47.8 0.7 collective-permute-start.9
  49.7 0.7 collective-permute-start.10
  51.7 24.5 %collective-permute-start.11 = (f32[6,16,256]{2,1,0:T(8,128)S(1)}, f32[6,16,256]{2,1,0:T(8,128)S(1)}, u32[]{:S(2)}, u32[]{:S(2)}) collective-permute-start(f32[6,16,256]{2,1,0:T(8,128)S(1)} %shard_map.53), channel_id=1, source_target_pairs={{8,0},{9,1},{10,2},{11,3},{12,4},{13,5},{14,6},{15,7}} | collective-permute-start | bytes 294920 | tf_op jit(solution)/shard_map/ppermute | solution.py:308

commit v2 on v1

v2 whole, which is shorter than its diff:
```python
import jax
import jax.numpy as jnp
from jax import lax
from jax.experimental import pallas as pl
from jax.experimental.pallas import tpu as pltpu
from jax.sharding import PartitionSpec as P

VARS = 6
LANES = 128
F32 = jnp.float32
WHOLE = pl.BlockSpec(memory_space=pltpu.VMEM)


def call(body, outs, *args, flops, limit=16 << 20, scratch=(), in_hbm=(), out_hbm=()):
    far = pl.BlockSpec(memory_space=pl.ANY)
    shapes = [
        jax.ShapeDtypeStruct(o[0], o[1]) if i in out_hbm else pltpu.VMEM(o[0], o[1])
        for i, o in enumerate(outs)
    ]
    moved = sum(a.size * a.dtype.itemsize for a in args)
    return pl.pallas_call(
        body,
        out_shape=shapes,
        in_specs=[far if i in in_hbm else WHOLE for i in range(len(args))],
        out_specs=[far if i in out_hbm else WHOLE for i in range(len(outs))],
        scratch_shapes=scratch,
        cost_estimate=pl.CostEstimate(flops=flops, bytes_accessed=moved, transcendentals=0),
        compiler_params=pltpu.CompilerParams(vmem_limit_bytes=limit),
    )(*[
        pltpu.with_memory_space_constraint(a, pltpu.HBM if i in in_hbm else pltpu.VMEM)
        for i, a in enumerate(args)
    ])


def lane_iota(rows):
    return lax.broadcasted_iota(jnp.int32, (rows, LANES), 1)


def row_iota(rows):
    return lax.broadcasted_iota(jnp.int32, (rows, LANES), 0)


def dot6(blocks, values):
    terms = [b.astype(F32) * v for b, v in zip(blocks, values)]
    return (terms[0] + terms[1]) + (terms[2] + terms[3]) + (terms[4] + terms[5])


def block(ref, *index, at):
    return lambda r, c: ref[(*index, r, c, slice(None), at)]


def apply_block(get, values):
    return [dot6([get(r, c) for c in range(VARS)], values) for r in range(VARS)]


def write_faces(value, x_face, y_face, z_count):
    y_count = value.shape[2]
    x_count = value.shape[3]
    lane = lane_iota(y_count)
    for side, start, source_lane in ((0, 0, 0), (1, x_count - LANES, LANES - 1)):
        for group in range(x_face.shape[1]):
            held = jnp.zeros((y_count, LANES), F32)
            for slot in range(min(LANES, z_count * VARS - group * LANES)):
                z, var = divmod(group * LANES + slot, VARS)
                tile = value[z, var, :, start : start + LANES]
                moved = pltpu.roll(tile, (slot - source_lane) % LANES, 1)
                held = jnp.where(lane == slot, moved, held)
            x_face[side, group] = held
    if y_face.shape[0] == 1:
        first = lax.axis_index("gy") == 0
        for z in range(z_count):
            for var in range(VARS):
                low = value[z, var, 0:1, :]
                high = value[z, var, y_count - 1 : y_count, :]
                y_face[0, z, var : var + 1, :] = jnp.where(first, high, low)
    else:
        for z in range(z_count):
            for var in range(VARS):
                y_face[0, z, var : var + 1, :] = value[z, var, 0:1, :]
                y_face[1, z, var : var + 1, :] = value[z, var, y_count - 1 : y_count, :]


def neighbours(value, z, tile, tiles):
    y_count = value.shape[2]
    lane = lane_iota(y_count)
    row = row_iota(y_count)
    at = slice(tile * LANES, (tile + 1) * LANES)
    zero = jnp.zeros((y_count, LANES), F32)
    result = ([], [], [], [])
    for var in range(VARS):
        here = value[z, var, :, at]
        before, after = zero, zero
        if tile > 0:
            before = pltpu.roll(value[z, var, :, at.start - LANES : at.start], 1, 1)
        if tile < tiles - 1:
            after = pltpu.roll(value[z, var, :, at.stop : at.stop + LANES], LANES - 1, 1)
        result[0].append(jnp.where(lane == 0, before, pltpu.roll(here, 1, 1)))
        result[1].append(jnp.where(lane == LANES - 1, after, pltpu.roll(here, LANES - 1, 1)))
        result[2].append(jnp.where(row == 0, zero, pltpu.roll(here, 1, 0)))
        result[3].append(jnp.where(row == y_count - 1, zero, pltpu.roll(here, y_count - 1, 0)))
    return result


def inplane(jacobians, value, z, tile, tiles):
    at = slice(tile * LANES, (tile + 1) * LANES)
    total = None
    for n, values in enumerate(neighbours(value, z, tile, tiles)):
        part = apply_block(block(jacobians, z, n, at=at), values)
        total = part if total is None else [a + b for a, b in zip(total, part)]
    return total


def halo_terms(jacobians, x_all, y_all, z, tile, tiles, gx, gy):
    y_count = jacobians.shape[-2]
    lane = lane_iota(y_count)
    row = row_iota(y_count)
    at = slice(tile * LANES, (tile + 1) * LANES)
    zero = jnp.zeros((y_count, LANES), F32)
    parts = []

    def columns(there, side, mask, to_lane):
        exists = (there >= 0) & (there < gx)
        device = jnp.clip(there, 0, gx - 1)
        values = []
        for var in range(VARS):
            j = z * VARS + var
            face = x_all[device, side, j // LANES]
            moved = pltpu.roll(face, (to_lane + LANES - j % LANES) % LANES, 1)
            values.append(jnp.where(mask & exists, moved, zero))
        return values

    def rows(there, side, mask):
        exists = (there >= 0) & (there < gy)
        device = jnp.clip(there, 0, gy - 1)
        return [
            jnp.where(mask & exists, y_all[device, side, z, var : var + 1, at], zero)
            for var in range(VARS)
        ]

    me_x, me_y = lax.axis_index("gx"), lax.axis_index("gy")
    if tile == 0:
        values = columns(me_x - 1, 1, lane == 0, 0)
        parts.append(apply_block(block(jacobians, z, 0, at=at), values))
    if tile == tiles - 1:
        values = columns(me_x + 1, 0, lane == LANES - 1, LANES - 1)
        parts.append(apply_block(block(jacobians, z, 1, at=at), values))
    if gy == 2:
        edge = jnp.where(me_y == 0, y_count - 1, 0)
        values = rows(1 - me_y, 0, row == edge)
        parts.append(apply_block(block(jacobians, z, 3 - me_y, at=at), values))
    else:
        parts.append(apply_block(block(jacobians, z, 2, at=at), rows(me_y - 1, 1, row == 0)))
        last = row == y_count - 1
        parts.append(apply_block(block(jacobians, z, 3, at=at), rows(me_y + 1, 0, last)))
    total = parts[0]
    for part in parts[1:]:
        total = [a + b for a, b in zip(total, part)]
    return total


def planes_of(ref, z, at):
    return [ref[z, var, :, at] for var in range(VARS)]


def solution(mesh):
    gz, gx, gy = (mesh.shape[a] for a in ("gz", "gx", "gy"))

    def body(right_side, previous, diag_inverse, jacobians):
        rhs = jnp.transpose(right_side, (0, 2, 1, 3))
        prev = jnp.transpose(previous, (0, 2, 1, 3))
        inv = jnp.transpose(diag_inverse, (0, 2, 3, 1, 4))
        jac = jnp.transpose(jacobians, (0, 2, 3, 4, 1, 5))
        nz, _, ny, nx = rhs.shape
        tiles = nx // LANES
        assert nx % LANES == 0
        spans = [slice(t * LANES, (t + 1) * LANES) for t in range(tiles)]
        plane = (VARS, ny, nx)
        volume = (nz, VARS, ny, nx)
        x_face = ((2, -(-nz * VARS // LANES), ny, LANES), F32)
        y_face = ((1 if gy == 2 else 2, nz, VARS, nx), F32)
        plane, volume = (plane, F32), (volume, F32)
        cells = nz * ny * nx
        block_flops = 2 * VARS * VARS * cells

        def exchange(x_face, y_face):
            return lax.all_gather(x_face, "gx"), lax.all_gather(y_face, "gy")

        def faces_kernel(prev_hbm, prev_ref, x_face, y_face, sem):
            copy = pltpu.make_async_copy(prev_hbm, prev_ref, sem)
            copy.start()
            copy.wait()
            write_faces(prev_ref, x_face, y_face, nz)

        def forward_plane(source, inv_ref, jac_ref, z, at, earlier):
            lagged = apply_block(block(jac_ref, z, 4, at=at), earlier)
            return apply_block(block(inv_ref, z, at=at), [a - b for a, b in zip(source, lagged)])

        def load_kernel(rhs_hbm, inv_hbm, jac_hbm, prev_ref, source_ref, inv_ref, jac_ref, rhs_ref, sems):
            def copies(z):
                pairs = ((jac_hbm, jac_ref), (rhs_hbm, rhs_ref), (inv_hbm, inv_ref))
                return [
                    pltpu.make_async_copy(far.at[z], near.at[z], sems.at[i, z])
                    for i, (far, near) in enumerate(pairs)
                ]

            for z in range(nz):
                for copy in copies(z):
                    copy.start()

            def step(z, carry):
                waits = copies(z)
                waits[0].wait()
                waits[1].wait()
                for tile, at in enumerate(spans):
                    lagged = inplane(jac_ref, prev_ref, z, tile, tiles)
                    source = planes_of(rhs_ref, z, at)
                    for var in range(VARS):
                        source_ref[z, var, :, at] = source[var] - lagged[var]
                waits[2].wait()
                return carry

            lax.fori_loop(0, nz, step, 0)

        def first_kernel(part_ref, inv_ref, jac_ref, x_all, y_all, source_ref, top_ref):
            for tile, at in enumerate(spans):

                def step(z, earlier, tile=tile, at=at):
                    extra = halo_terms(jac_ref, x_all, y_all, z, tile, tiles, gx, gy)
                    source = [a - b for a, b in zip(planes_of(part_ref, z, at), extra)]
                    for var in range(VARS):
                        source_ref[z, var, :, at] = source[var]
                    return tuple(forward_plane(source, inv_ref, jac_ref, z, at, earlier))

                zero = tuple(jnp.zeros((ny, LANES), F32) for _ in range(VARS))
                top = lax.fori_loop(0, nz, step, zero)
                for var in range(VARS):
                    top_ref[var, :, at] = top[var]

        def incoming(refs, at):
            total = [refs[0][var, :, at] for var in range(VARS)]
            for ref in refs[1:]:
                total = [a + ref[var, :, at] for var, a in enumerate(total)]
            return tuple(total)

        def forward_kernel(source_ref, inv_ref, jac_ref, *rest):
            came, top_ref = rest[:-1], rest[-1]
            for at in spans:

                def step(z, earlier, at=at):
                    source = planes_of(source_ref, z, at)
                    return tuple(forward_plane(source, inv_ref, jac_ref, z, at, earlier))

                top = lax.fori_loop(0, nz, step, incoming(came, at))
                for var in range(VARS):
                    top_ref[var, :, at] = top[var]

        def forward_last_kernel(source_ref, prev_ref, inv_ref, jac_ref, *rest):
            came, (sweep_ref, change_ref, x_face, y_face) = rest[:-4], rest[-4:]
            for at in spans:

                def step(z, earlier, at=at):
                    source = planes_of(source_ref, z, at)
                    result = forward_plane(source, inv_ref, jac_ref, z, at, earlier)
                    before = planes_of(prev_ref, z, at)
                    for var in range(VARS):
                        sweep_ref[z, var, :, at] = result[var]
                        change_ref[z, var, :, at] = result[var] - before[var]
                    return tuple(result)

                lax.fori_loop(0, nz, step, incoming(came, at))
            write_faces(change_ref, x_face, y_face, nz)

        def backward_plane(sweep, inner, inv_ref, jac_ref, z, at, later):
            change = apply_block(block(jac_ref, z, 5, at=at), later)
            change = apply_block(block(inv_ref, z, at=at), [a + b for a, b in zip(change, inner)])
            return [a - b for a, b in zip(sweep, change)]

        def inner_kernel(change_ref, jac_ref, inner_ref):
            def step(z, carry):
                for tile, at in enumerate(spans):
                    inner = inplane(jac_ref, change_ref, z, tile, tiles)
                    for var in range(VARS):
                        inner_ref[z, var, :, at] = inner[var]
                return carry

            lax.fori_loop(0, nz, step, 0)

        def turn_kernel(sweep_ref, part_ref, inv_ref, jac_ref, x_all, y_all, inner_ref, low_ref):
            for tile, at in enumerate(spans):

                def step(i, later, tile=tile, at=at):
                    z = nz - 1 - i
                    extra = halo_terms(jac_ref, x_all, y_all, z, tile, tiles, gx, gy)
                    inner = [a + b for a, b in zip(planes_of(part_ref, z, at), extra)]
                    for var in range(VARS):
                        inner_ref[z, var, :, at] = inner[var]
                    sweep = planes_of(sweep_ref, z, at)
                    return tuple(backward_plane(sweep, inner, inv_ref, jac_ref, z, at, later))

                zero = tuple(jnp.zeros((ny, LANES), F32) for _ in range(VARS))
                low = lax.fori_loop(0, nz, step, zero)
                for var in range(VARS):
                    low_ref[var, :, at] = low[var]

        def backward_kernel(sweep_ref, inner_ref, inv_ref, jac_ref, *rest):
            came, low_ref = rest[:-1], rest[-1]
            for at in spans:

                def step(i, later, at=at):
                    z = nz - 1 - i
                    sweep, inner = planes_of(sweep_ref, z, at), planes_of(inner_ref, z, at)
                    return tuple(backward_plane(sweep, inner, inv_ref, jac_ref, z, at, later))

                low = lax.fori_loop(0, nz, step, incoming(came, at))
                for var in range(VARS):
                    low_ref[var, :, at] = low[var]

        def update_kernel(sweep_ref, inner_ref, inv_ref, jac_ref, *rest):
            came, (out_hbm, held, sems) = rest[:-3], rest[-3:]

            def out_copy(z):
                return pltpu.make_async_copy(held.at[z], out_hbm.at[z], sems.at[z])

            def step(i, later):
                z = nz - 1 - i
                results = []
                for tile, at in enumerate(spans):
                    sweep, inner = planes_of(sweep_ref, z, at), planes_of(inner_ref, z, at)
                    result = backward_plane(sweep, inner, inv_ref, jac_ref, z, at, later[tile])
                    for var in range(VARS):
                        held[z, var, :, at] = result[var]
                    results.append(tuple(result))
                out_copy(z).start()
                return tuple(results)

            lax.fori_loop(0, nz, step, tuple(incoming(came, at) for at in spans))
            for z in range(nz):
                out_copy(z).wait()

        prev, *faces = call(
            faces_kernel,
            [volume, x_face, y_face],
            prev,
            flops=cells,
            in_hbm=(0,),
            scratch=[pltpu.SemaphoreType.DMA],
        )
        halo = exchange(*faces)
        part, inv, jac = call(
            load_kernel,
            [volume, (inv.shape, inv.dtype), (jac.shape, jac.dtype)],
            rhs,
            inv,
            jac,
            prev,
            flops=4 * block_flops,
            in_hbm=(0, 1, 2),
            scratch=[pltpu.VMEM(rhs.shape, F32), pltpu.SemaphoreType.DMA((3, nz))],
        )
        source, top = call(first_kernel, [volume, plane], part, inv, jac, *halo, flops=4 * block_flops)
        came = []
        for hop in range(gz - 1):
            if hop:
                (top,) = call(forward_kernel, [plane], source, inv, jac, *came, flops=2 * block_flops)
            came.append(lax.ppermute(top, "gz", [(hop, hop + 1)]))
        sweep, change, *faces = call(
            forward_last_kernel,
            [volume, volume, x_face, y_face],
            source,
            prev,
            inv,
            jac,
            *came,
            flops=2 * block_flops,
        )
        halo = exchange(*faces)
        (part,) = call(inner_kernel, [volume], change, jac, flops=4 * block_flops)
        inner, low = call(
            turn_kernel, [volume, plane], sweep, part, inv, jac, *halo, flops=4 * block_flops
        )
        came = []
        for hop in range(gz - 1, 0, -1):
            if came:
                (low,) = call(
                    backward_kernel, [plane], sweep, inner, inv, jac, *came, flops=2 * block_flops
                )
            came.append(lax.ppermute(low, "gz", [(hop, hop - 1)]))
        (update,) = call(
            update_kernel,
            [volume],
            sweep,
            inner,
            inv,
            jac,
            *came,
            flops=2 * block_flops,
            out_hbm=(0,),
            scratch=[pltpu.VMEM(volume[0], F32), pltpu.SemaphoreType.DMA((nz,))],
        )
        return jnp.transpose(update, (0, 2, 1, 3))

    placed = (
        P("gz", "gy", None, "gx"),
        P("gz", "gy", None, "gx"),
        P("gz", "gy", None, None, "gx"),
        P("gz", "gy", None, None, None, "gx"),
    )
    return jax.shard_map(
        body, mesh=mesh, in_specs=placed, out_specs=P("gz", "gy", None, "gx"), check_vma=False
    )
```

time: 78.9 us -> 82.9 us (1.051)
  blocking collectives: 0 us -> 22.4 us
  local copies, waits for them, and re-layouts: 11.2 us -> 0 us
  Pallas kernels: 17.4 us -> 28.3 us
  starting transfers between devices: 18.4 us -> 7.72 us
  waiting for transfers between devices: 31.2 us -> 24.2 us
    all_gather x0 -> x4, blocking collectives: none -> 22.4 us  [exchange(): return (lax.all_gather(x_face, 'gx'), lax.all_gather(y_face, 'gy'))]
    unnamed x11 -> x0, local copies, waits for them, and re-layouts: 11.2 us -> none
    pallas_call x9 -> x11, Pallas kernels: 17.4 us -> 28.3 us  [call(): pl.pallas_call(body, out_shape=shapes, in_specs=[far if i in in_hbm else...]
    ppermute x6 -> x0, starting transfers between devices: 10.8 us -> none  [the longest x2 4.61 us: exchange(): before_x = lax.ppermute(right, 'gx', up)]
    ppermute x6 -> x0, waiting for transfers between devices: 5.78 us -> none  [the longest x2 5.77 us: exchange(): after_x = lax.ppermute(left, 'gx', [(j, i) for i, j in up])]
    ppermute x3, waiting for transfers between devices: 23.2 us -> 22 us  [body(): came.append(lax.ppermute(low, 'gz', [(hop, hop - 1)]))]
  transfers between devices with their start and end apart: 12 -> 6, of which waited for: 4 -> 2; matrix products, arithmetic and copies ran while one was open for 0% -> 0% of each run, Pallas kernels for 0% -> 0%
where the time goes in v2:
time: 82.9 us; the launch traced here: 82.7 us
  Pallas kernels  28.3 us (34%)
  waiting for transfers between devices  24.2 us (29%)
  blocking collectives  22.4 us (27%)
  starting transfers between devices  7.72 us (9%)
    pallas_call x11, Pallas kernels, call(): pl.pallas_call(body, out_shape=shapes, in_specs=[far if i in in_hbm else...  28.3 us
    all_gather x4, blocking collectives, exchange(): return (lax.all_gather(x_face, 'gx'), lax.all_gather(y_face, 'gy'))  22.4 us
    ppermute x3, waiting for transfers between devices, body(): came.append(lax.ppermute(low, 'gz', [(hop, hop - 1)]))  22 us
    ppermute x3, starting transfers between devices, body(): came.append(lax.ppermute(top, 'gz', [(hop, hop + 1)]))  5.09 us
    ppermute x3, starting transfers between devices, body(): came.append(lax.ppermute(low, 'gz', [(hop, hop - 1)]))  2.63 us
    ppermute x3, waiting for transfers between devices, body(): came.append(lax.ppermute(top, 'gz', [(hop, hop + 1)]))  2.2 us
  transfers between devices with their start and end apart: 6, of which 2 were waited for; matrix products, arithmetic and copies ran while one was open for 0% of the time, Pallas kernels for 0%

profile of v2, /device:TPU:0, one launch (start us, length us, event | category | flops | bytes accessed | tf_op | source)
XLA Modules:
  0.0 82.7 jit_solution(13559316503759793904)
XLA Ops:
  0.0 1.5 %shard_map.46 = (f32[10,6,16,256]{3,2,1,0:T(8,128)S(1)}, f32[2,1,16,128]{3,2,1,0:T(8,128)S(1)}, f32[1,10,6,256]{3,2,1,0:T(8,128)S(1)}) custom-call(f32[10,6,16,256]{3,2,1,0:T(8,128)} %bitcast.15), custom_call_target="tpu_custom_call" | custom-call | flops 40960 | bytes 983040 | tf_op jit(solution)/shard_map/pallas_call | solution.py:21
  1.5 6.2 %all-gather = f32[8,1,16,128]{3,2,1,0:T(8,128)S(1)} all-gather(f32[2,1,16,128]{3,2,1,0:T(8,128)S(1)} %get-tuple-element.23), channel_id=2, replica_groups=mesh['gz'=4,'gx'=4,'gy'=2] {'gx'}, dimensions={0}, use_global_device_ids=true | all-gather | bytes 81920 | tf_op jit(solution)/shard_map/all_gather | solution.py:186
  7.7 5.6 %all-gather.1 = f32[2,10,6,256]{3,2,1,0:T(8,128)S(1)} all-gather(f32[1,10,6,256]{3,2,1,0:T(8,128)S(1)} %get-tuple-element.24), channel_id=3, replica_groups=mesh['gz'=4,'gx'=4,'gy'=2] {'gy'}, dimensions={0}, use_global_device_ids=true | all-gather | bytes 184320 | tf_op jit(solution)/shard_map/all_gather | solution.py:186
  13.3 7.6 %shard_map.47 = (f32[10,6,16,256]{3,2,1,0:T(8,128)S(1)}, bf16[10,6,6,16,256]{4,3,2,1,0:T(8,128)(2,1)S(1)}, bf16[10,6,6,6,16,256]{5,4,3,2,1,0:T(8,128)(2,1)S(1)}) custom-call(f32[10,6,16,256]{3,2,1,0:T(8,128)} %bitcast.16, bf16[10,6,6,16,256]{4,3,2,1,0:T(8,128)(2,1)} %bitcast.14, bf16[10,6,6,6,16,256]{5,4,3,2,1,0:T(8,128)(2,1)} %bitcast.13, ...), custom_call_target="tpu_custom_call" | custom-call | flops 11796480 | bytes 22609920 | tf_op jit(solution)/shard_map/pallas_call | solution.py:21
  21.0 4.1 %shard_map.48 = (f32[10,6,16,256]{3,2,1,0:T(8,128)S(1)}, f32[6,16,256]{2,1,0:T(8,128)S(1)}) custom-call(f32[10,6,16,256]{3,2,1,0:T(8,128)S(1)} %get-tuple-element.20.part_ref, bf16[10,6,6,16,256]{4,3,2,1,0:T(8,128)(2,1)S(1)} %get-tuple-element.21.inv_ref, bf16[10,6,6,6,16,256]{5,4,3,2,1,0:T(8,128)(2,1)S(1)} %get-tuple-element.22.jac_ref, ...), custom_call_target="tpu_custom_call" | custom-call | flops 11796480 | bytes 21815296 | tf_op jit(solution)/shard_map/pallas_call | solution.py:21
  25.0 3.8 %collective-permute-start = (f32[6,16,256]{2,1,0:T(8,128)S(1)}, f32[6,16,256]{2,1,0:T(8,128)S(1)}, u32[]{:S(2)}, u32[]{:S(2)}) collective-permute-start(f32[6,16,256]{2,1,0:T(8,128)S(1)} %get-tuple-element.26), channel_id=1, source_target_pairs={{0,8},{1,9},{2,10},{3,11},{4,12},{5,13},{6,14},{7,15}} | collective-permute-start | bytes 294920 | tf_op jit(solution)/shard_map/ppermute | solution.py:365
  28.8 2.2 %collective-permute-done.rest_0_ = f32[6,16,256]{2,1,0:T(8,128)S(1)} collective-permute-done((f32[6,16,256]{2,1,0:T(8,128)S(1)}, f32[6,16,256]{2,1,0:T(8,128)S(1)}, u32[]{:S(2)}, u32[]{:S(2)}) %collective-permute-start) | collective-permute-done | bytes 98336 | tf_op jit(solution)/shard_map/ppermute | solution.py:365
  31.0 1.2 %shard_map.49 = f32[6,16,256]{2,1,0:T(8,128)S(1)} custom-call(f32[10,6,16,256]{3,2,1,0:T(8,128)S(1)} %get-tuple-element.25.source_ref, bf16[10,6,6,16,256]{4,3,2,1,0:T(8,128)(2,1)S(1)} %get-tuple-element.21.inv_ref, bf16[10,6,6,6,16,256]{5,4,3,2,1,0:T(8,128)(2,1)S(1)} %get-tuple-element.22.jac_ref, f32[6,16,256]{2,1,0:T(8,128)S(1)} %collective-permute-done.rest_0_), custom_call_target="tpu_custom_call" | custom-call | flops 5898240 | bytes 21725184 | tf_op jit(solution)/shard_map/pallas_call | solution.py:21
  32.2 0.7 collective-permute-start.1
  32.9 0.0 collective-permute-done.1.rest_1_
  32.9 1.2 %shard_map.50 = f32[6,16,256]{2,1,0:T(8,128)S(1)} custom-call(f32[10,6,16,256]{3,2,1,0:T(8,128)S(1)} %get-tuple-element.25.source_ref, bf16[10,6,6,16,256]{4,3,2,1,0:T(8,128)(2,1)S(1)} %get-tuple-element.21.inv_ref, bf16[10,6,6,6,16,256]{5,4,3,2,1,0:T(8,128)(2,1)S(1)} %get-tuple-element.22.jac_ref, f32[6,16,256]{2,1,0:T(8,128)S(1)} %collective-permute-done.rest_0_, ...), custom_call_target="tpu_custom_call" | custom-call | flops 5898240 | bytes 21823488 | tf_op jit(solution)/shard_map/pallas_call | solution.py:21
  34.1 0.7 collective-permute-start.2
  34.8 0.0 collective-permute-done.2.rest_2_
  34.8 1.6 %shard_map.51 = (f32[10,6,16,256]{3,2,1,0:T(8,128)S(1)}, f32[10,6,16,256]{3,2,1,0:T(8,128)S(1)}, f32[2,1,16,128]{3,2,1,0:T(8,128)S(1)}, f32[1,10,6,256]{3,2,1,0:T(8,128)S(1)}) custom-call(f32[10,6,16,256]{3,2,1,0:T(8,128)S(1)} %get-tuple-element.25.source_ref, f32[10,6,16,256]{3,2,1,0:T(8,128)S(1)} %get-tuple-element.19.prev_ref, ...), custom_call_target="tpu_custom_call" | custom-call | flops 5898240 | bytes 22904832 | tf_op jit(solution)/shard_map/pallas_call | solution.py:21
  36.4 2.6 %shard_map.52.part_ref = f32[10,6,16,256]{3,2,1,0:T(8,128)S(1)} custom-call(f32[10,6,16,256]{3,2,1,0:T(8,128)S(1)} %get-tuple-element.28.change_ref, bf16[10,6,6,6,16,256]{5,4,3,2,1,0:T(8,128)(2,1)S(1)} %get-tuple-element.22.jac_ref), custom_call_target="tpu_custom_call" | custom-call | flops 11796480 | bytes 18677760 | tf_op jit(solution)/shard_map/pallas_call | solution.py:21
  39.0 5.2 %all-gather.2 = f32[8,1,16,128]{3,2,1,0:T(8,128)S(1)} all-gather(f32[2,1,16,128]{3,2,1,0:T(8,128)S(1)} %get-tuple-element.29), channel_id=4, replica_groups=mesh['gz'=4,'gx'=4,'gy'=2] {'gx'}, dimensions={0}, use_global_device_ids=true | all-gather | bytes 81920 | tf_op jit(solution)/shard_map/all_gather | solution.py:186
  44.3 5.3 %all-gather.3 = f32[2,10,6,256]{3,2,1,0:T(8,128)S(1)} all-gather(f32[1,10,6,256]{3,2,1,0:T(8,128)S(1)} %get-tuple-element.30), channel_id=5, replica_groups=mesh['gz'=4,'gx'=4,'gy'=2] {'gy'}, dimensions={0}, use_global_device_ids=true | all-gather | bytes 184320 | tf_op jit(solution)/shard_map/all_gather | solution.py:186
  49.6 3.9 %shard_map.53 = (f32[10,6,16,256]{3,2,1,0:T(8,128)S(1)}, f32[6,16,256]{2,1,0:T(8,128)S(1)}) custom-call(f32[10,6,16,256]{3,2,1,0:T(8,128)S(1)} %get-tuple-element.27.sweep_ref, f32[10,6,16,256]{3,2,1,0:T(8,128)S(1)} %shard_map.52.part_ref, bf16[10,6,6,16,256]{4,3,2,1,0:T(8,128)(2,1)S(1)} %get-tuple-element.21.inv_ref, ...), custom_call_target="tpu_custom_call" | custom-call | flops 11796480 | bytes 22798336 | tf_op jit(solution)/shard_map/pallas_call | solution.py:21
  53.6 0.7 collective-permute-start.3
  54.2 0.0 collective-permute-done.3.rest_0_
  54.2 1.2 %shard_map.54 = f32[6,16,256]{2,1,0:T(8,128)S(1)} custom-call(f32[10,6,16,256]{3,2,1,0:T(8,128)S(1)} %get-tuple-element.27.sweep_ref, f32[10,6,16,256]{3,2,1,0:T(8,128)S(1)} %get-tuple-element.31.inner_ref, bf16[10,6,6,16,256]{4,3,2,1,0:T(8,128)(2,1)S(1)} %get-tuple-element.21.inv_ref, bf16[10,6,6,6,16,256]{5,4,3,2,1,0:T(8,128)(2,1)S(1)} %get-tuple-element.22.jac_ref, ...), custom_call_target="tpu_custom_call" | custom-call | flops 5898240 | bytes 22708224 | tf_op jit(solution)/shard_map/pallas_call | solution.py:21
  55.5 0.7 collective-permute-start.4
  56.2 0.0 collective-permute-done.4.rest_1_
  56.2 1.2 %shard_map.55 = f32[6,16,256]{2,1,0:T(8,128)S(1)} custom-call(f32[10,6,16,256]{3,2,1,0:T(8,128)S(1)} %get-tuple-element.27.sweep_ref, f32[10,6,16,256]{3,2,1,0:T(8,128)S(1)} %get-tuple-element.31.inner_ref, bf16[10,6,6,16,256]{4,3,2,1,0:T(8,128)(2,1)S(1)} %get-tuple-element.21.inv_ref, bf16[10,6,6,6,16,256]{5,4,3,2,1,0:T(8,128)(2,1)S(1)} %get-tuple-element.22.jac_ref, ...), custom_call_target="tpu_custom_call" | custom-call | flops 5898240 | bytes 22806528 | tf_op jit(solution)/shard_map/pallas_call | solution.py:21
  57.4 1.3 %collective-permute-start.5 = (f32[6,16,256]{2,1,0:T(8,128)S(1)}, f32[6,16,256]{2,1,0:T(8,128)S(1)}, u32[]{:S(2)}, u32[]{:S(2)}) collective-permute-start(f32[6,16,256]{2,1,0:T(8,128)S(1)} %shard_map.55), channel_id=1, source_target_pairs={{8,0},{9,1},{10,2},{11,3},{12,4},{13,5},{14,6},{15,7}} | collective-permute-start | bytes 294920 | tf_op jit(solution)/shard_map/ppermute | solution.py:387
  58.7 22.0 %collective-permute-done.5.rest_2_ = f32[6,16,256]{2,1,0:T(8,128)S(1)} collective-permute-done((f32[6,16,256]{2,1,0:T(8,128)S(1)}, f32[6,16,256]{2,1,0:T(8,128)S(1)}, u32[]{:S(2)}, u32[]{:S(2)}) %collective-permute-start.5) | collective-permute-done | bytes 98336 | tf_op jit(solution)/shard_map/ppermute | solution.py:387
  80.7 2.0 %shard_map.56 = f32[10,6,16,256]{3,2,1,0:T(8,128)} custom-call(f32[10,6,16,256]{3,2,1,0:T(8,128)S(1)} %get-tuple-element.27.sweep_ref, f32[10,6,16,256]{3,2,1,0:T(8,128)S(1)} %get-tuple-element.31.inner_ref, bf16[10,6,6,16,256]{4,3,2,1,0:T(8,128)(2,1)S(1)} %get-tuple-element.21.inv_ref, bf16[10,6,6,6,16,256]{5,4,3,2,1,0:T(8,128)(2,1)S(1)} %get-tuple-element.22.jac_ref, ...), custom_call_target="tpu_custom_call" | custom-call | flops 5898240 | bytes 22904832 | tf_op jit(solution)/shard_map/pallas_call | solution.py:21
Async XLA Ops:
  25.0 6.0 %collective-permute-start = (f32[6,16,256]{2,1,0:T(8,128)S(1)}, f32[6,16,256]{2,1,0:T(8,128)S(1)}, u32[]{:S(2)}, u32[]{:S(2)}) collective-permute-start(f32[6,16,256]{2,1,0:T(8,128)S(1)} %get-tuple-element.26), channel_id=1, source_target_pairs={{0,8},{1,9},{2,10},{3,11},{4,12},{5,13},{6,14},{7,15}} | collective-permute-start | bytes 294920 | tf_op jit(solution)/shard_map/ppermute | solution.py:365
  32.2 0.7 collective-permute-start.1
  34.1 0.7 collective-permute-start.2
  53.6 0.7 collective-permute-start.3
  55.5 0.7 collective-permute-start.4
  57.4 23.3 %collective-permute-start.5 = (f32[6,16,256]{2,1,0:T(8,128)S(1)}, f32[6,16,256]{2,1,0:T(8,128)S(1)}, u32[]{:S(2)}, u32[]{:S(2)}) collective-permute-start(f32[6,16,256]{2,1,0:T(8,128)S(1)} %shard_map.55), channel_id=1, source_target_pairs={{8,0},{9,1},{10,2},{11,3},{12,4},{13,5},{14,6},{15,7}} | collective-permute-start | bytes 294920 | tf_op jit(solution)/shard_map/ppermute | solution.py:387

commit v3 on v2

--- a/solution.py
+++ b/solution.py
@@ -80,81 +80,64 @@
                 y_face[1, z, var : var + 1, :] = value[z, var, y_count - 1 : y_count, :]
 
 
-def neighbours(value, z, tile, tiles):
+def halo_reader(x_all, y_rows, gx, gy):
+    me_x = lax.axis_index("gx")
+
+    def column(there, side, to_lane):
+        exists = (there >= 0) & (there < gx)
+        device = jnp.clip(there, 0, gx - 1)
+
+        def read(z, var):
+            j = z * VARS + var
+            face = x_all[device, side, j // LANES]
+            moved = pltpu.roll(face, (to_lane + LANES - j % LANES) % LANES, 1)
+            return jnp.where(exists, moved, jnp.zeros_like(moved))
+
+        return read
+
+    def row(which):
+        def read(z, var, at):
+            if len(y_rows) > 1:
+                return y_rows[which][z, var : var + 1, at]
+            here = y_rows[0][z, var : var + 1, at]
+            return jnp.where(lax.axis_index("gy") == 1 - which, here, jnp.zeros_like(here))
+
+        return read
+
+    return column(me_x - 1, 1, 0), column(me_x + 1, 0, LANES - 1), row(0), row(1)
+
+
+def neighbours(value, z, tile, tiles, halo):
     y_count = value.shape[2]
     lane = lane_iota(y_count)
     row = row_iota(y_count)
     at = slice(tile * LANES, (tile + 1) * LANES)
-    zero = jnp.zeros((y_count, LANES), F32)
     result = ([], [], [], [])
     for var in range(VARS):
         here = value[z, var, :, at]
-        before, after = zero, zero
         if tile > 0:
             before = pltpu.roll(value[z, var, :, at.start - LANES : at.start], 1, 1)
+        else:
+            before = halo[0](z, var)
         if tile < tiles - 1:
             after = pltpu.roll(value[z, var, :, at.stop : at.stop + LANES], LANES - 1, 1)
+        else:
+            after = halo[1](z, var)
         result[0].append(jnp.where(lane == 0, before, pltpu.roll(here, 1, 1)))
         result[1].append(jnp.where(lane == LANES - 1, after, pltpu.roll(here, LANES - 1, 1)))
-        result[2].append(jnp.where(row == 0, zero, pltpu.roll(here, 1, 0)))
-        result[3].append(jnp.where(row == y_count - 1, zero, pltpu.roll(here, y_count - 1, 0)))
+        result[2].append(jnp.where(row == 0, halo[2](z, var, at), pltpu.roll(here, 1, 0)))
+        result[3].append(
+            jnp.where(row == y_count - 1, halo[3](z, var, at), pltpu.roll(here, y_count - 1, 0))
+        )
     return result
 
 
-def inplane(jacobians, value, z, tile, tiles):
+def inplane(jacobians, value, z, tile, tiles, halo):
     at = slice(tile * LANES, (tile + 1) * LANES)
     total = None
-    for n, values in enumerate(neighbours(value, z, tile, tiles)):
+    for n, values in enumerate(neighbours(value, z, tile, tiles, halo)):
         part = apply_block(block(jacobians, z, n, at=at), values)
         total = part if total is None else [a + b for a, b in zip(total, part)]
-    return total
-
-
-def halo_terms(jacobians, x_all, y_all, z, tile, tiles, gx, gy):
-    y_count = jacobians.shape[-2]
-    lane = lane_iota(y_count)
-    row = row_iota(y_count)
-    at = slice(tile * LANES, (tile + 1) * LANES)
-    zero = jnp.zeros((y_count, LANES), F32)
-    parts = []
-
-    def columns(there, side, mask, to_lane):
-        exists = (there >= 0) & (there < gx)
-        device = jnp.clip(there, 0, gx - 1)
-        values = []
-        for var in range(VARS):
-            j = z * VARS + var
-            face = x_all[device, side, j // LANES]
-            moved = pltpu.roll(face, (to_lane + LANES - j % LANES) % LANES, 1)
-            values.append(jnp.where(mask & exists, moved, zero))
-        return values
-
-    def rows(there, side, mask):
-        exists = (there >= 0) & (there < gy)
-        device = jnp.clip(there, 0, gy - 1)
-        return [
-            jnp.where(mask & exists, y_all[device, side, z, var : var + 1, at], zero)
-            for var in range(VARS)
-        ]
-
-    me_x, me_y = lax.axis_index("gx"), lax.axis_index("gy")
-    if tile == 0:
-        values = columns(me_x - 1, 1, lane == 0, 0)
-        parts.append(apply_block(block(jacobians, z, 0, at=at), values))
-    if tile == tiles - 1:
-        values = columns(me_x + 1, 0, lane == LANES - 1, LANES - 1)
-        parts.append(apply_block(block(jacobians, z, 1, at=at), values))
-    if gy == 2:
-        edge = jnp.where(me_y == 0, y_count - 1, 0)
-        values = rows(1 - me_y, 0, row == edge)
-        parts.append(apply_block(block(jacobians, z, 3 - me_y, at=at), values))
-    else:
-        parts.append(apply_block(block(jacobians, z, 2, at=at), rows(me_y - 1, 1, row == 0)))
-        last = row == y_count - 1
-        parts.append(apply_block(block(jacobians, z, 3, at=at), rows(me_y + 1, 0, last)))
-    total = parts[0]
-    for part in parts[1:]:
-        total = [a + b for a, b in zip(total, part)]
     return total
 
 
@@ -183,7 +166,15 @@
         block_flops = 2 * VARS * VARS * cells
 
         def exchange(x_face, y_face):
-            return lax.all_gather(x_face, "gx"), lax.all_gather(y_face, "gy")
+            if gy == 2:
+                rows = [lax.ppermute(y_face[0], "gy", [(0, 1), (1, 0)])]
+            else:
+                up = [(i, i + 1) for i in range(gy - 1)]
+                rows = [
+                    lax.ppermute(y_face[1], "gy", up),
+                    lax.ppermute(y_face[0], "gy", [(j, i) for i, j in up]),
+                ]
+            return lax.all_gather(x_face, "gx"), *rows
 
         def faces_kernel(prev_hbm, prev_ref, x_face, y_face, sem):
             copy = pltpu.make_async_copy(prev_hbm, prev_ref, sem)
@@ -195,7 +186,10 @@
             lagged = apply_block(block(jac_ref, z, 4, at=at), earlier)
             return apply_block(block(inv_ref, z, at=at), [a - b for a, b in zip(source, lagged)])
 
-        def load_kernel(rhs_hbm, inv_hbm, jac_hbm, prev_ref, source_ref, inv_ref, jac_ref, rhs_ref, sems):
+        def first_kernel(rhs_hbm, inv_hbm, jac_hbm, prev_ref, x_all, *rest):
+            y_rows, (source_ref, top_ref, inv_ref, jac_ref, rhs_ref, sems) = rest[:-6], rest[-6:]
+            halo = halo_reader(x_all, y_rows, gx, gy)
+
             def copies(z):
                 pairs = ((jac_hbm, jac_ref), (rhs_hbm, rhs_ref), (inv_hbm, inv_ref))
                 return [
@@ -207,34 +201,24 @@
                 for copy in copies(z):
                     copy.start()
 
-            def step(z, carry):
-                waits = copies(z)
-                waits[0].wait()
-                waits[1].wait()
+            def step(z, earlier):
+                for copy in copies(z):
+                    copy.wait()
+                results = []
                 for tile, at in enumerate(spans):
-                    lagged = inplane(jac_ref, prev_ref, z, tile, tiles)
-                    source = planes_of(rhs_ref, z, at)
-                    for var in range(VARS):
-                        source_ref[z, var, :, at] = source[var] - lagged[var]
-                waits[2].wait()
-                return carry
-
-            lax.fori_loop(0, nz, step, 0)
-
-        def first_kernel(part_ref, inv_ref, jac_ref, x_all, y_all, source_ref, top_ref):
-            for tile, at in enumerate(spans):
-
-                def step(z, earlier, tile=tile, at=at):
-                    extra = halo_terms(jac_ref, x_all, y_all, z, tile, tiles, gx, gy)
-                    source = [a - b for a, b in zip(planes_of(part_ref, z, at), extra)]
+                    lagged = inplane(jac_ref, prev_ref, z, tile, tiles, halo)
+                    source = [a - b for a, b in zip(planes_of(rhs_ref, z, at), lagged)]
                     for var in range(VARS):
                         source_ref[z, var, :, at] = source[var]
-                    return tuple(forward_plane(source, inv_ref, jac_ref, z, at, earlier))
-
-                zero = tuple(jnp.zeros((ny, LANES), F32) for _ in range(VARS))
-                top = lax.fori_loop(0, nz, step, zero)
+                    result = forward_plane(source, inv_ref, jac_ref, z, at, earlier[tile])
+                    results.append(tuple(result))
+                return tuple(results)
+
+            zero = tuple(jnp.zeros((ny, LANES), F32) for _ in range(VARS))
+            top = lax.fori_loop(0, nz, step, (zero,) * tiles)
+            for tile, at in enumerate(spans):
                 for var in range(VARS):
-                    top_ref[var, :, at] = top[var]
+                    top_ref[var, :, at] = top[tile][var]
 
         def incoming(refs, at):
             total = [refs[0][var, :, at] for var in range(VARS)]
@@ -275,23 +259,14 @@
             change = apply_block(block(inv_ref, z, at=at), [a + b for a, b in zip(change, inner)])
             return [a - b for a, b in zip(sweep, change)]
 
-        def inner_kernel(change_ref, jac_ref, inner_ref):
-            def step(z, carry):
-                for tile, at in enumerate(spans):
-                    inner = inplane(jac_ref, change_ref, z, tile, tiles)
-                    for var in range(VARS):
-                        inner_ref[z, var, :, at] = inner[var]
-                return carry
-
-            lax.fori_loop(0, nz, step, 0)
-
-        def turn_kernel(sweep_ref, part_ref, inv_ref, jac_ref, x_all, y_all, inner_ref, low_ref):
+        def turn_kernel(sweep_ref, change_ref, inv_ref, jac_ref, x_all, *rest):
+            y_rows, (inner_ref, low_ref) = rest[:-2], rest[-2:]
+            halo = halo_reader(x_all, y_rows, gx, gy)
             for tile, at in enumerate(spans):
 
                 def step(i, later, tile=tile, at=at):
                     z = nz - 1 - i
-                    extra = halo_terms(jac_ref, x_all, y_all, z, tile, tiles, gx, gy)
-                    inner = [a + b for a, b in zip(planes_of(part_ref, z, at), extra)]
+                    inner = inplane(jac_ref, change_ref, z, tile, tiles, halo)
                     for var in range(VARS):
                         inner_ref[z, var, :, at] = inner[var]
                     sweep = planes_of(sweep_ref, z, at)
@@ -346,18 +321,18 @@
             scratch=[pltpu.SemaphoreType.DMA],
         )
         halo = exchange(*faces)
-        part, inv, jac = call(
-            load_kernel,
-            [volume, (inv.shape, inv.dtype), (jac.shape, jac.dtype)],
+        source, top, inv, jac = call(
+            first_kernel,
+            [volume, plane, (inv.shape, inv.dtype), (jac.shape, jac.dtype)],
             rhs,
             inv,
             jac,
             prev,
-            flops=4 * block_flops,
+            *halo,
+            flops=6 * block_flops,
             in_hbm=(0, 1, 2),
             scratch=[pltpu.VMEM(rhs.shape, F32), pltpu.SemaphoreType.DMA((3, nz))],
         )
-        source, top = call(first_kernel, [volume, plane], part, inv, jac, *halo, flops=4 * block_flops)
         came = []
         for hop in range(gz - 1):
             if hop:
@@ -374,9 +349,8 @@
             flops=2 * block_flops,
         )
         halo = exchange(*faces)
-        (part,) = call(inner_kernel, [volume], change, jac, flops=4 * block_flops)
         inner, low = call(
-            turn_kernel, [volume, plane], sweep, part, inv, jac, *halo, flops=4 * block_flops
+            turn_kernel, [volume, plane], sweep, change, inv, jac, *halo, flops=6 * block_flops
         )
         came = []
         for hop in range(gz - 1, 0, -1):

time: 82.9 us -> 69.6 us (0.84)
  blocking collectives: 22.4 us -> 10.5 us
  Pallas kernels: 28.3 us -> 22.6 us
  starting transfers between devices: 7.72 us -> 11 us
  waiting for transfers between devices: 24.2 us -> 25.1 us
    all_gather x4 -> x2, blocking collectives: 22.4 us -> 10.5 us  [exchange(): return (lax.all_gather(x_face, 'gx'), *rows)]
    pallas_call x11 -> x9, Pallas kernels: 28.3 us -> 22.6 us  [call(): pl.pallas_call(body, out_shape=shapes, in_specs=[far if i in in_hbm else...]
    ppermute x0 -> x2, starting transfers between devices: none -> 3.6 us  [exchange(): rows = [lax.ppermute(y_face[0], 'gy', [(0, 1), (1, 0)])]]
  transfers between devices with their start and end apart: 6 -> 8, of which waited for: 2 -> 2; matrix products, arithmetic and copies ran while one was open for 0% -> 0% of each run, Pallas kernels for 0% -> 0%
where the time goes in v3:
time: 69.6 us; the launch traced here: 69.4 us
  waiting for transfers between devices  25.1 us (36%)
  Pallas kernels  22.6 us (32%)
  starting transfers between devices  11 us (16%)
  blocking collectives  10.5 us (15%)
    pallas_call x9, Pallas kernels, call(): pl.pallas_call(body, out_shape=shapes, in_specs=[far if i in in_hbm else...  22.6 us
    ppermute x3, waiting for transfers between devices, body(): came.append(lax.ppermute(low, 'gz', [(hop, hop - 1)]))  22.5 us
    all_gather x2, blocking collectives, exchange(): return (lax.all_gather(x_face, 'gx'), *rows)  10.5 us
    ppermute x3, starting transfers between devices, body(): came.append(lax.ppermute(top, 'gz', [(hop, hop + 1)]))  4.82 us
    ppermute x2, starting transfers between devices, exchange(): rows = [lax.ppermute(y_face[0], 'gy', [(0, 1), (1, 0)])]  3.6 us
    ppermute x3, starting transfers between devices, body(): came.append(lax.ppermute(low, 'gz', [(hop, hop - 1)]))  2.63 us
    ppermute x3, waiting for transfers between devices, body(): came.append(lax.ppermute(top, 'gz', [(hop, hop + 1)]))  2.54 us
  transfers between devices with their start and end apart: 8, of which 2 were waited for; matrix products, arithmetic and copies ran while one was open for 0% of the time, Pallas kernels for 0%

profile of v3, /device:TPU:0, one launch (start us, length us, event | category | flops | bytes accessed | tf_op | source)
XLA Modules:
  0.0 69.4 jit_solution(4559174034886020307)
XLA Ops:
  0.0 1.5 %shard_map.46 = (f32[10,6,16,256]{3,2,1,0:T(8,128)S(1)}, f32[2,1,16,128]{3,2,1,0:T(8,128)S(1)}, f32[1,10,6,256]{3,2,1,0:T(8,128)S(1)}) custom-call(f32[10,6,16,256]{3,2,1,0:T(8,128)} %bitcast.15), custom_call_target="tpu_custom_call" | custom-call | flops 40960 | bytes 983040 | tf_op jit(solution)/shard_map/pallas_call | solution.py:21
  1.5 3.0 %collective-permute-start = (f32[10,6,256]{2,1,0:T(8,128)S(1)}, f32[10,6,256]{2,1,0:T(8,128)S(1)}, u32[]{:S(2)}, u32[]{:S(2)}) collective-permute-start(f32[10,6,256]{2,1,0:T(8,128)S(1)} %bitcast.12), channel_id=1, source_target_pairs={{0,1},{1,0},{2,3},{3,2},{4,5},{5,4},{6,7},{7,6},{8,9},{9,8},{10,11... | collective-permute-start | bytes 184328 | tf_op jit(solution)/shard_map/ppermute | solution.py:170
  4.5 5.2 %all-gather = f32[8,1,16,128]{3,2,1,0:T(8,128)S(1)} all-gather(f32[2,1,16,128]{3,2,1,0:T(8,128)S(1)} %get-tuple-element.19), channel_id=2, replica_groups=mesh['gz'=4,'gx'=4,'gy'=2] {'gx'}, dimensions={0}, use_global_device_ids=true | all-gather | bytes 81920 | tf_op jit(solution)/shard_map/all_gather | solution.py:177
  9.8 0.0 collective-permute-done.rest_0_
  9.8 7.8 %shard_map.47 = (f32[10,6,16,256]{3,2,1,0:T(8,128)S(1)}, f32[6,16,256]{2,1,0:T(8,128)S(1)}, bf16[10,6,6,16,256]{4,3,2,1,0:T(8,128)(2,1)S(1)}, bf16[10,6,6,6,16,256]{5,4,3,2,1,0:T(8,128)(2,1)S(1)}) custom-call(f32[10,6,16,256]{3,2,1,0:T(8,128)} %bitcast.16, bf16[10,6,6,16,256]{4,3,2,1,0:T(8,128)(2,1)} %bitcast.14, bf16[10,6,6,6,16,256]{5,4,3,2,1,0:T(8,128)(2,1)} %bitcast.13, ...), custom_call_target="tpu_custom_call" | custom-call | flops 17694720 | bytes 22736896 | tf_op jit(solution)/shard_map/pallas_call | solution.py:21
  17.6 3.5 %collective-permute-start.1 = (f32[6,16,256]{2,1,0:T(8,128)S(1)}, f32[6,16,256]{2,1,0:T(8,128)S(1)}, u32[]{:S(2)}, u32[]{:S(2)}) collective-permute-start(f32[6,16,256]{2,1,0:T(8,128)S(1)} %get-tuple-element.24), channel_id=1, source_target_pairs={{0,8},{1,9},{2,10},{3,11},{4,12},{5,13},{6,14},{7,15}} | collective-permute-start | bytes 294920 | tf_op jit(solution)/shard_map/ppermute | solution.py:340
  21.1 2.5 %collective-permute-done.1.rest_0_ = f32[6,16,256]{2,1,0:T(8,128)S(1)} collective-permute-done((f32[6,16,256]{2,1,0:T(8,128)S(1)}, f32[6,16,256]{2,1,0:T(8,128)S(1)}, u32[]{:S(2)}, u32[]{:S(2)}) %collective-permute-start.1) | collective-permute-done | bytes 98336 | tf_op jit(solution)/shard_map/ppermute | solution.py:340
  23.6 1.2 %shard_map.48 = f32[6,16,256]{2,1,0:T(8,128)S(1)} custom-call(f32[10,6,16,256]{3,2,1,0:T(8,128)S(1)} %get-tuple-element.21.source_ref, bf16[10,6,6,16,256]{4,3,2,1,0:T(8,128)(2,1)S(1)} %get-tuple-element.22.inv_ref, bf16[10,6,6,6,16,256]{5,4,3,2,1,0:T(8,128)(2,1)S(1)} %get-tuple-element.23.jac_ref, f32[6,16,256]{2,1,0:T(8,128)S(1)} %collective-permute-done.1.rest_0_), custom_call_target="tpu_custom_call" | custom-call | flops 5898240 | bytes 21725184 | tf_op jit(solution)/shard_map/pallas_call | solution.py:21
  24.8 0.7 collective-permute-start.2
  25.5 0.0 collective-permute-done.2.rest_1_
  25.5 1.2 %shard_map.49 = f32[6,16,256]{2,1,0:T(8,128)S(1)} custom-call(f32[10,6,16,256]{3,2,1,0:T(8,128)S(1)} %get-tuple-element.21.source_ref, bf16[10,6,6,16,256]{4,3,2,1,0:T(8,128)(2,1)S(1)} %get-tuple-element.22.inv_ref, bf16[10,6,6,6,16,256]{5,4,3,2,1,0:T(8,128)(2,1)S(1)} %get-tuple-element.23.jac_ref, f32[6,16,256]{2,1,0:T(8,128)S(1)} %collective-permute-done.1.rest_0_, ...), custom_call_target="tpu_custom_call" | custom-call | flops 5898240 | bytes 21823488 | tf_op jit(solution)/shard_map/pallas_call | solution.py:21
  26.7 0.7 collective-permute-start.3
  27.4 0.0 collective-permute-done.3.rest_2_
  27.4 1.6 %shard_map.50 = (f32[10,6,16,256]{3,2,1,0:T(8,128)S(1)}, f32[10,6,16,256]{3,2,1,0:T(8,128)S(1)}, f32[2,1,16,128]{3,2,1,0:T(8,128)S(1)}, f32[1,10,6,256]{3,2,1,0:T(8,128)S(1)}) custom-call(f32[10,6,16,256]{3,2,1,0:T(8,128)S(1)} %get-tuple-element.21.source_ref, f32[10,6,16,256]{3,2,1,0:T(8,128)S(1)} %get-tuple-element.18.prev_ref, ...), custom_call_target="tpu_custom_call" | custom-call | flops 5898240 | bytes 22904832 | tf_op jit(solution)/shard_map/pallas_call | solution.py:21
  29.0 0.6 collective-permute-start.4
  29.6 5.2 %all-gather.1 = f32[8,1,16,128]{3,2,1,0:T(8,128)S(1)} all-gather(f32[2,1,16,128]{3,2,1,0:T(8,128)S(1)} %get-tuple-element.27), channel_id=3, replica_groups=mesh['gz'=4,'gx'=4,'gy'=2] {'gx'}, dimensions={0}, use_global_device_ids=true | all-gather | bytes 81920 | tf_op jit(solution)/shard_map/all_gather | solution.py:177
  34.9 0.0 collective-permute-done.4.rest_0_
  34.9 4.8 %shard_map.51 = (f32[10,6,16,256]{3,2,1,0:T(8,128)S(1)}, f32[6,16,256]{2,1,0:T(8,128)S(1)}) custom-call(f32[10,6,16,256]{3,2,1,0:T(8,128)S(1)} %get-tuple-element.25.sweep_ref, f32[10,6,16,256]{3,2,1,0:T(8,128)S(1)} %get-tuple-element.26.change_ref, bf16[10,6,6,16,256]{4,3,2,1,0:T(8,128)(2,1)S(1)} %get-tuple-element.22.inv_ref, ...), custom_call_target="tpu_custom_call" | custom-call | flops 17694720 | bytes 22736896 | tf_op jit(solution)/shard_map/pallas_call | solution.py:21
  39.7 0.7 collective-permute-start.5
  40.4 0.0 collective-permute-done.5.rest_0_
  40.4 1.2 %shard_map.52 = f32[6,16,256]{2,1,0:T(8,128)S(1)} custom-call(f32[10,6,16,256]{3,2,1,0:T(8,128)S(1)} %get-tuple-element.25.sweep_ref, f32[10,6,16,256]{3,2,1,0:T(8,128)S(1)} %get-tuple-element.29.inner_ref, bf16[10,6,6,16,256]{4,3,2,1,0:T(8,128)(2,1)S(1)} %get-tuple-element.22.inv_ref, bf16[10,6,6,6,16,256]{5,4,3,2,1,0:T(8,128)(2,1)S(1)} %get-tuple-element.23.jac_ref, ...), custom_call_target="tpu_custom_call" | custom-call | flops 5898240 | bytes 22708224 | tf_op jit(solution)/shard_map/pallas_call | solution.py:21
  41.6 0.7 collective-permute-start.6
  42.3 0.0 collective-permute-done.6.rest_1_
  42.3 1.2 %shard_map.53 = f32[6,16,256]{2,1,0:T(8,128)S(1)} custom-call(f32[10,6,16,256]{3,2,1,0:T(8,128)S(1)} %get-tuple-element.25.sweep_ref, f32[10,6,16,256]{3,2,1,0:T(8,128)S(1)} %get-tuple-element.29.inner_ref, bf16[10,6,6,16,256]{4,3,2,1,0:T(8,128)(2,1)S(1)} %get-tuple-element.22.inv_ref, bf16[10,6,6,6,16,256]{5,4,3,2,1,0:T(8,128)(2,1)S(1)} %get-tuple-element.23.jac_ref, ...), custom_call_target="tpu_custom_call" | custom-call | flops 5898240 | bytes 22806528 | tf_op jit(solution)/shard_map/pallas_call | solution.py:21
  43.6 1.3 %collective-permute-start.7 = (f32[6,16,256]{2,1,0:T(8,128)S(1)}, f32[6,16,256]{2,1,0:T(8,128)S(1)}, u32[]{:S(2)}, u32[]{:S(2)}) collective-permute-start(f32[6,16,256]{2,1,0:T(8,128)S(1)} %shard_map.53), channel_id=1, source_target_pairs={{8,0},{9,1},{10,2},{11,3},{12,4},{13,5},{14,6},{15,7}} | collective-permute-start | bytes 294920 | tf_op jit(solution)/shard_map/ppermute | solution.py:361
  44.9 22.5 %collective-permute-done.7.rest_2_ = f32[6,16,256]{2,1,0:T(8,128)S(1)} collective-permute-done((f32[6,16,256]{2,1,0:T(8,128)S(1)}, f32[6,16,256]{2,1,0:T(8,128)S(1)}, u32[]{:S(2)}, u32[]{:S(2)}) %collective-permute-start.7) | collective-permute-done | bytes 98336 | tf_op jit(solution)/shard_map/ppermute | solution.py:361
  67.4 2.0 %shard_map.54 = f32[10,6,16,256]{3,2,1,0:T(8,128)} custom-call(f32[10,6,16,256]{3,2,1,0:T(8,128)S(1)} %get-tuple-element.25.sweep_ref, f32[10,6,16,256]{3,2,1,0:T(8,128)S(1)} %get-tuple-element.29.inner_ref, bf16[10,6,6,16,256]{4,3,2,1,0:T(8,128)(2,1)S(1)} %get-tuple-element.22.inv_ref, bf16[10,6,6,6,16,256]{5,4,3,2,1,0:T(8,128)(2,1)S(1)} %get-tuple-element.23.jac_ref, ...), custom_call_target="tpu_custom_call" | custom-call | flops 5898240 | bytes 22904832 | tf_op jit(solution)/shard_map/pallas_call | solution.py:21
Async XLA Ops:
  1.5 8.2 %collective-permute-start = (f32[10,6,256]{2,1,0:T(8,128)S(1)}, f32[10,6,256]{2,1,0:T(8,128)S(1)}, u32[]{:S(2)}, u32[]{:S(2)}) collective-permute-start(f32[10,6,256]{2,1,0:T(8,128)S(1)} %bitcast.12), channel_id=1, source_target_pairs={{0,1},{1,0},{2,3},{3,2},{4,5},{5,4},{6,7},{7,6},{8,9},{9,8},{10,11... | collective-permute-start | bytes 184328 | tf_op jit(solution)/shard_map/ppermute | solution.py:170
  17.6 6.0 %collective-permute-start.1 = (f32[6,16,256]{2,1,0:T(8,128)S(1)}, f32[6,16,256]{2,1,0:T(8,128)S(1)}, u32[]{:S(2)}, u32[]{:S(2)}) collective-permute-start(f32[6,16,256]{2,1,0:T(8,128)S(1)} %get-tuple-element.24), channel_id=1, source_target_pairs={{0,8},{1,9},{2,10},{3,11},{4,12},{5,13},{6,14},{7,15}} | collective-permute-start | bytes 294920 | tf_op jit(solution)/shard_map/ppermute | solution.py:340
  24.8 0.7 collective-permute-start.2
  26.7 0.7 collective-permute-start.3
  29.0 5.8 %collective-permute-start.4 = (f32[10,6,256]{2,1,0:T(8,128)S(1)}, f32[10,6,256]{2,1,0:T(8,128)S(1)}, u32[]{:S(2)}, u32[]{:S(2)}) collective-permute-start(f32[10,6,256]{2,1,0:T(8,128)S(1)} %bitcast.11), channel_id=1, source_target_pairs={{0,1},{1,0},{2,3},{3,2},{4,5},{5,4},{6,7},{7,6},{8,9},{9,8},{10,11... | collective-permute-start | bytes 184328 | tf_op jit(solution)/shard_map/ppermute | solution.py:170
  39.7 0.7 collective-permute-start.5
  41.6 0.7 collective-permute-start.6
  43.6 23.8 %collective-permute-start.7 = (f32[6,16,256]{2,1,0:T(8,128)S(1)}, f32[6,16,256]{2,1,0:T(8,128)S(1)}, u32[]{:S(2)}, u32[]{:S(2)}) collective-permute-start(f32[6,16,256]{2,1,0:T(8,128)S(1)} %shard_map.53), channel_id=1, source_target_pairs={{8,0},{9,1},{10,2},{11,3},{12,4},{13,5},{14,6},{15,7}} | collective-permute-start | bytes 294920 | tf_op jit(solution)/shard_map/ppermute | solution.py:361

commit v4 on v3

--- a/solution.py
+++ b/solution.py
@@ -11,20 +11,20 @@
 WHOLE = pl.BlockSpec(memory_space=pltpu.VMEM)
 
 
-def call(body, outs, *args, flops, limit=16 << 20, scratch=(), in_hbm=(), out_hbm=()):
+def call(body, outs, *args, cost, limit=16 << 20, scratch=(), in_hbm=(), out_hbm=(), aliases={}):
     far = pl.BlockSpec(memory_space=pl.ANY)
     shapes = [
         jax.ShapeDtypeStruct(o[0], o[1]) if i in out_hbm else pltpu.VMEM(o[0], o[1])
         for i, o in enumerate(outs)
     ]
-    moved = sum(a.size * a.dtype.itemsize for a in args)
     return pl.pallas_call(
         body,
         out_shape=shapes,
         in_specs=[far if i in in_hbm else WHOLE for i in range(len(args))],
         out_specs=[far if i in out_hbm else WHOLE for i in range(len(outs))],
         scratch_shapes=scratch,
-        cost_estimate=pl.CostEstimate(flops=flops, bytes_accessed=moved, transcendentals=0),
+        input_output_aliases=aliases,
+        cost_estimate=pl.CostEstimate(flops=0, bytes_accessed=cost, transcendentals=0),
         compiler_params=pltpu.CompilerParams(vmem_limit_bytes=limit),
     )(*[
         pltpu.with_memory_space_constraint(a, pltpu.HBM if i in in_hbm else pltpu.VMEM)
@@ -147,6 +147,7 @@
 
 def solution(mesh):
     gz, gx, gy = (mesh.shape[a] for a in ("gz", "gx", "gy"))
+    short = gz == 4
 
     def body(right_side, previous, diag_inverse, jacobians):
         rhs = jnp.transpose(right_side, (0, 2, 1, 3))
@@ -163,7 +164,7 @@
         y_face = ((1 if gy == 2 else 2, nz, VARS, nx), F32)
         plane, volume = (plane, F32), (volume, F32)
         cells = nz * ny * nx
-        block_flops = 2 * VARS * VARS * cells
+        unit = 40 * cells
 
         def exchange(x_face, y_face):
             if gy == 2:
@@ -176,7 +177,8 @@
                 ]
             return lax.all_gather(x_face, "gx"), *rows
 
-        def faces_kernel(prev_hbm, prev_ref, x_face, y_face, sem):
+        def faces_kernel(prev_hbm, *rest):
+            prev_ref, x_face, y_face, sem = rest[-4:]
             copy = pltpu.make_async_copy(prev_hbm, prev_ref, sem)
             copy.start()
             copy.wait()
@@ -226,6 +228,133 @@
                 total = [a + ref[var, :, at] for var, a in enumerate(total)]
             return tuple(total)
 
+        def transfer(matrix_ref, inv_ref, jac_at, wait):
+            half = VARS // 2
+
+            def plane(z, at, group, vectors):
+                couple, inverse = jac_at(z), block(inv_ref, z, at=at)
+                middle = [[] for _ in group]
+                for r in range(VARS):
+                    row = [couple(r, c, at).astype(F32) for c in range(VARS)]
+                    for i in range(len(group)):
+                        middle[i].append(row[group[i]] if vectors is None else dot6(row, vectors[i]))
+                for r in range(VARS):
+                    row = [inverse(r, c).astype(F32) for c in range(VARS)]
+                    for i, c in enumerate(group):
+                        matrix_ref[r, c, :, at] = -dot6(row, middle[i])
+
+            groups = [range(g * half, (g + 1) * half) for g in range(VARS // half)]
+
+            def step(i, carry):
+                z = wait(i)
+                for at in spans:
+                    for group in groups:
+                        vectors = [[matrix_ref[r, c, :, at] for r in range(VARS)] for c in group]
+                        plane(z, at, group, vectors)
+                return carry
+
+            z = wait(0)
+            for at in spans:
+                for group in groups:
+                    plane(z, at, group, None)
+            lax.fori_loop(1, nz, step, 0)
+
+        def only_on(device, work, matrix_ref):
+            here = lax.axis_index("gz") == device
+            pl.when(here)(work)
+
+            @pl.when(jnp.logical_not(here))
+            def _():
+                matrix_ref[...] = jnp.zeros(matrix_ref.shape, F32)
+
+        def up_matrix_kernel(inv_hbm, jac_hbm, matrix_ref, inv_ref, jac_ref, sems):
+            def copies(z):
+                return [
+                    pltpu.make_async_copy(inv_hbm.at[z], inv_ref.at[z], sems.at[0, z]),
+                    pltpu.make_async_copy(jac_hbm.at[z, 4], jac_ref.at[z], sems.at[1, z]),
+                ]
+
+            def wait(z):
+                for copy in copies(z):
+                    copy.wait()
+                return z
+
+            def work():
+                for z in range(nz):
+                    for copy in copies(z):
+                        copy.start()
+                transfer(matrix_ref, inv_ref, lambda z: lambda r, c, at: jac_ref[z, r, c, :, at], wait)
+
+            only_on(2, work, matrix_ref)
+
+        def down_matrix_kernel(inv_ref, jac_ref, matrix_ref):
+            def work():
+                def couple(z):
+                    return lambda r, c, at: jac_ref[z, 5, r, c, :, at]
+
+                transfer(matrix_ref, inv_ref, couple, lambda i: nz - 1 - i)
+
+            only_on(1, work, matrix_ref)
+
+        def apply_matrix(matrix_ref, vector, at):
+            return apply_block(block(matrix_ref, at=at), vector)
+
+        def arrived(parts, at):
+            *plain, matrix_ref, vector_ref = parts
+            total = apply_matrix(matrix_ref, [vector_ref[var, :, at] for var in range(VARS)], at)
+            for ref in plain:
+                total = [a + ref[var, :, at] for var, a in enumerate(total)]
+            return tuple(total)
+
+        def forward_mid_kernel(low_ref, came_ref, after_ref, source_ref, inv_ref, jac_ref, _, top_ref):
+            top_ref[...] = low_ref[...]
+
+            @pl.when(lax.axis_index("gz") == 1)
+            def _():
+                def step(z, earlier):
+                    return tuple(
+                        tuple(
+                            forward_plane(
+                                planes_of(source_ref, z, at), inv_ref, jac_ref, z, at, earlier[tile]
+                            )
+                        )
+                        for tile, at in enumerate(spans)
+                    )
+
+                start = tuple(incoming([came_ref], at) for at in spans)
+                top = lax.fori_loop(0, nz, step, start)
+                for tile, at in enumerate(spans):
+                    for var in range(VARS):
+                        top_ref[var, :, at] = top[tile][var]
+
+        def backward_mid_kernel(high_ref, came_ref, sweep_ref, inner_ref, inv_ref, jac_ref, low_ref):
+            low_ref[...] = high_ref[...]
+
+            @pl.when(lax.axis_index("gz") == 2)
+            def _():
+                def step(i, later):
+                    z = nz - 1 - i
+                    return tuple(
+                        tuple(
+                            backward_plane(
+                                planes_of(sweep_ref, z, at),
+                                planes_of(inner_ref, z, at),
+                                inv_ref,
+                                jac_ref,
+                                z,
+                                at,
+                                later[tile],
+                            )
+                        )
+                        for tile, at in enumerate(spans)
+                    )
+
+                start = tuple(incoming([came_ref], at) for at in spans)
+                low = lax.fori_loop(0, nz, step, start)
+                for tile, at in enumerate(spans):
+                    for var in range(VARS):
+                        low_ref[var, :, at] = low[tile][var]
+
         def forward_kernel(source_ref, inv_ref, jac_ref, *rest):
             came, top_ref = rest[:-1], rest[-1]
             for at in spans:
@@ -239,7 +368,10 @@
                     top_ref[var, :, at] = top[var]
 
         def forward_last_kernel(source_ref, prev_ref, inv_ref, jac_ref, *rest):
-            came, (sweep_ref, change_ref, x_face, y_face) = rest[:-4], rest[-4:]
+            if short:
+                came, (sweep_ref, change_ref, x_face, y_face) = rest[:4], rest[5:9]
+            else:
+                came, (sweep_ref, change_ref, x_face, y_face) = rest[:-4], rest[-4:]
             for at in spans:
 
                 def step(z, earlier, at=at):
@@ -251,7 +383,8 @@
                         change_ref[z, var, :, at] = result[var] - before[var]
                     return tuple(result)
 
-                lax.fori_loop(0, nz, step, incoming(came, at))
+                start = arrived(came, at) if short else incoming(came, at)
+                lax.fori_loop(0, nz, step, start)
             write_faces(change_ref, x_face, y_face, nz)
 
         def backward_plane(sweep, inner, inv_ref, jac_ref, z, at, later):
@@ -308,15 +441,33 @@
                 out_copy(z).start()
                 return tuple(results)
 
-            lax.fori_loop(0, nz, step, tuple(incoming(came, at) for at in spans))
+            entered = arrived if short else incoming
+            lax.fori_loop(0, nz, step, tuple(entered(came, at) for at in spans))
             for z in range(nz):
                 out_copy(z).wait()
 
+        if short:
+            matrix_shape = ((VARS, VARS, ny, nx), F32)
+            (up_matrix,) = call(
+                up_matrix_kernel,
+                [matrix_shape],
+                inv,
+                jac,
+                cost=12 * unit,
+                in_hbm=(0, 1),
+                scratch=[
+                    pltpu.VMEM(inv.shape, inv.dtype),
+                    pltpu.VMEM(inv.shape, jac.dtype),
+                    pltpu.SemaphoreType.DMA((2, nz)),
+                ],
+            )
+            up_there = lax.ppermute(up_matrix, "gz", [(gz - 2, gz - 1)])
         prev, *faces = call(
             faces_kernel,
             [volume, x_face, y_face],
             prev,
-            flops=cells,
+            *([up_matrix] if short else []),
+            cost=3 * unit,
             in_hbm=(0,),
             scratch=[pltpu.SemaphoreType.DMA],
         )
@@ -329,36 +480,77 @@
             jac,
             prev,
             *halo,
-            flops=6 * block_flops,
+            cost=18 * unit,
             in_hbm=(0, 1, 2),
             scratch=[pltpu.VMEM(rhs.shape, F32), pltpu.SemaphoreType.DMA((3, nz))],
         )
-        came = []
-        for hop in range(gz - 1):
-            if hop:
-                (top,) = call(forward_kernel, [plane], source, inv, jac, *came, flops=2 * block_flops)
-            came.append(lax.ppermute(top, "gz", [(hop, hop + 1)]))
-        sweep, change, *faces = call(
+        if short:
+            first = lax.ppermute(top, "gz", [(0, 1)])
+            (down_matrix,) = call(down_matrix_kernel, [matrix_shape], inv, jac, cost=12 * unit)
+            (top,) = call(
+                forward_mid_kernel,
+                [plane],
+                top,
+                first,
+                up_there,
+                source,
+                inv,
+                jac,
+                down_matrix,
+                cost=3 * unit,
+            )
+            far = lax.ppermute(top, "gz", [(1, 3)])
+            near = lax.ppermute(top, "gz", [(1, 2), (2, 3)])
+            came = [first, near, up_there, far]
+            extra = [down_matrix]
+        else:
+            extra = []
+            came = []
+            for hop in range(gz - 1):
+                if hop:
+                    (top,) = call(
+                        forward_kernel, [plane], source, inv, jac, *came, cost=3 * unit)
+                came.append(lax.ppermute(top, "gz", [(hop, hop + 1)]))
+        sweep, change, x_side, y_side, *extra = call(
             forward_last_kernel,
-            [volume, volume, x_face, y_face],
+            [volume, volume, x_face, y_face] + [matrix_shape] * len(extra),
             source,
             prev,
             inv,
             jac,
             *came,
-            flops=2 * block_flops,
+            *extra,
+            cost=4 * unit,
+            aliases={4 + len(came): 4} if short else {},
         )
-        halo = exchange(*faces)
+        if short:
+            down_there = lax.ppermute(extra[0], "gz", [(1, 0)])
+        halo = exchange(x_side, y_side)
         inner, low = call(
-            turn_kernel, [volume, plane], sweep, change, inv, jac, *halo, flops=6 * block_flops
-        )
-        came = []
-        for hop in range(gz - 1, 0, -1):
-            if came:
-                (low,) = call(
-                    backward_kernel, [plane], sweep, inner, inv, jac, *came, flops=2 * block_flops
-                )
-            came.append(lax.ppermute(low, "gz", [(hop, hop - 1)]))
+            turn_kernel, [volume, plane], sweep, change, inv, jac, *halo, cost=11 * unit)
+        if short:
+            first = lax.ppermute(low, "gz", [(3, 2)])
+            (low,) = call(
+                backward_mid_kernel, [plane], low, first, sweep, inner, inv, jac, cost=3 * unit
+            )
+            far = lax.ppermute(low, "gz", [(2, 0)])
+            near = lax.ppermute(low, "gz", [(2, 1), (1, 0)])
+            came = [first, near, down_there, far]
+        else:
+            came = []
+            for hop in range(gz - 1, 0, -1):
+                if came:
+                    (low,) = call(
+                        backward_kernel,
+                        [plane],
+                        sweep,
+                        inner,
+                        inv,
+                        jac,
+                        *came,
+                        cost=3 * unit,
+                    )
+                came.append(lax.ppermute(low, "gz", [(hop, hop - 1)]))
         (update,) = call(
             update_kernel,
             [volume],
@@ -367,7 +559,7 @@
             inv,
             jac,
             *came,
-            flops=2 * block_flops,
+            cost=5 * unit,
             out_hbm=(0,),
             scratch=[pltpu.VMEM(volume[0], F32), pltpu.SemaphoreType.DMA((nz,))],
         )

time: 69.6 us -> 64.4 us (0.925)
  Pallas kernels: 22.6 us -> 18.1 us
  waiting for transfers between devices: 25.1 us -> 21.7 us
  starting transfers between devices: 11 us -> 13.7 us
    pallas_call x9, Pallas kernels: 22.6 us -> 18.1 us  [call(): pl.pallas_call(body, out_shape=shapes, in_specs=[far if i in in_hbm else...]
    ppermute x6 -> x8, waiting for transfers between devices: 25.1 us -> 21.7 us  [the longest x1 19.2 us: body(): far = lax.ppermute(low, 'gz', [(2, 0)])]
    ppermute x6 -> x8, starting transfers between devices: 7.45 us -> 10.1 us  [the longest x1 3.49 us: body(): first = lax.ppermute(top, 'gz', [(0, 1)])]
  transfers between devices with their start and end apart: 8 -> 10, of which waited for: 2 -> 2; matrix products, arithmetic and copies ran while one was open for 0% -> 0% of each run, Pallas kernels for 0% -> 22%
where the time goes in v4:
time: 64.4 us; the launch traced here: 64.1 us
  waiting for transfers between devices  21.7 us (34%)
  Pallas kernels  18.1 us (28%)
  starting transfers between devices  13.7 us (21%)
  blocking collectives  10.5 us (16%)
    ppermute x1, waiting for transfers between devices, body(): far = lax.ppermute(low, 'gz', [(2, 0)])  19.2 us
    pallas_call x9, Pallas kernels, call(): pl.pallas_call(body, out_shape=shapes, in_specs=[far if i in in_hbm else...  18.1 us
    all_gather x2, blocking collectives, exchange(): return (lax.all_gather(x_face, 'gx'), *rows)  10.5 us
    ppermute x2, starting transfers between devices, exchange(): rows = [lax.ppermute(y_face[0], 'gy', [(0, 1), (1, 0)])]  3.6 us
    ppermute x1, starting transfers between devices, body(): first = lax.ppermute(top, 'gz', [(0, 1)])  3.49 us
    ppermute x1, waiting for transfers between devices, body(): first = lax.ppermute(top, 'gz', [(0, 1)])  2.47 us
    ppermute x1, starting transfers between devices, body(): down_there = lax.ppermute(extra[0], 'gz', [(1, 0)])  1.29 us
    ppermute x1, starting transfers between devices, body(): far = lax.ppermute(low, 'gz', [(2, 0)])  1.29 us
  transfers between devices with their start and end apart: 10, of which 2 were waited for; matrix products, arithmetic and copies ran while one was open for 0% of the time, Pallas kernels for 22%

profile of v4, /device:TPU:0, one launch (start us, length us, event | category | flops | bytes accessed | tf_op | source)
XLA Modules:
  0.0 64.1 jit_solution(15122272296054922512)
XLA Ops:
  0.0 0.2 shard_map.46.rest_0_
  0.2 0.7 %collective-permute-start.2 = (f32[6,6,16,256]{3,2,1,0:T(8,128)S(1)}, f32[6,6,16,256]{3,2,1,0:T(8,128)S(1)}, u32[]{:S(2)}, u32[]{:S(2)}) collective-permute-start(f32[6,6,16,256]{3,2,1,0:T(8,128)S(1)} %shard_map.46.rest_0_), channel_id=1, source_target_pairs={{16,24},{17,25},{18,26},{19,27},{20,28},{21,29},{22,30},{23,31}} | collective-permute-start | bytes 1769480 | tf_op jit(solution)/shard_map/ppermute | solution.py:464
  0.9 1.5 %shard_map.47 = (f32[10,6,16,256]{3,2,1,0:T(8,128)S(1)}, f32[2,1,16,128]{3,2,1,0:T(8,128)S(1)}, f32[1,10,6,256]{3,2,1,0:T(8,128)S(1)}) custom-call(f32[10,6,16,256]{3,2,1,0:T(8,128)} %bitcast.17, f32[6,6,16,256]{3,2,1,0:T(8,128)S(1)} %shard_map.46.rest_0_), custom_call_target="tpu_custom_call" | custom-call | bytes 4915200 | tf_op jit(solution)/shard_map/pallas_call | solution.py:20
  2.5 3.0 %collective-permute-start = (f32[10,6,256]{2,1,0:T(8,128)S(1)}, f32[10,6,256]{2,1,0:T(8,128)S(1)}, u32[]{:S(2)}, u32[]{:S(2)}) collective-permute-start(f32[10,6,256]{2,1,0:T(8,128)S(1)} %bitcast.12), channel_id=1, source_target_pairs={{0,1},{1,0},{2,3},{3,2},{4,5},{5,4},{6,7},{7,6},{8,9},{9,8},{10,11... | collective-permute-start | bytes 184328 | tf_op jit(solution)/shard_map/ppermute | solution.py:171
  5.5 5.2 %all-gather = f32[8,1,16,128]{3,2,1,0:T(8,128)S(1)} all-gather(f32[2,1,16,128]{3,2,1,0:T(8,128)S(1)} %get-tuple-element.20), channel_id=2, replica_groups=mesh['gz'=4,'gx'=4,'gy'=2] {'gx'}, dimensions={0}, use_global_device_ids=true | all-gather | bytes 81920 | tf_op jit(solution)/shard_map/all_gather | solution.py:178
  10.7 0.0 collective-permute-done.rest_0_
  10.7 7.8 %shard_map.48 = (f32[10,6,16,256]{3,2,1,0:T(8,128)S(1)}, f32[6,16,256]{2,1,0:T(8,128)S(1)}, bf16[10,6,6,16,256]{4,3,2,1,0:T(8,128)(2,1)S(1)}, bf16[10,6,6,6,16,256]{5,4,3,2,1,0:T(8,128)(2,1)S(1)}) custom-call(f32[10,6,16,256]{3,2,1,0:T(8,128)} %bitcast.18, bf16[10,6,6,16,256]{4,3,2,1,0:T(8,128)(2,1)} %bitcast.16, bf16[10,6,6,6,16,256]{5,4,3,2,1,0:T(8,128)(2,1)} %bitcast.14, ...), custom_call_target="tpu_custom_call" | custom-call | bytes 29491200 | tf_op jit(solution)/shard_map/pallas_call | solution.py:20
  18.5 3.5 %collective-permute-start.1 = (f32[6,16,256]{2,1,0:T(8,128)S(1)}, f32[6,16,256]{2,1,0:T(8,128)S(1)}, u32[]{:S(2)}, u32[]{:S(2)}) collective-permute-start(f32[6,16,256]{2,1,0:T(8,128)S(1)} %get-tuple-element.25.low_ref), channel_id=1, source_target_pairs={{0,8},{1,9},{2,10},{3,11},{4,12},{5,13},{6,14},{7,15}} | collective-permute-start | bytes 294920 | tf_op jit(solution)/shard_map/ppermute | solution.py:488
  22.0 0.1 shard_map.49._.rest_4_
  22.1 2.5 %collective-permute-done.1.came_ref.rest_0_ = f32[6,16,256]{2,1,0:T(8,128)S(1)} collective-permute-done((f32[6,16,256]{2,1,0:T(8,128)S(1)}, f32[6,16,256]{2,1,0:T(8,128)S(1)}, u32[]{:S(2)}, u32[]{:S(2)}) %collective-permute-start.1) | collective-permute-done | bytes 98336 | tf_op jit(solution)/shard_map/ppermute | solution.py:488
  24.5 0.0 collective-permute-done.2.after_ref.rest_2_
  24.6 0.7 %collective-permute-start.4 = (f32[6,16,256]{2,1,0:T(8,128)S(1)}, f32[6,16,256]{2,1,0:T(8,128)S(1)}, u32[]{:S(2)}, u32[]{:S(2)}) collective-permute-start(f32[6,16,256]{2,1,0:T(8,128)S(1)} %shard_map.50), channel_id=1, source_target_pairs={{8,24},{9,25},{10,26},{11,27},{12,28},{13,29},{14,30},{15,31}} | collective-permute-start | bytes 294920 | tf_op jit(solution)/shard_map/ppermute | solution.py:502
  25.2 0.7 %collective-permute-start.3 = (f32[6,16,256]{2,1,0:T(8,128)S(1)}, f32[6,16,256]{2,1,0:T(8,128)S(1)}, u32[]{:S(2)}, u32[]{:S(2)}) collective-permute-start(f32[6,16,256]{2,1,0:T(8,128)S(1)} %shard_map.50), channel_id=1, source_target_pairs={{8,16},{16,24},{9,17},{17,25},{10,18},{18,26},{11,19},{19,27},{12,... | collective-permute-start | bytes 294920 | tf_op jit(solution)/shard_map/ppermute | solution.py:503
  25.9 0.0 collective-permute-done.4.rest_3_
  25.9 0.0 collective-permute-done.3.rest_1_
  25.9 1.6 %shard_map.51 = (f32[10,6,16,256]{3,2,1,0:T(8,128)S(1)}, f32[10,6,16,256]{3,2,1,0:T(8,128)S(1)}, f32[2,1,16,128]{3,2,1,0:T(8,128)S(1)}, f32[1,10,6,256]{3,2,1,0:T(8,128)S(1)}, f32[6,6,16,256]{3,2,1,0:T(8,128)S(1)}) custom-call(f32[10,6,16,256]{3,2,1,0:T(8,128)S(1)} %get-tuple-element.22.source_ref, ...), custom_call_target="tpu_custom_call", output_to_operand_aliasing={{4}: (8, {})} | custom-call | bytes 6553600 | tf_op jit(solution)/shard_map/pallas_call | solution.py:20
  27.6 1.3 %collective-permute-start.8 = (f32[6,6,16,256]{3,2,1,0:T(8,128)S(1)}, f32[6,6,16,256]{3,2,1,0:T(8,128)S(1)}, u32[]{:S(2)}, u32[]{:S(2)}) collective-permute-start(f32[6,6,16,256]{3,2,1,0:T(8,128)S(1)} %get-tuple-element.32), channel_id=1, source_target_pairs={{8,0},{9,1},{10,2},{11,3},{12,4},{13,5},{14,6},{15,7}} | collective-permute-start | bytes 1769480 | tf_op jit(solution)/shard_map/ppermute | solution.py:527
  28.9 0.6 collective-permute-start.5
  29.5 5.2 %all-gather.1 = f32[8,1,16,128]{3,2,1,0:T(8,128)S(1)} all-gather(f32[2,1,16,128]{3,2,1,0:T(8,128)S(1)} %get-tuple-element.28), channel_id=3, replica_groups=mesh['gz'=4,'gx'=4,'gy'=2] {'gx'}, dimensions={0}, use_global_device_ids=true | all-gather | bytes 81920 | tf_op jit(solution)/shard_map/all_gather | solution.py:178
  34.7 0.0 collective-permute-done.5.rest_0_
  34.7 4.8 %shard_map.52 = (f32[10,6,16,256]{3,2,1,0:T(8,128)S(1)}, f32[6,16,256]{2,1,0:T(8,128)S(1)}) custom-call(f32[10,6,16,256]{3,2,1,0:T(8,128)S(1)} %get-tuple-element.26.sweep_ref, f32[10,6,16,256]{3,2,1,0:T(8,128)S(1)} %get-tuple-element.27.change_ref, bf16[10,6,6,16,256]{4,3,2,1,0:T(8,128)(2,1)S(1)} %get-tuple-element.23.inv_ref, ...), custom_call_target="tpu_custom_call" | custom-call | bytes 18022400 | tf_op jit(solution)/shard_map/pallas_call | solution.py:20
  39.5 0.7 %collective-permute-start.6 = (f32[6,16,256]{2,1,0:T(8,128)S(1)}, f32[6,16,256]{2,1,0:T(8,128)S(1)}, u32[]{:S(2)}, u32[]{:S(2)}) collective-permute-start(f32[6,16,256]{2,1,0:T(8,128)S(1)} %get-tuple-element.31.high_ref), channel_id=1, source_target_pairs={{24,16},{25,17},{26,18},{27,19},{28,20},{29,21},{30,22},{31,23}} | collective-permute-start | bytes 294920 | tf_op jit(solution)/shard_map/ppermute | solution.py:532
  40.2 0.0 collective-permute-done.6.came_ref.rest_0_
  40.2 1.3 %collective-permute-start.9 = (f32[6,16,256]{2,1,0:T(8,128)S(1)}, f32[6,16,256]{2,1,0:T(8,128)S(1)}, u32[]{:S(2)}, u32[]{:S(2)}) collective-permute-start(f32[6,16,256]{2,1,0:T(8,128)S(1)} %shard_map.53), channel_id=1, source_target_pairs={{16,0},{17,1},{18,2},{19,3},{20,4},{21,5},{22,6},{23,7}} | collective-permute-start | bytes 294920 | tf_op jit(solution)/shard_map/ppermute | solution.py:536
  41.5 1.3 %collective-permute-start.7 = (f32[6,16,256]{2,1,0:T(8,128)S(1)}, f32[6,16,256]{2,1,0:T(8,128)S(1)}, u32[]{:S(2)}, u32[]{:S(2)}) collective-permute-start(f32[6,16,256]{2,1,0:T(8,128)S(1)} %shard_map.53), channel_id=1, source_target_pairs={{16,8},{8,0},{17,9},{9,1},{18,10},{10,2},{19,11},{11,3},{20,12},{1... | collective-permute-start | bytes 294920 | tf_op jit(solution)/shard_map/ppermute | solution.py:537
  42.8 19.2 %collective-permute-done.9.rest_3_ = f32[6,16,256]{2,1,0:T(8,128)S(1)} collective-permute-done((f32[6,16,256]{2,1,0:T(8,128)S(1)}, f32[6,16,256]{2,1,0:T(8,128)S(1)}, u32[]{:S(2)}, u32[]{:S(2)}) %collective-permute-start.9) | collective-permute-done | bytes 98336 | tf_op jit(solution)/shard_map/ppermute | solution.py:536
  62.1 0.0 collective-permute-done.7.rest_1_
  62.1 0.0 collective-permute-done.8.rest_2_
  62.1 2.0 %shard_map.54 = f32[10,6,16,256]{3,2,1,0:T(8,128)} custom-call(f32[10,6,16,256]{3,2,1,0:T(8,128)S(1)} %get-tuple-element.26.sweep_ref, f32[10,6,16,256]{3,2,1,0:T(8,128)S(1)} %get-tuple-element.30.inner_ref, bf16[10,6,6,16,256]{4,3,2,1,0:T(8,128)(2,1)S(1)} %get-tuple-element.23.inv_ref, bf16[10,6,6,6,16,256]{5,4,3,2,1,0:T(8,128)(2,1)S(1)} %get-tuple-element.24.jac_ref, ...), custom_call_target="tpu_custom_call" | custom-call | bytes 8192000 | tf_op jit(solution)/shard_map/pallas_call | solution.py:20
  (2 shorter events, 0.0 us)
Async XLA Ops:
  0.2 24.3 %collective-permute-start.2 = (f32[6,6,16,256]{3,2,1,0:T(8,128)S(1)}, f32[6,6,16,256]{3,2,1,0:T(8,128)S(1)}, u32[]{:S(2)}, u32[]{:S(2)}) collective-permute-start(f32[6,6,16,256]{3,2,1,0:T(8,128)S(1)} %shard_map.46.rest_0_), channel_id=1, source_target_pairs={{16,24},{17,25},{18,26},{19,27},{20,28},{21,29},{22,30},{23,31}} | collective-permute-start | bytes 1769480 | tf_op jit(solution)/shard_map/ppermute | solution.py:464
  2.5 8.2 %collective-permute-start = (f32[10,6,256]{2,1,0:T(8,128)S(1)}, f32[10,6,256]{2,1,0:T(8,128)S(1)}, u32[]{:S(2)}, u32[]{:S(2)}) collective-permute-start(f32[10,6,256]{2,1,0:T(8,128)S(1)} %bitcast.12), channel_id=1, source_target_pairs={{0,1},{1,0},{2,3},{3,2},{4,5},{5,4},{6,7},{7,6},{8,9},{9,8},{10,11... | collective-permute-start | bytes 184328 | tf_op jit(solution)/shard_map/ppermute | solution.py:171
  18.5 6.0 %collective-permute-start.1 = (f32[6,16,256]{2,1,0:T(8,128)S(1)}, f32[6,16,256]{2,1,0:T(8,128)S(1)}, u32[]{:S(2)}, u32[]{:S(2)}) collective-permute-start(f32[6,16,256]{2,1,0:T(8,128)S(1)} %get-tuple-element.25.low_ref), channel_id=1, source_target_pairs={{0,8},{1,9},{2,10},{3,11},{4,12},{5,13},{6,14},{7,15}} | collective-permute-start | bytes 294920 | tf_op jit(solution)/shard_map/ppermute | solution.py:488
  24.6 1.4 %collective-permute-start.4 = (f32[6,16,256]{2,1,0:T(8,128)S(1)}, f32[6,16,256]{2,1,0:T(8,128)S(1)}, u32[]{:S(2)}, u32[]{:S(2)}) collective-permute-start(f32[6,16,256]{2,1,0:T(8,128)S(1)} %shard_map.50), channel_id=1, source_target_pairs={{8,24},{9,25},{10,26},{11,27},{12,28},{13,29},{14,30},{15,31}} | collective-permute-start | bytes 294920 | tf_op jit(solution)/shard_map/ppermute | solution.py:502
  25.2 0.7 %collective-permute-start.3 = (f32[6,16,256]{2,1,0:T(8,128)S(1)}, f32[6,16,256]{2,1,0:T(8,128)S(1)}, u32[]{:S(2)}, u32[]{:S(2)}) collective-permute-start(f32[6,16,256]{2,1,0:T(8,128)S(1)} %shard_map.50), channel_id=1, source_target_pairs={{8,16},{16,24},{9,17},{17,25},{10,18},{18,26},{11,19},{19,27},{12,... | collective-permute-start | bytes 294920 | tf_op jit(solution)/shard_map/ppermute | solution.py:503
  27.6 34.5 %collective-permute-start.8 = (f32[6,6,16,256]{3,2,1,0:T(8,128)S(1)}, f32[6,6,16,256]{3,2,1,0:T(8,128)S(1)}, u32[]{:S(2)}, u32[]{:S(2)}) collective-permute-start(f32[6,6,16,256]{3,2,1,0:T(8,128)S(1)} %get-tuple-element.32), channel_id=1, source_target_pairs={{8,0},{9,1},{10,2},{11,3},{12,4},{13,5},{14,6},{15,7}} | collective-permute-start | bytes 1769480 | tf_op jit(solution)/shard_map/ppermute | solution.py:527
  28.9 5.8 %collective-permute-start.5 = (f32[10,6,256]{2,1,0:T(8,128)S(1)}, f32[10,6,256]{2,1,0:T(8,128)S(1)}, u32[]{:S(2)}, u32[]{:S(2)}) collective-permute-start(f32[10,6,256]{2,1,0:T(8,128)S(1)} %bitcast.11), channel_id=1, source_target_pairs={{0,1},{1,0},{2,3},{3,2},{4,5},{5,4},{6,7},{7,6},{8,9},{9,8},{10,11... | collective-permute-start | bytes 184328 | tf_op jit(solution)/shard_map/ppermute | solution.py:171
  39.5 0.7 %collective-permute-start.6 = (f32[6,16,256]{2,1,0:T(8,128)S(1)}, f32[6,16,256]{2,1,0:T(8,128)S(1)}, u32[]{:S(2)}, u32[]{:S(2)}) collective-permute-start(f32[6,16,256]{2,1,0:T(8,128)S(1)} %get-tuple-element.31.high_ref), channel_id=1, source_target_pairs={{24,16},{25,17},{26,18},{27,19},{28,20},{29,21},{30,22},{31,23}} | collective-permute-start | bytes 294920 | tf_op jit(solution)/shard_map/ppermute | solution.py:532
  40.2 21.8 %collective-permute-start.9 = (f32[6,16,256]{2,1,0:T(8,128)S(1)}, f32[6,16,256]{2,1,0:T(8,128)S(1)}, u32[]{:S(2)}, u32[]{:S(2)}) collective-permute-start(f32[6,16,256]{2,1,0:T(8,128)S(1)} %shard_map.53), channel_id=1, source_target_pairs={{16,0},{17,1},{18,2},{19,3},{20,4},{21,5},{22,6},{23,7}} | collective-permute-start | bytes 294920 | tf_op jit(solution)/shard_map/ppermute | solution.py:536
  41.5 20.5 %collective-permute-start.7 = (f32[6,16,256]{2,1,0:T(8,128)S(1)}, f32[6,16,256]{2,1,0:T(8,128)S(1)}, u32[]{:S(2)}, u32[]{:S(2)}) collective-permute-start(f32[6,16,256]{2,1,0:T(8,128)S(1)} %shard_map.53), channel_id=1, source_target_pairs={{16,8},{8,0},{17,9},{9,1},{18,10},{10,2},{19,11},{11,3},{20,12},{1... | collective-permute-start | bytes 294920 | tf_op jit(solution)/shard_map/ppermute | solution.py:537

commit v5 on v3

v5 whole, which is shorter than its diff:
```python
import functools

import jax
import jax.numpy as jnp
from jax import lax
from jax.experimental import pallas as pl
from jax.experimental.pallas import tpu as pltpu
from jax.sharding import PartitionSpec as P

VARS = 6
LANES = 128
F32 = jnp.float32
WHOLE = pl.BlockSpec(memory_space=pltpu.VMEM)


def call(body, outs, *args, cost, limit=16 << 20, scratch=(), in_hbm=(), out_hbm=(), aliases={}):
    far = pl.BlockSpec(memory_space=pl.ANY)
    shapes = [
        jax.ShapeDtypeStruct(o[0], o[1]) if i in out_hbm else pltpu.VMEM(o[0], o[1])
        for i, o in enumerate(outs)
    ]
    return pl.pallas_call(
        body,
        out_shape=shapes,
        in_specs=[far if i in in_hbm else WHOLE for i in range(len(args))],
        out_specs=[far if i in out_hbm else WHOLE for i in range(len(outs))],
        scratch_shapes=scratch,
        input_output_aliases=aliases,
        cost_estimate=pl.CostEstimate(flops=0, bytes_accessed=cost, transcendentals=0),
        compiler_params=pltpu.CompilerParams(vmem_limit_bytes=limit),
    )(*[
        pltpu.with_memory_space_constraint(a, pltpu.HBM if i in in_hbm else pltpu.VMEM)
        for i, a in enumerate(args)
    ])


def lane_iota(rows):
    return lax.broadcasted_iota(jnp.int32, (rows, LANES), 1)


def row_iota(rows):
    return lax.broadcasted_iota(jnp.int32, (rows, LANES), 0)


def dot6(blocks, values):
    terms = [b.astype(F32) * v for b, v in zip(blocks, values)]
    return (terms[0] + terms[1]) + (terms[2] + terms[3]) + (terms[4] + terms[5])


def block(ref, *index, at):
    return lambda r, c: ref[(*index, r, c, slice(None), at)]


def apply_block(get, values):
    return [dot6([get(r, c) for c in range(VARS)], values) for r in range(VARS)]


def write_faces(value, x_face, y_face, z_count):
    y_count = value.shape[2]
    x_count = value.shape[3]
    lane = lane_iota(y_count)
    for side, start, source_lane in ((0, 0, 0), (1, x_count - LANES, LANES - 1)):
        for group in range(x_face.shape[1]):
            held = jnp.zeros((y_count, LANES), F32)
            for slot in range(min(LANES, z_count * VARS - group * LANES)):
                z, var = divmod(group * LANES + slot, VARS)
                tile = value[z, var, :, start : start + LANES]
                moved = pltpu.roll(tile, (slot - source_lane) % LANES, 1)
                held = jnp.where(lane == slot, moved, held)
            x_face[side, group] = held
    if y_face.shape[0] == 1:
        first = lax.axis_index("gy") == 0
        for z in range(z_count):
            for var in range(VARS):
                low = value[z, var, 0:1, :]
                high = value[z, var, y_count - 1 : y_count, :]
                y_face[0, z, var : var + 1, :] = jnp.where(first, high, low)
    else:
        for z in range(z_count):
            for var in range(VARS):
                y_face[0, z, var : var + 1, :] = value[z, var, 0:1, :]
                y_face[1, z, var : var + 1, :] = value[z, var, y_count - 1 : y_count, :]


def halo_reader(x_all, y_rows, gx, gy):
    me_x = lax.axis_index("gx")

    def column(there, side, to_lane):
        exists = (there >= 0) & (there < gx)
        device = jnp.clip(there, 0, gx - 1)

        def read(z, var):
            j = z * VARS + var
            face = x_all[device, side, j // LANES]
            moved = pltpu.roll(face, (to_lane + LANES - j % LANES) % LANES, 1)
            return jnp.where(exists, moved, jnp.zeros_like(moved))

        return read

    def row(which):
        def read(z, var, at):
            if len(y_rows) > 1:
                return y_rows[which][z, var : var + 1, at]
            here = y_rows[0][z, var : var + 1, at]
            return jnp.where(lax.axis_index("gy") == 1 - which, here, jnp.zeros_like(here))

        return read

    return column(me_x - 1, 1, 0), column(me_x + 1, 0, LANES - 1), row(0), row(1)


def neighbours(value, z, tile, tiles, halo):
    y_count = value.shape[2]
    lane = lane_iota(y_count)
    row = row_iota(y_count)
    at = slice(tile * LANES, (tile + 1) * LANES)
    result = ([], [], [], [])
    for var in range(VARS):
        here = value[z, var, :, at]
        if tile > 0:
            before = pltpu.roll(value[z, var, :, at.start - LANES : at.start], 1, 1)
        else:
            before = halo[0](z, var)
        if tile < tiles - 1:
            after = pltpu.roll(value[z, var, :, at.stop : at.stop + LANES], LANES - 1, 1)
        else:
            after = halo[1](z, var)
        result[0].append(jnp.where(lane == 0, before, pltpu.roll(here, 1, 1)))
        result[1].append(jnp.where(lane == LANES - 1, after, pltpu.roll(here, LANES - 1, 1)))
        result[2].append(jnp.where(row == 0, halo[2](z, var, at), pltpu.roll(here, 1, 0)))
        result[3].append(
            jnp.where(row == y_count - 1, halo[3](z, var, at), pltpu.roll(here, y_count - 1, 0))
        )
    return result


def inplane(jacobians, value, z, tile, tiles, halo):
    at = slice(tile * LANES, (tile + 1) * LANES)
    total = None
    for n, values in enumerate(neighbours(value, z, tile, tiles, halo)):
        part = apply_block(block(jacobians, z, n, at=at), values)
        total = part if total is None else [a + b for a, b in zip(total, part)]
    return total


def planes_of(ref, z, at):
    return [ref[z, var, :, at] for var in range(VARS)]


def solution(mesh):
    gz, gx, gy = (mesh.shape[a] for a in ("gz", "gx", "gy"))
    short = gz == 4

    def body(right_side, previous, diag_inverse, jacobians):
        rhs = jnp.transpose(right_side, (0, 2, 1, 3))
        prev = jnp.transpose(previous, (0, 2, 1, 3))
        inv = jnp.transpose(diag_inverse, (0, 2, 3, 1, 4))
        jac = jnp.transpose(jacobians, (0, 2, 3, 4, 1, 5))
        nz, _, ny, nx = rhs.shape
        tiles = nx // LANES
        assert nx % LANES == 0
        spans = [slice(t * LANES, (t + 1) * LANES) for t in range(tiles)]
        plane = ((VARS, ny, nx), F32)
        volume = ((nz, VARS, ny, nx), F32)
        x_face = ((2, -(-nz * VARS // LANES), ny, LANES), F32)
        y_face = ((1 if gy == 2 else 2, nz, VARS, nx), F32)
        matrix = ((VARS, VARS, ny, nx), F32)
        blocks = ((nz, VARS, VARS, ny, nx), jac.dtype)
        side_blocks = ((nz, 4, VARS, VARS, ny, nx), jac.dtype)
        unit = 40 * nz * ny * nx

        def exchange(x_face, y_face):
            if gy == 2:
                rows = [lax.ppermute(y_face[0], "gy", [(0, 1), (1, 0)])]
            else:
                up = [(i, i + 1) for i in range(gy - 1)]
                rows = [
                    lax.ppermute(y_face[1], "gy", up),
                    lax.ppermute(y_face[0], "gy", [(j, i) for i, j in up]),
                ]
            return lax.all_gather(x_face, "gx"), *rows


        def forward_plane(source, inv_ref, low_jac, z, at, earlier):
            lagged = apply_block(block(low_jac, z, at=at), earlier)
            return apply_block(block(inv_ref, z, at=at), [a - b for a, b in zip(source, lagged)])

        def backward_plane(sweep, inner, inv_ref, high_jac, z, at, later):
            change = apply_block(block(high_jac, z, at=at), later)
            change = apply_block(block(inv_ref, z, at=at), [a + b for a, b in zip(change, inner)])
            return [a - b for a, b in zip(sweep, change)]

        def put(ref, values, at):
            for var in range(VARS):
                ref[var, :, at] = values[var]

        def incoming(refs, at):
            total = [refs[0][var, :, at] for var in range(VARS)]
            for ref in refs[1:]:
                total = [a + ref[var, :, at] for var, a in enumerate(total)]
            return tuple(total)

        def apply_matrix(matrix_ref, vector, at):
            return apply_block(block(matrix_ref, at=at), vector)

        def arrived(plain, matrix_ref, vector_ref, at):
            total = apply_matrix(matrix_ref, [vector_ref[var, :, at] for var in range(VARS)], at)
            for ref in plain:
                total = [a + ref[var, :, at] for var, a in enumerate(total)]
            return tuple(total)

        def forward_sweep(source_ref, inv_ref, low_jac, starts, keep=None):
            def step(z, earlier):
                results = []
                for tile, at in enumerate(spans):
                    source = planes_of(source_ref, z, at)
                    result = forward_plane(source, inv_ref, low_jac, z, at, earlier[tile])
                    if keep is not None:
                        keep(z, at, result)
                    results.append(tuple(result))
                return tuple(results)

            return lax.fori_loop(0, nz, step, starts)

        def backward_sweep(sweep_ref, inner_ref, inv_ref, high_jac, starts, keep=None):
            def step(i, later):
                z = nz - 1 - i
                results = []
                for tile, at in enumerate(spans):
                    sweep, inner = planes_of(sweep_ref, z, at), planes_of(inner_ref, z, at)
                    result = backward_plane(sweep, inner, inv_ref, high_jac, z, at, later[tile])
                    if keep is not None:
                        keep(z, tile, at, result)
                    results.append(tuple(result))
                return tuple(results)

            return lax.fori_loop(0, nz, step, starts)

        def transfer(matrix_ref, inv_ref, couple_ref, wait):
            half = VARS // 2
            groups = [range(g * half, (g + 1) * half) for g in range(VARS // half)]

            def plane_step(z, at, group, vectors):
                couple, inverse = block(couple_ref, z, at=at), block(inv_ref, z, at=at)
                middle = [[] for _ in group]
                for r in range(VARS):
                    row = [couple(r, c).astype(F32) for c in range(VARS)]
                    for i in range(len(group)):
                        middle[i].append(row[group[i]] if vectors is None else dot6(row, vectors[i]))
                for r in range(VARS):
                    row = [inverse(r, c).astype(F32) for c in range(VARS)]
                    for i, c in enumerate(group):
                        matrix_ref[r, c, :, at] = -dot6(row, middle[i])

            def step(i, carry):
                z = wait(i)
                for at in spans:
                    for group in groups:
                        vectors = [[matrix_ref[r, c, :, at] for r in range(VARS)] for c in group]
                        plane_step(z, at, group, vectors)
                return carry

            z = wait(0)
            for at in spans:
                for group in groups:
                    plane_step(z, at, group, None)
            lax.fori_loop(1, nz, step, 0)


        def open_kernel(prev_hbm, inv_hbm, jac_hbm, *rest):
            prev_ref, inv_ref, low_jac, x_side, y_side, *matrices, sem, sems = rest

            def copies(z):
                return [
                    pltpu.make_async_copy(inv_hbm.at[z], inv_ref.at[z], sems.at[0, z]),
                    pltpu.make_async_copy(jac_hbm.at[z, 4], low_jac.at[z], sems.at[1, z]),
                ]

            def wait(z):
                for copy in copies(z):
                    copy.wait()
                return z

            first_copy = pltpu.make_async_copy(prev_hbm, prev_ref, sem)
            first_copy.start()
            for z in range(nz):
                for copy in copies(z):
                    copy.start()
            first_copy.wait()
            write_faces(prev_ref, x_side, y_side, nz)
            if not matrices:
                for z in range(nz):
                    wait(z)
                return
            here = lax.axis_index("gz") == 2

            @pl.when(here)
            def _():
                transfer(matrices[0], inv_ref, low_jac, wait)

            @pl.when(jnp.logical_not(here))
            def _():
                matrices[0][...] = jnp.zeros(matrix[0], F32)
                for z in range(nz):
                    wait(z)

        def first_kernel(rhs_hbm, jac_hbm, prev_ref, inv_ref, low_jac, x_all, *rest):
            y_rows, (source_ref, top_ref, sides, high_jac, rhs_ref, sems) = rest[:-6], rest[-6:]
            halo = halo_reader(x_all, y_rows, gx, gy)

            def copies(z):
                return [
                    pltpu.make_async_copy(jac_hbm.at[z, 0:4], sides.at[z], sems.at[0, z]),
                    pltpu.make_async_copy(rhs_hbm.at[z], rhs_ref.at[z], sems.at[1, z]),
                ]

            def high_copy(z):
                return pltpu.make_async_copy(jac_hbm.at[z, 5], high_jac.at[z], sems.at[2, z])

            for z in range(nz):
                for copy in copies(z):
                    copy.start()
            for z in range(nz):
                high_copy(z).start()

            def step(z, earlier):
                for copy in copies(z):
                    copy.wait()
                results = []
                for tile, at in enumerate(spans):
                    lagged = inplane(sides, prev_ref, z, tile, tiles, halo)
                    source = [a - b for a, b in zip(planes_of(rhs_ref, z, at), lagged)]
                    for var in range(VARS):
                        source_ref[z, var, :, at] = source[var]
                    results.append(tuple(forward_plane(source, inv_ref, low_jac, z, at, earlier[tile])))
                return tuple(results)

            zero = tuple(jnp.zeros((ny, LANES), F32) for _ in range(VARS))
            top = lax.fori_loop(0, nz, step, (zero,) * tiles)
            for tile, at in enumerate(spans):
                put(top_ref, top[tile], at)
            for z in range(nz):
                high_copy(z).wait()

        def forward_kernel(source_ref, inv_ref, low_jac, *rest):
            came, top_ref = rest[:-1], rest[-1]
            starts = tuple(incoming(came, at) for at in spans)
            top = forward_sweep(source_ref, inv_ref, low_jac, starts)
            for tile, at in enumerate(spans):
                put(top_ref, top[tile], at)

        def forward_mid_kernel(low_ref, came_ref, _, source_ref, inv_ref, low_jac, __, top_ref):
            top_ref[...] = low_ref[...]

            @pl.when(lax.axis_index("gz") == 1)
            def _():
                forward_kernel(source_ref, inv_ref, low_jac, came_ref, top_ref)

        def forward_last_kernel(source_ref, prev_ref, inv_ref, low_jac, *rest):
            if short:
                (first, near, matrix_ref, far), outs = rest[:4], rest[5:9]
                starts = tuple(arrived((first, near), matrix_ref, far, at) for at in spans)
            else:
                came, outs = rest[:-4], rest[-4:]
                starts = tuple(incoming(came, at) for at in spans)
            sweep_ref, change_ref, x_side, y_side = outs

            def keep(z, at, result):
                before = planes_of(prev_ref, z, at)
                for var in range(VARS):
                    sweep_ref[z, var, :, at] = result[var]
                    change_ref[z, var, :, at] = result[var] - before[var]

            forward_sweep(source_ref, inv_ref, low_jac, starts, keep)
            write_faces(change_ref, x_side, y_side, nz)

        def turn_kernel(sweep_ref, change_ref, inv_ref, sides, high_jac, x_all, *rest):
            y_rows, (inner_ref, low_ref) = rest[:-2], rest[-2:]
            halo = halo_reader(x_all, y_rows, gx, gy)
            for tile, at in enumerate(spans):

                def step(i, later, tile=tile, at=at):
                    z = nz - 1 - i
                    inner = inplane(sides, change_ref, z, tile, tiles, halo)
                    for var in range(VARS):
                        inner_ref[z, var, :, at] = inner[var]
                    sweep = planes_of(sweep_ref, z, at)
                    return tuple(backward_plane(sweep, inner, inv_ref, high_jac, z, at, later))

                zero = tuple(jnp.zeros((ny, LANES), F32) for _ in range(VARS))
                put(low_ref, lax.fori_loop(0, nz, step, zero), at)

        def down_matrix_kernel(device, inv_ref, high_jac, matrix_ref):
            here = lax.axis_index("gz") == device

            @pl.when(here)
            def _():
                transfer(matrix_ref, inv_ref, high_jac, lambda i: nz - 1 - i)

            @pl.when(jnp.logical_not(here))
            def _():
                matrix_ref[...] = jnp.zeros(matrix[0], F32)

        def backward_kernel(sweep_ref, inner_ref, inv_ref, high_jac, *rest):
            came, low_ref = rest[:-1], rest[-1]
            starts = tuple(incoming(came, at) for at in spans)
            low = backward_sweep(sweep_ref, inner_ref, inv_ref, high_jac, starts)
            for tile, at in enumerate(spans):
                put(low_ref, low[tile], at)

        def backward_mid_kernel(own_ref, near, there_ref, far, matrix_ref, came_ref, low_ref):
            for at in spans:
                came = arrived((near,), there_ref, far, at)
                moved = apply_matrix(matrix_ref, came, at)
                put(came_ref, came, at)
                put(low_ref, [own_ref[var, :, at] + moved[var] for var in range(VARS)], at)

        def update_kernel(sweep_ref, inner_ref, inv_ref, high_jac, *rest):
            came, (out_hbm, held, sems) = rest[:-3], rest[-3:]

            def out_copy(z):
                return pltpu.make_async_copy(held.at[z], out_hbm.at[z], sems.at[z])

            def keep(z, tile, at, result):
                for var in range(VARS):
                    held[z, var, :, at] = result[var]
                if tile == tiles - 1:
                    out_copy(z).start()

            starts = tuple(incoming(came, at) for at in spans)
            backward_sweep(sweep_ref, inner_ref, inv_ref, high_jac, starts, keep)
            for z in range(nz):
                out_copy(z).wait()


        prev, inv, low_jac, x_side, y_side, *up_matrix = call(
            open_kernel,
            [volume, blocks, blocks, x_face, y_face] + [matrix] * (1 if short else 0),
            prev,
            inv,
            jac,
            cost=12 * unit,
            in_hbm=(0, 1, 2),
            scratch=[pltpu.SemaphoreType.DMA, pltpu.SemaphoreType.DMA((2, nz))],
        )
        if short:
            up_there = lax.ppermute(up_matrix[0], "gz", [(2, 3)])
        halo = exchange(x_side, y_side)
        source, top, sides, high_jac = call(
            first_kernel,
            [volume, plane, side_blocks, blocks],
            rhs,
            jac,
            prev,
            inv,
            low_jac,
            *halo,
            cost=14 * unit,
            in_hbm=(0, 1),
            scratch=[pltpu.VMEM(rhs.shape, F32), pltpu.SemaphoreType.DMA((3, nz))],
        )
        if short:
            first = lax.ppermute(top, "gz", [(0, 1)])
            (own_matrix,) = call(
                functools.partial(down_matrix_kernel, 1), [matrix], inv, high_jac, cost=12 * unit
            )
            (top,) = call(
                forward_mid_kernel,
                [plane],
                top,
                first,
                up_there,
                source,
                inv,
                low_jac,
                own_matrix,
                cost=3 * unit,
            )
            far = lax.ppermute(top, "gz", [(1, 3)])
            near = lax.ppermute(top, "gz", [(1, 2), (2, 3)])
            (down_matrix,) = call(
                functools.partial(down_matrix_kernel, 2), [matrix], inv, high_jac, cost=12 * unit
            )
            came = [first, near, up_there, far]
            extra = [down_matrix]
        else:
            came, extra = [], []
            for hop in range(gz - 1):
                if hop:
                    (top,) = call(
                        forward_kernel, [plane], source, inv, low_jac, *came, cost=3 * unit
                    )
                came.append(lax.ppermute(top, "gz", [(hop, hop + 1)]))
        sweep, change, x_side, y_side, *extra = call(
            forward_last_kernel,
            [volume, volume, x_face, y_face] + [matrix] * len(extra),
            source,
            prev,
            inv,
            low_jac,
            *came,
            *extra,
            cost=4 * unit,
            aliases={4 + len(came): 4} if short else {},
        )
        if short:
            down_there = lax.ppermute(extra[0], "gz", [(2, 1)])
        halo = exchange(x_side, y_side)
        inner, low = call(
            turn_kernel, [volume, plane], sweep, change, inv, sides, high_jac, *halo, cost=11 * unit
        )
        if short:
            far = lax.ppermute(low, "gz", [(3, 1)])
            near = lax.ppermute(low, "gz", [(3, 2), (2, 1)])
            entered, low = call(
                backward_mid_kernel,
                [plane, plane],
                low,
                near,
                down_there,
                far,
                own_matrix,
                cost=unit,
            )
            came = [entered, lax.ppermute(low, "gz", [(1, 0)])]
        else:
            came = []
            for hop in range(gz - 1, 0, -1):
                if came:
                    (low,) = call(
                        backward_kernel, [plane], sweep, inner, inv, high_jac, *came, cost=3 * unit
                    )
                came.append(lax.ppermute(low, "gz", [(hop, hop - 1)]))
        (update,) = call(
            update_kernel,
            [volume],
            sweep,
            inner,
            inv,
            high_jac,
            *came,
            cost=5 * unit,
            out_hbm=(0,),
            scratch=[pltpu.VMEM(volume[0], F32), pltpu.SemaphoreType.DMA((nz,))],
        )
        return jnp.transpose(update, (0, 2, 1, 3))

    placed = (
        P("gz", "gy", None, "gx"),
        P("gz", "gy", None, "gx"),
        P("gz", "gy", None, None, "gx"),
        P("gz", "gy", None, None, None, "gx"),
    )
    return jax.shard_map(
        body, mesh=mesh, in_specs=placed, out_specs=P("gz", "gy", None, "gx"), check_vma=False
    )
```

time: 69.6 us -> 66 us (0.948)
  Pallas kernels: 22.6 us -> 17.8 us
  starting transfers between devices: 11 us -> 12.4 us
    pallas_call x9, Pallas kernels: 22.6 us -> 17.8 us  [call(): pl.pallas_call(body, out_shape=shapes, in_specs=[far if i in in_hbm else...]
    ppermute x6 -> x8, starting transfers between devices: 7.45 us -> 8.84 us  [the longest x1 3.49 us: body(): first = lax.ppermute(top, 'gz', [(0, 1)])]
    ppermute x6 -> x8, waiting for transfers between devices: 25.1 us -> 24.8 us  [the longest x1 22.4 us: body(): came = [entered, lax.ppermute(low, 'gz', [(1, 0)])]]
  transfers between devices with their start and end apart: 8 -> 10, of which waited for: 2 -> 2; matrix products, arithmetic and copies ran while one was open for 0% -> 0% of each run, Pallas kernels for 0% -> 16%
where the time goes in v5:
time: 66 us; the launch traced here: 65.7 us
  waiting for transfers between devices  24.8 us (38%)
  Pallas kernels  17.8 us (27%)
  starting transfers between devices  12.4 us (19%)
  blocking collectives  10.5 us (16%)
    ppermute x1, waiting for transfers between devices, body(): came = [entered, lax.ppermute(low, 'gz', [(1, 0)])]  22.4 us
    pallas_call x9, Pallas kernels, call(): pl.pallas_call(body, out_shape=shapes, in_specs=[far if i in in_hbm else...  17.8 us
    all_gather x2, blocking collectives, exchange(): return (lax.all_gather(x_face, 'gx'), *rows)  10.5 us
    ppermute x2, starting transfers between devices, exchange(): rows = [lax.ppermute(y_face[0], 'gy', [(0, 1), (1, 0)])]  3.6 us
    ppermute x1, starting transfers between devices, body(): first = lax.ppermute(top, 'gz', [(0, 1)])  3.49 us
    ppermute x1, waiting for transfers between devices, body(): first = lax.ppermute(top, 'gz', [(0, 1)])  2.47 us
  transfers between devices with their start and end apart: 10, of which 2 were waited for; matrix products, arithmetic and copies ran while one was open for 0% of the time, Pallas kernels for 16%

profile of v5, /device:TPU:0, one launch (start us, length us, event | category | flops | bytes accessed | tf_op | source)
XLA Modules:
  0.0 65.7 jit_solution(2212829341619546876)
XLA Ops:
  0.0 3.5 %shard_map.46 = (f32[10,6,16,256]{3,2,1,0:T(8,128)S(1)}, bf16[10,6,6,16,256]{4,3,2,1,0:T(8,128)(2,1)S(1)}, bf16[10,6,6,16,256]{4,3,2,1,0:T(8,128)(2,1)S(1)}, f32...) custom-call(f32[10,6,16,256]{3,2,1,0:T(8,128)} %bitcast.17, ...), custom_call_target="tpu_custom_call" | custom-call | bytes 19660800 | tf_op jit(solution)/shard_map/pallas_call | solution.py:22
  3.5 0.7 %collective-permute-start.2 = (f32[6,6,16,256]{3,2,1,0:T(8,128)S(1)}, f32[6,6,16,256]{3,2,1,0:T(8,128)S(1)}, u32[]{:S(2)}, u32[]{:S(2)}) collective-permute-start(f32[6,6,16,256]{3,2,1,0:T(8,128)S(1)} %get-tuple-element.31), channel_id=1, source_target_pairs={{16,24},{17,25},{18,26},{19,27},{20,28},{21,29},{22,30},{23,31}} | collective-permute-start | bytes 1769480 | tf_op jit(solution)/shard_map/ppermute | solution.py:447
  4.2 3.0 %collective-permute-start = (f32[10,6,256]{2,1,0:T(8,128)S(1)}, f32[10,6,256]{2,1,0:T(8,128)S(1)}, u32[]{:S(2)}, u32[]{:S(2)}) collective-permute-start(f32[10,6,256]{2,1,0:T(8,128)S(1)} %bitcast.12), channel_id=1, source_target_pairs={{0,1},{1,0},{2,3},{3,2},{4,5},{5,4},{6,7},{7,6},{8,9},{9,8},{10,11... | collective-permute-start | bytes 184328 | tf_op jit(solution)/shard_map/ppermute | solution.py:174
  7.2 5.2 %all-gather = f32[8,1,16,128]{3,2,1,0:T(8,128)S(1)} all-gather(f32[2,1,16,128]{3,2,1,0:T(8,128)S(1)} %get-tuple-element.27), channel_id=2, replica_groups=mesh['gz'=4,'gx'=4,'gy'=2] {'gx'}, dimensions={0}, use_global_device_ids=true | all-gather | bytes 81920 | tf_op jit(solution)/shard_map/all_gather | solution.py:181
  12.4 0.0 collective-permute-done.rest_0_
  12.4 5.7 %shard_map.47 = (f32[10,6,16,256]{3,2,1,0:T(8,128)S(1)}, f32[6,16,256]{2,1,0:T(8,128)S(1)}, bf16[10,4,6,6,16,256]{5,4,3,2,1,0:T(8,128)(2,1)S(1)}, bf16[10,6,6,16,256]{4,3,2,1,0:T(8,128)(2,1)S(1)}) custom-call(f32[10,6,16,256]{3,2,1,0:T(8,128)} %bitcast.16, bf16[10,6,6,6,16,256]{5,4,3,2,1,0:T(8,128)(2,1)} %bitcast.14, ...), custom_call_target="tpu_custom_call" | custom-call | bytes 22937600 | tf_op jit(solution)/shard_map/pallas_call | solution.py:22
  18.1 3.5 %collective-permute-start.1 = (f32[6,16,256]{2,1,0:T(8,128)S(1)}, f32[6,16,256]{2,1,0:T(8,128)S(1)}, u32[]{:S(2)}, u32[]{:S(2)}) collective-permute-start(f32[6,16,256]{2,1,0:T(8,128)S(1)} %get-tuple-element.30.low_ref), channel_id=1, source_target_pairs={{0,8},{1,9},{2,10},{3,11},{4,12},{5,13},{6,14},{7,15}} | collective-permute-start | bytes 294920 | tf_op jit(solution)/shard_map/ppermute | solution.py:463
  21.6 0.1 shard_map.48.__.matrix_ref
  21.7 2.5 %collective-permute-done.1.came_ref.rest_0_ = f32[6,16,256]{2,1,0:T(8,128)S(1)} collective-permute-done((f32[6,16,256]{2,1,0:T(8,128)S(1)}, f32[6,16,256]{2,1,0:T(8,128)S(1)}, u32[]{:S(2)}, u32[]{:S(2)}) %collective-permute-start.1) | collective-permute-done | bytes 98336 | tf_op jit(solution)/shard_map/ppermute | solution.py:463
  24.2 0.0 collective-permute-done.2._.rest_2_
  24.2 0.7 %collective-permute-start.4 = (f32[6,16,256]{2,1,0:T(8,128)S(1)}, f32[6,16,256]{2,1,0:T(8,128)S(1)}, u32[]{:S(2)}, u32[]{:S(2)}) collective-permute-start(f32[6,16,256]{2,1,0:T(8,128)S(1)} %shard_map.49), channel_id=1, source_target_pairs={{8,24},{9,25},{10,26},{11,27},{12,28},{13,29},{14,30},{15,31}} | collective-permute-start | bytes 294920 | tf_op jit(solution)/shard_map/ppermute | solution.py:479
  24.9 0.7 %collective-permute-start.3 = (f32[6,16,256]{2,1,0:T(8,128)S(1)}, f32[6,16,256]{2,1,0:T(8,128)S(1)}, u32[]{:S(2)}, u32[]{:S(2)}) collective-permute-start(f32[6,16,256]{2,1,0:T(8,128)S(1)} %shard_map.49), channel_id=1, source_target_pairs={{8,16},{16,24},{9,17},{17,25},{10,18},{18,26},{11,19},{19,27},{12,... | collective-permute-start | bytes 294920 | tf_op jit(solution)/shard_map/ppermute | solution.py:480
  25.5 0.1 shard_map.50.rest_4_
  25.6 0.0 collective-permute-done.4.rest_3_
  25.6 0.0 collective-permute-done.3.rest_1_
  25.6 1.6 %shard_map.51 = (f32[10,6,16,256]{3,2,1,0:T(8,128)S(1)}, f32[10,6,16,256]{3,2,1,0:T(8,128)S(1)}, f32[2,1,16,128]{3,2,1,0:T(8,128)S(1)}, f32[1,10,6,256]{3,2,1,0:T(8,128)S(1)}, f32[6,6,16,256]{3,2,1,0:T(8,128)S(1)}) custom-call(f32[10,6,16,256]{3,2,1,0:T(8,128)S(1)} %get-tuple-element.29.source_ref, ...), custom_call_target="tpu_custom_call", output_to_operand_aliasing={{4}: (8, {})} | custom-call | bytes 6553600 | tf_op jit(solution)/shard_map/pallas_call | solution.py:22
  27.2 0.7 %collective-permute-start.7 = (f32[6,6,16,256]{3,2,1,0:T(8,128)S(1)}, f32[6,6,16,256]{3,2,1,0:T(8,128)S(1)}, u32[]{:S(2)}, u32[]{:S(2)}) collective-permute-start(f32[6,6,16,256]{3,2,1,0:T(8,128)S(1)} %get-tuple-element.40), channel_id=1, source_target_pairs={{16,8},{17,9},{18,10},{19,11},{20,12},{21,13},{22,14},{23,15}} | collective-permute-start | bytes 1769480 | tf_op jit(solution)/shard_map/ppermute | solution.py:507
  27.9 0.6 collective-permute-start.5
  28.5 5.2 %all-gather.1 = f32[8,1,16,128]{3,2,1,0:T(8,128)S(1)} all-gather(f32[2,1,16,128]{3,2,1,0:T(8,128)S(1)} %get-tuple-element.36), channel_id=3, replica_groups=mesh['gz'=4,'gx'=4,'gy'=2] {'gx'}, dimensions={0}, use_global_device_ids=true | all-gather | bytes 81920 | tf_op jit(solution)/shard_map/all_gather | solution.py:181
  33.7 0.0 collective-permute-done.5.rest_0_
  33.7 4.9 %shard_map.52 = (f32[10,6,16,256]{3,2,1,0:T(8,128)S(1)}, f32[6,16,256]{2,1,0:T(8,128)S(1)}) custom-call(f32[10,6,16,256]{3,2,1,0:T(8,128)S(1)} %get-tuple-element.33.sweep_ref, f32[10,6,16,256]{3,2,1,0:T(8,128)S(1)} %get-tuple-element.34.change_ref, bf16[10,6,6,16,256]{4,3,2,1,0:T(8,128)(2,1)S(1)} %get-tuple-element.25.inv_ref, ...), custom_call_target="tpu_custom_call" | custom-call | bytes 18022400 | tf_op jit(solution)/shard_map/pallas_call | solution.py:22
  38.6 0.7 %collective-permute-start.8 = (f32[6,16,256]{2,1,0:T(8,128)S(1)}, f32[6,16,256]{2,1,0:T(8,128)S(1)}, u32[]{:S(2)}, u32[]{:S(2)}) collective-permute-start(f32[6,16,256]{2,1,0:T(8,128)S(1)} %get-tuple-element.39.own_ref), channel_id=1, source_target_pairs={{24,8},{25,9},{26,10},{27,11},{28,12},{29,13},{30,14},{31,15}} | collective-permute-start | bytes 294920 | tf_op jit(solution)/shard_map/ppermute | solution.py:513
  39.3 0.7 %collective-permute-start.6 = (f32[6,16,256]{2,1,0:T(8,128)S(1)}, f32[6,16,256]{2,1,0:T(8,128)S(1)}, u32[]{:S(2)}, u32[]{:S(2)}) collective-permute-start(f32[6,16,256]{2,1,0:T(8,128)S(1)} %get-tuple-element.39.own_ref), channel_id=1, source_target_pairs={{24,16},{16,8},{25,17},{17,9},{26,18},{18,10},{27,19},{19,11},{28,... | collective-permute-start | bytes 294920 | tf_op jit(solution)/shard_map/ppermute | solution.py:514
  40.0 0.0 collective-permute-done.8.far
  40.0 0.0 collective-permute-done.6.near
  40.0 0.0 collective-permute-done.7.there_ref
  40.0 0.1 shard_map.53
  40.1 1.3 %collective-permute-start.9 = (f32[6,16,256]{2,1,0:T(8,128)S(1)}, f32[6,16,256]{2,1,0:T(8,128)S(1)}, u32[]{:S(2)}, u32[]{:S(2)}) collective-permute-start(f32[6,16,256]{2,1,0:T(8,128)S(1)} %get-tuple-element.42), channel_id=1, source_target_pairs={{8,0},{9,1},{10,2},{11,3},{12,4},{13,5},{14,6},{15,7}} | collective-permute-start | bytes 294920 | tf_op jit(solution)/shard_map/ppermute | solution.py:525
  41.4 22.4 %collective-permute-done.9.rest_1_ = f32[6,16,256]{2,1,0:T(8,128)S(1)} collective-permute-done((f32[6,16,256]{2,1,0:T(8,128)S(1)}, f32[6,16,256]{2,1,0:T(8,128)S(1)}, u32[]{:S(2)}, u32[]{:S(2)}) %collective-permute-start.9) | collective-permute-done | bytes 98336 | tf_op jit(solution)/shard_map/ppermute | solution.py:525
  63.8 2.0 %shard_map.54 = f32[10,6,16,256]{3,2,1,0:T(8,128)} custom-call(f32[10,6,16,256]{3,2,1,0:T(8,128)S(1)} %get-tuple-element.33.sweep_ref, f32[10,6,16,256]{3,2,1,0:T(8,128)S(1)} %get-tuple-element.38.inner_ref, bf16[10,6,6,16,256]{4,3,2,1,0:T(8,128)(2,1)S(1)} %get-tuple-element.25.inv_ref, bf16[10,6,6,16,256]{4,3,2,1,0:T(8,128)(2,1)S(1)} %get-tuple-element.32.high_jac, ...), custom_call_target="tpu_custom_call" | custom-call | bytes 8192000 | tf_op jit(solution)/shard_map/pallas_call | solution.py:22
  (1 shorter events, 0.0 us)
Async XLA Ops:
  3.5 20.7 %collective-permute-start.2 = (f32[6,6,16,256]{3,2,1,0:T(8,128)S(1)}, f32[6,6,16,256]{3,2,1,0:T(8,128)S(1)}, u32[]{:S(2)}, u32[]{:S(2)}) collective-permute-start(f32[6,6,16,256]{3,2,1,0:T(8,128)S(1)} %get-tuple-element.31), channel_id=1, source_target_pairs={{16,24},{17,25},{18,26},{19,27},{20,28},{21,29},{22,30},{23,31}} | collective-permute-start | bytes 1769480 | tf_op jit(solution)/shard_map/ppermute | solution.py:447
  4.2 8.2 %collective-permute-start = (f32[10,6,256]{2,1,0:T(8,128)S(1)}, f32[10,6,256]{2,1,0:T(8,128)S(1)}, u32[]{:S(2)}, u32[]{:S(2)}) collective-permute-start(f32[10,6,256]{2,1,0:T(8,128)S(1)} %bitcast.12), channel_id=1, source_target_pairs={{0,1},{1,0},{2,3},{3,2},{4,5},{5,4},{6,7},{7,6},{8,9},{9,8},{10,11... | collective-permute-start | bytes 184328 | tf_op jit(solution)/shard_map/ppermute | solution.py:174
  18.1 6.0 %collective-permute-start.1 = (f32[6,16,256]{2,1,0:T(8,128)S(1)}, f32[6,16,256]{2,1,0:T(8,128)S(1)}, u32[]{:S(2)}, u32[]{:S(2)}) collective-permute-start(f32[6,16,256]{2,1,0:T(8,128)S(1)} %get-tuple-element.30.low_ref), channel_id=1, source_target_pairs={{0,8},{1,9},{2,10},{3,11},{4,12},{5,13},{6,14},{7,15}} | collective-permute-start | bytes 294920 | tf_op jit(solution)/shard_map/ppermute | solution.py:463
  24.2 1.4 %collective-permute-start.4 = (f32[6,16,256]{2,1,0:T(8,128)S(1)}, f32[6,16,256]{2,1,0:T(8,128)S(1)}, u32[]{:S(2)}, u32[]{:S(2)}) collective-permute-start(f32[6,16,256]{2,1,0:T(8,128)S(1)} %shard_map.49), channel_id=1, source_target_pairs={{8,24},{9,25},{10,26},{11,27},{12,28},{13,29},{14,30},{15,31}} | collective-permute-start | bytes 294920 | tf_op jit(solution)/shard_map/ppermute | solution.py:479
  24.9 0.8 %collective-permute-start.3 = (f32[6,16,256]{2,1,0:T(8,128)S(1)}, f32[6,16,256]{2,1,0:T(8,128)S(1)}, u32[]{:S(2)}, u32[]{:S(2)}) collective-permute-start(f32[6,16,256]{2,1,0:T(8,128)S(1)} %shard_map.49), channel_id=1, source_target_pairs={{8,16},{16,24},{9,17},{17,25},{10,18},{18,26},{11,19},{19,27},{12,... | collective-permute-start | bytes 294920 | tf_op jit(solution)/shard_map/ppermute | solution.py:480
  27.2 12.8 %collective-permute-start.7 = (f32[6,6,16,256]{3,2,1,0:T(8,128)S(1)}, f32[6,6,16,256]{3,2,1,0:T(8,128)S(1)}, u32[]{:S(2)}, u32[]{:S(2)}) collective-permute-start(f32[6,6,16,256]{3,2,1,0:T(8,128)S(1)} %get-tuple-element.40), channel_id=1, source_target_pairs={{16,8},{17,9},{18,10},{19,11},{20,12},{21,13},{22,14},{23,15}} | collective-permute-start | bytes 1769480 | tf_op jit(solution)/shard_map/ppermute | solution.py:507
  27.9 5.8 %collective-permute-start.5 = (f32[10,6,256]{2,1,0:T(8,128)S(1)}, f32[10,6,256]{2,1,0:T(8,128)S(1)}, u32[]{:S(2)}, u32[]{:S(2)}) collective-permute-start(f32[10,6,256]{2,1,0:T(8,128)S(1)} %bitcast.11), channel_id=1, source_target_pairs={{0,1},{1,0},{2,3},{3,2},{4,5},{5,4},{6,7},{7,6},{8,9},{9,8},{10,11... | collective-permute-start | bytes 184328 | tf_op jit(solution)/shard_map/ppermute | solution.py:174
  38.6 1.4 %collective-permute-start.8 = (f32[6,16,256]{2,1,0:T(8,128)S(1)}, f32[6,16,256]{2,1,0:T(8,128)S(1)}, u32[]{:S(2)}, u32[]{:S(2)}) collective-permute-start(f32[6,16,256]{2,1,0:T(8,128)S(1)} %get-tuple-element.39.own_ref), channel_id=1, source_target_pairs={{24,8},{25,9},{26,10},{27,11},{28,12},{29,13},{30,14},{31,15}} | collective-permute-start | bytes 294920 | tf_op jit(solution)/shard_map/ppermute | solution.py:513
  39.3 0.7 %collective-permute-start.6 = (f32[6,16,256]{2,1,0:T(8,128)S(1)}, f32[6,16,256]{2,1,0:T(8,128)S(1)}, u32[]{:S(2)}, u32[]{:S(2)}) collective-permute-start(f32[6,16,256]{2,1,0:T(8,128)S(1)} %get-tuple-element.39.own_ref), channel_id=1, source_target_pairs={{24,16},{16,8},{25,17},{17,9},{26,18},{18,10},{27,19},{19,11},{28,... | collective-permute-start | bytes 294920 | tf_op jit(solution)/shard_map/ppermute | solution.py:514
  40.1 23.7 %collective-permute-start.9 = (f32[6,16,256]{2,1,0:T(8,128)S(1)}, f32[6,16,256]{2,1,0:T(8,128)S(1)}, u32[]{:S(2)}, u32[]{:S(2)}) collective-permute-start(f32[6,16,256]{2,1,0:T(8,128)S(1)} %get-tuple-element.42), channel_id=1, source_target_pairs={{8,0},{9,1},{10,2},{11,3},{12,4},{13,5},{14,6},{15,7}} | collective-permute-start | bytes 294920 | tf_op jit(solution)/shard_map/ppermute | solution.py:525

commit v6 on v5

--- a/solution.py
+++ b/solution.py
@@ -55,19 +55,26 @@
     return [dot6([get(r, c) for c in range(VARS)], values) for r in range(VARS)]
 
 
-def write_faces(value, x_face, y_face, z_count):
+def write_faces(value, x_face, y_face, z_count, slots):
     y_count = value.shape[2]
     x_count = value.shape[3]
     lane = lane_iota(y_count)
-    for side, start, source_lane in ((0, 0, 0), (1, x_count - LANES, LANES - 1)):
-        for group in range(x_face.shape[1]):
+    for group in range(x_face.shape[1]):
+        faces = []
+        for start, source_lane in ((0, 0), (x_count - LANES, LANES - 1)):
             held = jnp.zeros((y_count, LANES), F32)
             for slot in range(min(LANES, z_count * VARS - group * LANES)):
                 z, var = divmod(group * LANES + slot, VARS)
                 tile = value[z, var, :, start : start + LANES]
                 moved = pltpu.roll(tile, (slot - source_lane) % LANES, 1)
                 held = jnp.where(lane == slot, moved, held)
-            x_face[side, group] = held
+            faces.append(held)
+        if slots:
+            for device in range(x_face.shape[0]):
+                above = device > lax.axis_index("gx")
+                x_face[device, group] = jnp.where(above, faces[1], faces[0])
+        else:
+            x_face[0, group], x_face[1, group] = faces
     if y_face.shape[0] == 1:
         first = lax.axis_index("gy") == 0
         for z in range(z_count):
@@ -82,7 +89,7 @@
                 y_face[1, z, var : var + 1, :] = value[z, var, y_count - 1 : y_count, :]
 
 
-def halo_reader(x_all, y_rows, gx, gy):
+def halo_reader(x_all, y_rows, gx, gy, slots):
     me_x = lax.axis_index("gx")
 
     def column(there, side, to_lane):
@@ -91,7 +98,7 @@
 
         def read(z, var):
             j = z * VARS + var
-            face = x_all[device, side, j // LANES]
+            face = x_all[(device, *side, j // LANES)]
             moved = pltpu.roll(face, (to_lane + LANES - j % LANES) % LANES, 1)
             return jnp.where(exists, moved, jnp.zeros_like(moved))
 
@@ -106,7 +113,9 @@
 
         return read
 
-    return column(me_x - 1, 1, 0), column(me_x + 1, 0, LANES - 1), row(0), row(1)
+    sides = ((), ()) if slots else ((1,), (0,))
+    before, after = column(me_x - 1, sides[0], 0), column(me_x + 1, sides[1], LANES - 1)
+    return before, after, row(0), row(1)
 
 
 def neighbours(value, z, tile, tiles, halo):
@@ -162,23 +171,27 @@
         spans = [slice(t * LANES, (t + 1) * LANES) for t in range(tiles)]
         plane = ((VARS, ny, nx), F32)
         volume = ((nz, VARS, ny, nx), F32)
-        x_face = ((2, -(-nz * VARS // LANES), ny, LANES), F32)
+        x_groups = -(-nz * VARS // LANES)
+        x_face = ((2, x_groups, ny, LANES), F32)
+        x_slots = ((gx, x_groups, ny, LANES), F32)
         y_face = ((1 if gy == 2 else 2, nz, VARS, nx), F32)
         matrix = ((VARS, VARS, ny, nx), F32)
         blocks = ((nz, VARS, VARS, ny, nx), jac.dtype)
         side_blocks = ((nz, 4, VARS, VARS, ny, nx), jac.dtype)
         unit = 40 * nz * ny * nx
 
-        def exchange(x_face, y_face):
+        def exchange(x_side, y_side, slots):
             if gy == 2:
-                rows = [lax.ppermute(y_face[0], "gy", [(0, 1), (1, 0)])]
+                rows = [lax.ppermute(y_side[0], "gy", [(0, 1), (1, 0)])]
             else:
                 up = [(i, i + 1) for i in range(gy - 1)]
                 rows = [
-                    lax.ppermute(y_face[1], "gy", up),
-                    lax.ppermute(y_face[0], "gy", [(j, i) for i, j in up]),
+                    lax.ppermute(y_side[1], "gy", up),
+                    lax.ppermute(y_side[0], "gy", [(j, i) for i, j in up]),
                 ]
-            return lax.all_gather(x_face, "gx"), *rows
+            if slots:
+                return lax.all_to_all(x_side, "gx", 0, 0, tiled=True), *rows
+            return lax.all_gather(x_side, "gx"), *rows
 
 
         def forward_plane(source, inv_ref, low_jac, z, at, earlier):
@@ -286,27 +299,33 @@
             for z in range(nz):
                 for copy in copies(z):
                     copy.start()
+            here = lax.axis_index("gz") == 2
+            if matrices:
+
+                @pl.when(here)
+                def _():
+                    transfer(matrices[0], inv_ref, low_jac, wait)
+
             first_copy.wait()
-            write_faces(prev_ref, x_side, y_side, nz)
-            if not matrices:
+            write_faces(prev_ref, x_side, y_side, nz, True)
+
+            def rest_of_copies():
                 for z in range(nz):
                     wait(z)
-                return
-            here = lax.axis_index("gz") == 2
-
-            @pl.when(here)
-            def _():
-                transfer(matrices[0], inv_ref, low_jac, wait)
-
-            @pl.when(jnp.logical_not(here))
-            def _():
-                matrices[0][...] = jnp.zeros(matrix[0], F32)
-                for z in range(nz):
-                    wait(z)
+
+            if matrices:
+
+                @pl.when(jnp.logical_not(here))
+                def _():
+                    matrices[0][...] = jnp.zeros(matrix[0], F32)
+                    rest_of_copies()
+
+            else:
+                rest_of_copies()
 
         def first_kernel(rhs_hbm, jac_hbm, prev_ref, inv_ref, low_jac, x_all, *rest):
             y_rows, (source_ref, top_ref, sides, high_jac, rhs_ref, sems) = rest[:-6], rest[-6:]
-            halo = halo_reader(x_all, y_rows, gx, gy)
+            halo = halo_reader(x_all, y_rows, gx, gy, True)
 
             def copies(z):
                 return [
@@ -349,7 +368,7 @@
             for tile, at in enumerate(spans):
                 put(top_ref, top[tile], at)
 
-        def forward_mid_kernel(low_ref, came_ref, _, source_ref, inv_ref, low_jac, __, top_ref):
+        def forward_mid_kernel(low_ref, came_ref, source_ref, inv_ref, low_jac, _, top_ref):
             top_ref[...] = low_ref[...]
 
             @pl.when(lax.axis_index("gz") == 1)
@@ -372,11 +391,11 @@
                     change_ref[z, var, :, at] = result[var] - before[var]
 
             forward_sweep(source_ref, inv_ref, low_jac, starts, keep)
-            write_faces(change_ref, x_side, y_side, nz)
+            write_faces(change_ref, x_side, y_side, nz, False)
 
         def turn_kernel(sweep_ref, change_ref, inv_ref, sides, high_jac, x_all, *rest):
             y_rows, (inner_ref, low_ref) = rest[:-2], rest[-2:]
-            halo = halo_reader(x_all, y_rows, gx, gy)
+            halo = halo_reader(x_all, y_rows, gx, gy, False)
             for tile, at in enumerate(spans):
 
                 def step(i, later, tile=tile, at=at):
@@ -390,7 +409,8 @@
                 zero = tuple(jnp.zeros((ny, LANES), F32) for _ in range(VARS))
                 put(low_ref, lax.fori_loop(0, nz, step, zero), at)
 
-        def down_matrix_kernel(device, inv_ref, high_jac, matrix_ref):
+        def down_matrix_kernel(device, inv_ref, high_jac, *rest):
+            matrix_ref = rest[-1]
             here = lax.axis_index("gz") == device
 
             @pl.when(here)
@@ -435,7 +455,7 @@
 
         prev, inv, low_jac, x_side, y_side, *up_matrix = call(
             open_kernel,
-            [volume, blocks, blocks, x_face, y_face] + [matrix] * (1 if short else 0),
+            [volume, blocks, blocks, x_slots, y_face] + [matrix] * (1 if short else 0),
             prev,
             inv,
             jac,
@@ -445,7 +465,7 @@
         )
         if short:
             up_there = lax.ppermute(up_matrix[0], "gz", [(2, 3)])
-        halo = exchange(x_side, y_side)
+        halo = exchange(x_side, y_side, True)
         source, top, sides, high_jac = call(
             first_kernel,
             [volume, plane, side_blocks, blocks],
@@ -455,31 +475,35 @@
             inv,
             low_jac,
             *halo,
-            cost=14 * unit,
+            cost=unit // 8,
             in_hbm=(0, 1),
             scratch=[pltpu.VMEM(rhs.shape, F32), pltpu.SemaphoreType.DMA((3, nz))],
         )
         if short:
             first = lax.ppermute(top, "gz", [(0, 1)])
             (own_matrix,) = call(
-                functools.partial(down_matrix_kernel, 1), [matrix], inv, high_jac, cost=12 * unit
+                functools.partial(down_matrix_kernel, 1), [matrix], inv, high_jac, cost=unit // 8
             )
             (top,) = call(
                 forward_mid_kernel,
                 [plane],
                 top,
                 first,
-                up_there,
                 source,
                 inv,
                 low_jac,
                 own_matrix,
-                cost=3 * unit,
+                cost=unit // 8,
             )
             far = lax.ppermute(top, "gz", [(1, 3)])
             near = lax.ppermute(top, "gz", [(1, 2), (2, 3)])
             (down_matrix,) = call(
-                functools.partial(down_matrix_kernel, 2), [matrix], inv, high_jac, cost=12 * unit
+                functools.partial(down_matrix_kernel, 2),
+                [matrix],
+                inv,
+                high_jac,
+                up_there,
+                cost=unit // 8,
             )
             came = [first, near, up_there, far]
             extra = [down_matrix]
@@ -505,7 +529,7 @@
         )
         if short:
             down_there = lax.ppermute(extra[0], "gz", [(2, 1)])
-        halo = exchange(x_side, y_side)
+        halo = exchange(x_side, y_side, False)
         inner, low = call(
             turn_kernel, [volume, plane], sweep, change, inv, sides, high_jac, *halo, cost=11 * unit
         )

time: 66 us -> 64.4 us (0.976)
  waiting for transfers between devices: 24.8 us -> 22 us
  blocking collectives: 10.5 us -> 11.8 us
    all_to_all x0 -> x1, blocking collectives: none -> 6.52 us  [exchange(): return (lax.all_to_all(x_side, 'gx', 0, 0, tiled=True), *rows)]
    all_gather x2 -> x1, blocking collectives: 10.5 us -> 5.23 us  [exchange(): return (lax.all_gather(x_side, 'gx'), *rows)]
    ppermute x1, waiting for transfers between devices: 22.4 us -> 19.8 us  [body(): came = [entered, lax.ppermute(low, 'gz', [(1, 0)])]]
  transfers between devices with their start and end apart: 10 -> 10, of which waited for: 2 -> 2; matrix products, arithmetic and copies ran while one was open for 0% -> 0% of each run, Pallas kernels for 16% -> 17%
where the time goes in v6:
time: 64.4 us; the launch traced here: 64.2 us
  waiting for transfers between devices  22 us (34%)
  Pallas kernels  17.8 us (28%)
  starting transfers between devices  12.4 us (19%)
  blocking collectives  11.8 us (18%)
    ppermute x1, waiting for transfers between devices, body(): came = [entered, lax.ppermute(low, 'gz', [(1, 0)])]  19.8 us
    pallas_call x9, Pallas kernels, call(): pl.pallas_call(body, out_shape=shapes, in_specs=[far if i in in_hbm else...  17.8 us
    all_to_all x1, blocking collectives, exchange(): return (lax.all_to_all(x_side, 'gx', 0, 0, tiled=True), *rows)  6.52 us
    all_gather x1, blocking collectives, exchange(): return (lax.all_gather(x_side, 'gx'), *rows)  5.23 us
    ppermute x2, starting transfers between devices, exchange(): rows = [lax.ppermute(y_side[0], 'gy', [(0, 1), (1, 0)])]  3.6 us
    ppermute x1, starting transfers between devices, body(): first = lax.ppermute(top, 'gz', [(0, 1)])  3.49 us
    ppermute x1, waiting for transfers between devices, body(): first = lax.ppermute(top, 'gz', [(0, 1)])  2.13 us
    ppermute x1, starting transfers between devices, body(): came = [entered, lax.ppermute(low, 'gz', [(1, 0)])]  1.29 us
  transfers between devices with their start and end apart: 10, of which 2 were waited for; matrix products, arithmetic and copies ran while one was open for 0% of the time, Pallas kernels for 17%

profile of v6, /device:TPU:0, one launch (start us, length us, event | category | flops | bytes accessed | tf_op | source)
XLA Modules:
  0.0 64.2 jit_solution(13419109704202150339)
XLA Ops:
  0.0 3.5 %shard_map.46 = (f32[10,6,16,256]{3,2,1,0:T(8,128)S(1)}, bf16[10,6,6,16,256]{4,3,2,1,0:T(8,128)(2,1)S(1)}, bf16[10,6,6,16,256]{4,3,2,1,0:T(8,128)(2,1)S(1)}, f32...) custom-call(f32[10,6,16,256]{3,2,1,0:T(8,128)} %bitcast.15, ...), custom_call_target="tpu_custom_call" | custom-call | bytes 19660800 | tf_op jit(solution)/shard_map/pallas_call | solution.py:22
  3.5 0.7 %collective-permute-start.3 = (f32[6,6,16,256]{3,2,1,0:T(8,128)S(1)}, f32[6,6,16,256]{3,2,1,0:T(8,128)S(1)}, u32[]{:S(2)}, u32[]{:S(2)}) collective-permute-start(f32[6,6,16,256]{3,2,1,0:T(8,128)S(1)} %get-tuple-element.32), channel_id=1, source_target_pairs={{16,24},{17,25},{18,26},{19,27},{20,28},{21,29},{22,30},{23,31}} | collective-permute-start | bytes 1769480 | tf_op jit(solution)/shard_map/ppermute | solution.py:467
  4.2 3.0 %collective-permute-start = (f32[10,6,256]{2,1,0:T(8,128)S(1)}, f32[10,6,256]{2,1,0:T(8,128)S(1)}, u32[]{:S(2)}, u32[]{:S(2)}) collective-permute-start(f32[10,6,256]{2,1,0:T(8,128)S(1)} %bitcast.10), channel_id=1, source_target_pairs={{0,1},{1,0},{2,3},{3,2},{4,5},{5,4},{6,7},{7,6},{8,9},{9,8},{10,11... | collective-permute-start | bytes 184328 | tf_op jit(solution)/shard_map/ppermute | solution.py:185
  7.2 6.5 %all_to_all.5.x_all = f32[4,1,16,128]{3,2,1,0:T(8,128)S(1)} all-to-all(f32[4,1,16,128]{3,2,1,0:T(8,128)S(1)} %get-tuple-element.27), channel_id=1, replica_groups=mesh['gz'=4,'gx'=4,'gy'=2] {'gx'}, dimensions={0} | all-to-all | bytes 65536 | tf_op jit(solution)/shard_map/all_to_all | solution.py:193
  13.7 0.0 collective-permute-done.rest_0_
  13.7 5.7 %shard_map.47 = (f32[10,6,16,256]{3,2,1,0:T(8,128)S(1)}, f32[6,16,256]{2,1,0:T(8,128)S(1)}, bf16[10,4,6,6,16,256]{5,4,3,2,1,0:T(8,128)(2,1)S(1)}, bf16[10,6,6,16,256]{4,3,2,1,0:T(8,128)(2,1)S(1)}) custom-call(f32[10,6,16,256]{3,2,1,0:T(8,128)} %bitcast.14, bf16[10,6,6,6,16,256]{5,4,3,2,1,0:T(8,128)(2,1)} %bitcast.12, ...), custom_call_target="tpu_custom_call" | custom-call | bytes 204800 | tf_op jit(solution)/shard_map/pallas_call | solution.py:22
  19.4 3.5 %collective-permute-start.1 = (f32[6,16,256]{2,1,0:T(8,128)S(1)}, f32[6,16,256]{2,1,0:T(8,128)S(1)}, u32[]{:S(2)}, u32[]{:S(2)}) collective-permute-start(f32[6,16,256]{2,1,0:T(8,128)S(1)} %get-tuple-element.30.low_ref), channel_id=1, source_target_pairs={{0,8},{1,9},{2,10},{3,11},{4,12},{5,13},{6,14},{7,15}} | collective-permute-start | bytes 294920 | tf_op jit(solution)/shard_map/ppermute | solution.py:483
  22.9 0.1 shard_map.48._.matrix_ref
  23.0 2.1 %collective-permute-done.1.came_ref.rest_0_ = f32[6,16,256]{2,1,0:T(8,128)S(1)} collective-permute-done((f32[6,16,256]{2,1,0:T(8,128)S(1)}, f32[6,16,256]{2,1,0:T(8,128)S(1)}, u32[]{:S(2)}, u32[]{:S(2)}) %collective-permute-start.1) | collective-permute-done | bytes 98336 | tf_op jit(solution)/shard_map/ppermute | solution.py:483
  25.1 0.7 %collective-permute-start.4 = (f32[6,16,256]{2,1,0:T(8,128)S(1)}, f32[6,16,256]{2,1,0:T(8,128)S(1)}, u32[]{:S(2)}, u32[]{:S(2)}) collective-permute-start(f32[6,16,256]{2,1,0:T(8,128)S(1)} %shard_map.49), channel_id=1, source_target_pairs={{8,24},{9,25},{10,26},{11,27},{12,28},{13,29},{14,30},{15,31}} | collective-permute-start | bytes 294920 | tf_op jit(solution)/shard_map/ppermute | solution.py:498
  25.8 0.7 %collective-permute-start.2 = (f32[6,16,256]{2,1,0:T(8,128)S(1)}, f32[6,16,256]{2,1,0:T(8,128)S(1)}, u32[]{:S(2)}, u32[]{:S(2)}) collective-permute-start(f32[6,16,256]{2,1,0:T(8,128)S(1)} %shard_map.49), channel_id=1, source_target_pairs={{8,16},{16,24},{9,17},{17,25},{10,18},{18,26},{11,19},{19,27},{12,... | collective-permute-start | bytes 294920 | tf_op jit(solution)/shard_map/ppermute | solution.py:499
  26.5 0.0 collective-permute-done.3.rest_0_.rest_2_
  26.5 0.1 shard_map.50.rest_4_
  26.5 0.0 collective-permute-done.4.rest_3_
  26.6 0.0 collective-permute-done.2.rest_1_
  26.6 1.6 %shard_map.51 = (f32[10,6,16,256]{3,2,1,0:T(8,128)S(1)}, f32[10,6,16,256]{3,2,1,0:T(8,128)S(1)}, f32[2,1,16,128]{3,2,1,0:T(8,128)S(1)}, f32[1,10,6,256]{3,2,1,0:T(8,128)S(1)}, f32[6,6,16,256]{3,2,1,0:T(8,128)S(1)}) custom-call(f32[10,6,16,256]{3,2,1,0:T(8,128)S(1)} %get-tuple-element.29.source_ref, ...), custom_call_target="tpu_custom_call", output_to_operand_aliasing={{4}: (8, {})} | custom-call | bytes 6553600 | tf_op jit(solution)/shard_map/pallas_call | solution.py:22
  28.2 0.7 %collective-permute-start.7 = (f32[6,6,16,256]{3,2,1,0:T(8,128)S(1)}, f32[6,6,16,256]{3,2,1,0:T(8,128)S(1)}, u32[]{:S(2)}, u32[]{:S(2)}) collective-permute-start(f32[6,6,16,256]{3,2,1,0:T(8,128)S(1)} %get-tuple-element.40), channel_id=1, source_target_pairs={{16,8},{17,9},{18,10},{19,11},{20,12},{21,13},{22,14},{23,15}} | collective-permute-start | bytes 1769480 | tf_op jit(solution)/shard_map/ppermute | solution.py:531
  28.9 0.6 collective-permute-start.5
  29.5 5.2 %all-gather = f32[8,1,16,128]{3,2,1,0:T(8,128)S(1)} all-gather(f32[2,1,16,128]{3,2,1,0:T(8,128)S(1)} %get-tuple-element.36), channel_id=2, replica_groups=mesh['gz'=4,'gx'=4,'gy'=2] {'gx'}, dimensions={0}, use_global_device_ids=true | all-gather | bytes 81920 | tf_op jit(solution)/shard_map/all_gather | solution.py:194
  34.7 0.0 collective-permute-done.5.rest_0_
  34.7 4.9 %shard_map.52 = (f32[10,6,16,256]{3,2,1,0:T(8,128)S(1)}, f32[6,16,256]{2,1,0:T(8,128)S(1)}) custom-call(f32[10,6,16,256]{3,2,1,0:T(8,128)S(1)} %get-tuple-element.33.sweep_ref, f32[10,6,16,256]{3,2,1,0:T(8,128)S(1)} %get-tuple-element.34.change_ref, bf16[10,6,6,16,256]{4,3,2,1,0:T(8,128)(2,1)S(1)} %get-tuple-element.25.inv_ref, ...), custom_call_target="tpu_custom_call" | custom-call | bytes 18022400 | tf_op jit(solution)/shard_map/pallas_call | solution.py:22
  39.6 0.7 %collective-permute-start.8 = (f32[6,16,256]{2,1,0:T(8,128)S(1)}, f32[6,16,256]{2,1,0:T(8,128)S(1)}, u32[]{:S(2)}, u32[]{:S(2)}) collective-permute-start(f32[6,16,256]{2,1,0:T(8,128)S(1)} %get-tuple-element.39.own_ref), channel_id=1, source_target_pairs={{24,8},{25,9},{26,10},{27,11},{28,12},{29,13},{30,14},{31,15}} | collective-permute-start | bytes 294920 | tf_op jit(solution)/shard_map/ppermute | solution.py:537
  40.3 0.7 %collective-permute-start.6 = (f32[6,16,256]{2,1,0:T(8,128)S(1)}, f32[6,16,256]{2,1,0:T(8,128)S(1)}, u32[]{:S(2)}, u32[]{:S(2)}) collective-permute-start(f32[6,16,256]{2,1,0:T(8,128)S(1)} %get-tuple-element.39.own_ref), channel_id=1, source_target_pairs={{24,16},{16,8},{25,17},{17,9},{26,18},{18,10},{27,19},{19,11},{28,... | collective-permute-start | bytes 294920 | tf_op jit(solution)/shard_map/ppermute | solution.py:538
  40.9 0.0 collective-permute-done.8.far
  40.9 0.0 collective-permute-done.6.near
  40.9 0.0 collective-permute-done.7.there_ref
  41.0 0.1 shard_map.53
  41.1 1.3 %collective-permute-start.9 = (f32[6,16,256]{2,1,0:T(8,128)S(1)}, f32[6,16,256]{2,1,0:T(8,128)S(1)}, u32[]{:S(2)}, u32[]{:S(2)}) collective-permute-start(f32[6,16,256]{2,1,0:T(8,128)S(1)} %get-tuple-element.42), channel_id=1, source_target_pairs={{8,0},{9,1},{10,2},{11,3},{12,4},{13,5},{14,6},{15,7}} | collective-permute-start | bytes 294920 | tf_op jit(solution)/shard_map/ppermute | solution.py:549
  42.4 19.8 %collective-permute-done.9.rest_1_ = f32[6,16,256]{2,1,0:T(8,128)S(1)} collective-permute-done((f32[6,16,256]{2,1,0:T(8,128)S(1)}, f32[6,16,256]{2,1,0:T(8,128)S(1)}, u32[]{:S(2)}, u32[]{:S(2)}) %collective-permute-start.9) | collective-permute-done | bytes 98336 | tf_op jit(solution)/shard_map/ppermute | solution.py:549
  62.2 2.0 %shard_map.54 = f32[10,6,16,256]{3,2,1,0:T(8,128)} custom-call(f32[10,6,16,256]{3,2,1,0:T(8,128)S(1)} %get-tuple-element.33.sweep_ref, f32[10,6,16,256]{3,2,1,0:T(8,128)S(1)} %get-tuple-element.38.inner_ref, bf16[10,6,6,16,256]{4,3,2,1,0:T(8,128)(2,1)S(1)} %get-tuple-element.25.inv_ref, bf16[10,6,6,16,256]{4,3,2,1,0:T(8,128)(2,1)S(1)} %get-tuple-element.31.high_jac, ...), custom_call_target="tpu_custom_call" | custom-call | bytes 8192000 | tf_op jit(solution)/shard_map/pallas_call | solution.py:22
  (1 shorter events, 0.0 us)
Async XLA Ops:
  3.5 23.0 %collective-permute-start.3 = (f32[6,6,16,256]{3,2,1,0:T(8,128)S(1)}, f32[6,6,16,256]{3,2,1,0:T(8,128)S(1)}, u32[]{:S(2)}, u32[]{:S(2)}) collective-permute-start(f32[6,6,16,256]{3,2,1,0:T(8,128)S(1)} %get-tuple-element.32), channel_id=1, source_target_pairs={{16,24},{17,25},{18,26},{19,27},{20,28},{21,29},{22,30},{23,31}} | collective-permute-start | bytes 1769480 | tf_op jit(solution)/shard_map/ppermute | solution.py:467
  4.2 9.5 %collective-permute-start = (f32[10,6,256]{2,1,0:T(8,128)S(1)}, f32[10,6,256]{2,1,0:T(8,128)S(1)}, u32[]{:S(2)}, u32[]{:S(2)}) collective-permute-start(f32[10,6,256]{2,1,0:T(8,128)S(1)} %bitcast.10), channel_id=1, source_target_pairs={{0,1},{1,0},{2,3},{3,2},{4,5},{5,4},{6,7},{7,6},{8,9},{9,8},{10,11... | collective-permute-start | bytes 184328 | tf_op jit(solution)/shard_map/ppermute | solution.py:185
  19.4 5.7 %collective-permute-start.1 = (f32[6,16,256]{2,1,0:T(8,128)S(1)}, f32[6,16,256]{2,1,0:T(8,128)S(1)}, u32[]{:S(2)}, u32[]{:S(2)}) collective-permute-start(f32[6,16,256]{2,1,0:T(8,128)S(1)} %get-tuple-element.30.low_ref), channel_id=1, source_target_pairs={{0,8},{1,9},{2,10},{3,11},{4,12},{5,13},{6,14},{7,15}} | collective-permute-start | bytes 294920 | tf_op jit(solution)/shard_map/ppermute | solution.py:483
  25.1 1.4 %collective-permute-start.4 = (f32[6,16,256]{2,1,0:T(8,128)S(1)}, f32[6,16,256]{2,1,0:T(8,128)S(1)}, u32[]{:S(2)}, u32[]{:S(2)}) collective-permute-start(f32[6,16,256]{2,1,0:T(8,128)S(1)} %shard_map.49), channel_id=1, source_target_pairs={{8,24},{9,25},{10,26},{11,27},{12,28},{13,29},{14,30},{15,31}} | collective-permute-start | bytes 294920 | tf_op jit(solution)/shard_map/ppermute | solution.py:498
  25.8 0.8 %collective-permute-start.2 = (f32[6,16,256]{2,1,0:T(8,128)S(1)}, f32[6,16,256]{2,1,0:T(8,128)S(1)}, u32[]{:S(2)}, u32[]{:S(2)}) collective-permute-start(f32[6,16,256]{2,1,0:T(8,128)S(1)} %shard_map.49), channel_id=1, source_target_pairs={{8,16},{16,24},{9,17},{17,25},{10,18},{18,26},{11,19},{19,27},{12,... | collective-permute-start | bytes 294920 | tf_op jit(solution)/shard_map/ppermute | solution.py:499
  28.2 12.8 %collective-permute-start.7 = (f32[6,6,16,256]{3,2,1,0:T(8,128)S(1)}, f32[6,6,16,256]{3,2,1,0:T(8,128)S(1)}, u32[]{:S(2)}, u32[]{:S(2)}) collective-permute-start(f32[6,6,16,256]{3,2,1,0:T(8,128)S(1)} %get-tuple-element.40), channel_id=1, source_target_pairs={{16,8},{17,9},{18,10},{19,11},{20,12},{21,13},{22,14},{23,15}} | collective-permute-start | bytes 1769480 | tf_op jit(solution)/shard_map/ppermute | solution.py:531
  28.9 5.8 %collective-permute-start.5 = (f32[10,6,256]{2,1,0:T(8,128)S(1)}, f32[10,6,256]{2,1,0:T(8,128)S(1)}, u32[]{:S(2)}, u32[]{:S(2)}) collective-permute-start(f32[10,6,256]{2,1,0:T(8,128)S(1)} %bitcast.9), channel_id=1, source_target_pairs={{0,1},{1,0},{2,3},{3,2},{4,5},{5,4},{6,7},{7,6},{8,9},{9,8},{10,11... | collective-permute-start | bytes 184328 | tf_op jit(solution)/shard_map/ppermute | solution.py:185
  39.6 1.4 %collective-permute-start.8 = (f32[6,16,256]{2,1,0:T(8,128)S(1)}, f32[6,16,256]{2,1,0:T(8,128)S(1)}, u32[]{:S(2)}, u32[]{:S(2)}) collective-permute-start(f32[6,16,256]{2,1,0:T(8,128)S(1)} %get-tuple-element.39.own_ref), channel_id=1, source_target_pairs={{24,8},{25,9},{26,10},{27,11},{28,12},{29,13},{30,14},{31,15}} | collective-permute-start | bytes 294920 | tf_op jit(solution)/shard_map/ppermute | solution.py:537
  40.3 0.7 %collective-permute-start.6 = (f32[6,16,256]{2,1,0:T(8,128)S(1)}, f32[6,16,256]{2,1,0:T(8,128)S(1)}, u32[]{:S(2)}, u32[]{:S(2)}) collective-permute-start(f32[6,16,256]{2,1,0:T(8,128)S(1)} %get-tuple-element.39.own_ref), channel_id=1, source_target_pairs={{24,16},{16,8},{25,17},{17,9},{26,18},{18,10},{27,19},{19,11},{28,... | collective-permute-start | bytes 294920 | tf_op jit(solution)/shard_map/ppermute | solution.py:538
  41.1 21.1 %collective-permute-start.9 = (f32[6,16,256]{2,1,0:T(8,128)S(1)}, f32[6,16,256]{2,1,0:T(8,128)S(1)}, u32[]{:S(2)}, u32[]{:S(2)}) collective-permute-start(f32[6,16,256]{2,1,0:T(8,128)S(1)} %get-tuple-element.42), channel_id=1, source_target_pairs={{8,0},{9,1},{10,2},{11,3},{12,4},{13,5},{14,6},{15,7}} | collective-permute-start | bytes 294920 | tf_op jit(solution)/shard_map/ppermute | solution.py:549

commit v7 on v6

--- a/solution.py
+++ b/solution.py
@@ -55,7 +55,7 @@
     return [dot6([get(r, c) for c in range(VARS)], values) for r in range(VARS)]
 
 
-def write_faces(value, x_face, y_face, z_count, slots):
+def write_faces(value, x_face, y_face, z_count):
     y_count = value.shape[2]
     x_count = value.shape[3]
     lane = lane_iota(y_count)
@@ -69,12 +69,7 @@
                 moved = pltpu.roll(tile, (slot - source_lane) % LANES, 1)
                 held = jnp.where(lane == slot, moved, held)
             faces.append(held)
-        if slots:
-            for device in range(x_face.shape[0]):
-                above = device > lax.axis_index("gx")
-                x_face[device, group] = jnp.where(above, faces[1], faces[0])
-        else:
-            x_face[0, group], x_face[1, group] = faces
+        x_face[0, group], x_face[1, group] = faces
     if y_face.shape[0] == 1:
         first = lax.axis_index("gy") == 0
         for z in range(z_count):
@@ -89,7 +84,7 @@
                 y_face[1, z, var : var + 1, :] = value[z, var, y_count - 1 : y_count, :]
 
 
-def halo_reader(x_all, y_rows, gx, gy, slots):
+def halo_reader(x_all, y_rows, gx, gy):
     me_x = lax.axis_index("gx")
 
     def column(there, side, to_lane):
@@ -98,7 +93,7 @@
 
         def read(z, var):
             j = z * VARS + var
-            face = x_all[(device, *side, j // LANES)]
+            face = x_all[device, side, j // LANES]
             moved = pltpu.roll(face, (to_lane + LANES - j % LANES) % LANES, 1)
             return jnp.where(exists, moved, jnp.zeros_like(moved))
 
@@ -113,9 +108,7 @@
 
         return read
 
-    sides = ((), ()) if slots else ((1,), (0,))
-    before, after = column(me_x - 1, sides[0], 0), column(me_x + 1, sides[1], LANES - 1)
-    return before, after, row(0), row(1)
+    return column(me_x - 1, 1, 0), column(me_x + 1, 0, LANES - 1), row(0), row(1)
 
 
 def neighbours(value, z, tile, tiles, halo):
@@ -173,14 +166,13 @@
         volume = ((nz, VARS, ny, nx), F32)
         x_groups = -(-nz * VARS // LANES)
         x_face = ((2, x_groups, ny, LANES), F32)
-        x_slots = ((gx, x_groups, ny, LANES), F32)
         y_face = ((1 if gy == 2 else 2, nz, VARS, nx), F32)
         matrix = ((VARS, VARS, ny, nx), F32)
         blocks = ((nz, VARS, VARS, ny, nx), jac.dtype)
         side_blocks = ((nz, 4, VARS, VARS, ny, nx), jac.dtype)
         unit = 40 * nz * ny * nx
 
-        def exchange(x_side, y_side, slots):
+        def exchange(x_side, y_side):
             if gy == 2:
                 rows = [lax.ppermute(y_side[0], "gy", [(0, 1), (1, 0)])]
             else:
@@ -189,8 +181,6 @@
                     lax.ppermute(y_side[1], "gy", up),
                     lax.ppermute(y_side[0], "gy", [(j, i) for i, j in up]),
                 ]
-            if slots:
-                return lax.all_to_all(x_side, "gx", 0, 0, tiled=True), *rows
             return lax.all_gather(x_side, "gx"), *rows
 
 
@@ -212,6 +202,9 @@
             for ref in refs[1:]:
                 total = [a + ref[var, :, at] for var, a in enumerate(total)]
             return tuple(total)
+
+        def planes_in(ref, at):
+            return [ref[var, :, at] for var in range(VARS)]
 
         def apply_matrix(matrix_ref, vector, at):
             return apply_block(block(matrix_ref, at=at), vector)
@@ -307,7 +300,7 @@
                     transfer(matrices[0], inv_ref, low_jac, wait)
 
             first_copy.wait()
-            write_faces(prev_ref, x_side, y_side, nz, True)
+            write_faces(prev_ref, x_side, y_side, nz)
 
             def rest_of_copies():
                 for z in range(nz):
@@ -323,9 +316,30 @@
             else:
                 rest_of_copies()
 
-        def first_kernel(rhs_hbm, jac_hbm, prev_ref, inv_ref, low_jac, x_all, *rest):
-            y_rows, (source_ref, top_ref, sides, high_jac, rhs_ref, sems) = rest[:-6], rest[-6:]
-            halo = halo_reader(x_all, y_rows, gx, gy, True)
+        def on(wanted, work):
+            if wanted is None:
+                work()
+            else:
+                pl.when(wanted(lax.axis_index("gz")))(work)
+
+        def first_kernel(wanted, rhs_hbm, jac_hbm, prev_ref, inv_ref, low_jac, x_all, *rest):
+            y_rows, outs = rest[: 1 if gy == 2 else 2], rest[-6:]
+            on(
+                wanted,
+                lambda: first_work(
+                    rhs_hbm, jac_hbm, prev_ref, inv_ref, low_jac, x_all, y_rows, *outs
+                ),
+            )
+
+        def first_again_kernel(wanted, *refs):
+            refs[-5][...] = refs[-9][...]
+            first_kernel(wanted, *refs)
+
+        def first_work(
+            rhs_hbm, jac_hbm, prev_ref, inv_ref, low_jac, x_all, y_rows,
+            source_ref, top_ref, sides, high_jac, rhs_ref, sems,
+        ):
+            halo = halo_reader(x_all, y_rows, gx, gy)
 
             def copies(z):
                 return [
@@ -391,11 +405,25 @@
                     change_ref[z, var, :, at] = result[var] - before[var]
 
             forward_sweep(source_ref, inv_ref, low_jac, starts, keep)
-            write_faces(change_ref, x_side, y_side, nz, False)
-
-        def turn_kernel(sweep_ref, change_ref, inv_ref, sides, high_jac, x_all, *rest):
-            y_rows, (inner_ref, low_ref) = rest[:-2], rest[-2:]
-            halo = halo_reader(x_all, y_rows, gx, gy, False)
+            write_faces(change_ref, x_side, y_side, nz)
+
+        def turn_kernel(wanted, sweep_ref, change_ref, inv_ref, sides, high_jac, x_all, *rest):
+            y_rows, outs = rest[: 1 if gy == 2 else 2], rest[-2:]
+            on(
+                wanted,
+                lambda: turn_work(
+                    sweep_ref, change_ref, inv_ref, sides, high_jac, x_all, y_rows, *outs
+                ),
+            )
+
+        def turn_again_kernel(wanted, *refs):
+            refs[-1][...] = refs[-3][...]
+            turn_kernel(wanted, *refs)
+
+        def turn_work(
+            sweep_ref, change_ref, inv_ref, sides, high_jac, x_all, y_rows, inner_ref, low_ref
+        ):
+            halo = halo_reader(x_all, y_rows, gx, gy)
             for tile, at in enumerate(spans):
 
                 def step(i, later, tile=tile, at=at):
@@ -428,12 +456,16 @@
             for tile, at in enumerate(spans):
                 put(low_ref, low[tile], at)
 
-        def backward_mid_kernel(own_ref, near, there_ref, far, matrix_ref, came_ref, low_ref):
+        def far_kernel(far_ref, matrix_ref, moved_ref):
             for at in spans:
-                came = arrived((near,), there_ref, far, at)
+                put(moved_ref, apply_matrix(matrix_ref, planes_in(far_ref, at), at), at)
+
+        def backward_mid_kernel(own_ref, near_ref, moved_ref, matrix_ref, came_ref, low_ref):
+            for at in spans:
+                came = incoming((near_ref, moved_ref), at)
                 moved = apply_matrix(matrix_ref, came, at)
                 put(came_ref, came, at)
-                put(low_ref, [own_ref[var, :, at] + moved[var] for var in range(VARS)], at)
+                put(low_ref, [a + b for a, b in zip(planes_in(own_ref, at), moved)], at)
 
         def update_kernel(sweep_ref, inner_ref, inv_ref, high_jac, *rest):
             came, (out_hbm, held, sems) = rest[:-3], rest[-3:]
@@ -455,7 +487,7 @@
 
         prev, inv, low_jac, x_side, y_side, *up_matrix = call(
             open_kernel,
-            [volume, blocks, blocks, x_slots, y_face] + [matrix] * (1 if short else 0),
+            [volume, blocks, blocks, x_face, y_face] + [matrix] * (1 if short else 0),
             prev,
             inv,
             jac,
@@ -465,22 +497,34 @@
         )
         if short:
             up_there = lax.ppermute(up_matrix[0], "gz", [(2, 3)])
-        halo = exchange(x_side, y_side, True)
-        source, top, sides, high_jac = call(
-            first_kernel,
-            [volume, plane, side_blocks, blocks],
-            rhs,
-            jac,
-            prev,
-            inv,
-            low_jac,
-            *halo,
+        halo = exchange(x_side, y_side)
+        ahead, behind = None, None
+        if short:
+            ahead, behind = (lambda device: device == 0), (lambda device: device != 0)
+        first_args = [rhs, jac, prev, inv, low_jac, *halo]
+        first_options = dict(
             cost=unit // 8,
             in_hbm=(0, 1),
             scratch=[pltpu.VMEM(rhs.shape, F32), pltpu.SemaphoreType.DMA((3, nz))],
         )
+        first_outs = [volume, plane, side_blocks, blocks]
+        source, top, sides, high_jac = call(
+            functools.partial(first_kernel, ahead), first_outs, *first_args, **first_options
+        )
         if short:
             first = lax.ppermute(top, "gz", [(0, 1)])
+            n = len(first_args)
+            source, top, sides, high_jac = call(
+                functools.partial(first_again_kernel, behind),
+                first_outs,
+                *first_args,
+                source,
+                top,
+                sides,
+                high_jac,
+                aliases={n: 0, n + 2: 2, n + 3: 3},
+                **first_options,
+            )
             (own_matrix,) = call(
                 functools.partial(down_matrix_kernel, 1), [matrix], inv, high_jac, cost=unit // 8
             )
@@ -529,22 +573,29 @@
         )
         if short:
             down_there = lax.ppermute(extra[0], "gz", [(2, 1)])
-        halo = exchange(x_side, y_side, False)
+        halo = exchange(x_side, y_side)
+        if short:
+            ahead, behind = (lambda device: device == 3), (lambda device: device != 3)
+        turn_args = [sweep, change, inv, sides, high_jac, *halo]
         inner, low = call(
-            turn_kernel, [volume, plane], sweep, change, inv, sides, high_jac, *halo, cost=11 * unit
+            functools.partial(turn_kernel, ahead), [volume, plane], *turn_args, cost=11 * unit
         )
         if short:
-            far = lax.ppermute(low, "gz", [(3, 1)])
+            ahead_low = low
+            inner, low = call(
+                functools.partial(turn_again_kernel, behind),
+                [volume, plane],
+                *turn_args,
+                inner,
+                low,
+                aliases={len(turn_args): 0},
+                cost=unit // 8,
+            )
             near = lax.ppermute(low, "gz", [(3, 2), (2, 1)])
+            far = lax.ppermute(ahead_low, "gz", [(3, 1)])
+            (moved,) = call(far_kernel, [plane], far, down_there, cost=unit // 8)
             entered, low = call(
-                backward_mid_kernel,
-                [plane, plane],
-                low,
-                near,
-                down_there,
-                far,
-                own_matrix,
-                cost=unit,
+                backward_mid_kernel, [plane, plane], low, near, moved, own_matrix, cost=unit // 8
             )
             came = [entered, lax.ppermute(low, "gz", [(1, 0)])]
         else:

time: 64.4 us -> 62.8 us (0.975)
  starting transfers between devices: 12.4 us -> 9.73 us
  waiting for transfers between devices: 22 us -> 24.1 us
  blocking collectives: 11.8 us -> 10.5 us
    all_to_all x1 -> x0, blocking collectives: 6.52 us -> none  [exchange(): return (lax.all_to_all(x_side, 'gx', 0, 0, tiled=True), *rows)]
    all_gather x1 -> x2, blocking collectives: 5.23 us -> 10.5 us  [exchange(): return (lax.all_gather(x_side, 'gx'), *rows)]
    ppermute x1, starting transfers between devices: 3.49 us -> 1.3 us  [body(): first = lax.ppermute(top, 'gz', [(0, 1)])]
    ppermute x1, waiting for transfers between devices: 19.8 us -> 21.6 us  [body(): came = [entered, lax.ppermute(low, 'gz', [(1, 0)])]]
    pallas_call x9 -> x12, Pallas kernels: 17.8 us -> 18.1 us  [call(): pl.pallas_call(body, out_shape=shapes, in_specs=[far if i in in_hbm else...]
  transfers between devices with their start and end apart: 10 -> 10, of which waited for: 2 -> 2; matrix products, arithmetic and copies ran while one was open for 0% -> 0% of each run, Pallas kernels for 17% -> 18%
where the time goes in v7:
time: 62.8 us; the launch traced here: 62.6 us
  waiting for transfers between devices  24.1 us (38%)
  Pallas kernels  18.1 us (29%)
  blocking collectives  10.5 us (17%)
  starting transfers between devices  9.73 us (15%)
    ppermute x1, waiting for transfers between devices, body(): came = [entered, lax.ppermute(low, 'gz', [(1, 0)])]  21.6 us
    pallas_call x12, Pallas kernels, call(): pl.pallas_call(body, out_shape=shapes, in_specs=[far if i in in_hbm else...  18.1 us
    all_gather x2, blocking collectives, exchange(): return (lax.all_gather(x_side, 'gx'), *rows)  10.5 us
    ppermute x2, starting transfers between devices, exchange(): rows = [lax.ppermute(y_side[0], 'gy', [(0, 1), (1, 0)])]  3.1 us
    ppermute x1, waiting for transfers between devices, body(): first = lax.ppermute(top, 'gz', [(0, 1)])  2.45 us
    ppermute x1, starting transfers between devices, body(): first = lax.ppermute(top, 'gz', [(0, 1)])  1.3 us
    ppermute x1, starting transfers between devices, body(): came = [entered, lax.ppermute(low, 'gz', [(1, 0)])]  1.29 us
  transfers between devices with their start and end apart: 10, of which 2 were waited for; matrix products, arithmetic and copies ran while one was open for 0% of the time, Pallas kernels for 18%

profile of v7, /device:TPU:0, one launch (start us, length us, event | category | flops | bytes accessed | tf_op | source)
XLA Modules:
  0.0 62.6 jit_solution(14297133964904673184)
XLA Ops:
  0.0 3.4 %shard_map.46 = (f32[10,6,16,256]{3,2,1,0:T(8,128)S(1)}, bf16[10,6,6,16,256]{4,3,2,1,0:T(8,128)(2,1)S(1)}, bf16[10,6,6,16,256]{4,3,2,1,0:T(8,128)(2,1)S(1)}, f32...) custom-call(f32[10,6,16,256]{3,2,1,0:T(8,128)} %bitcast.21, ...), custom_call_target="tpu_custom_call" | custom-call | bytes 19660800 | tf_op jit(solution)/shard_map/pallas_call | solution.py:22
  3.5 0.7 %collective-permute-start.3 = (f32[6,6,16,256]{3,2,1,0:T(8,128)S(1)}, f32[6,6,16,256]{3,2,1,0:T(8,128)S(1)}, u32[]{:S(2)}, u32[]{:S(2)}) collective-permute-start(f32[6,6,16,256]{3,2,1,0:T(8,128)S(1)} %get-tuple-element.42), channel_id=1, source_target_pairs={{16,24},{17,25},{18,26},{19,27},{20,28},{21,29},{22,30},{23,31}} | collective-permute-start | bytes 1769480 | tf_op jit(solution)/shard_map/ppermute | solution.py:499
  4.2 3.0 %collective-permute-start = (f32[10,6,256]{2,1,0:T(8,128)S(1)}, f32[10,6,256]{2,1,0:T(8,128)S(1)}, u32[]{:S(2)}, u32[]{:S(2)}) collective-permute-start(f32[10,6,256]{2,1,0:T(8,128)S(1)} %bitcast.14), channel_id=1, source_target_pairs={{0,1},{1,0},{2,3},{3,2},{4,5},{5,4},{6,7},{7,6},{8,9},{9,8},{10,11... | collective-permute-start | bytes 184328 | tf_op jit(solution)/shard_map/ppermute | solution.py:177
  7.2 5.2 %all-gather = f32[8,1,16,128]{3,2,1,0:T(8,128)S(1)} all-gather(f32[2,1,16,128]{3,2,1,0:T(8,128)S(1)} %get-tuple-element.33), channel_id=2, replica_groups=mesh['gz'=4,'gx'=4,'gy'=2] {'gx'}, dimensions={0}, use_global_device_ids=true | all-gather | bytes 81920 | tf_op jit(solution)/shard_map/all_gather | solution.py:184
  12.4 0.0 collective-permute-done.rest_0_.refs_6_
  12.4 5.7 %shard_map.47 = (f32[10,6,16,256]{3,2,1,0:T(8,128)S(1)}, f32[6,16,256]{2,1,0:T(8,128)S(1)}, bf16[10,4,6,6,16,256]{5,4,3,2,1,0:T(8,128)(2,1)S(1)}, bf16[10,6,6,16,256]{4,3,2,1,0:T(8,128)(2,1)S(1)}) custom-call(f32[10,6,16,256]{3,2,1,0:T(8,128)} %bitcast.18, bf16[10,6,6,6,16,256]{5,4,3,2,1,0:T(8,128)(2,1)} %bitcast.16, ...), custom_call_target="tpu_custom_call" | custom-call | bytes 204800 | tf_op jit(solution)/shard_map/pallas_call | solution.py:22
  18.1 1.3 %collective-permute-start.1 = (f32[6,16,256]{2,1,0:T(8,128)S(1)}, f32[6,16,256]{2,1,0:T(8,128)S(1)}, u32[]{:S(2)}, u32[]{:S(2)}) collective-permute-start(f32[6,16,256]{2,1,0:T(8,128)S(1)} %get-tuple-element.36.refs_8_), channel_id=1, source_target_pairs={{0,8},{1,9},{2,10},{3,11},{4,12},{5,13},{6,14},{7,15}} | collective-permute-start | bytes 294920 | tf_op jit(solution)/shard_map/ppermute | solution.py:515
  19.4 0.3 shard_map.48
  19.7 0.1 shard_map.49._.matrix_ref
  19.8 2.5 %collective-permute-done.1.came_ref.rest_0_ = f32[6,16,256]{2,1,0:T(8,128)S(1)} collective-permute-done((f32[6,16,256]{2,1,0:T(8,128)S(1)}, f32[6,16,256]{2,1,0:T(8,128)S(1)}, u32[]{:S(2)}, u32[]{:S(2)}) %collective-permute-start.1) | collective-permute-done | bytes 98336 | tf_op jit(solution)/shard_map/ppermute | solution.py:515
  22.2 0.7 %collective-permute-start.4 = (f32[6,16,256]{2,1,0:T(8,128)S(1)}, f32[6,16,256]{2,1,0:T(8,128)S(1)}, u32[]{:S(2)}, u32[]{:S(2)}) collective-permute-start(f32[6,16,256]{2,1,0:T(8,128)S(1)} %shard_map.50), channel_id=1, source_target_pairs={{8,24},{9,25},{10,26},{11,27},{12,28},{13,29},{14,30},{15,31}} | collective-permute-start | bytes 294920 | tf_op jit(solution)/shard_map/ppermute | solution.py:542
  22.9 0.7 %collective-permute-start.2 = (f32[6,16,256]{2,1,0:T(8,128)S(1)}, f32[6,16,256]{2,1,0:T(8,128)S(1)}, u32[]{:S(2)}, u32[]{:S(2)}) collective-permute-start(f32[6,16,256]{2,1,0:T(8,128)S(1)} %shard_map.50), channel_id=1, source_target_pairs={{8,16},{16,24},{9,17},{17,25},{10,18},{18,26},{11,19},{19,27},{12,... | collective-permute-start | bytes 294920 | tf_op jit(solution)/shard_map/ppermute | solution.py:543
  23.6 0.0 collective-permute-done.3.rest_0_.rest_2_
  23.6 0.1 shard_map.51.rest_4_
  23.6 0.0 collective-permute-done.4.rest_3_
  23.7 0.0 collective-permute-done.2.rest_1_
  23.7 1.6 %shard_map.52 = (f32[10,6,16,256]{3,2,1,0:T(8,128)S(1)}, f32[10,6,16,256]{3,2,1,0:T(8,128)S(1)}, f32[2,1,16,128]{3,2,1,0:T(8,128)S(1)}, f32[1,10,6,256]{3,2,1,0:T(8,128)S(1)}, f32[6,6,16,256]{3,2,1,0:T(8,128)S(1)}) custom-call(f32[10,6,16,256]{3,2,1,0:T(8,128)S(1)} %get-tuple-element.39.source_ref, ...), custom_call_target="tpu_custom_call", output_to_operand_aliasing={{4}: (8, {})} | custom-call | bytes 6553600 | tf_op jit(solution)/shard_map/pallas_call | solution.py:22
  25.3 0.7 %collective-permute-start.8 = (f32[6,6,16,256]{3,2,1,0:T(8,128)S(1)}, f32[6,6,16,256]{3,2,1,0:T(8,128)S(1)}, u32[]{:S(2)}, u32[]{:S(2)}) collective-permute-start(f32[6,6,16,256]{3,2,1,0:T(8,128)S(1)} %get-tuple-element.52), channel_id=1, source_target_pairs={{16,8},{17,9},{18,10},{19,11},{20,12},{21,13},{22,14},{23,15}} | collective-permute-start | bytes 1769480 | tf_op jit(solution)/shard_map/ppermute | solution.py:575
  26.0 0.1 collective-permute-start.5
  26.1 5.2 %all-gather.1 = f32[8,1,16,128]{3,2,1,0:T(8,128)S(1)} all-gather(f32[2,1,16,128]{3,2,1,0:T(8,128)S(1)} %get-tuple-element.46), channel_id=3, replica_groups=mesh['gz'=4,'gx'=4,'gy'=2] {'gx'}, dimensions={0}, use_global_device_ids=true | all-gather | bytes 81920 | tf_op jit(solution)/shard_map/all_gather | solution.py:184
  31.3 0.0 collective-permute-done.5.rest_0_.refs_6_
  31.3 0.7 %collective-permute-start.7 = (f32[6,16,256]{2,1,0:T(8,128)S(1)}, f32[6,16,256]{2,1,0:T(8,128)S(1)}, u32[]{:S(2)}, u32[]{:S(2)}) collective-permute-start(f32[6,16,256]{2,1,0:T(8,128)S(1)} %get-tuple-element.49.refs_8_), channel_id=1, source_target_pairs={{24,8},{25,9},{26,10},{27,11},{28,12},{29,13},{30,14},{31,15}} | collective-permute-start | bytes 294920 | tf_op jit(solution)/shard_map/ppermute | solution.py:595
  32.0 4.9 %shard_map.54 = (f32[10,6,16,256]{3,2,1,0:T(8,128)S(1)}, f32[6,16,256]{2,1,0:T(8,128)S(1)}) custom-call(f32[10,6,16,256]{3,2,1,0:T(8,128)S(1)} %get-tuple-element.43.sweep_ref.refs_0_, f32[10,6,16,256]{3,2,1,0:T(8,128)S(1)} %get-tuple-element.44.change_ref.refs_1_, ...), custom_call_target="tpu_custom_call", output_to_operand_aliasing={{0}: (7, {})} | custom-call | bytes 204800 | tf_op jit(solution)/shard_map/pallas_call | solution.py:22
  36.9 0.7 %collective-permute-start.6 = (f32[6,16,256]{2,1,0:T(8,128)S(1)}, f32[6,16,256]{2,1,0:T(8,128)S(1)}, u32[]{:S(2)}, u32[]{:S(2)}) collective-permute-start(f32[6,16,256]{2,1,0:T(8,128)S(1)} %get-tuple-element.51.own_ref), channel_id=1, source_target_pairs={{24,16},{16,8},{25,17},{17,9},{26,18},{18,10},{27,19},{19,11},{28,... | collective-permute-start | bytes 294920 | tf_op jit(solution)/shard_map/ppermute | solution.py:594
  37.5 0.0 collective-permute-done.7.far_ref
  37.5 0.0 collective-permute-done.8.matrix_ref
  37.6 0.1 shard_map.55.moved_ref
  37.6 0.0 collective-permute-done.6.near_ref
  37.6 0.1 shard_map.56
  37.7 1.3 %collective-permute-start.9 = (f32[6,16,256]{2,1,0:T(8,128)S(1)}, f32[6,16,256]{2,1,0:T(8,128)S(1)}, u32[]{:S(2)}, u32[]{:S(2)}) collective-permute-start(f32[6,16,256]{2,1,0:T(8,128)S(1)} %get-tuple-element.54), channel_id=1, source_target_pairs={{8,0},{9,1},{10,2},{11,3},{12,4},{13,5},{14,6},{15,7}} | collective-permute-start | bytes 294920 | tf_op jit(solution)/shard_map/ppermute | solution.py:600
  39.0 21.6 %collective-permute-done.9.rest_1_ = f32[6,16,256]{2,1,0:T(8,128)S(1)} collective-permute-done((f32[6,16,256]{2,1,0:T(8,128)S(1)}, f32[6,16,256]{2,1,0:T(8,128)S(1)}, u32[]{:S(2)}, u32[]{:S(2)}) %collective-permute-start.9) | collective-permute-done | bytes 98336 | tf_op jit(solution)/shard_map/ppermute | solution.py:600
  60.6 2.0 %shard_map.57 = f32[10,6,16,256]{3,2,1,0:T(8,128)} custom-call(f32[10,6,16,256]{3,2,1,0:T(8,128)S(1)} %get-tuple-element.43.sweep_ref.refs_0_, f32[10,6,16,256]{3,2,1,0:T(8,128)S(1)} %get-tuple-element.50.inner_ref, bf16[10,6,6,16,256]{4,3,2,1,0:T(8,128)(2,1)S(1)} %get-tuple-element.31.inv_ref.refs_3_.refs_2_, ...), custom_call_target="tpu_custom_call" | custom-call | bytes 8192000 | tf_op jit(solution)/shard_map/pallas_call | solution.py:22
  (2 shorter events, 0.0 us)
Async XLA Ops:
  3.5 20.1 %collective-permute-start.3 = (f32[6,6,16,256]{3,2,1,0:T(8,128)S(1)}, f32[6,6,16,256]{3,2,1,0:T(8,128)S(1)}, u32[]{:S(2)}, u32[]{:S(2)}) collective-permute-start(f32[6,6,16,256]{3,2,1,0:T(8,128)S(1)} %get-tuple-element.42), channel_id=1, source_target_pairs={{16,24},{17,25},{18,26},{19,27},{20,28},{21,29},{22,30},{23,31}} | collective-permute-start | bytes 1769480 | tf_op jit(solution)/shard_map/ppermute | solution.py:499
  4.2 8.2 %collective-permute-start = (f32[10,6,256]{2,1,0:T(8,128)S(1)}, f32[10,6,256]{2,1,0:T(8,128)S(1)}, u32[]{:S(2)}, u32[]{:S(2)}) collective-permute-start(f32[10,6,256]{2,1,0:T(8,128)S(1)} %bitcast.14), channel_id=1, source_target_pairs={{0,1},{1,0},{2,3},{3,2},{4,5},{5,4},{6,7},{7,6},{8,9},{9,8},{10,11... | collective-permute-start | bytes 184328 | tf_op jit(solution)/shard_map/ppermute | solution.py:177
  18.1 4.1 %collective-permute-start.1 = (f32[6,16,256]{2,1,0:T(8,128)S(1)}, f32[6,16,256]{2,1,0:T(8,128)S(1)}, u32[]{:S(2)}, u32[]{:S(2)}) collective-permute-start(f32[6,16,256]{2,1,0:T(8,128)S(1)} %get-tuple-element.36.refs_8_), channel_id=1, source_target_pairs={{0,8},{1,9},{2,10},{3,11},{4,12},{5,13},{6,14},{7,15}} | collective-permute-start | bytes 294920 | tf_op jit(solution)/shard_map/ppermute | solution.py:515
  22.2 1.4 %collective-permute-start.4 = (f32[6,16,256]{2,1,0:T(8,128)S(1)}, f32[6,16,256]{2,1,0:T(8,128)S(1)}, u32[]{:S(2)}, u32[]{:S(2)}) collective-permute-start(f32[6,16,256]{2,1,0:T(8,128)S(1)} %shard_map.50), channel_id=1, source_target_pairs={{8,24},{9,25},{10,26},{11,27},{12,28},{13,29},{14,30},{15,31}} | collective-permute-start | bytes 294920 | tf_op jit(solution)/shard_map/ppermute | solution.py:542
  22.9 0.8 %collective-permute-start.2 = (f32[6,16,256]{2,1,0:T(8,128)S(1)}, f32[6,16,256]{2,1,0:T(8,128)S(1)}, u32[]{:S(2)}, u32[]{:S(2)}) collective-permute-start(f32[6,16,256]{2,1,0:T(8,128)S(1)} %shard_map.50), channel_id=1, source_target_pairs={{8,16},{16,24},{9,17},{17,25},{10,18},{18,26},{11,19},{19,27},{12,... | collective-permute-start | bytes 294920 | tf_op jit(solution)/shard_map/ppermute | solution.py:543
  25.3 12.3 %collective-permute-start.8 = (f32[6,6,16,256]{3,2,1,0:T(8,128)S(1)}, f32[6,6,16,256]{3,2,1,0:T(8,128)S(1)}, u32[]{:S(2)}, u32[]{:S(2)}) collective-permute-start(f32[6,6,16,256]{3,2,1,0:T(8,128)S(1)} %get-tuple-element.52), channel_id=1, source_target_pairs={{16,8},{17,9},{18,10},{19,11},{20,12},{21,13},{22,14},{23,15}} | collective-permute-start | bytes 1769480 | tf_op jit(solution)/shard_map/ppermute | solution.py:575
  26.0 5.3 %collective-permute-start.5 = (f32[10,6,256]{2,1,0:T(8,128)S(1)}, f32[10,6,256]{2,1,0:T(8,128)S(1)}, u32[]{:S(2)}, u32[]{:S(2)}) collective-permute-start(f32[10,6,256]{2,1,0:T(8,128)S(1)} %bitcast.13), channel_id=1, source_target_pairs={{0,1},{1,0},{2,3},{3,2},{4,5},{5,4},{6,7},{7,6},{8,9},{9,8},{10,11... | collective-permute-start | bytes 184328 | tf_op jit(solution)/shard_map/ppermute | solution.py:177
  31.3 6.2 %collective-permute-start.7 = (f32[6,16,256]{2,1,0:T(8,128)S(1)}, f32[6,16,256]{2,1,0:T(8,128)S(1)}, u32[]{:S(2)}, u32[]{:S(2)}) collective-permute-start(f32[6,16,256]{2,1,0:T(8,128)S(1)} %get-tuple-element.49.refs_8_), channel_id=1, source_target_pairs={{24,8},{25,9},{26,10},{27,11},{28,12},{29,13},{30,14},{31,15}} | collective-permute-start | bytes 294920 | tf_op jit(solution)/shard_map/ppermute | solution.py:595
  36.9 0.8 %collective-permute-start.6 = (f32[6,16,256]{2,1,0:T(8,128)S(1)}, f32[6,16,256]{2,1,0:T(8,128)S(1)}, u32[]{:S(2)}, u32[]{:S(2)}) collective-permute-start(f32[6,16,256]{2,1,0:T(8,128)S(1)} %get-tuple-element.51.own_ref), channel_id=1, source_target_pairs={{24,16},{16,8},{25,17},{17,9},{26,18},{18,10},{27,19},{19,11},{28,... | collective-permute-start | bytes 294920 | tf_op jit(solution)/shard_map/ppermute | solution.py:594
  37.7 22.9 %collective-permute-start.9 = (f32[6,16,256]{2,1,0:T(8,128)S(1)}, f32[6,16,256]{2,1,0:T(8,128)S(1)}, u32[]{:S(2)}, u32[]{:S(2)}) collective-permute-start(f32[6,16,256]{2,1,0:T(8,128)S(1)} %get-tuple-element.54), channel_id=1, source_target_pairs={{8,0},{9,1},{10,2},{11,3},{12,4},{13,5},{14,6},{15,7}} | collective-permute-start | bytes 294920 | tf_op jit(solution)/shard_map/ppermute | solution.py:600

commit v8 on v7

--- a/solution.py
+++ b/solution.py
@@ -168,6 +168,7 @@
         x_face = ((2, x_groups, ny, LANES), F32)
         y_face = ((1 if gy == 2 else 2, nz, VARS, nx), F32)
         matrix = ((VARS, VARS, ny, nx), F32)
+        steps = ((nz, VARS, VARS, ny, nx), F32)
         blocks = ((nz, VARS, VARS, ny, nx), jac.dtype)
         side_blocks = ((nz, 4, VARS, VARS, ny, nx), jac.dtype)
         unit = 40 * nz * ny * nx
@@ -193,6 +194,30 @@
             change = apply_block(block(inv_ref, z, at=at), [a + b for a, b in zip(change, inner)])
             return [a - b for a, b in zip(sweep, change)]
 
+        def fast_plane(step_ref, plain_ref, z, at, before):
+            moved = apply_block(block(step_ref, z, at=at), before)
+            return [a + b for a, b in zip(planes_of(plain_ref, z, at), moved)]
+
+        def make_fast(step_ref, plain_ref, inv_ref, couple_ref, plain_of):
+            half = VARS // 2
+
+            def step(z, carry):
+                for at in spans:
+                    couple, inverse = block(couple_ref, z, at=at), block(inv_ref, z, at=at)
+                    for g in range(VARS // half):
+                        columns = range(g * half, (g + 1) * half)
+                        held = [[couple(k, c).astype(F32) for k in range(VARS)] for c in columns]
+                        for r in range(VARS):
+                            row = [inverse(r, k).astype(F32) for k in range(VARS)]
+                            for i, c in enumerate(columns):
+                                step_ref[z, r, c, :, at] = -dot6(row, held[i])
+                    plain = plain_of(z, at, lambda values: apply_block(inverse, values))
+                    for var in range(VARS):
+                        plain_ref[z, var, :, at] = plain[var]
+                return carry
+
+            lax.fori_loop(0, nz, step, 0)
+
         def put(ref, values, at):
             for var in range(VARS):
                 ref[var, :, at] = values[var]
@@ -215,12 +240,15 @@
                 total = [a + ref[var, :, at] for var, a in enumerate(total)]
             return tuple(total)
 
-        def forward_sweep(source_ref, inv_ref, low_jac, starts, keep=None):
+        def forward_sweep(source_ref, inv_ref, low_jac, starts, keep=None, fast=None):
             def step(z, earlier):
                 results = []
                 for tile, at in enumerate(spans):
-                    source = planes_of(source_ref, z, at)
-                    result = forward_plane(source, inv_ref, low_jac, z, at, earlier[tile])
+                    if fast is not None:
+                        result = fast_plane(*fast, z, at, earlier[tile])
+                    else:
+                        source = planes_of(source_ref, z, at)
+                        result = forward_plane(source, inv_ref, low_jac, z, at, earlier[tile])
                     if keep is not None:
                         keep(z, at, result)
                     results.append(tuple(result))
@@ -228,13 +256,16 @@
 
             return lax.fori_loop(0, nz, step, starts)
 
-        def backward_sweep(sweep_ref, inner_ref, inv_ref, high_jac, starts, keep=None):
+        def backward_sweep(sweep_ref, inner_ref, inv_ref, high_jac, starts, keep=None, fast=None):
             def step(i, later):
                 z = nz - 1 - i
                 results = []
                 for tile, at in enumerate(spans):
-                    sweep, inner = planes_of(sweep_ref, z, at), planes_of(inner_ref, z, at)
-                    result = backward_plane(sweep, inner, inv_ref, high_jac, z, at, later[tile])
+                    if fast is not None:
+                        result = fast_plane(*fast, z, at, later[tile])
+                    else:
+                        sweep, inner = planes_of(sweep_ref, z, at), planes_of(inner_ref, z, at)
+                        result = backward_plane(sweep, inner, inv_ref, high_jac, z, at, later[tile])
                     if keep is not None:
                         keep(z, tile, at, result)
                     results.append(tuple(result))
@@ -382,21 +413,26 @@
             for tile, at in enumerate(spans):
                 put(top_ref, top[tile], at)
 
-        def forward_mid_kernel(low_ref, came_ref, source_ref, inv_ref, low_jac, _, top_ref):
+        def forward_mid_kernel(low_ref, came_ref, source_ref, inv_ref, low_jac, top_ref):
             top_ref[...] = low_ref[...]
 
             @pl.when(lax.axis_index("gz") == 1)
             def _():
                 forward_kernel(source_ref, inv_ref, low_jac, came_ref, top_ref)
 
+        def either(device, work, fast):
+            if fast is None:
+                work(None)
+                return
+            here = lax.axis_index("gz") == device
+            pl.when(here)(lambda: work(fast))
+            pl.when(jnp.logical_not(here))(lambda: work(None))
+
         def forward_last_kernel(source_ref, prev_ref, inv_ref, low_jac, *rest):
+            came, (sweep_ref, change_ref, x_side, y_side) = rest[:-4], rest[-4:]
+            fast = None
             if short:
-                (first, near, matrix_ref, far), outs = rest[:4], rest[5:9]
-                starts = tuple(arrived((first, near), matrix_ref, far, at) for at in spans)
-            else:
-                came, outs = rest[:-4], rest[-4:]
-                starts = tuple(incoming(came, at) for at in spans)
-            sweep_ref, change_ref, x_side, y_side = outs
+                first, near, matrix_ref, far, *fast = came
 
             def keep(z, at, result):
                 before = planes_of(prev_ref, z, at)
@@ -404,7 +440,14 @@
                     sweep_ref[z, var, :, at] = result[var]
                     change_ref[z, var, :, at] = result[var] - before[var]
 
-            forward_sweep(source_ref, inv_ref, low_jac, starts, keep)
+            def work(fast):
+                if short:
+                    starts = tuple(arrived((first, near), matrix_ref, far, at) for at in spans)
+                else:
+                    starts = tuple(incoming(came, at) for at in spans)
+                forward_sweep(source_ref, inv_ref, low_jac, starts, keep, fast)
+
+            either(3, work, fast)
             write_faces(change_ref, x_side, y_side, nz)
 
         def turn_kernel(wanted, sweep_ref, change_ref, inv_ref, sides, high_jac, x_all, *rest):
@@ -437,17 +480,37 @@
                 zero = tuple(jnp.zeros((ny, LANES), F32) for _ in range(VARS))
                 put(low_ref, lax.fori_loop(0, nz, step, zero), at)
 
-        def down_matrix_kernel(device, inv_ref, high_jac, *rest):
-            matrix_ref = rest[-1]
+        def only(device, work, ref, shape):
             here = lax.axis_index("gz") == device
-
-            @pl.when(here)
-            def _():
-                transfer(matrix_ref, inv_ref, high_jac, lambda i: nz - 1 - i)
+            pl.when(here)(work)
 
             @pl.when(jnp.logical_not(here))
             def _():
-                matrix_ref[...] = jnp.zeros(matrix[0], F32)
+                ref[...] = jnp.zeros(shape, F32)
+
+        def down_matrix(inv_ref, high_jac, matrix_ref):
+            transfer(matrix_ref, inv_ref, high_jac, lambda i: nz - 1 - i)
+
+        def forward_idle_kernel(inv_ref, high_jac, low_jac, source_ref, _, matrix_ref, step_ref, plain_ref):
+            only(2, lambda: down_matrix(inv_ref, high_jac, matrix_ref), matrix_ref, matrix[0])
+
+            @pl.when(lax.axis_index("gz") == 3)
+            def _():
+                def plain_of(z, at, times):
+                    return times(planes_of(source_ref, z, at))
+
+                make_fast(step_ref, plain_ref, inv_ref, low_jac, plain_of)
+
+        def backward_idle_kernel(inv_ref, high_jac, sweep_ref, inner_ref, _, matrix_ref, step_ref, plain_ref):
+            only(1, lambda: down_matrix(inv_ref, high_jac, matrix_ref), matrix_ref, matrix[0])
+
+            @pl.when(lax.axis_index("gz") == 0)
+            def _():
+                def plain_of(z, at, times):
+                    moved = times(planes_of(inner_ref, z, at))
+                    return [a - b for a, b in zip(planes_of(sweep_ref, z, at), moved)]
+
+                make_fast(step_ref, plain_ref, inv_ref, high_jac, plain_of)
 
         def backward_kernel(sweep_ref, inner_ref, inv_ref, high_jac, *rest):
             came, low_ref = rest[:-1], rest[-1]
@@ -456,7 +519,10 @@
             for tile, at in enumerate(spans):
                 put(low_ref, low[tile], at)
 
-        def far_kernel(far_ref, matrix_ref, moved_ref):
+        def pass_kernel(*refs):
+            pass
+
+        def far_kernel(far_ref, matrix_ref, _, moved_ref):
             for at in spans:
                 put(moved_ref, apply_matrix(matrix_ref, planes_in(far_ref, at), at), at)
 
@@ -469,6 +535,9 @@
 
         def update_kernel(sweep_ref, inner_ref, inv_ref, high_jac, *rest):
             came, (out_hbm, held, sems) = rest[:-3], rest[-3:]
+            fast = None
+            if short:
+                came, fast = came[:2], came[2:]
 
             def out_copy(z):
                 return pltpu.make_async_copy(held.at[z], out_hbm.at[z], sems.at[z])
@@ -479,8 +548,11 @@
                 if tile == tiles - 1:
                     out_copy(z).start()
 
-            starts = tuple(incoming(came, at) for at in spans)
-            backward_sweep(sweep_ref, inner_ref, inv_ref, high_jac, starts, keep)
+            def work(fast):
+                starts = tuple(incoming(came, at) for at in spans)
+                backward_sweep(sweep_ref, inner_ref, inv_ref, high_jac, starts, keep, fast)
+
+            either(0, work, fast)
             for z in range(nz):
                 out_copy(z).wait()
 
@@ -525,9 +597,6 @@
                 aliases={n: 0, n + 2: 2, n + 3: 3},
                 **first_options,
             )
-            (own_matrix,) = call(
-                functools.partial(down_matrix_kernel, 1), [matrix], inv, high_jac, cost=unit // 8
-            )
             (top,) = call(
                 forward_mid_kernel,
                 [plane],
@@ -536,43 +605,43 @@
                 source,
                 inv,
                 low_jac,
-                own_matrix,
                 cost=unit // 8,
             )
             far = lax.ppermute(top, "gz", [(1, 3)])
             near = lax.ppermute(top, "gz", [(1, 2), (2, 3)])
-            (down_matrix,) = call(
-                functools.partial(down_matrix_kernel, 2),
-                [matrix],
+            down_one, *fast = call(
+                forward_idle_kernel,
+                [matrix, steps, volume],
                 inv,
                 high_jac,
+                low_jac,
+                source,
                 up_there,
                 cost=unit // 8,
             )
-            came = [first, near, up_there, far]
-            extra = [down_matrix]
+            (down_one,) = call(
+                pass_kernel, [matrix], down_one, near, far, cost=unit // 8, aliases={0: 0}
+            )
+            down_there = lax.ppermute(down_one, "gz", [(2, 1)])
+            came = [first, near, up_there, far, *fast]
         else:
-            came, extra = [], []
+            came = []
             for hop in range(gz - 1):
                 if hop:
                     (top,) = call(
                         forward_kernel, [plane], source, inv, low_jac, *came, cost=3 * unit
                     )
                 came.append(lax.ppermute(top, "gz", [(hop, hop + 1)]))
-        sweep, change, x_side, y_side, *extra = call(
+        sweep, change, x_side, y_side = call(
             forward_last_kernel,
-            [volume, volume, x_face, y_face] + [matrix] * len(extra),
+            [volume, volume, x_face, y_face],
             source,
             prev,
             inv,
             low_jac,
             *came,
-            *extra,
             cost=4 * unit,
-            aliases={4 + len(came): 4} if short else {},
         )
-        if short:
-            down_there = lax.ppermute(extra[0], "gz", [(2, 1)])
         halo = exchange(x_side, y_side)
         if short:
             ahead, behind = (lambda device: device == 3), (lambda device: device != 3)
@@ -593,11 +662,21 @@
             )
             near = lax.ppermute(low, "gz", [(3, 2), (2, 1)])
             far = lax.ppermute(ahead_low, "gz", [(3, 1)])
-            (moved,) = call(far_kernel, [plane], far, down_there, cost=unit // 8)
+            own_matrix, *fast = call(
+                backward_idle_kernel,
+                [matrix, steps, volume],
+                inv,
+                high_jac,
+                sweep,
+                inner,
+                low,
+                cost=unit // 8,
+            )
+            (moved,) = call(far_kernel, [plane], far, down_there, own_matrix, cost=unit // 8)
             entered, low = call(
                 backward_mid_kernel, [plane, plane], low, near, moved, own_matrix, cost=unit // 8
             )
-            came = [entered, lax.ppermute(low, "gz", [(1, 0)])]
+            came = [entered, lax.ppermute(low, "gz", [(1, 0)]), *fast]
         else:
             came = []
             for hop in range(gz - 1, 0, -1):

time: 62.8 us -> 59.4 us (0.946)
  waiting for transfers between devices: 24.1 us -> 17.9 us
  Pallas kernels: 18.1 us -> 20.8 us
    ppermute x2, waiting for transfers between devices: 21.6 us -> 15.4 us  [the longest x1 15.4 us: body(): came = [entered, lax.ppermute(low, 'gz', [(1, 0)]), *fast]]
    pallas_call x12 -> x13, Pallas kernels: 18.1 us -> 20.8 us  [call(): pl.pallas_call(body, out_shape=shapes, in_specs=[far if i in in_hbm else...]
  transfers between devices with their start and end apart: 10 -> 10, of which waited for: 2 -> 2; matrix products, arithmetic and copies ran while one was open for 0% -> 0% of each run, Pallas kernels for 18% -> 27%
where the time goes in v8:
time: 59.4 us; the launch traced here: 59.1 us
  Pallas kernels  20.8 us (35%)
  waiting for transfers between devices  17.9 us (30%)
  blocking collectives  10.5 us (18%)
  starting transfers between devices  9.73 us (16%)
    pallas_call x13, Pallas kernels, call(): pl.pallas_call(body, out_shape=shapes, in_specs=[far if i in in_hbm else...  20.8 us
    ppermute x1, waiting for transfers between devices, body(): came = [entered, lax.ppermute(low, 'gz', [(1, 0)]), *fast]  15.4 us
    all_gather x2, blocking collectives, exchange(): return (lax.all_gather(x_side, 'gx'), *rows)  10.5 us
    ppermute x2, starting transfers between devices, exchange(): rows = [lax.ppermute(y_side[0], 'gy', [(0, 1), (1, 0)])]  3.1 us
    ppermute x1, waiting for transfers between devices, body(): first = lax.ppermute(top, 'gz', [(0, 1)])  2.52 us
    ppermute x1, starting transfers between devices, body(): first = lax.ppermute(top, 'gz', [(0, 1)])  1.3 us
    ppermute x1, starting transfers between devices, body(): came = [entered, lax.ppermute(low, 'gz', [(1, 0)]), *fast]  1.29 us
  transfers between devices with their start and end apart: 10, of which 2 were waited for; matrix products, arithmetic and copies ran while one was open for 0% of the time, Pallas kernels for 27%

profile of v8, /device:TPU:0, one launch (start us, length us, event | category | flops | bytes accessed | tf_op | source)
XLA Modules:
  0.0 59.1 jit_solution(1332839860129772957)
XLA Ops:
  0.0 3.4 %shard_map.46 = (f32[10,6,16,256]{3,2,1,0:T(8,128)S(1)}, bf16[10,6,6,16,256]{4,3,2,1,0:T(8,128)(2,1)S(1)}, bf16[10,6,6,16,256]{4,3,2,1,0:T(8,128)(2,1)S(1)}, f32...) custom-call(f32[10,6,16,256]{3,2,1,0:T(8,128)} %bitcast.21, ...), custom_call_target="tpu_custom_call" | custom-call | bytes 19660800 | tf_op jit(solution)/shard_map/pallas_call | solution.py:22
  3.5 0.7 %collective-permute-start.3 = (f32[6,6,16,256]{3,2,1,0:T(8,128)S(1)}, f32[6,6,16,256]{3,2,1,0:T(8,128)S(1)}, u32[]{:S(2)}, u32[]{:S(2)}) collective-permute-start(f32[6,6,16,256]{3,2,1,0:T(8,128)S(1)} %get-tuple-element.46), channel_id=1, source_target_pairs={{16,24},{17,25},{18,26},{19,27},{20,28},{21,29},{22,30},{23,31}} | collective-permute-start | bytes 1769480 | tf_op jit(solution)/shard_map/ppermute | solution.py:571
  4.2 3.0 %collective-permute-start = (f32[10,6,256]{2,1,0:T(8,128)S(1)}, f32[10,6,256]{2,1,0:T(8,128)S(1)}, u32[]{:S(2)}, u32[]{:S(2)}) collective-permute-start(f32[10,6,256]{2,1,0:T(8,128)S(1)} %bitcast.14), channel_id=1, source_target_pairs={{0,1},{1,0},{2,3},{3,2},{4,5},{5,4},{6,7},{7,6},{8,9},{9,8},{10,11... | collective-permute-start | bytes 184328 | tf_op jit(solution)/shard_map/ppermute | solution.py:178
  7.2 5.2 %all-gather = f32[8,1,16,128]{3,2,1,0:T(8,128)S(1)} all-gather(f32[2,1,16,128]{3,2,1,0:T(8,128)S(1)} %get-tuple-element.38), channel_id=2, replica_groups=mesh['gz'=4,'gx'=4,'gy'=2] {'gx'}, dimensions={0}, use_global_device_ids=true | all-gather | bytes 81920 | tf_op jit(solution)/shard_map/all_gather | solution.py:185
  12.4 0.0 collective-permute-done.rest_0_.refs_6_
  12.4 5.7 %shard_map.47 = (f32[10,6,16,256]{3,2,1,0:T(8,128)S(1)}, f32[6,16,256]{2,1,0:T(8,128)S(1)}, bf16[10,4,6,6,16,256]{5,4,3,2,1,0:T(8,128)(2,1)S(1)}, bf16[10,6,6,16,256]{4,3,2,1,0:T(8,128)(2,1)S(1)}) custom-call(f32[10,6,16,256]{3,2,1,0:T(8,128)} %bitcast.18, bf16[10,6,6,6,16,256]{5,4,3,2,1,0:T(8,128)(2,1)} %bitcast.16, ...), custom_call_target="tpu_custom_call" | custom-call | bytes 204800 | tf_op jit(solution)/shard_map/pallas_call | solution.py:22
  18.1 1.3 %collective-permute-start.1 = (f32[6,16,256]{2,1,0:T(8,128)S(1)}, f32[6,16,256]{2,1,0:T(8,128)S(1)}, u32[]{:S(2)}, u32[]{:S(2)}) collective-permute-start(f32[6,16,256]{2,1,0:T(8,128)S(1)} %get-tuple-element.41.refs_8_), channel_id=1, source_target_pairs={{0,8},{1,9},{2,10},{3,11},{4,12},{5,13},{6,14},{7,15}} | collective-permute-start | bytes 294920 | tf_op jit(solution)/shard_map/ppermute | solution.py:587
  19.4 0.3 shard_map.48
  19.7 2.5 %collective-permute-done.1.came_ref.rest_0_ = f32[6,16,256]{2,1,0:T(8,128)S(1)} collective-permute-done((f32[6,16,256]{2,1,0:T(8,128)S(1)}, f32[6,16,256]{2,1,0:T(8,128)S(1)}, u32[]{:S(2)}, u32[]{:S(2)}) %collective-permute-start.1) | collective-permute-done | bytes 98336 | tf_op jit(solution)/shard_map/ppermute | solution.py:587
  22.2 0.7 %collective-permute-start.4 = (f32[6,16,256]{2,1,0:T(8,128)S(1)}, f32[6,16,256]{2,1,0:T(8,128)S(1)}, u32[]{:S(2)}, u32[]{:S(2)}) collective-permute-start(f32[6,16,256]{2,1,0:T(8,128)S(1)} %shard_map.49), channel_id=1, source_target_pairs={{8,24},{9,25},{10,26},{11,27},{12,28},{13,29},{14,30},{15,31}} | collective-permute-start | bytes 294920 | tf_op jit(solution)/shard_map/ppermute | solution.py:610
  22.9 0.7 %collective-permute-start.2 = (f32[6,16,256]{2,1,0:T(8,128)S(1)}, f32[6,16,256]{2,1,0:T(8,128)S(1)}, u32[]{:S(2)}, u32[]{:S(2)}) collective-permute-start(f32[6,16,256]{2,1,0:T(8,128)S(1)} %shard_map.49), channel_id=1, source_target_pairs={{8,16},{16,24},{9,17},{17,25},{10,18},{18,26},{11,19},{19,27},{12,... | collective-permute-start | bytes 294920 | tf_op jit(solution)/shard_map/ppermute | solution.py:611
  23.6 0.0 collective-permute-done.3._.rest_2_
  23.6 0.1 shard_map.50
  23.6 0.0 collective-permute-done.4.rest_3_.refs_2_
  23.7 0.0 collective-permute-done.2.rest_1_.refs_1_
  23.7 0.7 %collective-permute-start.8 = (f32[6,6,16,256]{3,2,1,0:T(8,128)S(1)}, f32[6,6,16,256]{3,2,1,0:T(8,128)S(1)}, u32[]{:S(2)}, u32[]{:S(2)}) collective-permute-start(f32[6,6,16,256]{3,2,1,0:T(8,128)S(1)} %shard_map.54), channel_id=1, source_target_pairs={{16,8},{17,9},{18,10},{19,11},{20,12},{21,13},{22,14},{23,15}} | collective-permute-start | bytes 1769480 | tf_op jit(solution)/shard_map/ppermute | solution.py:625
  24.4 1.6 %shard_map.51 = (f32[10,6,16,256]{3,2,1,0:T(8,128)S(1)}, f32[10,6,16,256]{3,2,1,0:T(8,128)S(1)}, f32[2,1,16,128]{3,2,1,0:T(8,128)S(1)}, f32[1,10,6,256]{3,2,1,0:T(8,128)S(1)}) custom-call(f32[10,6,16,256]{3,2,1,0:T(8,128)S(1)} %get-tuple-element.44.source_ref, f32[10,6,16,256]{3,2,1,0:T(8,128)S(1)} %get-tuple-element.35.prev_ref.refs_2_, ...), custom_call_target="tpu_custom_call" | custom-call | bytes 6553600 | tf_op jit(solution)/shard_map/pallas_call | solution.py:22
  26.0 0.1 collective-permute-start.5
  26.1 5.2 %all-gather.1 = f32[8,1,16,128]{3,2,1,0:T(8,128)S(1)} all-gather(f32[2,1,16,128]{3,2,1,0:T(8,128)S(1)} %get-tuple-element.53), channel_id=3, replica_groups=mesh['gz'=4,'gx'=4,'gy'=2] {'gx'}, dimensions={0}, use_global_device_ids=true | all-gather | bytes 81920 | tf_op jit(solution)/shard_map/all_gather | solution.py:185
  31.3 0.0 collective-permute-done.5.rest_0_.refs_6_
  31.3 0.7 %collective-permute-start.7 = (f32[6,16,256]{2,1,0:T(8,128)S(1)}, f32[6,16,256]{2,1,0:T(8,128)S(1)}, u32[]{:S(2)}, u32[]{:S(2)}) collective-permute-start(f32[6,16,256]{2,1,0:T(8,128)S(1)} %get-tuple-element.56.refs_8_), channel_id=1, source_target_pairs={{24,8},{25,9},{26,10},{27,11},{28,12},{29,13},{30,14},{31,15}} | collective-permute-start | bytes 294920 | tf_op jit(solution)/shard_map/ppermute | solution.py:664
  32.0 4.9 %shard_map.53 = (f32[10,6,16,256]{3,2,1,0:T(8,128)S(1)}, f32[6,16,256]{2,1,0:T(8,128)S(1)}) custom-call(f32[10,6,16,256]{3,2,1,0:T(8,128)S(1)} %get-tuple-element.50.sweep_ref.refs_0_, f32[10,6,16,256]{3,2,1,0:T(8,128)S(1)} %get-tuple-element.51.change_ref.refs_1_, ...), custom_call_target="tpu_custom_call", output_to_operand_aliasing={{0}: (7, {})} | custom-call | bytes 204800 | tf_op jit(solution)/shard_map/pallas_call | solution.py:22
  36.9 0.7 %collective-permute-start.6 = (f32[6,16,256]{2,1,0:T(8,128)S(1)}, f32[6,16,256]{2,1,0:T(8,128)S(1)}, u32[]{:S(2)}, u32[]{:S(2)}) collective-permute-start(f32[6,16,256]{2,1,0:T(8,128)S(1)} %get-tuple-element.58._.own_ref), channel_id=1, source_target_pairs={{24,16},{16,8},{25,17},{17,9},{26,18},{18,10},{27,19},{19,11},{28,... | collective-permute-start | bytes 294920 | tf_op jit(solution)/shard_map/ppermute | solution.py:663
  37.6 3.4 %shard_map.55 = (f32[6,6,16,256]{3,2,1,0:T(8,128)S(1)}, f32[10,6,6,16,256]{4,3,2,1,0:T(8,128)S(1)}, f32[10,6,16,256]{3,2,1,0:T(8,128)S(1)}) custom-call(bf16[10,6,6,16,256]{4,3,2,1,0:T(8,128)(2,1)S(1)} %get-tuple-element.36.inv_ref.refs_3_.refs_2_, bf16[10,6,6,16,256]{4,3,2,1,0:T(8,128)(2,1)S(1)} %get-tuple-element.47.high_jac.refs_4_, ...), custom_call_target="tpu_custom_call" | custom-call | bytes 204800 | tf_op jit(solution)/shard_map/pallas_call | solution.py:22
  41.0 0.0 collective-permute-done.7.far_ref
  41.0 0.0 collective-permute-done.8.matrix_ref
  41.0 0.1 shard_map.56.moved_ref
  41.1 0.0 collective-permute-done.6.near_ref
  41.1 0.1 shard_map.57
  41.2 1.3 %collective-permute-start.9 = (f32[6,16,256]{2,1,0:T(8,128)S(1)}, f32[6,16,256]{2,1,0:T(8,128)S(1)}, u32[]{:S(2)}, u32[]{:S(2)}) collective-permute-start(f32[6,16,256]{2,1,0:T(8,128)S(1)} %get-tuple-element.62), channel_id=1, source_target_pairs={{8,0},{9,1},{10,2},{11,3},{12,4},{13,5},{14,6},{15,7}} | collective-permute-start | bytes 294920 | tf_op jit(solution)/shard_map/ppermute | solution.py:679
  42.5 15.4 %collective-permute-done.9.rest_1_ = f32[6,16,256]{2,1,0:T(8,128)S(1)} collective-permute-done((f32[6,16,256]{2,1,0:T(8,128)S(1)}, f32[6,16,256]{2,1,0:T(8,128)S(1)}, u32[]{:S(2)}, u32[]{:S(2)}) %collective-permute-start.9) | collective-permute-done | bytes 98336 | tf_op jit(solution)/shard_map/ppermute | solution.py:679
  57.9 1.3 %shard_map.58 = f32[10,6,16,256]{3,2,1,0:T(8,128)} custom-call(f32[10,6,16,256]{3,2,1,0:T(8,128)S(1)} %get-tuple-element.50.sweep_ref.refs_0_, f32[10,6,16,256]{3,2,1,0:T(8,128)S(1)} %get-tuple-element.57.inner_ref, bf16[10,6,6,16,256]{4,3,2,1,0:T(8,128)(2,1)S(1)} %get-tuple-element.36.inv_ref.refs_3_.refs_2_, ...), custom_call_target="tpu_custom_call" | custom-call | bytes 8192000 | tf_op jit(solution)/shard_map/pallas_call | solution.py:22
  (3 shorter events, 0.0 us)
Async XLA Ops:
  3.5 20.1 %collective-permute-start.3 = (f32[6,6,16,256]{3,2,1,0:T(8,128)S(1)}, f32[6,6,16,256]{3,2,1,0:T(8,128)S(1)}, u32[]{:S(2)}, u32[]{:S(2)}) collective-permute-start(f32[6,6,16,256]{3,2,1,0:T(8,128)S(1)} %get-tuple-element.46), channel_id=1, source_target_pairs={{16,24},{17,25},{18,26},{19,27},{20,28},{21,29},{22,30},{23,31}} | collective-permute-start | bytes 1769480 | tf_op jit(solution)/shard_map/ppermute | solution.py:571
  4.2 8.2 %collective-permute-start = (f32[10,6,256]{2,1,0:T(8,128)S(1)}, f32[10,6,256]{2,1,0:T(8,128)S(1)}, u32[]{:S(2)}, u32[]{:S(2)}) collective-permute-start(f32[10,6,256]{2,1,0:T(8,128)S(1)} %bitcast.14), channel_id=1, source_target_pairs={{0,1},{1,0},{2,3},{3,2},{4,5},{5,4},{6,7},{7,6},{8,9},{9,8},{10,11... | collective-permute-start | bytes 184328 | tf_op jit(solution)/shard_map/ppermute | solution.py:178
  18.1 4.1 %collective-permute-start.1 = (f32[6,16,256]{2,1,0:T(8,128)S(1)}, f32[6,16,256]{2,1,0:T(8,128)S(1)}, u32[]{:S(2)}, u32[]{:S(2)}) collective-permute-start(f32[6,16,256]{2,1,0:T(8,128)S(1)} %get-tuple-element.41.refs_8_), channel_id=1, source_target_pairs={{0,8},{1,9},{2,10},{3,11},{4,12},{5,13},{6,14},{7,15}} | collective-permute-start | bytes 294920 | tf_op jit(solution)/shard_map/ppermute | solution.py:587
  22.2 1.4 %collective-permute-start.4 = (f32[6,16,256]{2,1,0:T(8,128)S(1)}, f32[6,16,256]{2,1,0:T(8,128)S(1)}, u32[]{:S(2)}, u32[]{:S(2)}) collective-permute-start(f32[6,16,256]{2,1,0:T(8,128)S(1)} %shard_map.49), channel_id=1, source_target_pairs={{8,24},{9,25},{10,26},{11,27},{12,28},{13,29},{14,30},{15,31}} | collective-permute-start | bytes 294920 | tf_op jit(solution)/shard_map/ppermute | solution.py:610
  22.9 0.8 %collective-permute-start.2 = (f32[6,16,256]{2,1,0:T(8,128)S(1)}, f32[6,16,256]{2,1,0:T(8,128)S(1)}, u32[]{:S(2)}, u32[]{:S(2)}) collective-permute-start(f32[6,16,256]{2,1,0:T(8,128)S(1)} %shard_map.49), channel_id=1, source_target_pairs={{8,16},{16,24},{9,17},{17,25},{10,18},{18,26},{11,19},{19,27},{12,... | collective-permute-start | bytes 294920 | tf_op jit(solution)/shard_map/ppermute | solution.py:611
  23.7 17.3 %collective-permute-start.8 = (f32[6,6,16,256]{3,2,1,0:T(8,128)S(1)}, f32[6,6,16,256]{3,2,1,0:T(8,128)S(1)}, u32[]{:S(2)}, u32[]{:S(2)}) collective-permute-start(f32[6,6,16,256]{3,2,1,0:T(8,128)S(1)} %shard_map.54), channel_id=1, source_target_pairs={{16,8},{17,9},{18,10},{19,11},{20,12},{21,13},{22,14},{23,15}} | collective-permute-start | bytes 1769480 | tf_op jit(solution)/shard_map/ppermute | solution.py:625
  26.0 5.3 %collective-permute-start.5 = (f32[10,6,256]{2,1,0:T(8,128)S(1)}, f32[10,6,256]{2,1,0:T(8,128)S(1)}, u32[]{:S(2)}, u32[]{:S(2)}) collective-permute-start(f32[10,6,256]{2,1,0:T(8,128)S(1)} %bitcast.13), channel_id=1, source_target_pairs={{0,1},{1,0},{2,3},{3,2},{4,5},{5,4},{6,7},{7,6},{8,9},{9,8},{10,11... | collective-permute-start | bytes 184328 | tf_op jit(solution)/shard_map/ppermute | solution.py:178
  31.3 9.7 %collective-permute-start.7 = (f32[6,16,256]{2,1,0:T(8,128)S(1)}, f32[6,16,256]{2,1,0:T(8,128)S(1)}, u32[]{:S(2)}, u32[]{:S(2)}) collective-permute-start(f32[6,16,256]{2,1,0:T(8,128)S(1)} %get-tuple-element.56.refs_8_), channel_id=1, source_target_pairs={{24,8},{25,9},{26,10},{27,11},{28,12},{29,13},{30,14},{31,15}} | collective-permute-start | bytes 294920 | tf_op jit(solution)/shard_map/ppermute | solution.py:664
  36.9 4.2 %collective-permute-start.6 = (f32[6,16,256]{2,1,0:T(8,128)S(1)}, f32[6,16,256]{2,1,0:T(8,128)S(1)}, u32[]{:S(2)}, u32[]{:S(2)}) collective-permute-start(f32[6,16,256]{2,1,0:T(8,128)S(1)} %get-tuple-element.58._.own_ref), channel_id=1, source_target_pairs={{24,16},{16,8},{25,17},{17,9},{26,18},{18,10},{27,19},{19,11},{28,... | collective-permute-start | bytes 294920 | tf_op jit(solution)/shard_map/ppermute | solution.py:663
  41.2 16.7 %collective-permute-start.9 = (f32[6,16,256]{2,1,0:T(8,128)S(1)}, f32[6,16,256]{2,1,0:T(8,128)S(1)}, u32[]{:S(2)}, u32[]{:S(2)}) collective-permute-start(f32[6,16,256]{2,1,0:T(8,128)S(1)} %get-tuple-element.62), channel_id=1, source_target_pairs={{8,0},{9,1},{10,2},{11,3},{12,4},{13,5},{14,6},{15,7}} | collective-permute-start | bytes 294920 | tf_op jit(solution)/shard_map/ppermute | solution.py:679

commit v9 on v8

--- a/solution.py
+++ b/solution.py
@@ -353,22 +353,51 @@
             else:
                 pl.when(wanted(lax.axis_index("gz")))(work)
 
-        def first_kernel(wanted, rhs_hbm, jac_hbm, prev_ref, inv_ref, low_jac, x_all, *rest):
-            y_rows, outs = rest[: 1 if gy == 2 else 2], rest[-6:]
-            on(
-                wanted,
-                lambda: first_work(
-                    rhs_hbm, jac_hbm, prev_ref, inv_ref, low_jac, x_all, y_rows, *outs
-                ),
-            )
-
-        def first_again_kernel(wanted, *refs):
-            refs[-5][...] = refs[-9][...]
-            first_kernel(wanted, *refs)
+        def load_high(jac_hbm, high_jac, sem):
+            return pltpu.make_async_copy(jac_hbm.at[:, 5], high_jac, sem)
+
+        def first_kernel(rhs_hbm, jac_hbm, prev_ref, inv_ref, low_jac, x_all, *rest):
+            *y_rows, source_ref, top_ref, sides, high_jac, rhs_ref, sems, high_sem = rest
+            high_copy = load_high(jac_hbm, high_jac, high_sem)
+            first_work(
+                rhs_hbm, jac_hbm, prev_ref, inv_ref, low_jac, x_all, y_rows,
+                source_ref, top_ref, sides, rhs_ref, sems, high_copy,
+            )
+            high_copy.wait()
+
+        def first_ahead_kernel(rhs_hbm, jac_hbm, prev_ref, inv_ref, low_jac, x_all, *rest):
+            *y_rows, source_ref, top_ref, sides, rhs_ref, sems = rest
+
+            @pl.when(lax.axis_index("gz") == 0)
+            def _():
+                first_work(
+                    rhs_hbm, jac_hbm, prev_ref, inv_ref, low_jac, x_all, y_rows,
+                    source_ref, top_ref, sides, rhs_ref, sems, None,
+                )
+
+        def first_behind_kernel(*refs):
+            jac_hbm, high_jac, high_sem = refs[1], refs[-4], refs[-1]
+            inputs, top_before = refs[: len(first_args)], refs[len(first_args) + 1]
+            source_ref, top_ref, sides, _, rhs_ref, sems, _ = refs[-7:]
+            high_copy = load_high(jac_hbm, high_jac, high_sem)
+            here = lax.axis_index("gz") == 0
+
+            @pl.when(here)
+            def _():
+                high_copy.start()
+                top_ref[...] = top_before[...]
+
+            @pl.when(jnp.logical_not(here))
+            def _():
+                first_work(
+                    *inputs[:6], inputs[6:], source_ref, top_ref, sides, rhs_ref, sems, high_copy
+                )
+
+            high_copy.wait()
 
         def first_work(
             rhs_hbm, jac_hbm, prev_ref, inv_ref, low_jac, x_all, y_rows,
-            source_ref, top_ref, sides, high_jac, rhs_ref, sems,
+            source_ref, top_ref, sides, rhs_ref, sems, also,
         ):
             halo = halo_reader(x_all, y_rows, gx, gy)
 
@@ -378,14 +407,11 @@
                     pltpu.make_async_copy(rhs_hbm.at[z], rhs_ref.at[z], sems.at[1, z]),
                 ]
 
-            def high_copy(z):
-                return pltpu.make_async_copy(jac_hbm.at[z, 5], high_jac.at[z], sems.at[2, z])
-
             for z in range(nz):
                 for copy in copies(z):
                     copy.start()
-            for z in range(nz):
-                high_copy(z).start()
+            if also is not None:
+                also.start()
 
             def step(z, earlier):
                 for copy in copies(z):
@@ -403,8 +429,6 @@
             top = lax.fori_loop(0, nz, step, (zero,) * tiles)
             for tile, at in enumerate(spans):
                 put(top_ref, top[tile], at)
-            for z in range(nz):
-                high_copy(z).wait()
 
         def forward_kernel(source_ref, inv_ref, low_jac, *rest):
             came, top_ref = rest[:-1], rest[-1]
@@ -414,11 +438,12 @@
                 put(top_ref, top[tile], at)
 
         def forward_mid_kernel(low_ref, came_ref, source_ref, inv_ref, low_jac, top_ref):
-            top_ref[...] = low_ref[...]
-
-            @pl.when(lax.axis_index("gz") == 1)
+            here = lax.axis_index("gz") == 1
+            pl.when(here)(lambda: forward_kernel(source_ref, inv_ref, low_jac, came_ref, top_ref))
+
+            @pl.when(jnp.logical_not(here))
             def _():
-                forward_kernel(source_ref, inv_ref, low_jac, came_ref, top_ref)
+                top_ref[...] = low_ref[...]
 
         def either(device, work, fast):
             if fast is None:
@@ -432,7 +457,7 @@
             came, (sweep_ref, change_ref, x_side, y_side) = rest[:-4], rest[-4:]
             fast = None
             if short:
-                first, near, matrix_ref, far, *fast = came
+                first, far, third, matrix_ref, near, *fast = came
 
             def keep(z, at, result):
                 before = planes_of(prev_ref, z, at)
@@ -442,7 +467,9 @@
 
             def work(fast):
                 if short:
-                    starts = tuple(arrived((first, near), matrix_ref, far, at) for at in spans)
+                    starts = tuple(
+                        arrived((first, near, third), matrix_ref, far, at) for at in spans
+                    )
                 else:
                     starts = tuple(incoming(came, at) for at in spans)
                 forward_sweep(source_ref, inv_ref, low_jac, starts, keep, fast)
@@ -570,45 +597,37 @@
         if short:
             up_there = lax.ppermute(up_matrix[0], "gz", [(2, 3)])
         halo = exchange(x_side, y_side)
-        ahead, behind = None, None
+        first_args = [rhs, jac, prev, inv, low_jac, *halo]
+        first_scratch = [pltpu.VMEM(rhs.shape, F32), pltpu.SemaphoreType.DMA((2, nz))]
         if short:
-            ahead, behind = (lambda device: device == 0), (lambda device: device != 0)
-        first_args = [rhs, jac, prev, inv, low_jac, *halo]
-        first_options = dict(
-            cost=unit // 8,
-            in_hbm=(0, 1),
-            scratch=[pltpu.VMEM(rhs.shape, F32), pltpu.SemaphoreType.DMA((3, nz))],
-        )
-        first_outs = [volume, plane, side_blocks, blocks]
-        source, top, sides, high_jac = call(
-            functools.partial(first_kernel, ahead), first_outs, *first_args, **first_options
-        )
-        if short:
+            source, top, sides = call(
+                first_ahead_kernel,
+                [volume, plane, side_blocks],
+                *first_args,
+                cost=unit // 8,
+                in_hbm=(0, 1),
+                scratch=first_scratch,
+            )
             first = lax.ppermute(top, "gz", [(0, 1)])
             n = len(first_args)
             source, top, sides, high_jac = call(
-                functools.partial(first_again_kernel, behind),
-                first_outs,
+                first_behind_kernel,
+                [volume, plane, side_blocks, blocks],
                 *first_args,
                 source,
                 top,
                 sides,
-                high_jac,
-                aliases={n: 0, n + 2: 2, n + 3: 3},
-                **first_options,
-            )
+                cost=unit // 8,
+                in_hbm=(0, 1),
+                aliases={n: 0, n + 2: 2},
+                scratch=first_scratch + [pltpu.SemaphoreType.DMA],
+            )
+            third = lax.ppermute(top, "gz", [(2, 3)])
             (top,) = call(
-                forward_mid_kernel,
-                [plane],
-                top,
-                first,
-                source,
-                inv,
-                low_jac,
-                cost=unit // 8,
-            )
+                forward_mid_kernel, [plane], top, first, source, inv, low_jac, cost=unit // 8
+            )
+            near = lax.ppermute(top, "gz", [(1, 2)])
             far = lax.ppermute(top, "gz", [(1, 3)])
-            near = lax.ppermute(top, "gz", [(1, 2), (2, 3)])
             down_one, *fast = call(
                 forward_idle_kernel,
                 [matrix, steps, volume],
@@ -620,11 +639,19 @@
                 cost=unit // 8,
             )
             (down_one,) = call(
-                pass_kernel, [matrix], down_one, near, far, cost=unit // 8, aliases={0: 0}
+                pass_kernel, [matrix], down_one, far, near, third, cost=unit // 8, aliases={0: 0}
             )
             down_there = lax.ppermute(down_one, "gz", [(2, 1)])
-            came = [first, near, up_there, far, *fast]
+            came = [first, far, third, up_there, near, *fast]
         else:
+            source, top, sides, high_jac = call(
+                first_kernel,
+                [volume, plane, side_blocks, blocks],
+                *first_args,
+                cost=14 * unit,
+                in_hbm=(0, 1),
+                scratch=first_scratch + [pltpu.SemaphoreType.DMA],
+            )
             came = []
             for hop in range(gz - 1):
                 if hop:

time: 59.4 us -> 60.3 us (1.015)
  Pallas kernels: 20.8 us -> 22.5 us
  waiting for transfers between devices: 17.9 us -> 16.5 us
  starting transfers between devices: 9.73 us -> 10.4 us
    ppermute x1, waiting for transfers between devices: 2.52 us -> 0.09 us  [body(): first = lax.ppermute(top, 'gz', [(0, 1)])]
    pallas_call x13, Pallas kernels: 20.8 us -> 22.5 us  [call(): pl.pallas_call(body, out_shape=shapes, in_specs=[far if i in in_hbm else...]
    ppermute x1, waiting for transfers between devices: 15.4 us -> 16.4 us  [body(): came = [entered, lax.ppermute(low, 'gz', [(1, 0)]), *fast]]
    ppermute x1 -> x2, starting transfers between devices: 0.67 us -> 1.33 us  [the longest x1 0.67 us: body(): third = lax.ppermute(top, 'gz', [(2, 3)])]
  transfers between devices with their start and end apart: 10 -> 11, of which waited for: 2 -> 2; matrix products, arithmetic and copies ran while one was open for 0% -> 0% of each run, Pallas kernels for 27% -> 29%
where the time goes in v9:
time: 60.3 us; the launch traced here: 60 us
  Pallas kernels  22.5 us (37%)
  waiting for transfers between devices  16.5 us (27%)
  blocking collectives  10.5 us (17%)
  starting transfers between devices  10.4 us (17%)
    pallas_call x13, Pallas kernels, call(): pl.pallas_call(body, out_shape=shapes, in_specs=[far if i in in_hbm else...  22.5 us
    ppermute x1, waiting for transfers between devices, body(): came = [entered, lax.ppermute(low, 'gz', [(1, 0)]), *fast]  16.4 us
    all_gather x2, blocking collectives, exchange(): return (lax.all_gather(x_side, 'gx'), *rows)  10.5 us
    ppermute x2, starting transfers between devices, exchange(): rows = [lax.ppermute(y_side[0], 'gy', [(0, 1), (1, 0)])]  3.1 us
    ppermute x1, starting transfers between devices, body(): first = lax.ppermute(top, 'gz', [(0, 1)])  1.3 us
    ppermute x1, starting transfers between devices, body(): came = [entered, lax.ppermute(low, 'gz', [(1, 0)]), *fast]  1.29 us
  transfers between devices with their start and end apart: 11, of which 2 were waited for; matrix products, arithmetic and copies ran while one was open for 0% of the time, Pallas kernels for 29%

profile of v9, /device:TPU:0, one launch (start us, length us, event | category | flops | bytes accessed | tf_op | source)
XLA Modules:
  0.0 60.0 jit_solution(10111317072959473971)
XLA Ops:
  0.0 3.4 %shard_map.46 = (f32[10,6,16,256]{3,2,1,0:T(8,128)S(1)}, bf16[10,6,6,16,256]{4,3,2,1,0:T(8,128)(2,1)S(1)}, bf16[10,6,6,16,256]{4,3,2,1,0:T(8,128)(2,1)S(1)}, f32...) custom-call(f32[10,6,16,256]{3,2,1,0:T(8,128)} %bitcast.21, ...), custom_call_target="tpu_custom_call" | custom-call | bytes 19660800 | tf_op jit(solution)/shard_map/pallas_call | solution.py:22
  3.5 0.7 %collective-permute-start.4 = (f32[6,6,16,256]{3,2,1,0:T(8,128)S(1)}, f32[6,6,16,256]{3,2,1,0:T(8,128)S(1)}, u32[]{:S(2)}, u32[]{:S(2)}) collective-permute-start(f32[6,6,16,256]{3,2,1,0:T(8,128)S(1)} %get-tuple-element.44), channel_id=1, source_target_pairs={{16,24},{17,25},{18,26},{19,27},{20,28},{21,29},{22,30},{23,31}} | collective-permute-start | bytes 1769480 | tf_op jit(solution)/shard_map/ppermute | solution.py:598
  4.2 3.0 %collective-permute-start = (f32[10,6,256]{2,1,0:T(8,128)S(1)}, f32[10,6,256]{2,1,0:T(8,128)S(1)}, u32[]{:S(2)}, u32[]{:S(2)}) collective-permute-start(f32[10,6,256]{2,1,0:T(8,128)S(1)} %bitcast.14), channel_id=1, source_target_pairs={{0,1},{1,0},{2,3},{3,2},{4,5},{5,4},{6,7},{7,6},{8,9},{9,8},{10,11... | collective-permute-start | bytes 184328 | tf_op jit(solution)/shard_map/ppermute | solution.py:178
  7.2 5.2 %all-gather = f32[8,1,16,128]{3,2,1,0:T(8,128)S(1)} all-gather(f32[2,1,16,128]{3,2,1,0:T(8,128)S(1)} %get-tuple-element.37), channel_id=2, replica_groups=mesh['gz'=4,'gx'=4,'gy'=2] {'gx'}, dimensions={0}, use_global_device_ids=true | all-gather | bytes 81920 | tf_op jit(solution)/shard_map/all_gather | solution.py:185
  12.4 0.0 collective-permute-done.rest_0_.refs_6_
  12.4 5.6 %shard_map.47 = (f32[10,6,16,256]{3,2,1,0:T(8,128)S(1)}, f32[6,16,256]{2,1,0:T(8,128)S(1)}, bf16[10,4,6,6,16,256]{5,4,3,2,1,0:T(8,128)(2,1)S(1)}) custom-call(f32[10,6,16,256]{3,2,1,0:T(8,128)} %bitcast.18, bf16[10,6,6,6,16,256]{5,4,3,2,1,0:T(8,128)(2,1)} %bitcast.16, f32[10,6,16,256]{3,2,1,0:T(8,128)S(1)} %get-tuple-element.34.prev_ref.refs_2_, ...), custom_call_target="tpu_custom_call" | custom-call | bytes 204800 | tf_op jit(solution)/shard_map/pallas_call | solution.py:22
  18.0 1.3 %collective-permute-start.1 = (f32[6,16,256]{2,1,0:T(8,128)S(1)}, f32[6,16,256]{2,1,0:T(8,128)S(1)}, u32[]{:S(2)}, u32[]{:S(2)}) collective-permute-start(f32[6,16,256]{2,1,0:T(8,128)S(1)} %get-tuple-element.40.refs_8_), channel_id=1, source_target_pairs={{0,8},{1,9},{2,10},{3,11},{4,12},{5,13},{6,14},{7,15}} | collective-permute-start | bytes 294920 | tf_op jit(solution)/shard_map/ppermute | solution.py:611
  19.3 2.0 %shard_map.48 = (f32[10,6,16,256]{3,2,1,0:T(8,128)S(1)}, f32[6,16,256]{2,1,0:T(8,128)S(1)}, bf16[10,4,6,6,16,256]{5,4,3,2,1,0:T(8,128)(2,1)S(1)}, bf16[10,6,6,16,256]{4,3,2,1,0:T(8,128)(2,1)S(1)}) custom-call(f32[10,6,16,256]{3,2,1,0:T(8,128)} %bitcast.19, bf16[10,6,6,6,16,256]{5,4,3,2,1,0:T(8,128)(2,1)} %bitcast.17, ...), custom_call_target="tpu_custom_call", output_to_operand_aliasing={{0}: (7, {}), {2}: (9, {})} | custom-call | bytes 204800 | tf_op jit(solution)/shard_map/pallas_call | solution.py:22
  21.3 0.7 %collective-permute-start.3 = (f32[6,16,256]{2,1,0:T(8,128)S(1)}, f32[6,16,256]{2,1,0:T(8,128)S(1)}, u32[]{:S(2)}, u32[]{:S(2)}) collective-permute-start(f32[6,16,256]{2,1,0:T(8,128)S(1)} %get-tuple-element.43.low_ref), channel_id=1, source_target_pairs={{16,24},{17,25},{18,26},{19,27},{20,28},{21,29},{22,30},{23,31}} | collective-permute-start | bytes 294920 | tf_op jit(solution)/shard_map/ppermute | solution.py:625
  22.0 0.1 collective-permute-done.1.came_ref.rest_0_
  22.1 0.7 %collective-permute-start.2 = (f32[6,16,256]{2,1,0:T(8,128)S(1)}, f32[6,16,256]{2,1,0:T(8,128)S(1)}, u32[]{:S(2)}, u32[]{:S(2)}) collective-permute-start(f32[6,16,256]{2,1,0:T(8,128)S(1)} %shard_map.49), channel_id=1, source_target_pairs={{8,24},{9,25},{10,26},{11,27},{12,28},{13,29},{14,30},{15,31}} | collective-permute-start | bytes 294920 | tf_op jit(solution)/shard_map/ppermute | solution.py:630
  22.8 0.7 %collective-permute-start.5 = (f32[6,16,256]{2,1,0:T(8,128)S(1)}, f32[6,16,256]{2,1,0:T(8,128)S(1)}, u32[]{:S(2)}, u32[]{:S(2)}) collective-permute-start(f32[6,16,256]{2,1,0:T(8,128)S(1)} %shard_map.49), channel_id=1, source_target_pairs={{8,16},{9,17},{10,18},{11,19},{12,20},{13,21},{14,22},{15,23}} | collective-permute-start | bytes 294920 | tf_op jit(solution)/shard_map/ppermute | solution.py:629
  23.5 0.0 collective-permute-done.4._.rest_3_
  23.5 0.1 shard_map.50
  23.5 0.0 collective-permute-done.3.rest_2_.refs_3_
  23.6 0.0 collective-permute-done.2.rest_1_.refs_1_
  23.6 0.0 collective-permute-done.5.rest_4_.refs_2_
  23.6 0.7 %collective-permute-start.9 = (f32[6,6,16,256]{3,2,1,0:T(8,128)S(1)}, f32[6,6,16,256]{3,2,1,0:T(8,128)S(1)}, u32[]{:S(2)}, u32[]{:S(2)}) collective-permute-start(f32[6,6,16,256]{3,2,1,0:T(8,128)S(1)} %shard_map.54), channel_id=1, source_target_pairs={{16,8},{17,9},{18,10},{19,11},{20,12},{21,13},{22,14},{23,15}} | collective-permute-start | bytes 1769480 | tf_op jit(solution)/shard_map/ppermute | solution.py:644
  24.3 1.6 %shard_map.51 = (f32[10,6,16,256]{3,2,1,0:T(8,128)S(1)}, f32[10,6,16,256]{3,2,1,0:T(8,128)S(1)}, f32[2,1,16,128]{3,2,1,0:T(8,128)S(1)}, f32[1,10,6,256]{3,2,1,0:T(8,128)S(1)}) custom-call(f32[10,6,16,256]{3,2,1,0:T(8,128)S(1)} %get-tuple-element.42.source_ref, f32[10,6,16,256]{3,2,1,0:T(8,128)S(1)} %get-tuple-element.34.prev_ref.refs_2_, ...), custom_call_target="tpu_custom_call" | custom-call | bytes 6553600 | tf_op jit(solution)/shard_map/pallas_call | solution.py:22
  25.9 0.1 collective-permute-start.6
  26.0 5.2 %all-gather.1 = f32[8,1,16,128]{3,2,1,0:T(8,128)S(1)} all-gather(f32[2,1,16,128]{3,2,1,0:T(8,128)S(1)} %get-tuple-element.51), channel_id=3, replica_groups=mesh['gz'=4,'gx'=4,'gy'=2] {'gx'}, dimensions={0}, use_global_device_ids=true | all-gather | bytes 81920 | tf_op jit(solution)/shard_map/all_gather | solution.py:185
  31.2 0.0 collective-permute-done.6.rest_0_.refs_6_
  31.2 0.7 %collective-permute-start.8 = (f32[6,16,256]{2,1,0:T(8,128)S(1)}, f32[6,16,256]{2,1,0:T(8,128)S(1)}, u32[]{:S(2)}, u32[]{:S(2)}) collective-permute-start(f32[6,16,256]{2,1,0:T(8,128)S(1)} %get-tuple-element.54.refs_8_), channel_id=1, source_target_pairs={{24,8},{25,9},{26,10},{27,11},{28,12},{29,13},{30,14},{31,15}} | collective-permute-start | bytes 294920 | tf_op jit(solution)/shard_map/ppermute | solution.py:691
  31.9 4.9 %shard_map.53 = (f32[10,6,16,256]{3,2,1,0:T(8,128)S(1)}, f32[6,16,256]{2,1,0:T(8,128)S(1)}) custom-call(f32[10,6,16,256]{3,2,1,0:T(8,128)S(1)} %get-tuple-element.48.sweep_ref.refs_0_, f32[10,6,16,256]{3,2,1,0:T(8,128)S(1)} %get-tuple-element.49.change_ref.refs_1_, ...), custom_call_target="tpu_custom_call", output_to_operand_aliasing={{0}: (7, {})} | custom-call | bytes 204800 | tf_op jit(solution)/shard_map/pallas_call | solution.py:22
  36.8 0.7 %collective-permute-start.7 = (f32[6,16,256]{2,1,0:T(8,128)S(1)}, f32[6,16,256]{2,1,0:T(8,128)S(1)}, u32[]{:S(2)}, u32[]{:S(2)}) collective-permute-start(f32[6,16,256]{2,1,0:T(8,128)S(1)} %get-tuple-element.56._.own_ref), channel_id=1, source_target_pairs={{24,16},{16,8},{25,17},{17,9},{26,18},{18,10},{27,19},{19,11},{28,... | collective-permute-start | bytes 294920 | tf_op jit(solution)/shard_map/ppermute | solution.py:690
  37.5 3.4 %shard_map.55 = (f32[6,6,16,256]{3,2,1,0:T(8,128)S(1)}, f32[10,6,6,16,256]{4,3,2,1,0:T(8,128)S(1)}, f32[10,6,16,256]{3,2,1,0:T(8,128)S(1)}) custom-call(bf16[10,6,6,16,256]{4,3,2,1,0:T(8,128)(2,1)S(1)} %get-tuple-element.35.inv_ref.refs_3_.refs_2_, bf16[10,6,6,16,256]{4,3,2,1,0:T(8,128)(2,1)S(1)} %get-tuple-element.45.high_jac.refs_4_, ...), custom_call_target="tpu_custom_call" | custom-call | bytes 204800 | tf_op jit(solution)/shard_map/pallas_call | solution.py:22
  40.9 0.0 collective-permute-done.8.far_ref
  40.9 0.1 shard_map.56.moved_ref
  41.0 0.1 shard_map.57
  41.1 1.3 %collective-permute-start.10 = (f32[6,16,256]{2,1,0:T(8,128)S(1)}, f32[6,16,256]{2,1,0:T(8,128)S(1)}, u32[]{:S(2)}, u32[]{:S(2)}) collective-permute-start(f32[6,16,256]{2,1,0:T(8,128)S(1)} %get-tuple-element.60), channel_id=1, source_target_pairs={{8,0},{9,1},{10,2},{11,3},{12,4},{13,5},{14,6},{15,7}} | collective-permute-start | bytes 294920 | tf_op jit(solution)/shard_map/ppermute | solution.py:706
  42.4 16.4 %collective-permute-done.10.rest_1_ = f32[6,16,256]{2,1,0:T(8,128)S(1)} collective-permute-done((f32[6,16,256]{2,1,0:T(8,128)S(1)}, f32[6,16,256]{2,1,0:T(8,128)S(1)}, u32[]{:S(2)}, u32[]{:S(2)}) %collective-permute-start.10) | collective-permute-done | bytes 98336 | tf_op jit(solution)/shard_map/ppermute | solution.py:706
  58.8 1.3 %shard_map.58 = f32[10,6,16,256]{3,2,1,0:T(8,128)} custom-call(f32[10,6,16,256]{3,2,1,0:T(8,128)S(1)} %get-tuple-element.48.sweep_ref.refs_0_, f32[10,6,16,256]{3,2,1,0:T(8,128)S(1)} %get-tuple-element.55.inner_ref, bf16[10,6,6,16,256]{4,3,2,1,0:T(8,128)(2,1)S(1)} %get-tuple-element.35.inv_ref.refs_3_.refs_2_, ...), custom_call_target="tpu_custom_call" | custom-call | bytes 8192000 | tf_op jit(solution)/shard_map/pallas_call | solution.py:22
  (5 shorter events, 0.0 us)
Async XLA Ops:
  3.5 20.0 %collective-permute-start.4 = (f32[6,6,16,256]{3,2,1,0:T(8,128)S(1)}, f32[6,6,16,256]{3,2,1,0:T(8,128)S(1)}, u32[]{:S(2)}, u32[]{:S(2)}) collective-permute-start(f32[6,6,16,256]{3,2,1,0:T(8,128)S(1)} %get-tuple-element.44), channel_id=1, source_target_pairs={{16,24},{17,25},{18,26},{19,27},{20,28},{21,29},{22,30},{23,31}} | collective-permute-start | bytes 1769480 | tf_op jit(solution)/shard_map/ppermute | solution.py:598
  4.2 8.2 %collective-permute-start = (f32[10,6,256]{2,1,0:T(8,128)S(1)}, f32[10,6,256]{2,1,0:T(8,128)S(1)}, u32[]{:S(2)}, u32[]{:S(2)}) collective-permute-start(f32[10,6,256]{2,1,0:T(8,128)S(1)} %bitcast.14), channel_id=1, source_target_pairs={{0,1},{1,0},{2,3},{3,2},{4,5},{5,4},{6,7},{7,6},{8,9},{9,8},{10,11... | collective-permute-start | bytes 184328 | tf_op jit(solution)/shard_map/ppermute | solution.py:178
  18.0 4.1 %collective-permute-start.1 = (f32[6,16,256]{2,1,0:T(8,128)S(1)}, f32[6,16,256]{2,1,0:T(8,128)S(1)}, u32[]{:S(2)}, u32[]{:S(2)}) collective-permute-start(f32[6,16,256]{2,1,0:T(8,128)S(1)} %get-tuple-element.40.refs_8_), channel_id=1, source_target_pairs={{0,8},{1,9},{2,10},{3,11},{4,12},{5,13},{6,14},{7,15}} | collective-permute-start | bytes 294920 | tf_op jit(solution)/shard_map/ppermute | solution.py:611
  21.3 2.2 %collective-permute-start.3 = (f32[6,16,256]{2,1,0:T(8,128)S(1)}, f32[6,16,256]{2,1,0:T(8,128)S(1)}, u32[]{:S(2)}, u32[]{:S(2)}) collective-permute-start(f32[6,16,256]{2,1,0:T(8,128)S(1)} %get-tuple-element.43.low_ref), channel_id=1, source_target_pairs={{16,24},{17,25},{18,26},{19,27},{20,28},{21,29},{22,30},{23,31}} | collective-permute-start | bytes 294920 | tf_op jit(solution)/shard_map/ppermute | solution.py:625
  22.1 1.4 %collective-permute-start.2 = (f32[6,16,256]{2,1,0:T(8,128)S(1)}, f32[6,16,256]{2,1,0:T(8,128)S(1)}, u32[]{:S(2)}, u32[]{:S(2)}) collective-permute-start(f32[6,16,256]{2,1,0:T(8,128)S(1)} %shard_map.49), channel_id=1, source_target_pairs={{8,24},{9,25},{10,26},{11,27},{12,28},{13,29},{14,30},{15,31}} | collective-permute-start | bytes 294920 | tf_op jit(solution)/shard_map/ppermute | solution.py:630
  22.8 0.8 %collective-permute-start.5 = (f32[6,16,256]{2,1,0:T(8,128)S(1)}, f32[6,16,256]{2,1,0:T(8,128)S(1)}, u32[]{:S(2)}, u32[]{:S(2)}) collective-permute-start(f32[6,16,256]{2,1,0:T(8,128)S(1)} %shard_map.49), channel_id=1, source_target_pairs={{8,16},{9,17},{10,18},{11,19},{12,20},{13,21},{14,22},{15,23}} | collective-permute-start | bytes 294920 | tf_op jit(solution)/shard_map/ppermute | solution.py:629
  23.6 17.4 %collective-permute-start.9 = (f32[6,6,16,256]{3,2,1,0:T(8,128)S(1)}, f32[6,6,16,256]{3,2,1,0:T(8,128)S(1)}, u32[]{:S(2)}, u32[]{:S(2)}) collective-permute-start(f32[6,6,16,256]{3,2,1,0:T(8,128)S(1)} %shard_map.54), channel_id=1, source_target_pairs={{16,8},{17,9},{18,10},{19,11},{20,12},{21,13},{22,14},{23,15}} | collective-permute-start | bytes 1769480 | tf_op jit(solution)/shard_map/ppermute | solution.py:644
  25.9 5.3 %collective-permute-start.6 = (f32[10,6,256]{2,1,0:T(8,128)S(1)}, f32[10,6,256]{2,1,0:T(8,128)S(1)}, u32[]{:S(2)}, u32[]{:S(2)}) collective-permute-start(f32[10,6,256]{2,1,0:T(8,128)S(1)} %bitcast.13), channel_id=1, source_target_pairs={{0,1},{1,0},{2,3},{3,2},{4,5},{5,4},{6,7},{7,6},{8,9},{9,8},{10,11... | collective-permute-start | bytes 184328 | tf_op jit(solution)/shard_map/ppermute | solution.py:178
  31.2 9.7 %collective-permute-start.8 = (f32[6,16,256]{2,1,0:T(8,128)S(1)}, f32[6,16,256]{2,1,0:T(8,128)S(1)}, u32[]{:S(2)}, u32[]{:S(2)}) collective-permute-start(f32[6,16,256]{2,1,0:T(8,128)S(1)} %get-tuple-element.54.refs_8_), channel_id=1, source_target_pairs={{24,8},{25,9},{26,10},{27,11},{28,12},{29,13},{30,14},{31,15}} | collective-permute-start | bytes 294920 | tf_op jit(solution)/shard_map/ppermute | solution.py:691
  36.8 4.2 %collective-permute-start.7 = (f32[6,16,256]{2,1,0:T(8,128)S(1)}, f32[6,16,256]{2,1,0:T(8,128)S(1)}, u32[]{:S(2)}, u32[]{:S(2)}) collective-permute-start(f32[6,16,256]{2,1,0:T(8,128)S(1)} %get-tuple-element.56._.own_ref), channel_id=1, source_target_pairs={{24,16},{16,8},{25,17},{17,9},{26,18},{18,10},{27,19},{19,11},{28,... | collective-permute-start | bytes 294920 | tf_op jit(solution)/shard_map/ppermute | solution.py:690
  41.1 17.7 %collective-permute-start.10 = (f32[6,16,256]{2,1,0:T(8,128)S(1)}, f32[6,16,256]{2,1,0:T(8,128)S(1)}, u32[]{:S(2)}, u32[]{:S(2)}) collective-permute-start(f32[6,16,256]{2,1,0:T(8,128)S(1)} %get-tuple-element.60), channel_id=1, source_target_pairs={{8,0},{9,1},{10,2},{11,3},{12,4},{13,5},{14,6},{15,7}} | collective-permute-start | bytes 294920 | tf_op jit(solution)/shard_map/ppermute | solution.py:706

commit v10 on v8

--- a/solution.py
+++ b/solution.py
@@ -492,7 +492,7 @@
             transfer(matrix_ref, inv_ref, high_jac, lambda i: nz - 1 - i)
 
         def forward_idle_kernel(inv_ref, high_jac, low_jac, source_ref, _, matrix_ref, step_ref, plain_ref):
-            only(2, lambda: down_matrix(inv_ref, high_jac, matrix_ref), matrix_ref, matrix[0])
+            only(1, lambda: down_matrix(inv_ref, high_jac, matrix_ref), matrix_ref, matrix[0])
 
             @pl.when(lax.axis_index("gz") == 3)
             def _():
@@ -501,10 +501,10 @@
 
                 make_fast(step_ref, plain_ref, inv_ref, low_jac, plain_of)
 
-        def backward_idle_kernel(inv_ref, high_jac, sweep_ref, inner_ref, _, matrix_ref, step_ref, plain_ref):
-            only(1, lambda: down_matrix(inv_ref, high_jac, matrix_ref), matrix_ref, matrix[0])
-
-            @pl.when(lax.axis_index("gz") == 0)
+        def backward_idle_kernel(inv_ref, high_jac, sweep_ref, inner_ref, step_ref, plain_ref):
+            me = lax.axis_index("gz")
+
+            @pl.when((me == 0) | (me == 2))
             def _():
                 def plain_of(z, at, times):
                     moved = times(planes_of(inner_ref, z, at))
@@ -522,22 +522,25 @@
         def pass_kernel(*refs):
             pass
 
-        def far_kernel(far_ref, matrix_ref, _, moved_ref):
-            for at in spans:
-                put(moved_ref, apply_matrix(matrix_ref, planes_in(far_ref, at), at), at)
-
-        def backward_mid_kernel(own_ref, near_ref, moved_ref, matrix_ref, came_ref, low_ref):
-            for at in spans:
-                came = incoming((near_ref, moved_ref), at)
-                moved = apply_matrix(matrix_ref, came, at)
-                put(came_ref, came, at)
-                put(low_ref, [a + b for a, b in zip(planes_in(own_ref, at), moved)], at)
+        def backward_mid_kernel(own_ref, came_ref, step_ref, plain_ref, low_ref):
+            here = lax.axis_index("gz") == 2
+
+            @pl.when(here)
+            def _():
+                starts = tuple(incoming((came_ref,), at) for at in spans)
+                low = backward_sweep(None, None, None, None, starts, fast=(step_ref, plain_ref))
+                for tile, at in enumerate(spans):
+                    put(low_ref, low[tile], at)
+
+            @pl.when(jnp.logical_not(here))
+            def _():
+                low_ref[...] = own_ref[...]
 
         def update_kernel(sweep_ref, inner_ref, inv_ref, high_jac, *rest):
             came, (out_hbm, held, sems) = rest[:-3], rest[-3:]
             fast = None
             if short:
-                came, fast = came[:2], came[2:]
+                first, near, matrix_ref, far, *fast = came
 
             def out_copy(z):
                 return pltpu.make_async_copy(held.at[z], out_hbm.at[z], sems.at[z])
@@ -549,7 +552,10 @@
                     out_copy(z).start()
 
             def work(fast):
-                starts = tuple(incoming(came, at) for at in spans)
+                if short:
+                    starts = tuple(arrived((first, near), matrix_ref, far, at) for at in spans)
+                else:
+                    starts = tuple(incoming(came, at) for at in spans)
                 backward_sweep(sweep_ref, inner_ref, inv_ref, high_jac, starts, keep, fast)
 
             either(0, work, fast)
@@ -622,7 +628,7 @@
             (down_one,) = call(
                 pass_kernel, [matrix], down_one, near, far, cost=unit // 8, aliases={0: 0}
             )
-            down_there = lax.ppermute(down_one, "gz", [(2, 1)])
+            down_there = lax.ppermute(down_one, "gz", [(1, 0)])
             came = [first, near, up_there, far, *fast]
         else:
             came = []
@@ -660,23 +666,20 @@
                 aliases={len(turn_args): 0},
                 cost=unit // 8,
             )
-            near = lax.ppermute(low, "gz", [(3, 2), (2, 1)])
-            far = lax.ppermute(ahead_low, "gz", [(3, 1)])
-            own_matrix, *fast = call(
+            first = lax.ppermute(ahead_low, "gz", [(3, 2)])
+            fast = call(
                 backward_idle_kernel,
-                [matrix, steps, volume],
+                [steps, volume],
                 inv,
                 high_jac,
                 sweep,
                 inner,
-                low,
                 cost=unit // 8,
             )
-            (moved,) = call(far_kernel, [plane], far, down_there, own_matrix, cost=unit // 8)
-            entered, low = call(
-                backward_mid_kernel, [plane, plane], low, near, moved, own_matrix, cost=unit // 8
-            )
-            came = [entered, lax.ppermute(low, "gz", [(1, 0)]), *fast]
+            (low,) = call(backward_mid_kernel, [plane], low, first, *fast, cost=unit // 8)
+            far = lax.ppermute(low, "gz", [(2, 0)])
+            near = lax.ppermute(low, "gz", [(2, 1), (1, 0)])
+            came = [first, near, down_there, far, *fast]
         else:
             came = []
             for hop in range(gz - 1, 0, -1):

time: 59.4 us -> 58.5 us (0.985)
  waiting for transfers between devices: 17.9 us -> 15.8 us
  starting transfers between devices: 9.73 us -> 10.9 us
    ppermute x4, waiting for transfers between devices: 15.4 us -> 13.3 us  [the longest x1 13.3 us: body(): far = lax.ppermute(low, 'gz', [(2, 0)])]
    ppermute x4, starting transfers between devices: 3.31 us -> 4.53 us  [the longest x1 1.29 us: body(): down_there = lax.ppermute(down_one, 'gz', [(1, 0)])]
    pallas_call x13 -> x12, Pallas kernels: 20.8 us -> 20.7 us  [call(): pl.pallas_call(body, out_shape=shapes, in_specs=[far if i in in_hbm else...]
where the time goes in v10:
time: 58.5 us; the launch traced here: 58.1 us
  Pallas kernels  20.7 us (35%)
  waiting for transfers between devices  15.8 us (27%)
  starting transfers between devices  10.9 us (19%)
  blocking collectives  10.5 us (18%)
    pallas_call x12, Pallas kernels, call(): pl.pallas_call(body, out_shape=shapes, in_specs=[far if i in in_hbm else...  20.7 us
    ppermute x1, waiting for transfers between devices, body(): far = lax.ppermute(low, 'gz', [(2, 0)])  13.3 us
    all_gather x2, blocking collectives, exchange(): return (lax.all_gather(x_side, 'gx'), *rows)  10.5 us
    ppermute x2, starting transfers between devices, exchange(): rows = [lax.ppermute(y_side[0], 'gy', [(0, 1), (1, 0)])]  3.1 us
    ppermute x1, waiting for transfers between devices, body(): first = lax.ppermute(top, 'gz', [(0, 1)])  2.52 us
    ppermute x1, starting transfers between devices, body(): first = lax.ppermute(top, 'gz', [(0, 1)])  1.3 us
    ppermute x1, starting transfers between devices, body(): down_there = lax.ppermute(down_one, 'gz', [(1, 0)])  1.29 us
    ppermute x1, starting transfers between devices, body(): far = lax.ppermute(low, 'gz', [(2, 0)])  1.29 us
  transfers between devices with their start and end apart: 10, of which 2 were waited for; matrix products, arithmetic and copies ran while one was open for 0% of the time, Pallas kernels for 27%

profile of v10, /device:TPU:0, one launch (start us, length us, event | category | flops | bytes accessed | tf_op | source)
XLA Modules:
  0.0 58.1 jit_solution(11033943695760245981)
XLA Ops:
  0.0 3.4 %shard_map.46 = (f32[10,6,16,256]{3,2,1,0:T(8,128)S(1)}, bf16[10,6,6,16,256]{4,3,2,1,0:T(8,128)(2,1)S(1)}, bf16[10,6,6,16,256]{4,3,2,1,0:T(8,128)(2,1)S(1)}, f32...) custom-call(f32[10,6,16,256]{3,2,1,0:T(8,128)} %bitcast.21, ...), custom_call_target="tpu_custom_call" | custom-call | bytes 19660800 | tf_op jit(solution)/shard_map/pallas_call | solution.py:22
  3.5 0.7 %collective-permute-start.3 = (f32[6,6,16,256]{3,2,1,0:T(8,128)S(1)}, f32[6,6,16,256]{3,2,1,0:T(8,128)S(1)}, u32[]{:S(2)}, u32[]{:S(2)}) collective-permute-start(f32[6,6,16,256]{3,2,1,0:T(8,128)S(1)} %get-tuple-element.43), channel_id=1, source_target_pairs={{16,24},{17,25},{18,26},{19,27},{20,28},{21,29},{22,30},{23,31}} | collective-permute-start | bytes 1769480 | tf_op jit(solution)/shard_map/ppermute | solution.py:577
  4.2 3.0 %collective-permute-start = (f32[10,6,256]{2,1,0:T(8,128)S(1)}, f32[10,6,256]{2,1,0:T(8,128)S(1)}, u32[]{:S(2)}, u32[]{:S(2)}) collective-permute-start(f32[10,6,256]{2,1,0:T(8,128)S(1)} %bitcast.14), channel_id=1, source_target_pairs={{0,1},{1,0},{2,3},{3,2},{4,5},{5,4},{6,7},{7,6},{8,9},{9,8},{10,11... | collective-permute-start | bytes 184328 | tf_op jit(solution)/shard_map/ppermute | solution.py:178
  7.2 5.2 %all-gather = f32[8,1,16,128]{3,2,1,0:T(8,128)S(1)} all-gather(f32[2,1,16,128]{3,2,1,0:T(8,128)S(1)} %get-tuple-element.35), channel_id=2, replica_groups=mesh['gz'=4,'gx'=4,'gy'=2] {'gx'}, dimensions={0}, use_global_device_ids=true | all-gather | bytes 81920 | tf_op jit(solution)/shard_map/all_gather | solution.py:185
  12.4 0.0 collective-permute-done.rest_0_.refs_6_
  12.4 5.7 %shard_map.47 = (f32[10,6,16,256]{3,2,1,0:T(8,128)S(1)}, f32[6,16,256]{2,1,0:T(8,128)S(1)}, bf16[10,4,6,6,16,256]{5,4,3,2,1,0:T(8,128)(2,1)S(1)}, bf16[10,6,6,16,256]{4,3,2,1,0:T(8,128)(2,1)S(1)}) custom-call(f32[10,6,16,256]{3,2,1,0:T(8,128)} %bitcast.18, bf16[10,6,6,6,16,256]{5,4,3,2,1,0:T(8,128)(2,1)} %bitcast.16, ...), custom_call_target="tpu_custom_call" | custom-call | bytes 204800 | tf_op jit(solution)/shard_map/pallas_call | solution.py:22
  18.1 1.3 %collective-permute-start.1 = (f32[6,16,256]{2,1,0:T(8,128)S(1)}, f32[6,16,256]{2,1,0:T(8,128)S(1)}, u32[]{:S(2)}, u32[]{:S(2)}) collective-permute-start(f32[6,16,256]{2,1,0:T(8,128)S(1)} %get-tuple-element.38.refs_8_), channel_id=1, source_target_pairs={{0,8},{1,9},{2,10},{3,11},{4,12},{5,13},{6,14},{7,15}} | collective-permute-start | bytes 294920 | tf_op jit(solution)/shard_map/ppermute | solution.py:593
  19.4 0.3 shard_map.48
  19.7 2.5 %collective-permute-done.1.came_ref.rest_0_ = f32[6,16,256]{2,1,0:T(8,128)S(1)} collective-permute-done((f32[6,16,256]{2,1,0:T(8,128)S(1)}, f32[6,16,256]{2,1,0:T(8,128)S(1)}, u32[]{:S(2)}, u32[]{:S(2)}) %collective-permute-start.1) | collective-permute-done | bytes 98336 | tf_op jit(solution)/shard_map/ppermute | solution.py:593
  22.2 0.7 %collective-permute-start.4 = (f32[6,16,256]{2,1,0:T(8,128)S(1)}, f32[6,16,256]{2,1,0:T(8,128)S(1)}, u32[]{:S(2)}, u32[]{:S(2)}) collective-permute-start(f32[6,16,256]{2,1,0:T(8,128)S(1)} %shard_map.49), channel_id=1, source_target_pairs={{8,24},{9,25},{10,26},{11,27},{12,28},{13,29},{14,30},{15,31}} | collective-permute-start | bytes 294920 | tf_op jit(solution)/shard_map/ppermute | solution.py:616
  22.9 0.7 %collective-permute-start.2 = (f32[6,16,256]{2,1,0:T(8,128)S(1)}, f32[6,16,256]{2,1,0:T(8,128)S(1)}, u32[]{:S(2)}, u32[]{:S(2)}) collective-permute-start(f32[6,16,256]{2,1,0:T(8,128)S(1)} %shard_map.49), channel_id=1, source_target_pairs={{8,16},{16,24},{9,17},{17,25},{10,18},{18,26},{11,19},{19,27},{12,... | collective-permute-start | bytes 294920 | tf_op jit(solution)/shard_map/ppermute | solution.py:617
  23.6 0.0 collective-permute-done.3._.rest_2_
  23.6 0.1 shard_map.50
  23.6 0.0 collective-permute-done.4.rest_3_.refs_2_
  23.7 0.0 collective-permute-done.2.rest_1_.refs_1_
  23.7 1.3 %collective-permute-start.8 = (f32[6,6,16,256]{3,2,1,0:T(8,128)S(1)}, f32[6,6,16,256]{3,2,1,0:T(8,128)S(1)}, u32[]{:S(2)}, u32[]{:S(2)}) collective-permute-start(f32[6,6,16,256]{3,2,1,0:T(8,128)S(1)} %shard_map.56), channel_id=1, source_target_pairs={{8,0},{9,1},{10,2},{11,3},{12,4},{13,5},{14,6},{15,7}} | collective-permute-start | bytes 1769480 | tf_op jit(solution)/shard_map/ppermute | solution.py:631
  25.0 1.6 %shard_map.51 = (f32[10,6,16,256]{3,2,1,0:T(8,128)S(1)}, f32[10,6,16,256]{3,2,1,0:T(8,128)S(1)}, f32[2,1,16,128]{3,2,1,0:T(8,128)S(1)}, f32[1,10,6,256]{3,2,1,0:T(8,128)S(1)}) custom-call(f32[10,6,16,256]{3,2,1,0:T(8,128)S(1)} %get-tuple-element.41.source_ref, f32[10,6,16,256]{3,2,1,0:T(8,128)S(1)} %get-tuple-element.32.prev_ref.refs_2_, ...), custom_call_target="tpu_custom_call" | custom-call | bytes 6553600 | tf_op jit(solution)/shard_map/pallas_call | solution.py:22
  26.6 0.1 collective-permute-start.5
  26.7 5.2 %all-gather.1 = f32[8,1,16,128]{3,2,1,0:T(8,128)S(1)} all-gather(f32[2,1,16,128]{3,2,1,0:T(8,128)S(1)} %get-tuple-element.50), channel_id=3, replica_groups=mesh['gz'=4,'gx'=4,'gy'=2] {'gx'}, dimensions={0}, use_global_device_ids=true | all-gather | bytes 81920 | tf_op jit(solution)/shard_map/all_gather | solution.py:185
  31.9 0.0 collective-permute-done.5.rest_0_.refs_6_
  31.9 0.7 %collective-permute-start.6 = (f32[6,16,256]{2,1,0:T(8,128)S(1)}, f32[6,16,256]{2,1,0:T(8,128)S(1)}, u32[]{:S(2)}, u32[]{:S(2)}) collective-permute-start(f32[6,16,256]{2,1,0:T(8,128)S(1)} %get-tuple-element.53.refs_8_), channel_id=1, source_target_pairs={{24,16},{25,17},{26,18},{27,19},{28,20},{29,21},{30,22},{31,23}} | collective-permute-start | bytes 294920 | tf_op jit(solution)/shard_map/ppermute | solution.py:669
  32.6 4.9 %shard_map.53 = (f32[10,6,16,256]{3,2,1,0:T(8,128)S(1)}, f32[6,16,256]{2,1,0:T(8,128)S(1)}) custom-call(f32[10,6,16,256]{3,2,1,0:T(8,128)S(1)} %get-tuple-element.47.sweep_ref.refs_0_, f32[10,6,16,256]{3,2,1,0:T(8,128)S(1)} %get-tuple-element.48.change_ref.refs_1_, ...), custom_call_target="tpu_custom_call", output_to_operand_aliasing={{0}: (7, {})} | custom-call | bytes 204800 | tf_op jit(solution)/shard_map/pallas_call | solution.py:22
  37.5 3.4 %shard_map.54 = (f32[10,6,6,16,256]{4,3,2,1,0:T(8,128)S(1)}, f32[10,6,16,256]{3,2,1,0:T(8,128)S(1)}) custom-call(bf16[10,6,6,16,256]{4,3,2,1,0:T(8,128)(2,1)S(1)} %get-tuple-element.33.inv_ref.refs_3_.refs_2_, bf16[10,6,6,16,256]{4,3,2,1,0:T(8,128)(2,1)S(1)} %get-tuple-element.44.high_jac.refs_4_, ...), custom_call_target="tpu_custom_call" | custom-call | bytes 204800 | tf_op jit(solution)/shard_map/pallas_call | solution.py:22
  40.9 0.0 collective-permute-done.6.came_ref.rest_0_
  40.9 1.3 %collective-permute-start.9 = (f32[6,16,256]{2,1,0:T(8,128)S(1)}, f32[6,16,256]{2,1,0:T(8,128)S(1)}, u32[]{:S(2)}, u32[]{:S(2)}) collective-permute-start(f32[6,16,256]{2,1,0:T(8,128)S(1)} %shard_map.55), channel_id=1, source_target_pairs={{16,0},{17,1},{18,2},{19,3},{20,4},{21,5},{22,6},{23,7}} | collective-permute-start | bytes 294920 | tf_op jit(solution)/shard_map/ppermute | solution.py:680
  42.2 1.3 %collective-permute-start.7 = (f32[6,16,256]{2,1,0:T(8,128)S(1)}, f32[6,16,256]{2,1,0:T(8,128)S(1)}, u32[]{:S(2)}, u32[]{:S(2)}) collective-permute-start(f32[6,16,256]{2,1,0:T(8,128)S(1)} %shard_map.55), channel_id=1, source_target_pairs={{16,8},{8,0},{17,9},{9,1},{18,10},{10,2},{19,11},{11,3},{20,12},{1... | collective-permute-start | bytes 294920 | tf_op jit(solution)/shard_map/ppermute | solution.py:681
  43.5 13.3 %collective-permute-done.9.rest_3_ = f32[6,16,256]{2,1,0:T(8,128)S(1)} collective-permute-done((f32[6,16,256]{2,1,0:T(8,128)S(1)}, f32[6,16,256]{2,1,0:T(8,128)S(1)}, u32[]{:S(2)}, u32[]{:S(2)}) %collective-permute-start.9) | collective-permute-done | bytes 98336 | tf_op jit(solution)/shard_map/ppermute | solution.py:680
  56.8 0.0 collective-permute-done.7.rest_1_
  56.8 0.0 collective-permute-done.8.rest_2_
  56.8 1.3 %shard_map.57 = f32[10,6,16,256]{3,2,1,0:T(8,128)} custom-call(f32[10,6,16,256]{3,2,1,0:T(8,128)S(1)} %get-tuple-element.47.sweep_ref.refs_0_, f32[10,6,16,256]{3,2,1,0:T(8,128)S(1)} %get-tuple-element.54.inner_ref, bf16[10,6,6,16,256]{4,3,2,1,0:T(8,128)(2,1)S(1)} %get-tuple-element.33.inv_ref.refs_3_.refs_2_, ...), custom_call_target="tpu_custom_call" | custom-call | bytes 8192000 | tf_op jit(solution)/shard_map/pallas_call | solution.py:22
  (4 shorter events, 0.0 us)
Async XLA Ops:
  3.5 20.1 %collective-permute-start.3 = (f32[6,6,16,256]{3,2,1,0:T(8,128)S(1)}, f32[6,6,16,256]{3,2,1,0:T(8,128)S(1)}, u32[]{:S(2)}, u32[]{:S(2)}) collective-permute-start(f32[6,6,16,256]{3,2,1,0:T(8,128)S(1)} %get-tuple-element.43), channel_id=1, source_target_pairs={{16,24},{17,25},{18,26},{19,27},{20,28},{21,29},{22,30},{23,31}} | collective-permute-start | bytes 1769480 | tf_op jit(solution)/shard_map/ppermute | solution.py:577
  4.2 8.2 %collective-permute-start = (f32[10,6,256]{2,1,0:T(8,128)S(1)}, f32[10,6,256]{2,1,0:T(8,128)S(1)}, u32[]{:S(2)}, u32[]{:S(2)}) collective-permute-start(f32[10,6,256]{2,1,0:T(8,128)S(1)} %bitcast.14), channel_id=1, source_target_pairs={{0,1},{1,0},{2,3},{3,2},{4,5},{5,4},{6,7},{7,6},{8,9},{9,8},{10,11... | collective-permute-start | bytes 184328 | tf_op jit(solution)/shard_map/ppermute | solution.py:178
  18.1 4.1 %collective-permute-start.1 = (f32[6,16,256]{2,1,0:T(8,128)S(1)}, f32[6,16,256]{2,1,0:T(8,128)S(1)}, u32[]{:S(2)}, u32[]{:S(2)}) collective-permute-start(f32[6,16,256]{2,1,0:T(8,128)S(1)} %get-tuple-element.38.refs_8_), channel_id=1, source_target_pairs={{0,8},{1,9},{2,10},{3,11},{4,12},{5,13},{6,14},{7,15}} | collective-permute-start | bytes 294920 | tf_op jit(solution)/shard_map/ppermute | solution.py:593
  22.2 1.4 %collective-permute-start.4 = (f32[6,16,256]{2,1,0:T(8,128)S(1)}, f32[6,16,256]{2,1,0:T(8,128)S(1)}, u32[]{:S(2)}, u32[]{:S(2)}) collective-permute-start(f32[6,16,256]{2,1,0:T(8,128)S(1)} %shard_map.49), channel_id=1, source_target_pairs={{8,24},{9,25},{10,26},{11,27},{12,28},{13,29},{14,30},{15,31}} | collective-permute-start | bytes 294920 | tf_op jit(solution)/shard_map/ppermute | solution.py:616
  22.9 0.8 %collective-permute-start.2 = (f32[6,16,256]{2,1,0:T(8,128)S(1)}, f32[6,16,256]{2,1,0:T(8,128)S(1)}, u32[]{:S(2)}, u32[]{:S(2)}) collective-permute-start(f32[6,16,256]{2,1,0:T(8,128)S(1)} %shard_map.49), channel_id=1, source_target_pairs={{8,16},{16,24},{9,17},{17,25},{10,18},{18,26},{11,19},{19,27},{12,... | collective-permute-start | bytes 294920 | tf_op jit(solution)/shard_map/ppermute | solution.py:617
  23.7 33.2 %collective-permute-start.8 = (f32[6,6,16,256]{3,2,1,0:T(8,128)S(1)}, f32[6,6,16,256]{3,2,1,0:T(8,128)S(1)}, u32[]{:S(2)}, u32[]{:S(2)}) collective-permute-start(f32[6,6,16,256]{3,2,1,0:T(8,128)S(1)} %shard_map.56), channel_id=1, source_target_pairs={{8,0},{9,1},{10,2},{11,3},{12,4},{13,5},{14,6},{15,7}} | collective-permute-start | bytes 1769480 | tf_op jit(solution)/shard_map/ppermute | solution.py:631
  26.6 5.3 %collective-permute-start.5 = (f32[10,6,256]{2,1,0:T(8,128)S(1)}, f32[10,6,256]{2,1,0:T(8,128)S(1)}, u32[]{:S(2)}, u32[]{:S(2)}) collective-permute-start(f32[10,6,256]{2,1,0:T(8,128)S(1)} %bitcast.13), channel_id=1, source_target_pairs={{0,1},{1,0},{2,3},{3,2},{4,5},{5,4},{6,7},{7,6},{8,9},{9,8},{10,11... | collective-permute-start | bytes 184328 | tf_op jit(solution)/shard_map/ppermute | solution.py:178
  31.9 9.0 %collective-permute-start.6 = (f32[6,16,256]{2,1,0:T(8,128)S(1)}, f32[6,16,256]{2,1,0:T(8,128)S(1)}, u32[]{:S(2)}, u32[]{:S(2)}) collective-permute-start(f32[6,16,256]{2,1,0:T(8,128)S(1)} %get-tuple-element.53.refs_8_), channel_id=1, source_target_pairs={{24,16},{25,17},{26,18},{27,19},{28,20},{29,21},{30,22},{31,23}} | collective-permute-start | bytes 294920 | tf_op jit(solution)/shard_map/ppermute | solution.py:669
  40.9 15.9 %collective-permute-start.9 = (f32[6,16,256]{2,1,0:T(8,128)S(1)}, f32[6,16,256]{2,1,0:T(8,128)S(1)}, u32[]{:S(2)}, u32[]{:S(2)}) collective-permute-start(f32[6,16,256]{2,1,0:T(8,128)S(1)} %shard_map.55), channel_id=1, source_target_pairs={{16,0},{17,1},{18,2},{19,3},{20,4},{21,5},{22,6},{23,7}} | collective-permute-start | bytes 294920 | tf_op jit(solution)/shard_map/ppermute | solution.py:680
  42.2 14.6 %collective-permute-start.7 = (f32[6,16,256]{2,1,0:T(8,128)S(1)}, f32[6,16,256]{2,1,0:T(8,128)S(1)}, u32[]{:S(2)}, u32[]{:S(2)}) collective-permute-start(f32[6,16,256]{2,1,0:T(8,128)S(1)} %shard_map.55), channel_id=1, source_target_pairs={{16,8},{8,0},{17,9},{9,1},{18,10},{10,2},{19,11},{11,3},{20,12},{1... | collective-permute-start | bytes 294920 | tf_op jit(solution)/shard_map/ppermute | solution.py:681

commit v11 on v9

--- a/solution.py
+++ b/solution.py
@@ -320,10 +320,18 @@
 
             first_copy = pltpu.make_async_copy(prev_hbm, prev_ref, sem)
             first_copy.start()
-            for z in range(nz):
-                for copy in copies(z):
-                    copy.start()
-            here = lax.axis_index("gz") == 2
+            me = lax.axis_index("gz")
+            here = me == 2
+
+            def start_copies():
+                for z in range(nz):
+                    for copy in copies(z):
+                        copy.start()
+
+            if matrices:
+                pl.when(me != 0)(start_copies)
+            else:
+                start_copies()
             if matrices:
 
                 @pl.when(here)
@@ -342,7 +350,7 @@
                 @pl.when(jnp.logical_not(here))
                 def _():
                     matrices[0][...] = jnp.zeros(matrix[0], F32)
-                    rest_of_copies()
+                    pl.when(me != 0)(rest_of_copies)
 
             else:
                 rest_of_copies()
@@ -365,14 +373,14 @@
             )
             high_copy.wait()
 
-        def first_ahead_kernel(rhs_hbm, jac_hbm, prev_ref, inv_ref, low_jac, x_all, *rest):
-            *y_rows, source_ref, top_ref, sides, rhs_ref, sems = rest
+        def first_ahead_kernel(rhs_hbm, jac_hbm, prev_ref, _, __, x_all, *rest):
+            *y_rows, inv_hbm, source_ref, top_ref, sides, inv_ref, low_jac, rhs_ref, sems = rest
 
             @pl.when(lax.axis_index("gz") == 0)
             def _():
                 first_work(
                     rhs_hbm, jac_hbm, prev_ref, inv_ref, low_jac, x_all, y_rows,
-                    source_ref, top_ref, sides, rhs_ref, sems, None,
+                    source_ref, top_ref, sides, rhs_ref, sems, None, inv_hbm,
                 )
 
         def first_behind_kernel(*refs):
@@ -397,14 +405,17 @@
 
         def first_work(
             rhs_hbm, jac_hbm, prev_ref, inv_ref, low_jac, x_all, y_rows,
-            source_ref, top_ref, sides, rhs_ref, sems, also,
+            source_ref, top_ref, sides, rhs_ref, sems, also, inv_hbm=None,
         ):
             halo = halo_reader(x_all, y_rows, gx, gy)
 
             def copies(z):
+                pairs = [(jac_hbm.at[z, 0:4], sides), (rhs_hbm.at[z], rhs_ref)]
+                if inv_hbm is not None:
+                    pairs += [(inv_hbm.at[z], inv_ref), (jac_hbm.at[z, 4], low_jac)]
                 return [
-                    pltpu.make_async_copy(jac_hbm.at[z, 0:4], sides.at[z], sems.at[0, z]),
-                    pltpu.make_async_copy(rhs_hbm.at[z], rhs_ref.at[z], sems.at[1, z]),
+                    pltpu.make_async_copy(far, near.at[z], sems.at[i, z])
+                    for i, (far, near) in enumerate(pairs)
                 ]
 
             for z in range(nz):
@@ -438,18 +449,17 @@
                 put(top_ref, top[tile], at)
 
         def forward_mid_kernel(low_ref, came_ref, source_ref, inv_ref, low_jac, top_ref):
-            here = lax.axis_index("gz") == 1
-            pl.when(here)(lambda: forward_kernel(source_ref, inv_ref, low_jac, came_ref, top_ref))
-
-            @pl.when(jnp.logical_not(here))
-            def _():
-                top_ref[...] = low_ref[...]
-
-        def either(device, work, fast):
+            top_ref[...] = low_ref[...]
+
+            @pl.when(lax.axis_index("gz") == 1)
+            def _():
+                forward_kernel(source_ref, inv_ref, low_jac, came_ref, top_ref)
+
+        def either(wanted, work, fast):
             if fast is None:
                 work(None)
                 return
-            here = lax.axis_index("gz") == device
+            here = wanted(lax.axis_index("gz"))
             pl.when(here)(lambda: work(fast))
             pl.when(jnp.logical_not(here))(lambda: work(None))
 
@@ -457,7 +467,7 @@
             came, (sweep_ref, change_ref, x_side, y_side) = rest[:-4], rest[-4:]
             fast = None
             if short:
-                first, far, third, matrix_ref, near, *fast = came
+                first, far, matrix_ref, near, *fast = came
 
             def keep(z, at, result):
                 before = planes_of(prev_ref, z, at)
@@ -467,14 +477,12 @@
 
             def work(fast):
                 if short:
-                    starts = tuple(
-                        arrived((first, near, third), matrix_ref, far, at) for at in spans
-                    )
+                    starts = tuple(arrived((first, near), matrix_ref, far, at) for at in spans)
                 else:
                     starts = tuple(incoming(came, at) for at in spans)
                 forward_sweep(source_ref, inv_ref, low_jac, starts, keep, fast)
 
-            either(3, work, fast)
+            either(lambda me: me == 3, work, fast)
             write_faces(change_ref, x_side, y_side, nz)
 
         def turn_kernel(wanted, sweep_ref, change_ref, inv_ref, sides, high_jac, x_all, *rest):
@@ -519,7 +527,7 @@
             transfer(matrix_ref, inv_ref, high_jac, lambda i: nz - 1 - i)
 
         def forward_idle_kernel(inv_ref, high_jac, low_jac, source_ref, _, matrix_ref, step_ref, plain_ref):
-            only(2, lambda: down_matrix(inv_ref, high_jac, matrix_ref), matrix_ref, matrix[0])
+            only(1, lambda: down_matrix(inv_ref, high_jac, matrix_ref), matrix_ref, matrix[0])
 
             @pl.when(lax.axis_index("gz") == 3)
             def _():
@@ -528,10 +536,10 @@
 
                 make_fast(step_ref, plain_ref, inv_ref, low_jac, plain_of)
 
-        def backward_idle_kernel(inv_ref, high_jac, sweep_ref, inner_ref, _, matrix_ref, step_ref, plain_ref):
-            only(1, lambda: down_matrix(inv_ref, high_jac, matrix_ref), matrix_ref, matrix[0])
-
-            @pl.when(lax.axis_index("gz") == 0)
+        def backward_idle_kernel(inv_ref, high_jac, sweep_ref, inner_ref, step_ref, plain_ref):
+            me = lax.axis_index("gz")
+
+            @pl.when(me != 3)
             def _():
                 def plain_of(z, at, times):
                     moved = times(planes_of(inner_ref, z, at))
@@ -549,22 +557,25 @@
         def pass_kernel(*refs):
             pass
 
-        def far_kernel(far_ref, matrix_ref, _, moved_ref):
-            for at in spans:
-                put(moved_ref, apply_matrix(matrix_ref, planes_in(far_ref, at), at), at)
-
-        def backward_mid_kernel(own_ref, near_ref, moved_ref, matrix_ref, came_ref, low_ref):
-            for at in spans:
-                came = incoming((near_ref, moved_ref), at)
-                moved = apply_matrix(matrix_ref, came, at)
-                put(came_ref, came, at)
-                put(low_ref, [a + b for a, b in zip(planes_in(own_ref, at), moved)], at)
+        def backward_mid_kernel(own_ref, came_ref, step_ref, plain_ref, low_ref):
+            here = lax.axis_index("gz") == 2
+
+            @pl.when(here)
+            def _():
+                starts = tuple(incoming((came_ref,), at) for at in spans)
+                low = backward_sweep(None, None, None, None, starts, fast=(step_ref, plain_ref))
+                for tile, at in enumerate(spans):
+                    put(low_ref, low[tile], at)
+
+            @pl.when(jnp.logical_not(here))
+            def _():
+                low_ref[...] = own_ref[...]
 
         def update_kernel(sweep_ref, inner_ref, inv_ref, high_jac, *rest):
             came, (out_hbm, held, sems) = rest[:-3], rest[-3:]
             fast = None
             if short:
-                came, fast = came[:2], came[2:]
+                first, far, matrix_ref, near, *fast = came
 
             def out_copy(z):
                 return pltpu.make_async_copy(held.at[z], out_hbm.at[z], sems.at[z])
@@ -576,14 +587,18 @@
                     out_copy(z).start()
 
             def work(fast):
-                starts = tuple(incoming(came, at) for at in spans)
+                if short:
+                    starts = tuple(arrived((first, near), matrix_ref, far, at) for at in spans)
+                else:
+                    starts = tuple(incoming(came, at) for at in spans)
                 backward_sweep(sweep_ref, inner_ref, inv_ref, high_jac, starts, keep, fast)
 
-            either(0, work, fast)
+            either(lambda me: me != 3, work, fast)
             for z in range(nz):
                 out_copy(z).wait()
 
 
+        inv_far = inv
         prev, inv, low_jac, x_side, y_side, *up_matrix = call(
             open_kernel,
             [volume, blocks, blocks, x_face, y_face] + [matrix] * (1 if short else 0),
@@ -598,18 +613,21 @@
             up_there = lax.ppermute(up_matrix[0], "gz", [(2, 3)])
         halo = exchange(x_side, y_side)
         first_args = [rhs, jac, prev, inv, low_jac, *halo]
-        first_scratch = [pltpu.VMEM(rhs.shape, F32), pltpu.SemaphoreType.DMA((2, nz))]
+        first_scratch = [pltpu.VMEM(rhs.shape, F32), pltpu.SemaphoreType.DMA((4, nz))]
         if short:
-            source, top, sides = call(
+            n = len(first_args)
+            source, top, sides, inv, low_jac = call(
                 first_ahead_kernel,
-                [volume, plane, side_blocks],
+                [volume, plane, side_blocks, blocks, blocks],
                 *first_args,
+                inv_far,
                 cost=unit // 8,
-                in_hbm=(0, 1),
+                in_hbm=(0, 1, n),
+                aliases={3: 3, 4: 4},
                 scratch=first_scratch,
             )
+            first_args[3:5] = inv, low_jac
             first = lax.ppermute(top, "gz", [(0, 1)])
-            n = len(first_args)
             source, top, sides, high_jac = call(
                 first_behind_kernel,
                 [volume, plane, side_blocks, blocks],
@@ -622,12 +640,18 @@
                 aliases={n: 0, n + 2: 2},
                 scratch=first_scratch + [pltpu.SemaphoreType.DMA],
             )
-            third = lax.ppermute(top, "gz", [(2, 3)])
             (top,) = call(
-                forward_mid_kernel, [plane], top, first, source, inv, low_jac, cost=unit // 8
-            )
-            near = lax.ppermute(top, "gz", [(1, 2)])
+                forward_mid_kernel,
+                [plane],
+                top,
+                first,
+                source,
+                inv,
+                low_jac,
+                cost=unit // 8,
+            )
             far = lax.ppermute(top, "gz", [(1, 3)])
+            near = lax.ppermute(top, "gz", [(1, 2), (2, 3)])
             down_one, *fast = call(
                 forward_idle_kernel,
                 [matrix, steps, volume],
@@ -639,10 +663,10 @@
                 cost=unit // 8,
             )
             (down_one,) = call(
-                pass_kernel, [matrix], down_one, far, near, third, cost=unit // 8, aliases={0: 0}
-            )
-            down_there = lax.ppermute(down_one, "gz", [(2, 1)])
-            came = [first, far, third, up_there, near, *fast]
+                pass_kernel, [matrix], down_one, near, far, cost=unit // 8, aliases={0: 0}
+            )
+            down_there = lax.ppermute(down_one, "gz", [(1, 0)])
+            came = [first, far, up_there, near, *fast]
         else:
             source, top, sides, high_jac = call(
                 first_kernel,
@@ -687,23 +711,20 @@
                 aliases={len(turn_args): 0},
                 cost=unit // 8,
             )
-            near = lax.ppermute(low, "gz", [(3, 2), (2, 1)])
-            far = lax.ppermute(ahead_low, "gz", [(3, 1)])
-            own_matrix, *fast = call(
+            first = lax.ppermute(ahead_low, "gz", [(3, 2)])
+            fast = call(
                 backward_idle_kernel,
-                [matrix, steps, volume],
+                [steps, volume],
                 inv,
                 high_jac,
                 sweep,
                 inner,
-                low,
                 cost=unit // 8,
             )
-            (moved,) = call(far_kernel, [plane], far, down_there, own_matrix, cost=unit // 8)
-            entered, low = call(
-                backward_mid_kernel, [plane, plane], low, near, moved, own_matrix, cost=unit // 8
-            )
-            came = [entered, lax.ppermute(low, "gz", [(1, 0)]), *fast]
+            (low,) = call(backward_mid_kernel, [plane], low, first, *fast, cost=unit // 8)
+            far = lax.ppermute(low, "gz", [(2, 0)])
+            near = lax.ppermute(low, "gz", [(2, 1), (1, 0)])
+            came = [first, far, down_there, near, *fast]
         else:
             came = []
             for hop in range(gz - 1, 0, -1):

time: 60.3 us -> 60 us (level)
  waiting for transfers between devices: 16.5 us -> 15.8 us
    ppermute x6 -> x5, waiting for transfers between devices: 16.4 us -> 15.2 us  [the longest x1 13.1 us: body(): far = lax.ppermute(low, 'gz', [(2, 0)])]
    ppermute x6 -> x5, starting transfers between devices: 4.65 us -> 5.2 us  [the longest x1 1.29 us: body(): far = lax.ppermute(low, 'gz', [(2, 0)])]
    pallas_call x13 -> x12, Pallas kernels: 22.5 us -> 22.3 us  [call(): pl.pallas_call(body, out_shape=shapes, in_specs=[far if i in in_hbm else...]
  transfers between devices with their start and end apart: 11 -> 10, of which waited for: 2 -> 3; matrix products, arithmetic and copies ran while one was open for 0% -> 0% of each run, Pallas kernels for 29% -> 32%
where the time goes in v11:
time: 60 us; the launch traced here: 59.6 us
  Pallas kernels  22.3 us (37%)
  waiting for transfers between devices  15.8 us (26%)
  starting transfers between devices  10.9 us (18%)
  blocking collectives  10.5 us (18%)
    pallas_call x12, Pallas kernels, call(): pl.pallas_call(body, out_shape=shapes, in_specs=[far if i in in_hbm else...  22.3 us
    ppermute x1, waiting for transfers between devices, body(): far = lax.ppermute(low, 'gz', [(2, 0)])  13.1 us
    all_gather x2, blocking collectives, exchange(): return (lax.all_gather(x_side, 'gx'), *rows)  10.5 us
    ppermute x2, starting transfers between devices, exchange(): rows = [lax.ppermute(y_side[0], 'gy', [(0, 1), (1, 0)])]  3.1 us
    ppermute x1, waiting for transfers between devices, body(): near = lax.ppermute(low, 'gz', [(2, 1), (1, 0)])  2.04 us
    ppermute x1, starting transfers between devices, body(): first = lax.ppermute(top, 'gz', [(0, 1)])  1.3 us
    ppermute x1, starting transfers between devices, body(): far = lax.ppermute(low, 'gz', [(2, 0)])  1.29 us
    ppermute x1, starting transfers between devices, body(): near = lax.ppermute(low, 'gz', [(2, 1), (1, 0)])  1.29 us
  transfers between devices with their start and end apart: 10, of which 3 were waited for; matrix products, arithmetic and copies ran while one was open for 0% of the time, Pallas kernels for 32%

profile of v11, /device:TPU:0, one launch (start us, length us, event | category | flops | bytes accessed | tf_op | source)
XLA Modules:
  0.0 59.6 jit_solution(2671980310697085244)
XLA Ops:
  0.0 1.7 %shard_map.46 = (f32[10,6,16,256]{3,2,1,0:T(8,128)S(1)}, bf16[10,6,6,16,256]{4,3,2,1,0:T(8,128)(2,1)S(1)}, bf16[10,6,6,16,256]{4,3,2,1,0:T(8,128)(2,1)S(1)}, f32...) custom-call(f32[10,6,16,256]{3,2,1,0:T(8,128)} %bitcast.22, ...), custom_call_target="tpu_custom_call" | custom-call | bytes 19660800 | tf_op jit(solution)/shard_map/pallas_call | solution.py:22
  1.7 0.7 %collective-permute-start.3 = (f32[6,6,16,256]{3,2,1,0:T(8,128)S(1)}, f32[6,6,16,256]{3,2,1,0:T(8,128)S(1)}, u32[]{:S(2)}, u32[]{:S(2)}) collective-permute-start(f32[6,6,16,256]{3,2,1,0:T(8,128)S(1)} %get-tuple-element.45), channel_id=1, source_target_pairs={{16,24},{17,25},{18,26},{19,27},{20,28},{21,29},{22,30},{23,31}} | collective-permute-start | bytes 1769480 | tf_op jit(solution)/shard_map/ppermute | solution.py:613
  2.5 3.0 %collective-permute-start = (f32[10,6,256]{2,1,0:T(8,128)S(1)}, f32[10,6,256]{2,1,0:T(8,128)S(1)}, u32[]{:S(2)}, u32[]{:S(2)}) collective-permute-start(f32[10,6,256]{2,1,0:T(8,128)S(1)} %bitcast.14), channel_id=1, source_target_pairs={{0,1},{1,0},{2,3},{3,2},{4,5},{5,4},{6,7},{7,6},{8,9},{9,8},{10,11... | collective-permute-start | bytes 184328 | tf_op jit(solution)/shard_map/ppermute | solution.py:178
  5.5 5.2 %all-gather = f32[8,1,16,128]{3,2,1,0:T(8,128)S(1)} all-gather(f32[2,1,16,128]{3,2,1,0:T(8,128)S(1)} %get-tuple-element.36), channel_id=2, replica_groups=mesh['gz'=4,'gx'=4,'gy'=2] {'gx'}, dimensions={0}, use_global_device_ids=true | all-gather | bytes 81920 | tf_op jit(solution)/shard_map/all_gather | solution.py:185
  10.7 0.0 collective-permute-done.rest_0_.refs_6_
  10.7 7.0 %shard_map.47 = (f32[10,6,16,256]{3,2,1,0:T(8,128)S(1)}, f32[6,16,256]{2,1,0:T(8,128)S(1)}, bf16[10,4,6,6,16,256]{5,4,3,2,1,0:T(8,128)(2,1)S(1)}, bf16[10,6,6,16...) custom-call(f32[10,6,16,256]{3,2,1,0:T(8,128)} %bitcast.20, ...), custom_call_target="tpu_custom_call", output_to_operand_aliasing={{3}: (3, {}), {4}: (4, {})} | custom-call | bytes 204800 | tf_op jit(solution)/shard_map/pallas_call | solution.py:22
  17.7 1.3 %collective-permute-start.1 = (f32[6,16,256]{2,1,0:T(8,128)S(1)}, f32[6,16,256]{2,1,0:T(8,128)S(1)}, u32[]{:S(2)}, u32[]{:S(2)}) collective-permute-start(f32[6,16,256]{2,1,0:T(8,128)S(1)} %get-tuple-element.41.refs_8_), channel_id=1, source_target_pairs={{0,8},{1,9},{2,10},{3,11},{4,12},{5,13},{6,14},{7,15}} | collective-permute-start | bytes 294920 | tf_op jit(solution)/shard_map/ppermute | solution.py:630
  19.0 2.2 %shard_map.48 = (f32[10,6,16,256]{3,2,1,0:T(8,128)S(1)}, f32[6,16,256]{2,1,0:T(8,128)S(1)}, bf16[10,4,6,6,16,256]{5,4,3,2,1,0:T(8,128)(2,1)S(1)}, bf16[10,6,6,16,256]{4,3,2,1,0:T(8,128)(2,1)S(1)}) custom-call(f32[10,6,16,256]{3,2,1,0:T(8,128)} %bitcast.21, bf16[10,6,6,6,16,256]{5,4,3,2,1,0:T(8,128)(2,1)} %bitcast.17, ...), custom_call_target="tpu_custom_call", output_to_operand_aliasing={{0}: (7, {}), {2}: (9, {})} | custom-call | bytes 204800 | tf_op jit(solution)/shard_map/pallas_call | solution.py:22
  21.3 0.6 collective-permute-done.1.came_ref.rest_0_
  21.9 0.7 %collective-permute-start.2 = (f32[6,16,256]{2,1,0:T(8,128)S(1)}, f32[6,16,256]{2,1,0:T(8,128)S(1)}, u32[]{:S(2)}, u32[]{:S(2)}) collective-permute-start(f32[6,16,256]{2,1,0:T(8,128)S(1)} %shard_map.49), channel_id=1, source_target_pairs={{8,24},{9,25},{10,26},{11,27},{12,28},{13,29},{14,30},{15,31}} | collective-permute-start | bytes 294920 | tf_op jit(solution)/shard_map/ppermute | solution.py:653
  22.5 0.7 %collective-permute-start.4 = (f32[6,16,256]{2,1,0:T(8,128)S(1)}, f32[6,16,256]{2,1,0:T(8,128)S(1)}, u32[]{:S(2)}, u32[]{:S(2)}) collective-permute-start(f32[6,16,256]{2,1,0:T(8,128)S(1)} %shard_map.49), channel_id=1, source_target_pairs={{8,16},{16,24},{9,17},{17,25},{10,18},{18,26},{11,19},{19,27},{12,... | collective-permute-start | bytes 294920 | tf_op jit(solution)/shard_map/ppermute | solution.py:654
  23.2 0.0 collective-permute-done.3._.rest_2_
  23.2 0.1 shard_map.50
  23.3 0.0 collective-permute-done.2.rest_1_.refs_2_
  23.3 0.0 collective-permute-done.4.rest_3_.refs_1_
  23.3 1.3 %collective-permute-start.8 = (f32[6,6,16,256]{3,2,1,0:T(8,128)S(1)}, f32[6,6,16,256]{3,2,1,0:T(8,128)S(1)}, u32[]{:S(2)}, u32[]{:S(2)}) collective-permute-start(f32[6,6,16,256]{3,2,1,0:T(8,128)S(1)} %shard_map.56), channel_id=1, source_target_pairs={{8,0},{9,1},{10,2},{11,3},{12,4},{13,5},{14,6},{15,7}} | collective-permute-start | bytes 1769480 | tf_op jit(solution)/shard_map/ppermute | solution.py:668
  24.6 1.6 %shard_map.51 = (f32[10,6,16,256]{3,2,1,0:T(8,128)S(1)}, f32[10,6,16,256]{3,2,1,0:T(8,128)S(1)}, f32[2,1,16,128]{3,2,1,0:T(8,128)S(1)}, f32[1,10,6,256]{3,2,1,0:T(8,128)S(1)}) custom-call(f32[10,6,16,256]{3,2,1,0:T(8,128)S(1)} %get-tuple-element.43.source_ref, f32[10,6,16,256]{3,2,1,0:T(8,128)S(1)} %get-tuple-element.33.prev_ref.refs_2_, ...), custom_call_target="tpu_custom_call" | custom-call | bytes 6553600 | tf_op jit(solution)/shard_map/pallas_call | solution.py:22
  26.2 0.1 collective-permute-start.5
  26.3 5.2 %all-gather.1 = f32[8,1,16,128]{3,2,1,0:T(8,128)S(1)} all-gather(f32[2,1,16,128]{3,2,1,0:T(8,128)S(1)} %get-tuple-element.52), channel_id=3, replica_groups=mesh['gz'=4,'gx'=4,'gy'=2] {'gx'}, dimensions={0}, use_global_device_ids=true | all-gather | bytes 81920 | tf_op jit(solution)/shard_map/all_gather | solution.py:185
  31.5 0.0 collective-permute-done.5.rest_0_.refs_6_
  31.5 0.7 %collective-permute-start.6 = (f32[6,16,256]{2,1,0:T(8,128)S(1)}, f32[6,16,256]{2,1,0:T(8,128)S(1)}, u32[]{:S(2)}, u32[]{:S(2)}) collective-permute-start(f32[6,16,256]{2,1,0:T(8,128)S(1)} %get-tuple-element.55.refs_8_), channel_id=1, source_target_pairs={{24,16},{25,17},{26,18},{27,19},{28,20},{29,21},{30,22},{31,23}} | collective-permute-start | bytes 294920 | tf_op jit(solution)/shard_map/ppermute | solution.py:714
  32.2 4.9 %shard_map.53 = (f32[10,6,16,256]{3,2,1,0:T(8,128)S(1)}, f32[6,16,256]{2,1,0:T(8,128)S(1)}) custom-call(f32[10,6,16,256]{3,2,1,0:T(8,128)S(1)} %get-tuple-element.49.sweep_ref.refs_0_, f32[10,6,16,256]{3,2,1,0:T(8,128)S(1)} %get-tuple-element.50.change_ref.refs_1_, ...), custom_call_target="tpu_custom_call", output_to_operand_aliasing={{0}: (7, {})} | custom-call | bytes 204800 | tf_op jit(solution)/shard_map/pallas_call | solution.py:22
  37.1 3.4 %shard_map.54 = (f32[10,6,6,16,256]{4,3,2,1,0:T(8,128)S(1)}, f32[10,6,16,256]{3,2,1,0:T(8,128)S(1)}) custom-call(bf16[10,6,6,16,256]{4,3,2,1,0:T(8,128)(2,1)S(1)} %get-tuple-element.38.refs_3_.inv_ref.refs_2_, bf16[10,6,6,16,256]{4,3,2,1,0:T(8,128)(2,1)S(1)} %get-tuple-element.46.high_jac.refs_4_, ...), custom_call_target="tpu_custom_call" | custom-call | bytes 204800 | tf_op jit(solution)/shard_map/pallas_call | solution.py:22
  40.5 0.0 collective-permute-done.6.came_ref.rest_0_
  40.6 1.3 %collective-permute-start.7 = (f32[6,16,256]{2,1,0:T(8,128)S(1)}, f32[6,16,256]{2,1,0:T(8,128)S(1)}, u32[]{:S(2)}, u32[]{:S(2)}) collective-permute-start(f32[6,16,256]{2,1,0:T(8,128)S(1)} %shard_map.55), channel_id=1, source_target_pairs={{16,0},{17,1},{18,2},{19,3},{20,4},{21,5},{22,6},{23,7}} | collective-permute-start | bytes 294920 | tf_op jit(solution)/shard_map/ppermute | solution.py:725
  41.9 1.3 %collective-permute-start.9 = (f32[6,16,256]{2,1,0:T(8,128)S(1)}, f32[6,16,256]{2,1,0:T(8,128)S(1)}, u32[]{:S(2)}, u32[]{:S(2)}) collective-permute-start(f32[6,16,256]{2,1,0:T(8,128)S(1)} %shard_map.55), channel_id=1, source_target_pairs={{16,8},{8,0},{17,9},{9,1},{18,10},{10,2},{19,11},{11,3},{20,12},{1... | collective-permute-start | bytes 294920 | tf_op jit(solution)/shard_map/ppermute | solution.py:726
  43.2 13.1 %collective-permute-done.7.rest_1_ = f32[6,16,256]{2,1,0:T(8,128)S(1)} collective-permute-done((f32[6,16,256]{2,1,0:T(8,128)S(1)}, f32[6,16,256]{2,1,0:T(8,128)S(1)}, u32[]{:S(2)}, u32[]{:S(2)}) %collective-permute-start.7) | collective-permute-done | bytes 98336 | tf_op jit(solution)/shard_map/ppermute | solution.py:725
  56.3 2.0 %collective-permute-done.9.rest_3_ = f32[6,16,256]{2,1,0:T(8,128)S(1)} collective-permute-done((f32[6,16,256]{2,1,0:T(8,128)S(1)}, f32[6,16,256]{2,1,0:T(8,128)S(1)}, u32[]{:S(2)}, u32[]{:S(2)}) %collective-permute-start.9) | collective-permute-done | bytes 98336 | tf_op jit(solution)/shard_map/ppermute | solution.py:726
  58.3 0.0 collective-permute-done.8.rest_2_
  58.3 1.3 %shard_map.57 = f32[10,6,16,256]{3,2,1,0:T(8,128)} custom-call(f32[10,6,16,256]{3,2,1,0:T(8,128)S(1)} %get-tuple-element.49.sweep_ref.refs_0_, f32[10,6,16,256]{3,2,1,0:T(8,128)S(1)} %get-tuple-element.56.inner_ref, bf16[10,6,6,16,256]{4,3,2,1,0:T(8,128)(2,1)S(1)} %get-tuple-element.38.refs_3_.inv_ref.refs_2_, ...), custom_call_target="tpu_custom_call" | custom-call | bytes 8192000 | tf_op jit(solution)/shard_map/pallas_call | solution.py:22
  (4 shorter events, 0.0 us)
Async XLA Ops:
  1.7 21.5 %collective-permute-start.3 = (f32[6,6,16,256]{3,2,1,0:T(8,128)S(1)}, f32[6,6,16,256]{3,2,1,0:T(8,128)S(1)}, u32[]{:S(2)}, u32[]{:S(2)}) collective-permute-start(f32[6,6,16,256]{3,2,1,0:T(8,128)S(1)} %get-tuple-element.45), channel_id=1, source_target_pairs={{16,24},{17,25},{18,26},{19,27},{20,28},{21,29},{22,30},{23,31}} | collective-permute-start | bytes 1769480 | tf_op jit(solution)/shard_map/ppermute | solution.py:613
  2.5 8.2 %collective-permute-start = (f32[10,6,256]{2,1,0:T(8,128)S(1)}, f32[10,6,256]{2,1,0:T(8,128)S(1)}, u32[]{:S(2)}, u32[]{:S(2)}) collective-permute-start(f32[10,6,256]{2,1,0:T(8,128)S(1)} %bitcast.14), channel_id=1, source_target_pairs={{0,1},{1,0},{2,3},{3,2},{4,5},{5,4},{6,7},{7,6},{8,9},{9,8},{10,11... | collective-permute-start | bytes 184328 | tf_op jit(solution)/shard_map/ppermute | solution.py:178
  17.7 4.1 %collective-permute-start.1 = (f32[6,16,256]{2,1,0:T(8,128)S(1)}, f32[6,16,256]{2,1,0:T(8,128)S(1)}, u32[]{:S(2)}, u32[]{:S(2)}) collective-permute-start(f32[6,16,256]{2,1,0:T(8,128)S(1)} %get-tuple-element.41.refs_8_), channel_id=1, source_target_pairs={{0,8},{1,9},{2,10},{3,11},{4,12},{5,13},{6,14},{7,15}} | collective-permute-start | bytes 294920 | tf_op jit(solution)/shard_map/ppermute | solution.py:630
  21.9 1.4 %collective-permute-start.2 = (f32[6,16,256]{2,1,0:T(8,128)S(1)}, f32[6,16,256]{2,1,0:T(8,128)S(1)}, u32[]{:S(2)}, u32[]{:S(2)}) collective-permute-start(f32[6,16,256]{2,1,0:T(8,128)S(1)} %shard_map.49), channel_id=1, source_target_pairs={{8,24},{9,25},{10,26},{11,27},{12,28},{13,29},{14,30},{15,31}} | collective-permute-start | bytes 294920 | tf_op jit(solution)/shard_map/ppermute | solution.py:653
  22.5 0.8 %collective-permute-start.4 = (f32[6,16,256]{2,1,0:T(8,128)S(1)}, f32[6,16,256]{2,1,0:T(8,128)S(1)}, u32[]{:S(2)}, u32[]{:S(2)}) collective-permute-start(f32[6,16,256]{2,1,0:T(8,128)S(1)} %shard_map.49), channel_id=1, source_target_pairs={{8,16},{16,24},{9,17},{17,25},{10,18},{18,26},{11,19},{19,27},{12,... | collective-permute-start | bytes 294920 | tf_op jit(solution)/shard_map/ppermute | solution.py:654
  23.3 35.0 %collective-permute-start.8 = (f32[6,6,16,256]{3,2,1,0:T(8,128)S(1)}, f32[6,6,16,256]{3,2,1,0:T(8,128)S(1)}, u32[]{:S(2)}, u32[]{:S(2)}) collective-permute-start(f32[6,6,16,256]{3,2,1,0:T(8,128)S(1)} %shard_map.56), channel_id=1, source_target_pairs={{8,0},{9,1},{10,2},{11,3},{12,4},{13,5},{14,6},{15,7}} | collective-permute-start | bytes 1769480 | tf_op jit(solution)/shard_map/ppermute | solution.py:668
  26.2 5.3 %collective-permute-start.5 = (f32[10,6,256]{2,1,0:T(8,128)S(1)}, f32[10,6,256]{2,1,0:T(8,128)S(1)}, u32[]{:S(2)}, u32[]{:S(2)}) collective-permute-start(f32[10,6,256]{2,1,0:T(8,128)S(1)} %bitcast.13), channel_id=1, source_target_pairs={{0,1},{1,0},{2,3},{3,2},{4,5},{5,4},{6,7},{7,6},{8,9},{9,8},{10,11... | collective-permute-start | bytes 184328 | tf_op jit(solution)/shard_map/ppermute | solution.py:178
  31.5 9.0 %collective-permute-start.6 = (f32[6,16,256]{2,1,0:T(8,128)S(1)}, f32[6,16,256]{2,1,0:T(8,128)S(1)}, u32[]{:S(2)}, u32[]{:S(2)}) collective-permute-start(f32[6,16,256]{2,1,0:T(8,128)S(1)} %get-tuple-element.55.refs_8_), channel_id=1, source_target_pairs={{24,16},{25,17},{26,18},{27,19},{28,20},{29,21},{30,22},{31,23}} | collective-permute-start | bytes 294920 | tf_op jit(solution)/shard_map/ppermute | solution.py:714
  40.6 15.7 %collective-permute-start.7 = (f32[6,16,256]{2,1,0:T(8,128)S(1)}, f32[6,16,256]{2,1,0:T(8,128)S(1)}, u32[]{:S(2)}, u32[]{:S(2)}) collective-permute-start(f32[6,16,256]{2,1,0:T(8,128)S(1)} %shard_map.55), channel_id=1, source_target_pairs={{16,0},{17,1},{18,2},{19,3},{20,4},{21,5},{22,6},{23,7}} | collective-permute-start | bytes 294920 | tf_op jit(solution)/shard_map/ppermute | solution.py:725
  41.9 16.5 %collective-permute-start.9 = (f32[6,16,256]{2,1,0:T(8,128)S(1)}, f32[6,16,256]{2,1,0:T(8,128)S(1)}, u32[]{:S(2)}, u32[]{:S(2)}) collective-permute-start(f32[6,16,256]{2,1,0:T(8,128)S(1)} %shard_map.55), channel_id=1, source_target_pairs={{16,8},{8,0},{17,9},{9,1},{18,10},{10,2},{19,11},{11,3},{20,12},{1... | collective-permute-start | bytes 294920 | tf_op jit(solution)/shard_map/ppermute | solution.py:726

commit v12 on v11

--- a/solution.py
+++ b/solution.py
@@ -536,16 +536,20 @@
 
                 make_fast(step_ref, plain_ref, inv_ref, low_jac, plain_of)
 
-        def backward_idle_kernel(inv_ref, high_jac, sweep_ref, inner_ref, step_ref, plain_ref):
+        def backward_fast(inv_ref, high_jac, sweep_ref, inner_ref, step_ref, plain_ref):
+            def plain_of(z, at, times):
+                moved = times(planes_of(inner_ref, z, at))
+                return [a - b for a, b in zip(planes_of(sweep_ref, z, at), moved)]
+
+            make_fast(step_ref, plain_ref, inv_ref, high_jac, plain_of)
+
+        def backward_idle_kernel(*refs):
             me = lax.axis_index("gz")
-
-            @pl.when(me != 3)
-            def _():
-                def plain_of(z, at, times):
-                    moved = times(planes_of(inner_ref, z, at))
-                    return [a - b for a, b in zip(planes_of(sweep_ref, z, at), moved)]
-
-                make_fast(step_ref, plain_ref, inv_ref, high_jac, plain_of)
+            pl.when((me == 0) | (me == 2))(lambda: backward_fast(*refs))
+
+        def late_idle_kernel(inv_ref, high_jac, sweep_ref, inner_ref, _, __, ___, *outs):
+            me = lax.axis_index("gz")
+            pl.when(me == 1)(lambda: backward_fast(inv_ref, high_jac, sweep_ref, inner_ref, *outs))
 
         def backward_kernel(sweep_ref, inner_ref, inv_ref, high_jac, *rest):
             came, low_ref = rest[:-1], rest[-1]
@@ -724,6 +728,18 @@
             (low,) = call(backward_mid_kernel, [plane], low, first, *fast, cost=unit // 8)
             far = lax.ppermute(low, "gz", [(2, 0)])
             near = lax.ppermute(low, "gz", [(2, 1), (1, 0)])
+            fast = call(
+                late_idle_kernel,
+                [steps, volume],
+                inv,
+                high_jac,
+                sweep,
+                inner,
+                *fast,
+                low,
+                cost=unit // 8,
+                aliases={4: 0, 5: 1},
+            )
             came = [first, far, down_there, near, *fast]
         else:
             came = []

time: 60 us -> 58.2 us (0.970)
  waiting for transfers between devices: 15.8 us -> 14 us
    ppermute x1, waiting for transfers between devices: 2.04 us -> 0.01 us  [body(): near = lax.ppermute(low, 'gz', [(2, 1), (1, 0)])]
    pallas_call x12 -> x13, Pallas kernels: 22.3 us -> 22.3 us  [call(): pl.pallas_call(body, out_shape=shapes, in_specs=[far if i in in_hbm else...]
  transfers between devices with their start and end apart: 10 -> 10, of which waited for: 3 -> 2; matrix products, arithmetic and copies ran while one was open for 0% -> 0% of each run, Pallas kernels for 32% -> 33%
where the time goes in v12:
time: 58.2 us; the launch traced here: 57.8 us
  Pallas kernels  22.3 us (38%)
  waiting for transfers between devices  14 us (24%)
  starting transfers between devices  10.9 us (19%)
  blocking collectives  10.5 us (18%)
    pallas_call x13, Pallas kernels, call(): pl.pallas_call(body, out_shape=shapes, in_specs=[far if i in in_hbm else...  22.3 us
    ppermute x1, waiting for transfers between devices, body(): far = lax.ppermute(low, 'gz', [(2, 0)])  13.3 us
    all_gather x2, blocking collectives, exchange(): return (lax.all_gather(x_side, 'gx'), *rows)  10.5 us
    ppermute x2, starting transfers between devices, exchange(): rows = [lax.ppermute(y_side[0], 'gy', [(0, 1), (1, 0)])]  3.1 us
    ppermute x1, starting transfers between devices, body(): first = lax.ppermute(top, 'gz', [(0, 1)])  1.3 us
    ppermute x1, starting transfers between devices, body(): down_there = lax.ppermute(down_one, 'gz', [(1, 0)])  1.29 us
    ppermute x1, starting transfers between devices, body(): far = lax.ppermute(low, 'gz', [(2, 0)])  1.29 us
    ppermute x1, starting transfers between devices, body(): near = lax.ppermute(low, 'gz', [(2, 1), (1, 0)])  1.29 us
  transfers between devices with their start and end apart: 10, of which 2 were waited for; matrix products, arithmetic and copies ran while one was open for 0% of the time, Pallas kernels for 33%

profile of v12, /device:TPU:0, one launch (start us, length us, event | category | flops | bytes accessed | tf_op | source)
XLA Modules:
  0.0 57.8 jit_solution(8012064946289114916)
XLA Ops:
  0.0 1.7 %shard_map.46 = (f32[10,6,16,256]{3,2,1,0:T(8,128)S(1)}, bf16[10,6,6,16,256]{4,3,2,1,0:T(8,128)(2,1)S(1)}, bf16[10,6,6,16,256]{4,3,2,1,0:T(8,128)(2,1)S(1)}, f32...) custom-call(f32[10,6,16,256]{3,2,1,0:T(8,128)} %bitcast.22, ...), custom_call_target="tpu_custom_call" | custom-call | bytes 19660800 | tf_op jit(solution)/shard_map/pallas_call | solution.py:22
  1.7 0.7 %collective-permute-start.3 = (f32[6,6,16,256]{3,2,1,0:T(8,128)S(1)}, f32[6,6,16,256]{3,2,1,0:T(8,128)S(1)}, u32[]{:S(2)}, u32[]{:S(2)}) collective-permute-start(f32[6,6,16,256]{3,2,1,0:T(8,128)S(1)} %get-tuple-element.47), channel_id=1, source_target_pairs={{16,24},{17,25},{18,26},{19,27},{20,28},{21,29},{22,30},{23,31}} | collective-permute-start | bytes 1769480 | tf_op jit(solution)/shard_map/ppermute | solution.py:617
  2.5 3.0 %collective-permute-start = (f32[10,6,256]{2,1,0:T(8,128)S(1)}, f32[10,6,256]{2,1,0:T(8,128)S(1)}, u32[]{:S(2)}, u32[]{:S(2)}) collective-permute-start(f32[10,6,256]{2,1,0:T(8,128)S(1)} %bitcast.14), channel_id=1, source_target_pairs={{0,1},{1,0},{2,3},{3,2},{4,5},{5,4},{6,7},{7,6},{8,9},{9,8},{10,11... | collective-permute-start | bytes 184328 | tf_op jit(solution)/shard_map/ppermute | solution.py:178
  5.5 5.2 %all-gather = f32[8,1,16,128]{3,2,1,0:T(8,128)S(1)} all-gather(f32[2,1,16,128]{3,2,1,0:T(8,128)S(1)} %get-tuple-element.38), channel_id=2, replica_groups=mesh['gz'=4,'gx'=4,'gy'=2] {'gx'}, dimensions={0}, use_global_device_ids=true | all-gather | bytes 81920 | tf_op jit(solution)/shard_map/all_gather | solution.py:185
  10.7 0.0 collective-permute-done.rest_0_.refs_6_
  10.7 7.0 %shard_map.47 = (f32[10,6,16,256]{3,2,1,0:T(8,128)S(1)}, f32[6,16,256]{2,1,0:T(8,128)S(1)}, bf16[10,4,6,6,16,256]{5,4,3,2,1,0:T(8,128)(2,1)S(1)}, bf16[10,6,6,16...) custom-call(f32[10,6,16,256]{3,2,1,0:T(8,128)} %bitcast.20, ...), custom_call_target="tpu_custom_call", output_to_operand_aliasing={{3}: (3, {}), {4}: (4, {})} | custom-call | bytes 204800 | tf_op jit(solution)/shard_map/pallas_call | solution.py:22
  17.7 1.3 %collective-permute-start.1 = (f32[6,16,256]{2,1,0:T(8,128)S(1)}, f32[6,16,256]{2,1,0:T(8,128)S(1)}, u32[]{:S(2)}, u32[]{:S(2)}) collective-permute-start(f32[6,16,256]{2,1,0:T(8,128)S(1)} %get-tuple-element.43.refs_8_), channel_id=1, source_target_pairs={{0,8},{1,9},{2,10},{3,11},{4,12},{5,13},{6,14},{7,15}} | collective-permute-start | bytes 294920 | tf_op jit(solution)/shard_map/ppermute | solution.py:634
  19.0 2.2 %shard_map.48 = (f32[10,6,16,256]{3,2,1,0:T(8,128)S(1)}, f32[6,16,256]{2,1,0:T(8,128)S(1)}, bf16[10,4,6,6,16,256]{5,4,3,2,1,0:T(8,128)(2,1)S(1)}, bf16[10,6,6,16,256]{4,3,2,1,0:T(8,128)(2,1)S(1)}) custom-call(f32[10,6,16,256]{3,2,1,0:T(8,128)} %bitcast.21, bf16[10,6,6,6,16,256]{5,4,3,2,1,0:T(8,128)(2,1)} %bitcast.17, ...), custom_call_target="tpu_custom_call", output_to_operand_aliasing={{0}: (7, {}), {2}: (9, {})} | custom-call | bytes 204800 | tf_op jit(solution)/shard_map/pallas_call | solution.py:22
  21.3 0.6 %collective-permute-done.1.came_ref.rest_0_ = f32[6,16,256]{2,1,0:T(8,128)S(1)} collective-permute-done((f32[6,16,256]{2,1,0:T(8,128)S(1)}, f32[6,16,256]{2,1,0:T(8,128)S(1)}, u32[]{:S(2)}, u32[]{:S(2)}) %collective-permute-start.1) | collective-permute-done | bytes 98336 | tf_op jit(solution)/shard_map/ppermute | solution.py:634
  21.9 0.7 %collective-permute-start.2 = (f32[6,16,256]{2,1,0:T(8,128)S(1)}, f32[6,16,256]{2,1,0:T(8,128)S(1)}, u32[]{:S(2)}, u32[]{:S(2)}) collective-permute-start(f32[6,16,256]{2,1,0:T(8,128)S(1)} %shard_map.49), channel_id=1, source_target_pairs={{8,24},{9,25},{10,26},{11,27},{12,28},{13,29},{14,30},{15,31}} | collective-permute-start | bytes 294920 | tf_op jit(solution)/shard_map/ppermute | solution.py:657
  22.5 0.7 %collective-permute-start.4 = (f32[6,16,256]{2,1,0:T(8,128)S(1)}, f32[6,16,256]{2,1,0:T(8,128)S(1)}, u32[]{:S(2)}, u32[]{:S(2)}) collective-permute-start(f32[6,16,256]{2,1,0:T(8,128)S(1)} %shard_map.49), channel_id=1, source_target_pairs={{8,16},{16,24},{9,17},{17,25},{10,18},{18,26},{11,19},{19,27},{12,... | collective-permute-start | bytes 294920 | tf_op jit(solution)/shard_map/ppermute | solution.py:658
  23.2 0.0 collective-permute-done.3._.rest_2_
  23.2 0.1 shard_map.50
  23.3 0.0 collective-permute-done.2.rest_1_.refs_2_
  23.3 0.0 collective-permute-done.4.rest_3_.refs_1_
  23.3 1.3 %collective-permute-start.8 = (f32[6,6,16,256]{3,2,1,0:T(8,128)S(1)}, f32[6,6,16,256]{3,2,1,0:T(8,128)S(1)}, u32[]{:S(2)}, u32[]{:S(2)}) collective-permute-start(f32[6,6,16,256]{3,2,1,0:T(8,128)S(1)} %shard_map.56), channel_id=1, source_target_pairs={{8,0},{9,1},{10,2},{11,3},{12,4},{13,5},{14,6},{15,7}} | collective-permute-start | bytes 1769480 | tf_op jit(solution)/shard_map/ppermute | solution.py:672
  24.6 1.6 %shard_map.51 = (f32[10,6,16,256]{3,2,1,0:T(8,128)S(1)}, f32[10,6,16,256]{3,2,1,0:T(8,128)S(1)}, f32[2,1,16,128]{3,2,1,0:T(8,128)S(1)}, f32[1,10,6,256]{3,2,1,0:T(8,128)S(1)}) custom-call(f32[10,6,16,256]{3,2,1,0:T(8,128)S(1)} %get-tuple-element.45.source_ref, f32[10,6,16,256]{3,2,1,0:T(8,128)S(1)} %get-tuple-element.35.prev_ref.refs_2_, ...), custom_call_target="tpu_custom_call" | custom-call | bytes 6553600 | tf_op jit(solution)/shard_map/pallas_call | solution.py:22
  26.2 0.1 collective-permute-start.5
  26.3 5.2 %all-gather.1 = f32[8,1,16,128]{3,2,1,0:T(8,128)S(1)} all-gather(f32[2,1,16,128]{3,2,1,0:T(8,128)S(1)} %get-tuple-element.54), channel_id=3, replica_groups=mesh['gz'=4,'gx'=4,'gy'=2] {'gx'}, dimensions={0}, use_global_device_ids=true | all-gather | bytes 81920 | tf_op jit(solution)/shard_map/all_gather | solution.py:185
  31.5 0.0 collective-permute-done.5.rest_0_.refs_6_
  31.5 0.7 %collective-permute-start.6 = (f32[6,16,256]{2,1,0:T(8,128)S(1)}, f32[6,16,256]{2,1,0:T(8,128)S(1)}, u32[]{:S(2)}, u32[]{:S(2)}) collective-permute-start(f32[6,16,256]{2,1,0:T(8,128)S(1)} %get-tuple-element.57.refs_8_), channel_id=1, source_target_pairs={{24,16},{25,17},{26,18},{27,19},{28,20},{29,21},{30,22},{31,23}} | collective-permute-start | bytes 294920 | tf_op jit(solution)/shard_map/ppermute | solution.py:718
  32.2 4.9 %shard_map.53 = (f32[10,6,16,256]{3,2,1,0:T(8,128)S(1)}, f32[6,16,256]{2,1,0:T(8,128)S(1)}) custom-call(f32[10,6,16,256]{3,2,1,0:T(8,128)S(1)} %get-tuple-element.51.sweep_ref.refs_0_.refs_2_, f32[10,6,16,256]{3,2,1,0:T(8,128)S(1)} %get-tuple-element.52.change_ref.refs_1_, ...), custom_call_target="tpu_custom_call", output_to_operand_aliasing={{0}: (7, {})} | custom-call | bytes 204800 | tf_op jit(solution)/shard_map/pallas_call | solution.py:22
  37.1 3.4 %shard_map.54 = (f32[10,6,6,16,256]{4,3,2,1,0:T(8,128)S(1)}, f32[10,6,16,256]{3,2,1,0:T(8,128)S(1)}) custom-call(bf16[10,6,6,16,256]{4,3,2,1,0:T(8,128)(2,1)S(1)} %get-tuple-element.40.refs_3_.inv_ref.refs_2_.refs_0_, bf16[10,6,6,16,256]{4,3,2,1,0:T(8,128)(2,1)S(1)} %get-tuple-element.48.high_jac.refs_4_.refs_1_, ...), custom_call_target="tpu_custom_call" | custom-call | bytes 204800 | tf_op jit(solution)/shard_map/pallas_call | solution.py:22
  40.5 0.0 collective-permute-done.6.came_ref.rest_0_
  40.6 1.3 %collective-permute-start.7 = (f32[6,16,256]{2,1,0:T(8,128)S(1)}, f32[6,16,256]{2,1,0:T(8,128)S(1)}, u32[]{:S(2)}, u32[]{:S(2)}) collective-permute-start(f32[6,16,256]{2,1,0:T(8,128)S(1)} %shard_map.55.___), channel_id=1, source_target_pairs={{16,0},{17,1},{18,2},{19,3},{20,4},{21,5},{22,6},{23,7}} | collective-permute-start | bytes 294920 | tf_op jit(solution)/shard_map/ppermute | solution.py:729
  41.9 1.3 %collective-permute-start.9 = (f32[6,16,256]{2,1,0:T(8,128)S(1)}, f32[6,16,256]{2,1,0:T(8,128)S(1)}, u32[]{:S(2)}, u32[]{:S(2)}) collective-permute-start(f32[6,16,256]{2,1,0:T(8,128)S(1)} %shard_map.55.___), channel_id=1, source_target_pairs={{16,8},{8,0},{17,9},{9,1},{18,10},{10,2},{19,11},{11,3},{20,12},{1... | collective-permute-start | bytes 294920 | tf_op jit(solution)/shard_map/ppermute | solution.py:730
  43.2 13.3 %collective-permute-done.7.rest_1_ = f32[6,16,256]{2,1,0:T(8,128)S(1)} collective-permute-done((f32[6,16,256]{2,1,0:T(8,128)S(1)}, f32[6,16,256]{2,1,0:T(8,128)S(1)}, u32[]{:S(2)}, u32[]{:S(2)}) %collective-permute-start.7) | collective-permute-done | bytes 98336 | tf_op jit(solution)/shard_map/ppermute | solution.py:729
  56.5 0.0 collective-permute-done.9.rest_3_
  56.5 0.0 collective-permute-done.8.rest_2_
  56.5 1.3 %shard_map.58 = f32[10,6,16,256]{3,2,1,0:T(8,128)} custom-call(f32[10,6,16,256]{3,2,1,0:T(8,128)S(1)} %get-tuple-element.51.sweep_ref.refs_0_.refs_2_, f32[10,6,16,256]{3,2,1,0:T(8,128)S(1)} %get-tuple-element.58.refs_3_.inner_ref, bf16[10,6,6,16,256]{4,3,2,1,0:T(8,128)(2,1)S(1)} %get-tuple-element.40.refs_3_.inv_ref.refs_2_.refs_0_, ...), custom_call_target="tpu_custom_call" | custom-call | bytes 8192000 | tf_op jit(solution)/shard_map/pallas_call | solution.py:22
  (5 shorter events, 0.1 us)
Async XLA Ops:
  1.7 21.5 %collective-permute-start.3 = (f32[6,6,16,256]{3,2,1,0:T(8,128)S(1)}, f32[6,6,16,256]{3,2,1,0:T(8,128)S(1)}, u32[]{:S(2)}, u32[]{:S(2)}) collective-permute-start(f32[6,6,16,256]{3,2,1,0:T(8,128)S(1)} %get-tuple-element.47), channel_id=1, source_target_pairs={{16,24},{17,25},{18,26},{19,27},{20,28},{21,29},{22,30},{23,31}} | collective-permute-start | bytes 1769480 | tf_op jit(solution)/shard_map/ppermute | solution.py:617
  2.5 8.2 %collective-permute-start = (f32[10,6,256]{2,1,0:T(8,128)S(1)}, f32[10,6,256]{2,1,0:T(8,128)S(1)}, u32[]{:S(2)}, u32[]{:S(2)}) collective-permute-start(f32[10,6,256]{2,1,0:T(8,128)S(1)} %bitcast.14), channel_id=1, source_target_pairs={{0,1},{1,0},{2,3},{3,2},{4,5},{5,4},{6,7},{7,6},{8,9},{9,8},{10,11... | collective-permute-start | bytes 184328 | tf_op jit(solution)/shard_map/ppermute | solution.py:178
  17.7 4.1 %collective-permute-start.1 = (f32[6,16,256]{2,1,0:T(8,128)S(1)}, f32[6,16,256]{2,1,0:T(8,128)S(1)}, u32[]{:S(2)}, u32[]{:S(2)}) collective-permute-start(f32[6,16,256]{2,1,0:T(8,128)S(1)} %get-tuple-element.43.refs_8_), channel_id=1, source_target_pairs={{0,8},{1,9},{2,10},{3,11},{4,12},{5,13},{6,14},{7,15}} | collective-permute-start | bytes 294920 | tf_op jit(solution)/shard_map/ppermute | solution.py:634
  21.9 1.4 %collective-permute-start.2 = (f32[6,16,256]{2,1,0:T(8,128)S(1)}, f32[6,16,256]{2,1,0:T(8,128)S(1)}, u32[]{:S(2)}, u32[]{:S(2)}) collective-permute-start(f32[6,16,256]{2,1,0:T(8,128)S(1)} %shard_map.49), channel_id=1, source_target_pairs={{8,24},{9,25},{10,26},{11,27},{12,28},{13,29},{14,30},{15,31}} | collective-permute-start | bytes 294920 | tf_op jit(solution)/shard_map/ppermute | solution.py:657
  22.5 0.8 %collective-permute-start.4 = (f32[6,16,256]{2,1,0:T(8,128)S(1)}, f32[6,16,256]{2,1,0:T(8,128)S(1)}, u32[]{:S(2)}, u32[]{:S(2)}) collective-permute-start(f32[6,16,256]{2,1,0:T(8,128)S(1)} %shard_map.49), channel_id=1, source_target_pairs={{8,16},{16,24},{9,17},{17,25},{10,18},{18,26},{11,19},{19,27},{12,... | collective-permute-start | bytes 294920 | tf_op jit(solution)/shard_map/ppermute | solution.py:658
  23.3 33.2 %collective-permute-start.8 = (f32[6,6,16,256]{3,2,1,0:T(8,128)S(1)}, f32[6,6,16,256]{3,2,1,0:T(8,128)S(1)}, u32[]{:S(2)}, u32[]{:S(2)}) collective-permute-start(f32[6,6,16,256]{3,2,1,0:T(8,128)S(1)} %shard_map.56), channel_id=1, source_target_pairs={{8,0},{9,1},{10,2},{11,3},{12,4},{13,5},{14,6},{15,7}} | collective-permute-start | bytes 1769480 | tf_op jit(solution)/shard_map/ppermute | solution.py:672
  26.2 5.3 %collective-permute-start.5 = (f32[10,6,256]{2,1,0:T(8,128)S(1)}, f32[10,6,256]{2,1,0:T(8,128)S(1)}, u32[]{:S(2)}, u32[]{:S(2)}) collective-permute-start(f32[10,6,256]{2,1,0:T(8,128)S(1)} %bitcast.13), channel_id=1, source_target_pairs={{0,1},{1,0},{2,3},{3,2},{4,5},{5,4},{6,7},{7,6},{8,9},{9,8},{10,11... | collective-permute-start | bytes 184328 | tf_op jit(solution)/shard_map/ppermute | solution.py:178
  31.5 9.0 %collective-permute-start.6 = (f32[6,16,256]{2,1,0:T(8,128)S(1)}, f32[6,16,256]{2,1,0:T(8,128)S(1)}, u32[]{:S(2)}, u32[]{:S(2)}) collective-permute-start(f32[6,16,256]{2,1,0:T(8,128)S(1)} %get-tuple-element.57.refs_8_), channel_id=1, source_target_pairs={{24,16},{25,17},{26,18},{27,19},{28,20},{29,21},{30,22},{31,23}} | collective-permute-start | bytes 294920 | tf_op jit(solution)/shard_map/ppermute | solution.py:718
  40.6 16.0 %collective-permute-start.7 = (f32[6,16,256]{2,1,0:T(8,128)S(1)}, f32[6,16,256]{2,1,0:T(8,128)S(1)}, u32[]{:S(2)}, u32[]{:S(2)}) collective-permute-start(f32[6,16,256]{2,1,0:T(8,128)S(1)} %shard_map.55.___), channel_id=1, source_target_pairs={{16,0},{17,1},{18,2},{19,3},{20,4},{21,5},{22,6},{23,7}} | collective-permute-start | bytes 294920 | tf_op jit(solution)/shard_map/ppermute | solution.py:729
  41.9 14.7 %collective-permute-start.9 = (f32[6,16,256]{2,1,0:T(8,128)S(1)}, f32[6,16,256]{2,1,0:T(8,128)S(1)}, u32[]{:S(2)}, u32[]{:S(2)}) collective-permute-start(f32[6,16,256]{2,1,0:T(8,128)S(1)} %shard_map.55.___), channel_id=1, source_target_pairs={{16,8},{8,0},{17,9},{9,1},{18,10},{10,2},{19,11},{11,3},{20,12},{1... | collective-permute-start | bytes 294920 | tf_op jit(solution)/shard_map/ppermute | solution.py:730
